TPU v7x, 32 devices: a whole 2x2x4 slice. The times are simulated.
32 devices in a mesh: brow: 8 (over y, x, core), bcol: 4 (over z).
Axes of the slice: x: 2, y: 2, z: 4, core: 2. Of those that a mesh axis runs over, the one named last changes fastest.
Arguments:
- vectors: bfloat16 [8, 65536], P(None, ('brow', 'bcol')), may hold values from -6 to 6
- tiles: bfloat16 [6144, 4096], P(('brow', 'bcol')), may hold values from -0.29882812 to 0.29882812
- tile_rows: int32 [6144], P(('brow', 'bcol')), may hold values from 0 to 127
- tile_cols: int32 [6144], P(('brow', 'bcol')), may hold values from 0 to 255
- counts: int32 [8, 4], P('brow', 'bcol'), may hold values from 64 to 192, as said below
Outputs:
- product: float32 [8, 65536], P(None, ('brow', 'bcol'))
Inputs may be any that keep to these rules, and one draw needn't show every extreme that they name: `counts`: some grid block uses all 192 slots in every draw; every block uses at least a third of them.
All inputs are finite; a program needn't handle non-finite values.
Results may differ from a plain program's by a relative error of at most 0.0003.
Values may be sent and summed in bfloat16 or wider, within the bound.
No kernel may reach another device: no remote copies, remote signals or barrier semaphores. Data moves between devices by JAX's collectives and lax.ppermute only.
A program may use at most 64 MiB of HBM per device.

v0:
```python
import jax
import jax.numpy as jnp
from jax import lax
from jax.sharding import PartitionSpec as P

TILE = 64


def body(vectors, tiles, tile_rows, tile_cols, counts):
    width = vectors.shape[0]
    piece = vectors.shape[1]
    slots = tiles.shape[0]
    side = TILE
    n_rows_axis = lax.axis_size("brow")
    n_cols_axis = lax.axis_size("bcol")
    row_tiles = piece * n_cols_axis // side
    col_tiles = piece * n_rows_axis // side
    live = (jnp.arange(slots, dtype=jnp.int32) < counts[0, 0]).astype(jnp.bfloat16)
    row_hot = (tile_rows[:, None] == jnp.arange(row_tiles, dtype=jnp.int32)[None, :]).astype(
        jnp.bfloat16
    ) * live[:, None]
    col_hot = (tile_cols[:, None] == jnp.arange(col_tiles, dtype=jnp.int32)[None, :]).astype(
        jnp.bfloat16
    ) * live[:, None]
    row_hot_wide = row_hot.astype(jnp.float32)
    col_hot_wide = col_hot.astype(jnp.float32)
    blocks = tiles.reshape(slots, side, side)
    col_seg = lax.all_gather(vectors, "brow", axis=1, tiled=True).reshape(width, col_tiles, side)
    at_cols = jnp.einsum(
        "tc,kcj->tkj", col_hot, col_seg, preferred_element_type=jnp.float32
    ).astype(jnp.bfloat16)
    forward = jnp.einsum("tkj,tij->tki", at_cols, blocks, preferred_element_type=jnp.float32)
    partial_rows = jnp.einsum("tr,tki->kri", row_hot_wide, forward, precision=lax.Precision.HIGHEST)
    partial_rows = partial_rows.reshape(width, row_tiles * side)
    from_rows = lax.psum_scatter(partial_rows, "bcol", scatter_dimension=1, tiled=True)
    row_seg = lax.all_gather(vectors, "bcol", axis=1, tiled=True).reshape(width, row_tiles, side)
    at_rows = jnp.einsum(
        "tr,kri->tki", row_hot, row_seg, preferred_element_type=jnp.float32
    ).astype(jnp.bfloat16)
    backward = jnp.einsum("tki,tij->tkj", at_rows, blocks, preferred_element_type=jnp.float32)
    partial_cols = jnp.einsum(
        "tc,tkj->kcj", col_hot_wide, backward, precision=lax.Precision.HIGHEST
    )
    partial_cols = partial_cols.reshape(width, col_tiles * side)
    from_cols = lax.psum_scatter(partial_cols, "brow", scatter_dimension=1, tiled=True)
    return from_rows + from_cols


def solution(mesh):
    return jax.shard_map(
        body,
        mesh=mesh,
        in_specs=(
            P(None, ("brow", "bcol")),
            P(("brow", "bcol"), None),
            P(("brow", "bcol")),
            P(("brow", "bcol")),
            P("brow", "bcol"),
        ),
        out_specs=P(None, ("brow", "bcol")),
        check_vma=False,
    )
```

profile of v0, /device:TPU:0, one launch (start us, length us, event | category | flops | bytes accessed | tf_op | source)
XLA Modules:
  0.0 101.0 jit_solution(13899705732351727752)
XLA Ops:
  6.5 0.0 reduce-scatter.3.cloned.1.call-start
  7.2 3.8 %copy.6 = bf16[192,4096]{0,1:T(8,128)(2,1)} copy(bf16[192,4096]{1,0:T(8,128)(2,1)} %param.6) | data formatting | bytes 3145728 | tf_op args[1]
  11.0 0.0 copy-start
  11.0 0.0 copy-start.2
  11.0 4.2 %copy.13 = bf16[192,64,64]{2,1,0:T(8,128)(2,1)S(1)} copy(bf16[192,64,64]{0,2,1:T(8,128)(2,1)} %bitcast.21) | data formatting | bytes 3145728 | tf_op jit(solution)/shard_map/reshape | solution.py:27
  15.3 0.0 copy-done
  15.3 10.8 %all_gather.6 = bf16[8,16384]{1,0:T(8,128)(2,1)S(1)} all-gather(bf16[8,2048]{1,0:T(8,128)(2,1)S(1)} %copy-done), channel_id=1, replica_groups=mesh['brow'=8,'bcol'=4] {'brow'}, dimensions={1}, use_global_device_ids=true | all-gather | bytes 294912 | tf_op jit(solution)/shard_map/all_gather | solution.py:28
  26.1 0.0 copy-start.1
  26.1 1.3 %reshape.22 = bf16[8,256,64]{2,1,0:T(8,128)(2,1)} reshape(bf16[8,16384]{1,0:T(8,128)(2,1)S(1)} %all_gather.6) | data formatting | bytes 524288 | tf_op jit(solution)/shard_map/reshape | solution.py:28
  27.4 0.0 copy-done.2
  27.4 2.1 %fusion.9 = bf16[192,8,64]{0,2,1:T(8,128)(2,1)} fusion(bf16[8,256,64]{2,1,0:T(8,128)(2,1)} %reshape.22, s32[192]{0:T(256)S(1)} %copy-done.2, bf16[192]{0:T(256)(128)(2,1)S(1)} %compare_convert_fusion), kind=kOutput, calls=%fused_computation.11 | convolution fusion | flops 50429952 | bytes 459904 | tf_op jit(solution)/shard_map/tc,kcj->tkj/dot_general | solution.py:29
  29.5 1.2 %copy.9 = bf16[192,8,64]{2,1,0:T(8,128)(2,1)S(1)} copy(bf16[192,8,64]{0,2,1:T(8,128)(2,1)} %fusion.9) | data formatting | bytes 393216 | tf_op jit(solution)/shard_map/tc,kcj->tkj/dot_general | solution.py:29
  30.7 1.7 %fusion.33 = f32[192,8,64]{2,1,0:T(8,128)S(1)} fusion(bf16[192,8,64]{2,1,0:T(8,128)(2,1)S(1)} %copy.9, bf16[192,64,64]{2,1,0:T(8,128)(2,1)S(1)} %copy.13), kind=kOutput, calls=%fused_computation.34 | convolution fusion | flops 12582912 | bytes 2162688 | tf_op jit(solution)/shard_map/tkj,tij->tki/dot_general | solution.py:32
  32.4 0.0 copy-done.1
  32.4 0.9 convolution_bitcast_fusion.1
  33.4 1.0 copy.7
  34.4 1.9 %reshape.24 = f32[8,8192]{1,0:T(8,128)} reshape(f32[8,128,64]{2,1,0:T(8,128)} %copy.7) | data formatting | bytes 524288 | tf_op jit(solution)/shard_map/reshape | solution.py:34
  36.3 0.0 reduce-scatter.3.cloned.1.call-update
  36.3 0.0 reduce-scatter.5.cloned.1.call-start
  36.4 14.1 %all_gather.7 = bf16[8,8192]{1,0:T(8,128)(2,1)S(1)} all-gather(bf16[8,2048]{1,0:T(8,128)(2,1)} %param.5), channel_id=1, replica_groups=mesh['brow'=8,'bcol'=4] {'bcol'}, dimensions={1}, use_global_device_ids=true | all-gather | bytes 163840 | tf_op jit(solution)/shard_map/all_gather | solution.py:36
  50.5 0.2 reshape.25
  50.7 1.0 %fusion.15 = bf16[192,8,64]{0,2,1:T(8,128)(2,1)} fusion(bf16[8,128,64]{2,1,0:T(8,128)(2,1)S(1)} %reshape.25, s32[192]{0:T(256)S(1)} %copy-done.1, bf16[192]{0:T(256)(128)(2,1)S(1)} %compare_convert_fusion), kind=kOutput, calls=%fused_computation.17 | convolution fusion | flops 25214976 | bytes 328832 | tf_op jit(solution)/shard_map/tr,kri->tki/dot_general | solution.py:37
  51.8 1.2 %copy.12 = bf16[192,8,64]{2,1,0:T(8,128)(2,1)S(1)} copy(bf16[192,8,64]{0,2,1:T(8,128)(2,1)} %fusion.15) | data formatting | bytes 393216 | tf_op jit(solution)/shard_map/tr,kri->tki/dot_general | solution.py:37
  53.0 0.9 fusion.32
  53.9 0.9 convolution_bitcast_fusion
  54.8 0.3 copy.8
  55.1 1.2 %reshape.26 = f32[8,16384]{1,0:T(8,128)} reshape(f32[8,256,64]{2,1,0:T(8,128)S(1)} %copy.8) | data formatting | bytes 1048576 | tf_op jit(solution)/shard_map/reshape | solution.py:44
  56.3 0.0 reduce-scatter.5.cloned.1.call-update
  56.3 0.8 reduce-scatter.3.cloned.1.call-done
  57.1 35.6 %reduce-scatter.5.cloned.1.call-done = f32[8,2048]{1,0:T(8,128)} async-done(((f32[8,16384]{1,0:T(8,128)}), f32[8,2048]{1,0:T(8,128)}) %reduce-scatter.5.cloned.1.call-update) | async-done | bytes 65552 | tf_op jit(solution)/shard_map/reduce_scatter | solution.py:45
  92.6 1.5 %add.7 = f32[8,2048]{1,0:T(8,128)} add(f32[8,2048]{1,0:T(8,128)} %reduce-scatter.3.cloned.1.call-done, f32[8,2048]{1,0:T(8,128)} %reduce-scatter.5.cloned.1.call-done) | non-fusion elementwise | flops 16384 | bytes 196608 | tf_op jit(solution)/shard_map/add | solution.py:46
  (1 shorter events, 0.0 us)
Async XLA Ops:
  6.5 50.5 %reduce-scatter.3.cloned.1.call-start = ((), (), s32[]{:S(2)}) async-start(), calls=%async_computation.2 | async-start | bytes 327680 | tf_op jit(solution)/shard_map/reduce_scatter | solution.py:35
  11.0 4.2 %copy-start = (bf16[8,2048]{1,0:T(8,128)(2,1)S(1)}, bf16[8,2048]{1,0:T(8,128)(2,1)}, u32[]{:S(2)}) copy-start(bf16[8,2048]{1,0:T(8,128)(2,1)} %param.5) | copy-start | bytes 98308
  11.0 16.4 %copy-start.2 = (s32[192]{0:T(256)S(1)}, s32[192]{0:T(256)}, u32[]{:S(2)}) copy-start(s32[192]{0:T(256)} %param.8) | copy-start | bytes 2308
  26.1 6.4 %copy-start.1 = (s32[192]{0:T(256)S(1)}, s32[192]{0:T(256)}, u32[]{:S(2)}) copy-start(s32[192]{0:T(256)} %param.7) | copy-start | bytes 2308
  36.3 56.3 %reduce-scatter.5.cloned.1.call-start = ((), (), s32[]{:S(2)}) async-start(), calls=%async_computation.3 | async-start | bytes 589824 | tf_op jit(solution)/shard_map/reduce_scatter | solution.py:45
Sparse Core Ops, SparseCore 0:
  36.4 20.6 reduce-scatter.2
  60.5 32.1 reduce-scatter.4
where the time goes:
time: 101 us
  waiting for transfers between devices  36.4 us (36%)
  blocking collectives  24.9 us (25%)
  local copies, waits for them, and re-layouts  16.4 us (16%)
  between operations  14.1 us (14%)
  matrix products  7.63 us (8%)
  other arithmetic  1.51 us (1%)
    reduce_scatter x1, waiting for transfers between devices, body(): lax.psum_scatter(partial_cols, 'brow', scatter_dimension=1, tiled=True)  35.6 us
    all_gather x1, blocking collectives, body(): lax.all_gather(vectors, 'bcol', axis=1, tiled=True)  14.1 us
    all_gather x1, blocking collectives, body(): lax.all_gather(vectors, 'brow', axis=1, tiled=True)  10.8 us
    reshape x1, local copies, waits for them, and re-layouts, body(): blocks = tiles.reshape(slots, side, side)  4.23 us
    unnamed x7, local copies, waits for them, and re-layouts  3.85 us
    dot_general x1, matrix products, body(): jnp.einsum('tc,kcj->tkj', col_hot, col_seg, preferred_element_type=jnp.fl...  2.13 us
  transfers between devices with their start and end apart: 2, of which 2 were waited for; matrix products, arithmetic and copies ran while one was open for 6% of the time, Pallas kernels for 0%

commit v1 on v0

v1 whole, which is shorter than its diff:
```python
import functools

import jax
import jax.numpy as jnp
import numpy as np
from jax import lax
from jax.experimental import pallas as pl
from jax.experimental.pallas import tpu as pltpu
from jax.sharding import PartitionSpec as P

TILE = 64
LANES = 128
HALF = TILE // 2
GROUP = LANES // HALF
F32 = jnp.float32
BF16 = jnp.bfloat16
VMEM = pl.BlockSpec(memory_space=pltpu.VMEM)
SMEM = pl.BlockSpec(memory_space=pltpu.SMEM)
PARAMS = pltpu.CompilerParams(vmem_limit_bytes=48 * 1024 * 1024)


def row_spread():
    out = np.zeros((LANES, 2, 2, GROUP, HALF), np.float32)
    for q in range(2):
        for e in range(2):
            for m in range(HALF):
                out[q * TILE + 2 * m + e, q, e, :, m] = 1
    return jnp.asarray(out.reshape(LANES, 4 * LANES), BF16)


def col_spread():
    out = np.zeros((LANES, 2, 2, 2, TILE), np.float32)
    for q in range(2):
        for e in range(2):
            for j in range(TILE):
                out[q * TILE + j, q, e, e, j] = 1
    return jnp.asarray(out.reshape(LANES, 4 * LANES), BF16)


def row_fold():
    return row_spread().T


def prep_kernel(tiles_ref, out_ref, wide):
    for b in range(tiles_ref.shape[0]):
        wide[b] = tiles_ref[b].astype(F32).reshape(HALF * 8, LANES)
        for s in range(8):
            out_ref[8 * b + s] = wide[b, pl.ds(s, HALF, stride=8), :].astype(BF16)


def prep(tiles):
    slots = tiles.shape[0]
    blocks = slots // 8
    steps = 4 if blocks % 4 == 0 else 1
    view = tiles.reshape(blocks, 8, HALF, LANES).swapaxes(1, 2)
    return pl.pallas_call(
        prep_kernel,
        grid=(steps,),
        in_specs=[pl.BlockSpec((blocks // steps, HALF, 8, LANES), lambda i: (i, 0, 0, 0))],
        out_specs=pl.BlockSpec((slots // steps, HALF, LANES), lambda i: (i, 0, 0)),
        out_shape=jax.ShapeDtypeStruct((slots, HALF, LANES), BF16),
        scratch_shapes=[pltpu.VMEM((blocks // steps, HALF * 8, LANES), F32)],
        compiler_params=PARAMS,
        cost_estimate=pl.CostEstimate(flops=0, bytes_accessed=8 * tiles.size, transcendentals=0),
        name="prep_tiles",
    )(view)


def build_table(piece_refs, spread, table):
    width, piece = piece_refs[0].shape
    pairs = piece // LANES
    for n, ref in enumerate(piece_refs):
        rows = jnp.concatenate([ref[:, p * LANES : (p + 1) * LANES] for p in range(pairs)], axis=0)
        wide = jnp.dot(rows, spread, preferred_element_type=F32)
        wide = wide.reshape(pairs, width, 4 * LANES)
        for q in range(2):
            both = jnp.concatenate(
                [wide[:, :, (2 * q + e) * LANES : (2 * q + e + 1) * LANES] for e in range(2)], axis=1
            ).astype(BF16)
            for p in range(pairs):
                table[n * 2 * pairs + 2 * p + q] = both[p]


def backward_kernel(n_in, n_out, rows_ref, cols_ref, count_ref, spread_ref, tiles_ref, *refs):
    pieces, (keep_ref, give_ref), (table, acc) = refs[:n_in], refs[n_in : n_in + 2], refs[n_in + 2 :]
    width, piece = pieces[0].shape
    per_piece = piece // TILE
    slots = tiles_ref.shape[0]
    build_table(pieces, spread_ref[...], table)
    acc[...] = jnp.zeros_like(acc)
    lane = lax.broadcasted_iota(jnp.int32, (2 * width, LANES), 1)
    masks = [(lane // HALF == s).astype(BF16) for s in range(GROUP)]
    low = lax.broadcasted_iota(jnp.int32, (width, LANES), 1) < TILE
    count = count_ref[0, 0]
    row_flip = lax.axis_index("bcol") * per_piece
    col_flip = lax.axis_index("brow") * per_piece
    spare = n_out * per_piece

    for g in range(slots // GROUP):
        at = [table[rows_ref[g * GROUP + s] ^ row_flip] * masks[s] for s in range(GROUP)]
        block = tiles_ref[g * GROUP : (g + 1) * GROUP].reshape(LANES, LANES)
        out = jnp.dot(jnp.concatenate(at, axis=0), block, preferred_element_type=F32)
        for s in range(GROUP):
            t = g * GROUP + s
            part = out[2 * width * s : 2 * width * (s + 1)]
            part = jnp.where(low, part[:width], part[width:])
            c = jnp.where(t < count, cols_ref[t] ^ col_flip, spare)
            acc[c] += part

    for n in range(n_out):
        dest = (keep_ref if n % 2 == 0 else give_ref).at[n // 2]
        for p in range(per_piece // 2):
            a = acc[n * per_piece + 2 * p]
            b = acc[n * per_piece + 2 * p + 1]
            dest[:, p * LANES : (p + 1) * LANES] = jnp.where(low, a, b) + pltpu.roll(
                jnp.where(low, b, a), TILE, 1
            )


def backward(row_pieces, tiles, tile_rows, tile_cols, counts, n_out):
    n_in = len(row_pieces)
    width, piece = row_pieces[0].shape
    per_piece = piece // TILE
    half = jax.ShapeDtypeStruct((n_out // 2, width, piece), F32)
    return pl.pallas_call(
        functools.partial(backward_kernel, n_in, n_out),
        in_specs=[SMEM] * 3 + [VMEM] * (2 + n_in),
        out_specs=[VMEM] * 2,
        out_shape=[half, half],
        scratch_shapes=[
            pltpu.VMEM((n_in * per_piece, 2 * width, LANES), BF16),
            pltpu.VMEM((n_out * per_piece + 1, width, LANES), F32),
        ],
        compiler_params=PARAMS,
        cost_estimate=pl.CostEstimate(
            flops=2 * tiles.size * 64, bytes_accessed=4 * tiles.size, transcendentals=0
        ),
        name="transpose_product",
    )(tile_rows, tile_cols, counts, row_spread(), tiles, *row_pieces)


def forward_kernel(n_in, n_out, rows_ref, cols_ref, count_ref, spread_ref, fold_ref, tiles_ref, *refs):
    pieces, outs, (table, acc) = refs[:n_in], refs[n_in : n_in + n_out], refs[n_in + n_out :]
    width, piece = pieces[0].shape
    per_piece = piece // TILE
    slots = tiles_ref.shape[0]
    build_table(pieces, spread_ref[...], table)
    acc[...] = jnp.zeros_like(acc)
    lane = lax.broadcasted_iota(jnp.int32, (2 * width, LANES), 1)
    masks = [lane // HALF == s for s in range(GROUP)]
    count = count_ref[0, 0]
    row_flip = lax.axis_index("bcol") * per_piece
    col_flip = lax.axis_index("brow") * per_piece
    spare = n_out * per_piece

    for g in range(slots // GROUP):
        at = [table[cols_ref[g * GROUP + s] ^ col_flip] for s in range(GROUP)]
        block = tiles_ref[g * GROUP : (g + 1) * GROUP].reshape(LANES, LANES)
        out = lax.dot_general(
            jnp.concatenate(at, axis=0),
            block,
            (((1,), (1,)), ((), ())),
            preferred_element_type=F32,
        )
        for s in range(GROUP):
            t = g * GROUP + s
            part = out[2 * width * s : 2 * width * (s + 1)]
            r = jnp.where(t < count, rows_ref[t] ^ row_flip, spare)
            acc[r] += jnp.where(masks[s], part, 0.0)

    fold = fold_ref[...]
    pairs = per_piece // 2
    for n in range(n_out):
        both = acc[n * per_piece : (n + 1) * per_piece].reshape(pairs, 4 * width, LANES)
        blocks = [
            both[:, x * width : (x + 1) * width, :].reshape(pairs * width, LANES) for x in range(4)
        ]
        wide = jnp.concatenate(blocks, axis=1)
        first = wide.astype(BF16)
        rest = (wide - first.astype(F32)).astype(BF16)
        out = jnp.dot(first, fold, preferred_element_type=F32)
        out = out + jnp.dot(rest, fold, preferred_element_type=F32)
        for p in range(pairs):
            outs[n][:, p * LANES : (p + 1) * LANES] = out[p * width : (p + 1) * width]


def forward(col_pieces, tiles, tile_rows, tile_cols, counts, n_out):
    n_in = len(col_pieces)
    width, piece = col_pieces[0].shape
    per_piece = piece // TILE
    return pl.pallas_call(
        functools.partial(forward_kernel, n_in, n_out),
        in_specs=[SMEM] * 3 + [VMEM] * (3 + n_in),
        out_specs=[VMEM] * n_out,
        out_shape=[jax.ShapeDtypeStruct((width, piece), F32)] * n_out,
        scratch_shapes=[
            pltpu.VMEM((n_in * per_piece, 2 * width, LANES), BF16),
            pltpu.VMEM((n_out * per_piece + 1, 2 * width, LANES), F32),
        ],
        compiler_params=PARAMS,
        cost_estimate=pl.CostEstimate(
            flops=2 * tiles.size * 64, bytes_accessed=4 * tiles.size, transcendentals=0
        ),
        name="forward_product",
    )(tile_rows, tile_cols, counts, col_spread(), row_fold(), tiles, *col_pieces)


def pair_sum_kernel(keep_ref, got_ref, *outs):
    for h, out in enumerate(outs):
        out[...] = keep_ref[h + 1] + got_ref[h + 1]


def pair_sum(keep, got):
    parts, width, piece = keep.shape
    return pl.pallas_call(
        pair_sum_kernel,
        in_specs=[VMEM] * 2,
        out_specs=[VMEM] * (parts - 1),
        out_shape=[jax.ShapeDtypeStruct((width, piece), F32)] * (parts - 1),
        compiler_params=PARAMS,
        name="core_pair_sum",
    )(keep, got)


def swap(x, axis, size, d):
    return lax.ppermute(x, axis, [(i, i ^ d) for i in range(size)])


def body(vectors, tiles, tile_rows, tile_cols, counts):
    n_rows = lax.axis_size("brow")
    n_cols = lax.axis_size("bcol")
    row_pieces = [vectors] + [swap(vectors, "bcol", n_cols, d) for d in range(1, n_cols)]
    same_core = [vectors] + [swap(vectors, "brow", n_rows, 2 * h) for h in range(1, n_rows // 2)]
    other_core = [swap(x, "brow", n_rows, 1) for x in same_core]
    col_pieces = [x for pair in zip(same_core, other_core) for x in pair]
    blocks = prep(tiles)

    keep, give = backward(row_pieces, blocks, tile_rows, tile_cols, counts, n_rows)
    got = swap(give, "brow", n_rows, 1)
    mine = forward(col_pieces, blocks, tile_rows, tile_cols, counts, n_cols)
    from_rows = [mine[0]] + [swap(mine[d], "bcol", n_cols, d) for d in range(1, n_cols)]
    sums = pair_sum(keep, got)
    from_cols = [keep[0], got[0]] + [swap(x, "brow", n_rows, 2 * (h + 1)) for h, x in enumerate(sums)]
    return sum(from_rows + from_cols)


def solution(mesh):
    return jax.shard_map(
        body,
        mesh=mesh,
        in_specs=(
            P(None, ("brow", "bcol")),
            P(("brow", "bcol"), None),
            P(("brow", "bcol")),
            P(("brow", "bcol")),
            P("brow", "bcol"),
        ),
        out_specs=P(None, ("brow", "bcol")),
        check_vma=False,
    )
```

time: 101 us -> 37.3 us (0.37)
  waiting for transfers between devices: 36.4 us -> 11.3 us
  blocking collectives: 24.9 us -> 0 us
  starting transfers between devices: 0.04 us -> 17.3 us
  local copies, waits for them, and re-layouts: 16.4 us -> 1.44 us
  between operations: 14.1 us -> 0.8 us
  matrix products: 7.63 us -> 0 us
  Pallas kernels: 0 us -> 5.47 us
    reduce_scatter x2 -> x0, waiting for transfers between devices: 36.3 us -> none  [the longest x1 35.6 us: body(): lax.psum_scatter(partial_cols, 'brow', scatter_dimension=1, tiled=True)]
    all_gather x2 -> x0, blocking collectives: 24.9 us -> none  [the longest x1 14.1 us: body(): lax.all_gather(vectors, 'bcol', axis=1, tiled=True)]
    ppermute x0 -> x17, starting transfers between devices: none -> 17.3 us  [swap(): return lax.ppermute(x, axis, [(i, i ^ d) for i in range(size)])]
    ppermute x0 -> x17, waiting for transfers between devices: none -> 11.3 us  [swap(): return lax.ppermute(x, axis, [(i, i ^ d) for i in range(size)])]
    reshape x5 -> x0, local copies, waits for them, and re-layouts: 8.87 us -> none  [the longest x1 4.23 us: body(): blocks = tiles.reshape(slots, side, side)]
    dot_general x6 -> x0, matrix products: 7.63 us -> none  [the longest x1 2.13 us: body(): jnp.einsum('tc,kcj->tkj', col_hot, col_seg, preferred_element_type=jnp.fl...]
    pallas_call x0 -> x4, Pallas kernels: none -> 5.47 us  [the longest x1 2.63 us: forward(): pl.pallas_call(functools.partial(forward_kernel, n_in, n_out), in_specs=[...]
    unnamed x7 -> x14, local copies, waits for them, and re-layouts: 3.85 us -> 1.44 us
  transfers between devices with their start and end apart: 2 -> 17, of which waited for: 2 -> 10; matrix products, arithmetic and copies ran while one was open for 6% -> 0% of each run, Pallas kernels for 0% -> 9%
where the time goes in v1:
time: 37.3 us; the launch traced here: 37 us
  starting transfers between devices  17.3 us (46%)
  waiting for transfers between devices  11.3 us (30%)
  Pallas kernels  5.47 us (15%)
  local copies, waits for them, and re-layouts  1.44 us (4%)
  between operations  0.8 us (2%)
  other arithmetic  0.67 us (2%)
    ppermute x17, starting transfers between devices, swap(): return lax.ppermute(x, axis, [(i, i ^ d) for i in range(size)])  17.3 us
    ppermute x17, waiting for transfers between devices, swap(): return lax.ppermute(x, axis, [(i, i ^ d) for i in range(size)])  11.3 us
    pallas_call x1, Pallas kernels, forward(): pl.pallas_call(functools.partial(forward_kernel, n_in, n_out), in_specs=[...  2.63 us
    pallas_call x1, Pallas kernels, backward(): pl.pallas_call(functools.partial(backward_kernel, n_in, n_out), in_specs=...  2.06 us
    unnamed x14, local copies, waits for them, and re-layouts  1.44 us
    pallas_call x1, Pallas kernels, prep(): pl.pallas_call(prep_kernel, grid=(steps,), in_specs=[pl.BlockSpec((blocks...  0.76 us
  transfers between devices with their start and end apart: 17, of which 10 were waited for; matrix products, arithmetic and copies ran while one was open for 0% of the time, Pallas kernels for 9%

profile of v1, /device:TPU:0, one launch (start us, length us, event | category | flops | bytes accessed | tf_op | source)
XLA Modules:
  0.0 37.0 jit_solution(6010815540122075330)
XLA Ops:
  0.0 3.0 %collective-permute-start.10 = (bf16[8,2048]{1,0:T(8,128)(2,1)}, bf16[8,2048]{1,0:T(8,128)(2,1)S(1)}, u32[]{:S(2)}, u32[]{:S(2)}) collective-permute-start(bf16[8,2048]{1,0:T(8,128)(2,1)} %refs_0_.3), channel_id=1, source_target_pairs={{0,1},{1,0},{2,3},{3,2},{4,5},{5,4},{6,7},{7,6},{8,9},{9,8},{10,11... | collective-permute-start | bytes 98312 | tf_op jit(solution)/shard_map/ppermute | solution.py:226
  3.0 2.6 %collective-permute-start.11 = (bf16[8,2048]{1,0:T(8,128)(2,1)}, bf16[8,2048]{1,0:T(8,128)(2,1)S(1)}, u32[]{:S(2)}, u32[]{:S(2)}) collective-permute-start(bf16[8,2048]{1,0:T(8,128)(2,1)} %refs_0_.3), channel_id=1, source_target_pairs={{0,2},{1,3},{2,0},{3,1},{4,6},{5,7},{6,4},{7,5},{8,10},{9,11},{10,... | collective-permute-start | bytes 98312 | tf_op jit(solution)/shard_map/ppermute | solution.py:226
  5.6 0.0 collective-permute-start.12
  5.6 1.4 %copy-done = bf16[192,4096]{1,0:T(8,128)(2,1)S(1)} copy-done((bf16[192,4096]{1,0:T(8,128)(2,1)S(1)}, bf16[192,4096]{1,0:T(8,128)(2,1)}, u32[]{:S(2)}) %copy-start) | copy-done | bytes 1572888
  7.0 0.8 %prep_tiles.1.tiles_ref = bf16[192,32,128]{2,1,0:T(8,128)(2,1)S(1)} custom-call(bf16[24,32,8,128]{3,2,1,0:T(8,128)(2,1)S(1)} %bitcast.17), custom_call_target="tpu_custom_call" | custom-call | bytes 6291456 | tf_op jit(solution)/shard_map/prep_tiles/pallas_call | solution.py:56
  7.8 0.0 copy-start.3
  7.8 0.0 copy-start.4
  8.5 0.0 collective-permute-done.10.refs_1_
  8.5 0.1 collective-permute-done.11.refs_2_
  8.6 2.9 %collective-permute-done.12.refs_3_ = bf16[8,2048]{1,0:T(8,128)(2,1)S(1)} collective-permute-done((bf16[8,2048]{1,0:T(8,128)(2,1)}, bf16[8,2048]{1,0:T(8,128)(2,1)S(1)}, u32[]{:S(2)}, u32[]{:S(2)}) %collective-permute-start.12) | collective-permute-done | bytes 32800 | tf_op jit(solution)/shard_map/ppermute | solution.py:226
  11.6 2.1 %transpose_product.1 = (f32[4,8,2048]{2,1,0:T(8,128)S(1)}, f32[4,8,2048]{2,1,0:T(8,128)S(1)}) custom-call(s32[192]{0:T(256)S(1)} %copy-done.5, s32[192]{0:T(256)S(1)} %copy-done.6, s32[1,1]{1,0:T(1,128)S(6)} %copy.9.count_ref, bf16[128,512]{1,0:T(8,128)(2,1)S(1)} %copy-done.2, bf16[192,32,128]{2,1,0:T(8,128)(2,1)S(1)} %prep_tiles.1.tiles_ref, ...), custom_call_target="tpu_custom_call" | custom-call | flops 100663296 | bytes 3145728 | tf_op jit(solution)/shard_map/transpose_product/pallas_call | solution.py:125
  13.6 0.1 collective-permute-start.13
  13.7 1.9 %collective-permute-start.1 = (bf16[8,2048]{1,0:T(8,128)(2,1)S(1)}, bf16[8,2048]{1,0:T(8,128)(2,1)S(1)}, u32[]{:S(2)}, u32[]{:S(2)}) collective-permute-start(bf16[8,2048]{1,0:T(8,128)(2,1)S(1)} %copy-done.1), channel_id=1, source_target_pairs={{0,8},{4,12},{8,0},{12,4},{16,24},{20,28},{24,16},{28,20},{1,9},{5... | collective-permute-start | bytes 98312 | tf_op jit(solution)/shard_map/ppermute | solution.py:226
  15.6 1.5 %collective-permute-start.3 = (bf16[8,2048]{1,0:T(8,128)(2,1)S(1)}, bf16[8,2048]{1,0:T(8,128)(2,1)S(1)}, u32[]{:S(2)}, u32[]{:S(2)}) collective-permute-start(bf16[8,2048]{1,0:T(8,128)(2,1)S(1)} %copy-done.1), channel_id=1, source_target_pairs={{0,16},{4,20},{8,24},{12,28},{16,0},{20,4},{24,8},{28,12},{1,17},{... | collective-permute-start | bytes 98312 | tf_op jit(solution)/shard_map/ppermute | solution.py:226
  17.1 0.2 collective-permute-start.5
  17.3 0.4 %collective-permute-done.1.refs_2_ = bf16[8,2048]{1,0:T(8,128)(2,1)S(1)} collective-permute-done((bf16[8,2048]{1,0:T(8,128)(2,1)S(1)}, bf16[8,2048]{1,0:T(8,128)(2,1)S(1)}, u32[]{:S(2)}, u32[]{:S(2)}) %collective-permute-start.1) | collective-permute-done | bytes 32800 | tf_op jit(solution)/shard_map/ppermute | solution.py:226
  17.7 0.1 collective-permute-start.2
  17.8 1.7 %collective-permute-done.3.refs_4_ = bf16[8,2048]{1,0:T(8,128)(2,1)S(1)} collective-permute-done((bf16[8,2048]{1,0:T(8,128)(2,1)S(1)}, bf16[8,2048]{1,0:T(8,128)(2,1)S(1)}, u32[]{:S(2)}, u32[]{:S(2)}) %collective-permute-start.3) | collective-permute-done | bytes 32800 | tf_op jit(solution)/shard_map/ppermute | solution.py:226
  19.5 2.4 %collective-permute-done.5.refs_6_ = bf16[8,2048]{1,0:T(8,128)(2,1)S(1)} collective-permute-done((bf16[8,2048]{1,0:T(8,128)(2,1)S(1)}, bf16[8,2048]{1,0:T(8,128)(2,1)S(1)}, u32[]{:S(2)}, u32[]{:S(2)}) %collective-permute-start.5) | collective-permute-done | bytes 32800 | tf_op jit(solution)/shard_map/ppermute | solution.py:226
  21.9 1.2 %collective-permute-done.6.refs_7_ = bf16[8,2048]{1,0:T(8,128)(2,1)S(1)} collective-permute-done((bf16[8,2048]{1,0:T(8,128)(2,1)S(1)}, bf16[8,2048]{1,0:T(8,128)(2,1)S(1)}, u32[]{:S(2)}, u32[]{:S(2)}) %collective-permute-start.6) | collective-permute-done | bytes 32800 | tf_op jit(solution)/shard_map/ppermute | solution.py:226
  23.1 2.6 %forward_product.1 = (f32[8,2048]{1,0:T(8,128)S(1)}, f32[8,2048]{1,0:T(8,128)S(1)}, f32[8,2048]{1,0:T(8,128)S(1)}, f32[8,2048]{1,0:T(8,128)S(1)}) custom-call(s32[192]{0:T(256)S(1)} %copy-done.5, s32[192]{0:T(256)S(1)} %copy-done.6, s32[1,1]{1,0:T(1,128)S(6)} %copy.9.count_ref, bf16[128,512]{1,0:T(8,128)(2,1)S(1)} %copy-done.3, ...), custom_call_target="tpu_custom_call" | custom-call | flops 100663296 | bytes 3145728 | tf_op jit(solution)/shard_map/forward_product/pallas_call | solution.py:191
  25.8 0.1 collective-permute-start.7
  25.8 1.7 %collective-permute-start.8 = (f32[8,2048]{1,0:T(8,128)S(1)}, f32[8,2048]{1,0:T(8,128)S(1)}, u32[]{:S(2)}, u32[]{:S(2)}) collective-permute-start(f32[8,2048]{1,0:T(8,128)S(1)} %get-tuple-element.16), channel_id=1, source_target_pairs={{0,2},{1,3},{2,0},{3,1},{4,6},{5,7},{6,4},{7,5},{8,10},{9,11},{10,... | collective-permute-start | bytes 196616 | tf_op jit(solution)/shard_map/ppermute | solution.py:226
  27.6 2.6 %collective-permute-start.9 = (f32[8,2048]{1,0:T(8,128)S(1)}, f32[8,2048]{1,0:T(8,128)S(1)}, u32[]{:S(2)}, u32[]{:S(2)}) collective-permute-start(f32[8,2048]{1,0:T(8,128)S(1)} %get-tuple-element.17), channel_id=1, source_target_pairs={{0,3},{1,2},{2,1},{3,0},{4,7},{5,6},{6,5},{7,4},{8,11},{9,10},{10,... | collective-permute-start | bytes 196616 | tf_op jit(solution)/shard_map/ppermute | solution.py:226
  30.2 0.6 %collective-permute-start.14 = (f32[8,2048]{1,0:T(8,128)S(1)}, f32[8,2048]{1,0:T(8,128)S(1)}, u32[]{:S(2)}, u32[]{:S(2)}) collective-permute-start(f32[8,2048]{1,0:T(8,128)S(1)} %get-tuple-element.20), channel_id=1, source_target_pairs={{0,8},{4,12},{8,0},{12,4},{16,24},{20,28},{24,16},{28,20},{1,9},{5... | collective-permute-start | bytes 196616 | tf_op jit(solution)/shard_map/ppermute | solution.py:226
  30.8 0.3 collective-permute-start.15
  31.2 2.6 %collective-permute-start.16 = (f32[8,2048]{1,0:T(8,128)S(1)}, f32[8,2048]{1,0:T(8,128)S(1)}, u32[]{:S(2)}, u32[]{:S(2)}) collective-permute-start(f32[8,2048]{1,0:T(8,128)S(1)} %get-tuple-element.22), channel_id=1, source_target_pairs={{0,24},{4,28},{8,16},{12,20},{16,8},{20,12},{24,0},{28,4},{1,25},{... | collective-permute-start | bytes 196616 | tf_op jit(solution)/shard_map/ppermute | solution.py:226
  33.8 0.7 %collective-permute-done.8 = f32[8,2048]{1,0:T(8,128)S(1)} collective-permute-done((f32[8,2048]{1,0:T(8,128)S(1)}, f32[8,2048]{1,0:T(8,128)S(1)}, u32[]{:S(2)}, u32[]{:S(2)}) %collective-permute-start.8) | collective-permute-done | bytes 65568 | tf_op jit(solution)/shard_map/ppermute | solution.py:226
  34.5 0.5 %collective-permute-done.14 = f32[8,2048]{1,0:T(8,128)S(1)} collective-permute-done((f32[8,2048]{1,0:T(8,128)S(1)}, f32[8,2048]{1,0:T(8,128)S(1)}, u32[]{:S(2)}, u32[]{:S(2)}) %collective-permute-start.14) | collective-permute-done | bytes 65568 | tf_op jit(solution)/shard_map/ppermute | solution.py:226
  35.1 0.2 collective-permute-done.15
  35.2 1.1 %collective-permute-done.16 = f32[8,2048]{1,0:T(8,128)S(1)} collective-permute-done((f32[8,2048]{1,0:T(8,128)S(1)}, f32[8,2048]{1,0:T(8,128)S(1)}, u32[]{:S(2)}, u32[]{:S(2)}) %collective-permute-start.16) | collective-permute-done | bytes 65568 | tf_op jit(solution)/shard_map/ppermute | solution.py:226
  36.3 0.7 %fusion.3 = f32[8,2048]{1,0:T(8,128)} fusion(f32[8,2048]{1,0:T(8,128)S(1)} %collective-permute-done.16, f32[8,2048]{1,0:T(8,128)S(1)} %collective-permute-done.15, f32[8,2048]{1,0:T(8,128)S(1)} %collective-permute-done.14, f32[4,8,2048]{2,1,0:T(8,128)S(1)} %collective-permute-done.13.got_ref, f32[4,8,2048]{2,1,0:T(8,128)S(1)} %get-tuple-element.18.keep_ref, ...), kind=kLoop, calls=%fused_computation.4 | loop fusion | flops 131072 | bytes 655360 | tf_op jit(solution)/shard_map/add | solution.py:244
  (21 shorter events, 0.1 us)
Async XLA Ops:
  0.0 8.5 %collective-permute-start.10 = (bf16[8,2048]{1,0:T(8,128)(2,1)}, bf16[8,2048]{1,0:T(8,128)(2,1)S(1)}, u32[]{:S(2)}, u32[]{:S(2)}) collective-permute-start(bf16[8,2048]{1,0:T(8,128)(2,1)} %refs_0_.3), channel_id=1, source_target_pairs={{0,1},{1,0},{2,3},{3,2},{4,5},{5,4},{6,7},{7,6},{8,9},{9,8},{10,11... | collective-permute-start | bytes 98312 | tf_op jit(solution)/shard_map/ppermute | solution.py:226
  3.0 5.6 %collective-permute-start.11 = (bf16[8,2048]{1,0:T(8,128)(2,1)}, bf16[8,2048]{1,0:T(8,128)(2,1)S(1)}, u32[]{:S(2)}, u32[]{:S(2)}) collective-permute-start(bf16[8,2048]{1,0:T(8,128)(2,1)} %refs_0_.3), channel_id=1, source_target_pairs={{0,2},{1,3},{2,0},{3,1},{4,6},{5,7},{6,4},{7,5},{8,10},{9,11},{10,... | collective-permute-start | bytes 98312 | tf_op jit(solution)/shard_map/ppermute | solution.py:226
  5.6 5.9 %collective-permute-start.12 = (bf16[8,2048]{1,0:T(8,128)(2,1)}, bf16[8,2048]{1,0:T(8,128)(2,1)S(1)}, u32[]{:S(2)}, u32[]{:S(2)}) collective-permute-start(bf16[8,2048]{1,0:T(8,128)(2,1)} %refs_0_.3), channel_id=1, source_target_pairs={{0,3},{1,2},{2,1},{3,0},{4,7},{5,6},{6,5},{7,4},{8,11},{9,10},{10,... | collective-permute-start | bytes 98312 | tf_op jit(solution)/shard_map/ppermute | solution.py:226
  5.6 1.4 %copy-start = (bf16[192,4096]{1,0:T(8,128)(2,1)S(1)}, bf16[192,4096]{1,0:T(8,128)(2,1)}, u32[]{:S(2)}) copy-start(bf16[192,4096]{1,0:T(8,128)(2,1)} %param.9) | copy-start | bytes 4718596
  7.0 4.5 %copy-start.1 = (bf16[8,2048]{1,0:T(8,128)(2,1)S(1)}, bf16[8,2048]{1,0:T(8,128)(2,1)}, u32[]{:S(2)}) copy-start(bf16[8,2048]{1,0:T(8,128)(2,1)} %refs_0_.3) | copy-start | bytes 98308
  7.0 4.5 %copy-start.2 = (bf16[128,512]{1,0:T(8,128)(2,1)S(1)}, bf16[128,512]{1,0:T(8,128)(2,1)}, u32[]{:S(2)}) copy-start(bf16[128,512]{1,0:T(8,128)(2,1)} %constant.4.clone.spread_ref) | copy-start | bytes 393220
  7.0 4.5 %copy-start.5 = (s32[192]{0:T(256)S(1)}, s32[192]{0:T(256)}, u32[]{:S(2)}) copy-start(s32[192]{0:T(256)} %rows_ref.3) | copy-start | bytes 2308
  7.0 4.5 %copy-start.6 = (s32[192]{0:T(256)S(1)}, s32[192]{0:T(256)}, u32[]{:S(2)}) copy-start(s32[192]{0:T(256)} %cols_ref.3) | copy-start | bytes 2308
  7.8 15.3 %copy-start.3 = (bf16[128,512]{1,0:T(8,128)(2,1)S(1)}, bf16[128,512]{1,0:T(8,128)(2,1)}, u32[]{:S(2)}) copy-start(bf16[128,512]{1,0:T(8,128)(2,1)} %constant.5.clone.spread_ref) | copy-start | bytes 393220
  7.8 15.3 %copy-start.4 = (bf16[512,128]{1,0:T(8,128)(2,1)S(1)}, bf16[512,128]{1,0:T(8,128)(2,1)}, u32[]{:S(2)}) copy-start(bf16[512,128]{1,0:T(8,128)(2,1)} %constant.7.fold_ref) | copy-start | bytes 393220
  13.6 16.6 %collective-permute-start.13 = (f32[4,8,2048]{2,1,0:T(8,128)S(1)}, f32[4,8,2048]{2,1,0:T(8,128)S(1)}, u32[]{:S(2)}, u32[]{:S(2)}) collective-permute-start(f32[4,8,2048]{2,1,0:T(8,128)S(1)} %get-tuple-element.19), channel_id=1, source_target_pairs={{0,4},{4,0},{8,12},{12,8},{16,20},{20,16},{24,28},{28,24},{1,5},{5... | collective-permute-start | bytes 786440 | tf_op jit(solution)/shard_map/ppermute | solution.py:226
  13.7 4.0 %collective-permute-start.1 = (bf16[8,2048]{1,0:T(8,128)(2,1)S(1)}, bf16[8,2048]{1,0:T(8,128)(2,1)S(1)}, u32[]{:S(2)}, u32[]{:S(2)}) collective-permute-start(bf16[8,2048]{1,0:T(8,128)(2,1)S(1)} %copy-done.1), channel_id=1, source_target_pairs={{0,8},{4,12},{8,0},{12,4},{16,24},{20,28},{24,16},{28,20},{1,9},{5... | collective-permute-start | bytes 98312 | tf_op jit(solution)/shard_map/ppermute | solution.py:226
  15.6 3.9 %collective-permute-start.3 = (bf16[8,2048]{1,0:T(8,128)(2,1)S(1)}, bf16[8,2048]{1,0:T(8,128)(2,1)S(1)}, u32[]{:S(2)}, u32[]{:S(2)}) collective-permute-start(bf16[8,2048]{1,0:T(8,128)(2,1)S(1)} %copy-done.1), channel_id=1, source_target_pairs={{0,16},{4,20},{8,24},{12,28},{16,0},{20,4},{24,8},{28,12},{1,17},{... | collective-permute-start | bytes 98312 | tf_op jit(solution)/shard_map/ppermute | solution.py:226
  17.1 4.8 %collective-permute-start.5 = (bf16[8,2048]{1,0:T(8,128)(2,1)S(1)}, bf16[8,2048]{1,0:T(8,128)(2,1)S(1)}, u32[]{:S(2)}, u32[]{:S(2)}) collective-permute-start(bf16[8,2048]{1,0:T(8,128)(2,1)S(1)} %copy-done.1), channel_id=1, source_target_pairs={{0,24},{4,28},{8,16},{12,20},{16,8},{20,12},{24,0},{28,4},{1,25},{... | collective-permute-start | bytes 98312 | tf_op jit(solution)/shard_map/ppermute | solution.py:226
  17.3 4.7 %collective-permute-start = (bf16[8,2048]{1,0:T(8,128)(2,1)S(1)}, bf16[8,2048]{1,0:T(8,128)(2,1)S(1)}, u32[]{:S(2)}, u32[]{:S(2)}) collective-permute-start(bf16[8,2048]{1,0:T(8,128)(2,1)S(1)} %copy-done.1), channel_id=1, source_target_pairs={{0,4},{4,0},{8,12},{12,8},{16,20},{20,16},{24,28},{28,24},{1,5},{5... | collective-permute-start | bytes 98312 | tf_op jit(solution)/shard_map/ppermute | solution.py:226
  17.7 4.2 %collective-permute-start.2 = (bf16[8,2048]{1,0:T(8,128)(2,1)S(1)}, bf16[8,2048]{1,0:T(8,128)(2,1)S(1)}, u32[]{:S(2)}, u32[]{:S(2)}) collective-permute-start(bf16[8,2048]{1,0:T(8,128)(2,1)S(1)} %collective-permute-done.1.refs_2_), channel_id=1, source_target_pairs={{0,4},{4,0},{8,12},{12,8},{16,20},{20,16},{24,28},{28,24},{1,5},{5... | collective-permute-start | bytes 98312 | tf_op jit(solution)/shard_map/ppermute | solution.py:226
  19.5 2.4 %collective-permute-start.4 = (bf16[8,2048]{1,0:T(8,128)(2,1)S(1)}, bf16[8,2048]{1,0:T(8,128)(2,1)S(1)}, u32[]{:S(2)}, u32[]{:S(2)}) collective-permute-start(bf16[8,2048]{1,0:T(8,128)(2,1)S(1)} %collective-permute-done.3.refs_4_), channel_id=1, source_target_pairs={{0,4},{4,0},{8,12},{12,8},{16,20},{20,16},{24,28},{28,24},{1,5},{5... | collective-permute-start | bytes 98312 | tf_op jit(solution)/shard_map/ppermute | solution.py:226
  21.9 1.2 %collective-permute-start.6 = (bf16[8,2048]{1,0:T(8,128)(2,1)S(1)}, bf16[8,2048]{1,0:T(8,128)(2,1)S(1)}, u32[]{:S(2)}, u32[]{:S(2)}) collective-permute-start(bf16[8,2048]{1,0:T(8,128)(2,1)S(1)} %collective-permute-done.5.refs_6_), channel_id=1, source_target_pairs={{0,4},{4,0},{8,12},{12,8},{16,20},{20,16},{24,28},{28,24},{1,5},{5... | collective-permute-start | bytes 98312 | tf_op jit(solution)/shard_map/ppermute | solution.py:226
  25.8 5.4 %collective-permute-start.7 = (f32[8,2048]{1,0:T(8,128)S(1)}, f32[8,2048]{1,0:T(8,128)S(1)}, u32[]{:S(2)}, u32[]{:S(2)}) collective-permute-start(f32[8,2048]{1,0:T(8,128)S(1)} %get-tuple-element.15), channel_id=1, source_target_pairs={{0,1},{1,0},{2,3},{3,2},{4,5},{5,4},{6,7},{7,6},{8,9},{9,8},{10,11... | collective-permute-start | bytes 196616 | tf_op jit(solution)/shard_map/ppermute | solution.py:226
  25.8 8.7 %collective-permute-start.8 = (f32[8,2048]{1,0:T(8,128)S(1)}, f32[8,2048]{1,0:T(8,128)S(1)}, u32[]{:S(2)}, u32[]{:S(2)}) collective-permute-start(f32[8,2048]{1,0:T(8,128)S(1)} %get-tuple-element.16), channel_id=1, source_target_pairs={{0,2},{1,3},{2,0},{3,1},{4,6},{5,7},{6,4},{7,5},{8,10},{9,11},{10,... | collective-permute-start | bytes 196616 | tf_op jit(solution)/shard_map/ppermute | solution.py:226
  27.6 7.0 %collective-permute-start.9 = (f32[8,2048]{1,0:T(8,128)S(1)}, f32[8,2048]{1,0:T(8,128)S(1)}, u32[]{:S(2)}, u32[]{:S(2)}) collective-permute-start(f32[8,2048]{1,0:T(8,128)S(1)} %get-tuple-element.17), channel_id=1, source_target_pairs={{0,3},{1,2},{2,1},{3,0},{4,7},{5,6},{6,5},{7,4},{8,11},{9,10},{10,... | collective-permute-start | bytes 196616 | tf_op jit(solution)/shard_map/ppermute | solution.py:226
  30.2 4.8 %collective-permute-start.14 = (f32[8,2048]{1,0:T(8,128)S(1)}, f32[8,2048]{1,0:T(8,128)S(1)}, u32[]{:S(2)}, u32[]{:S(2)}) collective-permute-start(f32[8,2048]{1,0:T(8,128)S(1)} %get-tuple-element.20), channel_id=1, source_target_pairs={{0,8},{4,12},{8,0},{12,4},{16,24},{20,28},{24,16},{28,20},{1,9},{5... | collective-permute-start | bytes 196616 | tf_op jit(solution)/shard_map/ppermute | solution.py:226
  30.8 4.4 %collective-permute-start.15 = (f32[8,2048]{1,0:T(8,128)S(1)}, f32[8,2048]{1,0:T(8,128)S(1)}, u32[]{:S(2)}, u32[]{:S(2)}) collective-permute-start(f32[8,2048]{1,0:T(8,128)S(1)} %get-tuple-element.21), channel_id=1, source_target_pairs={{0,16},{4,20},{8,24},{12,28},{16,0},{20,4},{24,8},{28,12},{1,17},{... | collective-permute-start | bytes 196616 | tf_op jit(solution)/shard_map/ppermute | solution.py:226
  31.2 5.2 %collective-permute-start.16 = (f32[8,2048]{1,0:T(8,128)S(1)}, f32[8,2048]{1,0:T(8,128)S(1)}, u32[]{:S(2)}, u32[]{:S(2)}) collective-permute-start(f32[8,2048]{1,0:T(8,128)S(1)} %get-tuple-element.22), channel_id=1, source_target_pairs={{0,24},{4,28},{8,16},{12,20},{16,8},{20,12},{24,0},{28,4},{1,25},{... | collective-permute-start | bytes 196616 | tf_op jit(solution)/shard_map/ppermute | solution.py:226

commit v2 on v1

--- a/solution.py
+++ b/solution.py
@@ -1,5 +1,3 @@
-import functools
-
 import jax
 import jax.numpy as jnp
 import numpy as np
@@ -15,6 +13,7 @@
 F32 = jnp.float32
 BF16 = jnp.bfloat16
 VMEM = pl.BlockSpec(memory_space=pltpu.VMEM)
+ANY = pl.BlockSpec(memory_space=pl.ANY)
 SMEM = pl.BlockSpec(memory_space=pltpu.SMEM)
 PARAMS = pltpu.CompilerParams(vmem_limit_bytes=48 * 1024 * 1024)
 
@@ -51,25 +50,23 @@
 def prep(tiles):
     slots = tiles.shape[0]
     blocks = slots // 8
-    steps = 4 if blocks % 4 == 0 else 1
     view = tiles.reshape(blocks, 8, HALF, LANES).swapaxes(1, 2)
     return pl.pallas_call(
         prep_kernel,
-        grid=(steps,),
-        in_specs=[pl.BlockSpec((blocks // steps, HALF, 8, LANES), lambda i: (i, 0, 0, 0))],
-        out_specs=pl.BlockSpec((slots // steps, HALF, LANES), lambda i: (i, 0, 0)),
+        in_specs=[VMEM],
+        out_specs=VMEM,
         out_shape=jax.ShapeDtypeStruct((slots, HALF, LANES), BF16),
-        scratch_shapes=[pltpu.VMEM((blocks // steps, HALF * 8, LANES), F32)],
-        compiler_params=PARAMS,
-        cost_estimate=pl.CostEstimate(flops=0, bytes_accessed=8 * tiles.size, transcendentals=0),
+        scratch_shapes=[pltpu.VMEM((blocks, HALF * 8, LANES), F32)],
+        compiler_params=PARAMS,
+        cost_estimate=pl.CostEstimate(flops=0, bytes_accessed=4 * tiles.size, transcendentals=0),
         name="prep_tiles",
     )(view)
 
 
-def build_table(piece_refs, spread, table):
-    width, piece = piece_refs[0].shape
+def build_table(pieces, spread, table):
+    width, piece = pieces[0].shape
     pairs = piece // LANES
-    for n, ref in enumerate(piece_refs):
+    for n, ref in enumerate(pieces):
         rows = jnp.concatenate([ref[:, p * LANES : (p + 1) * LANES] for p in range(pairs)], axis=0)
         wide = jnp.dot(rows, spread, preferred_element_type=F32)
         wide = wide.reshape(pairs, width, 4 * LANES)
@@ -81,8 +78,11 @@
                 table[n * 2 * pairs + 2 * p + q] = both[p]
 
 
-def backward_kernel(n_in, n_out, rows_ref, cols_ref, count_ref, spread_ref, tiles_ref, *refs):
-    pieces, (keep_ref, give_ref), (table, acc) = refs[:n_in], refs[n_in : n_in + 2], refs[n_in + 2 :]
+def backward_kernel(
+    rows_ref, cols_ref, count_ref, spread_ref, tiles_ref, seg_ref, after_ref, keep_ref, give_ref, table, acc
+):
+    pieces = [seg_ref.at[n] for n in range(seg_ref.shape[0])]
+    n_out = 2 * keep_ref.shape[0]
     width, piece = pieces[0].shape
     per_piece = piece // TILE
     slots = tiles_ref.shape[0]
@@ -117,14 +117,13 @@
             )
 
 
-def backward(row_pieces, tiles, tile_rows, tile_cols, counts, n_out):
-    n_in = len(row_pieces)
-    width, piece = row_pieces[0].shape
+def backward(segment, tiles, tile_rows, tile_cols, counts, n_out, after):
+    n_in, width, piece = segment.shape
     per_piece = piece // TILE
     half = jax.ShapeDtypeStruct((n_out // 2, width, piece), F32)
     return pl.pallas_call(
-        functools.partial(backward_kernel, n_in, n_out),
-        in_specs=[SMEM] * 3 + [VMEM] * (2 + n_in),
+        backward_kernel,
+        in_specs=[SMEM] * 3 + [VMEM] * 3 + [ANY],
         out_specs=[VMEM] * 2,
         out_shape=[half, half],
         scratch_shapes=[
@@ -136,11 +135,26 @@
             flops=2 * tiles.size * 64, bytes_accessed=4 * tiles.size, transcendentals=0
         ),
         name="transpose_product",
-    )(tile_rows, tile_cols, counts, row_spread(), tiles, *row_pieces)
-
-
-def forward_kernel(n_in, n_out, rows_ref, cols_ref, count_ref, spread_ref, fold_ref, tiles_ref, *refs):
-    pieces, outs, (table, acc) = refs[:n_in], refs[n_in : n_in + n_out], refs[n_in + n_out :]
+    )(tile_rows, tile_cols, counts, row_spread(), tiles, segment, after)
+
+
+def forward_kernel(
+    rows_ref,
+    cols_ref,
+    count_ref,
+    spread_ref,
+    fold_ref,
+    tiles_ref,
+    same_ref,
+    other_ref,
+    after_ref,
+    keep_ref,
+    give_ref,
+    table,
+    acc,
+):
+    pieces = [ref.at[h] for h in range(same_ref.shape[0]) for ref in (same_ref, other_ref)]
+    n_out = 2 * keep_ref.shape[0]
     width, piece = pieces[0].shape
     per_piece = piece // TILE
     slots = tiles_ref.shape[0]
@@ -180,21 +194,22 @@
         rest = (wide - first.astype(F32)).astype(BF16)
         out = jnp.dot(first, fold, preferred_element_type=F32)
         out = out + jnp.dot(rest, fold, preferred_element_type=F32)
+        dest = (keep_ref if n % 2 == 0 else give_ref).at[n // 2]
         for p in range(pairs):
-            outs[n][:, p * LANES : (p + 1) * LANES] = out[p * width : (p + 1) * width]
-
-
-def forward(col_pieces, tiles, tile_rows, tile_cols, counts, n_out):
-    n_in = len(col_pieces)
-    width, piece = col_pieces[0].shape
+            dest[:, p * LANES : (p + 1) * LANES] = out[p * width : (p + 1) * width]
+
+
+def forward(same, other, tiles, tile_rows, tile_cols, counts, n_out, after):
+    n_chips, width, piece = same.shape
     per_piece = piece // TILE
-    return pl.pallas_call(
-        functools.partial(forward_kernel, n_in, n_out),
-        in_specs=[SMEM] * 3 + [VMEM] * (3 + n_in),
-        out_specs=[VMEM] * n_out,
-        out_shape=[jax.ShapeDtypeStruct((width, piece), F32)] * n_out,
+    half = jax.ShapeDtypeStruct((n_out // 2, width, piece), F32)
+    return pl.pallas_call(
+        forward_kernel,
+        in_specs=[SMEM] * 3 + [VMEM] * 5 + [ANY],
+        out_specs=[VMEM] * 2,
+        out_shape=[half, half],
         scratch_shapes=[
-            pltpu.VMEM((n_in * per_piece, 2 * width, LANES), BF16),
+            pltpu.VMEM((2 * n_chips * per_piece, 2 * width, LANES), BF16),
             pltpu.VMEM((n_out * per_piece + 1, 2 * width, LANES), F32),
         ],
         compiler_params=PARAMS,
@@ -202,7 +217,30 @@
             flops=2 * tiles.size * 64, bytes_accessed=4 * tiles.size, transcendentals=0
         ),
         name="forward_product",
-    )(tile_rows, tile_cols, counts, col_spread(), row_fold(), tiles, *col_pieces)
+    )(tile_rows, tile_cols, counts, col_spread(), row_fold(), tiles, same, other, after)
+
+
+def stack_kernel(*refs):
+    out_ref, at = refs[-1], 0
+    for ref in refs[:-2]:
+        if len(ref.shape) == 2:
+            out_ref[at] = ref[...]
+            at += 1
+        else:
+            out_ref[at : at + ref.shape[0]] = ref[...]
+            at += ref.shape[0]
+
+
+def stack(*parts, after):
+    total = sum(x.shape[0] if x.ndim == 3 else 1 for x in parts)
+    return pl.pallas_call(
+        stack_kernel,
+        in_specs=[VMEM] * len(parts) + [ANY],
+        out_specs=VMEM,
+        out_shape=jax.ShapeDtypeStruct((total,) + parts[0].shape[-2:], parts[0].dtype),
+        compiler_params=PARAMS,
+        name="stack_pieces",
+    )(*parts, after)
 
 
 def pair_sum_kernel(keep_ref, got_ref, *outs):
@@ -222,6 +260,43 @@
     )(keep, got)
 
 
+def split_sum_kernel(keep_ref, got_ref, after_ref, next_keep, next_give):
+    for h in range(next_keep.shape[0]):
+        next_keep[h] = keep_ref[2 * h] + got_ref[2 * h]
+        next_give[h] = keep_ref[2 * h + 1] + got_ref[2 * h + 1]
+
+
+def split_sum(keep, got, after):
+    parts, width, piece = keep.shape
+    half = jax.ShapeDtypeStruct((parts // 2, width, piece), F32)
+    return pl.pallas_call(
+        split_sum_kernel,
+        in_specs=[VMEM] * 2 + [ANY],
+        out_specs=[VMEM] * 2,
+        out_shape=[half, half],
+        compiler_params=PARAMS,
+        name="halving_sum",
+    )(keep, got, after)
+
+
+def sum_kernel(*refs):
+    total = refs[0][...]
+    for ref in refs[1:-1]:
+        total = total + ref[...]
+    refs[-1][...] = total
+
+
+def sum_pieces(*parts):
+    return pl.pallas_call(
+        sum_kernel,
+        in_specs=[VMEM] * len(parts),
+        out_specs=VMEM,
+        out_shape=jax.ShapeDtypeStruct(parts[0].shape, F32),
+        compiler_params=PARAMS,
+        name="sum_pieces",
+    )(*parts)
+
+
 def swap(x, axis, size, d):
     return lax.ppermute(x, axis, [(i, i ^ d) for i in range(size)])
 
@@ -229,19 +304,27 @@
 def body(vectors, tiles, tile_rows, tile_cols, counts):
     n_rows = lax.axis_size("brow")
     n_cols = lax.axis_size("bcol")
-    row_pieces = [vectors] + [swap(vectors, "bcol", n_cols, d) for d in range(1, n_cols)]
-    same_core = [vectors] + [swap(vectors, "brow", n_rows, 2 * h) for h in range(1, n_rows // 2)]
-    other_core = [swap(x, "brow", n_rows, 1) for x in same_core]
-    col_pieces = [x for pair in zip(same_core, other_core) for x in pair]
+    chips = [swap(vectors, "brow", n_rows, 2 * h) for h in range(1, n_rows // 2)]
+    row_seg, d = vectors, 1
+    while d < n_cols:
+        row_seg = stack(row_seg, swap(row_seg, "bcol", n_cols, d), after=chips[0])
+        d *= 2
     blocks = prep(tiles)
-
-    keep, give = backward(row_pieces, blocks, tile_rows, tile_cols, counts, n_rows)
-    got = swap(give, "brow", n_rows, 1)
-    mine = forward(col_pieces, blocks, tile_rows, tile_cols, counts, n_cols)
-    from_rows = [mine[0]] + [swap(mine[d], "bcol", n_cols, d) for d in range(1, n_cols)]
-    sums = pair_sum(keep, got)
-    from_cols = [keep[0], got[0]] + [swap(x, "brow", n_rows, 2 * (h + 1)) for h, x in enumerate(sums)]
-    return sum(from_rows + from_cols)
+    same = stack(vectors, *chips, after=blocks)
+    other = swap(same, "brow", n_rows, 1)
+
+    col_keep, col_give = backward(row_seg, blocks, tile_rows, tile_cols, counts, n_rows, same)
+    row_keep, give = forward(same, other, blocks, tile_rows, tile_cols, counts, n_cols, col_give)
+    col_got = swap(col_give, "brow", n_rows, 1)
+    sums = pair_sum(col_keep, col_got)
+    from_chips = [swap(x, "brow", n_rows, 2 * (h + 1)) for h, x in enumerate(sums)]
+    row_got, d = swap(give, "bcol", n_cols, 1), 2
+    while d < n_cols:
+        row_keep, give = split_sum(row_keep, row_got, sums[0])
+        row_got = swap(give, "bcol", n_cols, d)
+        d *= 2
+    total = sum_pieces(col_keep[0] + col_got[0], *from_chips)
+    return total + (row_keep[0] + row_got[0])
 
 
 def solution(mesh):

time: 37.3 us -> 35.3 us (0.946)
  starting transfers between devices: 17.3 us -> 15.6 us
  waiting for transfers between devices: 11.3 us -> 9.61 us
  Pallas kernels: 5.47 us -> 7.05 us
    ppermute x17 -> x12, starting transfers between devices: 17.3 us -> 15.6 us  [swap(): return lax.ppermute(x, axis, [(i, i ^ d) for i in range(size)])]
    ppermute x17 -> x12, waiting for transfers between devices: 11.3 us -> 9.61 us  [swap(): return lax.ppermute(x, axis, [(i, i ^ d) for i in range(size)])]
    pallas_call x3 -> x8, Pallas kernels: 5.45 us -> 7.03 us  [the longest x1 2.67 us: forward(): pl.pallas_call(forward_kernel, in_specs=[SMEM] * 3 + [VMEM] * 5 + [ANY],...]
    unnamed x14 -> x12, local copies, waits for them, and re-layouts: 1.44 us -> 1.44 us
  transfers between devices with their start and end apart: 17 -> 12, of which waited for: 10 -> 8; matrix products, arithmetic and copies ran while one was open for 0% -> 0% of each run, Pallas kernels for 9% -> 18%
where the time goes in v2:
time: 35.3 us; the launch traced here: 35.1 us
  starting transfers between devices  15.6 us (44%)
  waiting for transfers between devices  9.61 us (27%)
  Pallas kernels  7.05 us (20%)
  local copies, waits for them, and re-layouts  1.44 us (4%)
  between operations  0.81 us (2%)
  other arithmetic  0.65 us (2%)
    ppermute x12, starting transfers between devices, swap(): return lax.ppermute(x, axis, [(i, i ^ d) for i in range(size)])  15.6 us
    ppermute x12, waiting for transfers between devices, swap(): return lax.ppermute(x, axis, [(i, i ^ d) for i in range(size)])  9.61 us
    pallas_call x1, Pallas kernels, forward(): pl.pallas_call(forward_kernel, in_specs=[SMEM] * 3 + [VMEM] * 5 + [ANY],...  2.67 us
    pallas_call x1, Pallas kernels, backward(): pl.pallas_call(backward_kernel, in_specs=[SMEM] * 3 + [VMEM] * 3 + [ANY],...  2.1 us
    pallas_call x3, Pallas kernels, stack(): pl.pallas_call(stack_kernel, in_specs=[VMEM] * len(parts) + [ANY], out_sp...  1.54 us
    unnamed x12, local copies, waits for them, and re-layouts  1.44 us
  transfers between devices with their start and end apart: 12, of which 8 were waited for; matrix products, arithmetic and copies ran while one was open for 0% of the time, Pallas kernels for 18%

profile of v2, /device:TPU:0, one launch (start us, length us, event | category | flops | bytes accessed | tf_op | source)
XLA Modules:
  0.0 35.1 jit_solution(305979584010770226)
XLA Ops:
  0.0 2.9 %collective-permute-start.1 = (bf16[8,2048]{1,0:T(8,128)(2,1)}, bf16[8,2048]{1,0:T(8,128)(2,1)S(1)}, u32[]{:S(2)}, u32[]{:S(2)}) collective-permute-start(bf16[8,2048]{1,0:T(8,128)(2,1)} %refs_0_.3), channel_id=1, source_target_pairs={{0,8},{4,12},{8,0},{12,4},{16,24},{20,28},{24,16},{28,20},{1,9},{5... | collective-permute-start | bytes 98312 | tf_op jit(solution)/shard_map/ppermute | solution.py:301
  2.9 1.6 %collective-permute-start = (bf16[8,2048]{1,0:T(8,128)(2,1)}, bf16[8,2048]{1,0:T(8,128)(2,1)S(1)}, u32[]{:S(2)}, u32[]{:S(2)}) collective-permute-start(bf16[8,2048]{1,0:T(8,128)(2,1)} %refs_0_.3), channel_id=1, source_target_pairs={{0,1},{1,0},{2,3},{3,2},{4,5},{5,4},{6,7},{7,6},{8,9},{9,8},{10,11... | collective-permute-start | bytes 98312 | tf_op jit(solution)/shard_map/ppermute | solution.py:301
  4.5 0.5 %collective-permute-done.1.refs_2_.refs_1_ = bf16[8,2048]{1,0:T(8,128)(2,1)S(1)} collective-permute-done((bf16[8,2048]{1,0:T(8,128)(2,1)}, bf16[8,2048]{1,0:T(8,128)(2,1)S(1)}, u32[]{:S(2)}, u32[]{:S(2)}) %collective-permute-start.1) | collective-permute-done | bytes 32800 | tf_op jit(solution)/shard_map/ppermute | solution.py:301
  5.0 2.0 %collective-permute-done.refs_1_ = bf16[8,2048]{1,0:T(8,128)(2,1)S(1)} collective-permute-done((bf16[8,2048]{1,0:T(8,128)(2,1)}, bf16[8,2048]{1,0:T(8,128)(2,1)S(1)}, u32[]{:S(2)}, u32[]{:S(2)}) %collective-permute-start) | collective-permute-done | bytes 32800 | tf_op jit(solution)/shard_map/ppermute | solution.py:301
  7.1 0.8 %stack_pieces.3.refs_0_ = bf16[2,8,2048]{2,1,0:T(8,128)(2,1)S(1)} custom-call(bf16[8,2048]{1,0:T(8,128)(2,1)} %refs_0_.3, bf16[8,2048]{1,0:T(8,128)(2,1)S(1)} %collective-permute-done.refs_1_, bf16[8,2048]{1,0:T(8,128)(2,1)S(1)} %collective-permute-done.1.refs_2_.refs_1_), custom_call_target="tpu_custom_call" | custom-call | tf_op jit(solution)/shard_map/stack_pieces/pallas_call | solution.py:236
  7.8 2.6 %collective-permute-start.2 = (bf16[2,8,2048]{2,1,0:T(8,128)(2,1)S(1)}, bf16[2,8,2048]{2,1,0:T(8,128)(2,1)S(1)}, u32[]{:S(2)}, u32[]{:S(2)}) collective-permute-start(bf16[2,8,2048]{2,1,0:T(8,128)(2,1)S(1)} %stack_pieces.3.refs_0_), channel_id=1, source_target_pairs={{0,2},{1,3},{2,0},{3,1},{4,6},{5,7},{6,4},{7,5},{8,10},{9,11},{10,... | collective-permute-start | bytes 196616 | tf_op jit(solution)/shard_map/ppermute | solution.py:301
  10.4 1.5 %collective-permute-start.3 = (bf16[8,2048]{1,0:T(8,128)(2,1)}, bf16[8,2048]{1,0:T(8,128)(2,1)S(1)}, u32[]{:S(2)}, u32[]{:S(2)}) collective-permute-start(bf16[8,2048]{1,0:T(8,128)(2,1)} %refs_0_.3), channel_id=1, source_target_pairs={{0,16},{4,20},{8,24},{12,28},{16,0},{20,4},{24,8},{28,12},{1,17},{... | collective-permute-start | bytes 98312 | tf_op jit(solution)/shard_map/ppermute | solution.py:301
  11.9 0.5 %collective-permute-start.4 = (bf16[8,2048]{1,0:T(8,128)(2,1)}, bf16[8,2048]{1,0:T(8,128)(2,1)S(1)}, u32[]{:S(2)}, u32[]{:S(2)}) collective-permute-start(bf16[8,2048]{1,0:T(8,128)(2,1)} %refs_0_.3), channel_id=1, source_target_pairs={{0,24},{4,28},{8,16},{12,20},{16,8},{20,12},{24,0},{28,4},{1,25},{... | collective-permute-start | bytes 98312 | tf_op jit(solution)/shard_map/ppermute | solution.py:301
  13.1 0.0 copy-start
  13.1 1.4 %copy-done = bf16[192,4096]{1,0:T(8,128)(2,1)S(1)} copy-done((bf16[192,4096]{1,0:T(8,128)(2,1)S(1)}, bf16[192,4096]{1,0:T(8,128)(2,1)}, u32[]{:S(2)}) %copy-start) | copy-done | bytes 1572888
  14.5 0.7 %prep_tiles.1.refs_4_.tiles_ref = bf16[192,32,128]{2,1,0:T(8,128)(2,1)S(1)} custom-call(bf16[24,32,8,128]{3,2,1,0:T(8,128)(2,1)S(1)} %bitcast.7), custom_call_target="tpu_custom_call" | custom-call | bytes 3145728 | tf_op jit(solution)/shard_map/prep_tiles/pallas_call | solution.py:54
  15.2 0.0 copy-start.3
  15.2 0.0 copy-start.5
  15.2 1.7 %collective-permute-done.4.refs_3_ = bf16[8,2048]{1,0:T(8,128)(2,1)S(1)} collective-permute-done((bf16[8,2048]{1,0:T(8,128)(2,1)}, bf16[8,2048]{1,0:T(8,128)(2,1)S(1)}, u32[]{:S(2)}, u32[]{:S(2)}) %collective-permute-start.4) | collective-permute-done | bytes 32800 | tf_op jit(solution)/shard_map/ppermute | solution.py:301
  17.0 0.8 %stack_pieces.5.after_ref.same_ref = bf16[4,8,2048]{2,1,0:T(8,128)(2,1)S(1)} custom-call(bf16[8,2048]{1,0:T(8,128)(2,1)} %refs_0_.3, bf16[8,2048]{1,0:T(8,128)(2,1)S(1)} %collective-permute-done.1.refs_2_.refs_1_, bf16[8,2048]{1,0:T(8,128)(2,1)S(1)} %collective-permute-done.3.refs_2_, bf16[8,2048]{1,0:T(8,128)(2,1)S(1)} %collective-permute-done.4.refs_3_, ...), custom_call_target="tpu_custom_call" | custom-call | tf_op jit(solution)/shard_map/stack_pieces/pallas_call | solution.py:236
  17.7 0.0 copy-start.1
  17.7 0.0 copy-start.2
  17.8 0.1 collective-permute-start.9
  17.9 2.1 %transpose_product.1 = (f32[4,8,2048]{2,1,0:T(8,128)S(1)}, f32[4,8,2048]{2,1,0:T(8,128)S(1)}) custom-call(s32[192]{0:T(256)S(1)} %copy-done.4, s32[192]{0:T(256)S(1)} %copy-done.5, s32[1,1]{1,0:T(1,128)S(6)} %copy.9.count_ref, bf16[128,512]{1,0:T(8,128)(2,1)S(1)} %copy-done.3, bf16[192,32,128]{2,1,0:T(8,128)(2,1)S(1)} %prep_tiles.1.refs_4_.tiles_ref, ...), custom_call_target="tpu_custom_call" | custom-call | flops 100663296 | bytes 3145728 | tf_op jit(solution)/shard_map/transpose_product/pallas_call | solution.py:124
  20.0 0.9 %collective-permute-start.5 = (f32[4,8,2048]{2,1,0:T(8,128)S(1)}, f32[4,8,2048]{2,1,0:T(8,128)S(1)}, u32[]{:S(2)}, u32[]{:S(2)}) collective-permute-start(f32[4,8,2048]{2,1,0:T(8,128)S(1)} %get-tuple-element.15.after_ref), channel_id=1, source_target_pairs={{0,4},{4,0},{8,12},{12,8},{16,20},{20,16},{24,28},{28,24},{1,5},{5... | collective-permute-start | bytes 786440 | tf_op jit(solution)/shard_map/ppermute | solution.py:301
  20.9 2.7 %forward_product.1 = (f32[2,8,2048]{2,1,0:T(8,128)S(1)}, f32[2,8,2048]{2,1,0:T(8,128)S(1)}) custom-call(s32[192]{0:T(256)S(1)} %copy-done.4, s32[192]{0:T(256)S(1)} %copy-done.5, s32[1,1]{1,0:T(1,128)S(6)} %copy.9.count_ref, bf16[128,512]{1,0:T(8,128)(2,1)S(1)} %copy-done.2, bf16[512,128]{1,0:T(8,128)(2,1)S(1)} %copy-done.1, ...), custom_call_target="tpu_custom_call" | custom-call | flops 100663296 | bytes 3145728 | tf_op jit(solution)/shard_map/forward_product/pallas_call | solution.py:206
  23.6 1.5 %collective-permute-start.10 = (f32[2,8,2048]{2,1,0:T(8,128)S(1)}, f32[2,8,2048]{2,1,0:T(8,128)S(1)}, u32[]{:S(2)}, u32[]{:S(2)}) collective-permute-start(f32[2,8,2048]{2,1,0:T(8,128)S(1)} %get-tuple-element.20), channel_id=1, source_target_pairs={{0,1},{1,0},{2,3},{3,2},{4,5},{5,4},{6,7},{7,6},{8,9},{9,8},{10,11... | collective-permute-start | bytes 393224 | tf_op jit(solution)/shard_map/ppermute | solution.py:301
  25.1 0.6 %collective-permute-start.7 = (f32[8,2048]{1,0:T(8,128)S(1)}, f32[8,2048]{1,0:T(8,128)S(1)}, u32[]{:S(2)}, u32[]{:S(2)}) collective-permute-start(f32[8,2048]{1,0:T(8,128)S(1)} %get-tuple-element.17), channel_id=1, source_target_pairs={{0,16},{4,20},{8,24},{12,28},{16,0},{20,4},{24,8},{28,12},{1,17},{... | collective-permute-start | bytes 196616 | tf_op jit(solution)/shard_map/ppermute | solution.py:301
  25.7 1.8 %collective-permute-start.8 = (f32[8,2048]{1,0:T(8,128)S(1)}, f32[8,2048]{1,0:T(8,128)S(1)}, u32[]{:S(2)}, u32[]{:S(2)}) collective-permute-start(f32[8,2048]{1,0:T(8,128)S(1)} %get-tuple-element.18), channel_id=1, source_target_pairs={{0,24},{4,28},{8,16},{12,20},{16,8},{20,12},{24,0},{28,4},{1,25},{... | collective-permute-start | bytes 196616 | tf_op jit(solution)/shard_map/ppermute | solution.py:301
  27.5 1.2 %collective-permute-start.6 = (f32[8,2048]{1,0:T(8,128)S(1)}, f32[8,2048]{1,0:T(8,128)S(1)}, u32[]{:S(2)}, u32[]{:S(2)}) collective-permute-start(f32[8,2048]{1,0:T(8,128)S(1)} %get-tuple-element.16.after_ref), channel_id=1, source_target_pairs={{0,8},{4,12},{8,0},{12,4},{16,24},{20,28},{24,16},{28,20},{1,9},{5... | collective-permute-start | bytes 196616 | tf_op jit(solution)/shard_map/ppermute | solution.py:301
  28.7 0.5 %collective-permute-done.10.got_ref = f32[2,8,2048]{2,1,0:T(8,128)S(1)} collective-permute-done((f32[2,8,2048]{2,1,0:T(8,128)S(1)}, f32[2,8,2048]{2,1,0:T(8,128)S(1)}, u32[]{:S(2)}, u32[]{:S(2)}) %collective-permute-start.10) | collective-permute-done | bytes 131104 | tf_op jit(solution)/shard_map/ppermute | solution.py:301
  29.3 0.4 %collective-permute-start.11 = (f32[1,8,2048]{2,1,0:T(8,128)S(1)}, f32[1,8,2048]{2,1,0:T(8,128)S(1)}, u32[]{:S(2)}, u32[]{:S(2)}) collective-permute-start(f32[1,8,2048]{2,1,0:T(8,128)S(1)} %get-tuple-element.22), channel_id=1, source_target_pairs={{0,2},{1,3},{2,0},{3,1},{4,6},{5,7},{6,4},{7,5},{8,10},{9,11},{10,... | collective-permute-start | bytes 196616 | tf_op jit(solution)/shard_map/ppermute | solution.py:301
  29.7 0.5 %collective-permute-done.7.refs_2_ = f32[8,2048]{1,0:T(8,128)S(1)} collective-permute-done((f32[8,2048]{1,0:T(8,128)S(1)}, f32[8,2048]{1,0:T(8,128)S(1)}, u32[]{:S(2)}, u32[]{:S(2)}) %collective-permute-start.7) | collective-permute-done | bytes 65568 | tf_op jit(solution)/shard_map/ppermute | solution.py:301
  30.2 0.8 %collective-permute-done.8.refs_3_ = f32[8,2048]{1,0:T(8,128)S(1)} collective-permute-done((f32[8,2048]{1,0:T(8,128)S(1)}, f32[8,2048]{1,0:T(8,128)S(1)}, u32[]{:S(2)}, u32[]{:S(2)}) %collective-permute-start.8) | collective-permute-done | bytes 65568 | tf_op jit(solution)/shard_map/ppermute | solution.py:301
  30.9 0.8 %collective-permute-done.6.refs_1_ = f32[8,2048]{1,0:T(8,128)S(1)} collective-permute-done((f32[8,2048]{1,0:T(8,128)S(1)}, f32[8,2048]{1,0:T(8,128)S(1)}, u32[]{:S(2)}, u32[]{:S(2)}) %collective-permute-start.6) | collective-permute-done | bytes 65568 | tf_op jit(solution)/shard_map/ppermute | solution.py:301
  31.7 2.7 %collective-permute-done.11 = f32[1,8,2048]{2,1,0:T(8,128)S(1)} collective-permute-done((f32[1,8,2048]{2,1,0:T(8,128)S(1)}, f32[1,8,2048]{2,1,0:T(8,128)S(1)}, u32[]{:S(2)}, u32[]{:S(2)}) %collective-permute-start.11) | collective-permute-done | bytes 65568 | tf_op jit(solution)/shard_map/ppermute | solution.py:301
  34.5 0.6 %bitcast_add_fusion = f32[8,2048]{1,0:T(8,128)} fusion(f32[8,2048]{1,0:T(8,128)S(1)} %sum_pieces.1, f32[1,8,2048]{2,1,0:T(8,128)S(1)} %get-tuple-element.21, f32[1,8,2048]{2,1,0:T(8,128)S(1)} %collective-permute-done.11), kind=kLoop, calls=%fused_computation.2 | loop fusion | flops 32768 | bytes 262144 | tf_op jit(solution)/shard_map/add | solution.py:327
  (15 shorter events, 0.1 us)
Async XLA Ops:
  0.0 5.0 %collective-permute-start.1 = (bf16[8,2048]{1,0:T(8,128)(2,1)}, bf16[8,2048]{1,0:T(8,128)(2,1)S(1)}, u32[]{:S(2)}, u32[]{:S(2)}) collective-permute-start(bf16[8,2048]{1,0:T(8,128)(2,1)} %refs_0_.3), channel_id=1, source_target_pairs={{0,8},{4,12},{8,0},{12,4},{16,24},{20,28},{24,16},{28,20},{1,9},{5... | collective-permute-start | bytes 98312 | tf_op jit(solution)/shard_map/ppermute | solution.py:301
  2.9 4.1 %collective-permute-start = (bf16[8,2048]{1,0:T(8,128)(2,1)}, bf16[8,2048]{1,0:T(8,128)(2,1)S(1)}, u32[]{:S(2)}, u32[]{:S(2)}) collective-permute-start(bf16[8,2048]{1,0:T(8,128)(2,1)} %refs_0_.3), channel_id=1, source_target_pairs={{0,1},{1,0},{2,3},{3,2},{4,5},{5,4},{6,7},{7,6},{8,9},{9,8},{10,11... | collective-permute-start | bytes 98312 | tf_op jit(solution)/shard_map/ppermute | solution.py:301
  7.8 10.0 %collective-permute-start.2 = (bf16[2,8,2048]{2,1,0:T(8,128)(2,1)S(1)}, bf16[2,8,2048]{2,1,0:T(8,128)(2,1)S(1)}, u32[]{:S(2)}, u32[]{:S(2)}) collective-permute-start(bf16[2,8,2048]{2,1,0:T(8,128)(2,1)S(1)} %stack_pieces.3.refs_0_), channel_id=1, source_target_pairs={{0,2},{1,3},{2,0},{3,1},{4,6},{5,7},{6,4},{7,5},{8,10},{9,11},{10,... | collective-permute-start | bytes 196616 | tf_op jit(solution)/shard_map/ppermute | solution.py:301
  10.4 4.8 %collective-permute-start.3 = (bf16[8,2048]{1,0:T(8,128)(2,1)}, bf16[8,2048]{1,0:T(8,128)(2,1)S(1)}, u32[]{:S(2)}, u32[]{:S(2)}) collective-permute-start(bf16[8,2048]{1,0:T(8,128)(2,1)} %refs_0_.3), channel_id=1, source_target_pairs={{0,16},{4,20},{8,24},{12,28},{16,0},{20,4},{24,8},{28,12},{1,17},{... | collective-permute-start | bytes 98312 | tf_op jit(solution)/shard_map/ppermute | solution.py:301
  11.9 5.0 %collective-permute-start.4 = (bf16[8,2048]{1,0:T(8,128)(2,1)}, bf16[8,2048]{1,0:T(8,128)(2,1)S(1)}, u32[]{:S(2)}, u32[]{:S(2)}) collective-permute-start(bf16[8,2048]{1,0:T(8,128)(2,1)} %refs_0_.3), channel_id=1, source_target_pairs={{0,24},{4,28},{8,16},{12,20},{16,8},{20,12},{24,0},{28,4},{1,25},{... | collective-permute-start | bytes 98312 | tf_op jit(solution)/shard_map/ppermute | solution.py:301
  13.1 1.4 %copy-start = (bf16[192,4096]{1,0:T(8,128)(2,1)S(1)}, bf16[192,4096]{1,0:T(8,128)(2,1)}, u32[]{:S(2)}) copy-start(bf16[192,4096]{1,0:T(8,128)(2,1)} %param.9) | copy-start | bytes 4718596
  15.2 2.7 %copy-start.3 = (bf16[128,512]{1,0:T(8,128)(2,1)S(1)}, bf16[128,512]{1,0:T(8,128)(2,1)}, u32[]{:S(2)}) copy-start(bf16[128,512]{1,0:T(8,128)(2,1)} %constant.4.clone.spread_ref) | copy-start | bytes 393220
  15.2 2.7 %copy-start.4 = (s32[192]{0:T(256)S(1)}, s32[192]{0:T(256)}, u32[]{:S(2)}) copy-start(s32[192]{0:T(256)} %rows_ref.3) | copy-start | bytes 2308
  15.2 2.7 %copy-start.5 = (s32[192]{0:T(256)S(1)}, s32[192]{0:T(256)}, u32[]{:S(2)}) copy-start(s32[192]{0:T(256)} %cols_ref.3) | copy-start | bytes 2308
  17.7 3.2 %copy-start.1 = (bf16[512,128]{1,0:T(8,128)(2,1)S(1)}, bf16[512,128]{1,0:T(8,128)(2,1)}, u32[]{:S(2)}) copy-start(bf16[512,128]{1,0:T(8,128)(2,1)} %constant.7.fold_ref) | copy-start | bytes 393220
  17.7 3.2 %copy-start.2 = (bf16[128,512]{1,0:T(8,128)(2,1)S(1)}, bf16[128,512]{1,0:T(8,128)(2,1)}, u32[]{:S(2)}) copy-start(bf16[128,512]{1,0:T(8,128)(2,1)} %constant.5.clone.spread_ref) | copy-start | bytes 393220
  17.8 3.1 %collective-permute-start.9 = (bf16[4,8,2048]{2,1,0:T(8,128)(2,1)S(1)}, bf16[4,8,2048]{2,1,0:T(8,128)(2,1)S(1)}, u32[]{:S(2)}, u32[]{:S(2)}) collective-permute-start(bf16[4,8,2048]{2,1,0:T(8,128)(2,1)S(1)} %stack_pieces.5.after_ref.same_ref), channel_id=1, source_target_pairs={{0,4},{4,0},{8,12},{12,8},{16,20},{20,16},{24,28},{28,24},{1,5},{5... | collective-permute-start | bytes 393224 | tf_op jit(solution)/shard_map/ppermute | solution.py:301
  20.0 5.1 %collective-permute-start.5 = (f32[4,8,2048]{2,1,0:T(8,128)S(1)}, f32[4,8,2048]{2,1,0:T(8,128)S(1)}, u32[]{:S(2)}, u32[]{:S(2)}) collective-permute-start(f32[4,8,2048]{2,1,0:T(8,128)S(1)} %get-tuple-element.15.after_ref), channel_id=1, source_target_pairs={{0,4},{4,0},{8,12},{12,8},{16,20},{20,16},{24,28},{28,24},{1,5},{5... | collective-permute-start | bytes 786440 | tf_op jit(solution)/shard_map/ppermute | solution.py:301
  23.6 5.7 %collective-permute-start.10 = (f32[2,8,2048]{2,1,0:T(8,128)S(1)}, f32[2,8,2048]{2,1,0:T(8,128)S(1)}, u32[]{:S(2)}, u32[]{:S(2)}) collective-permute-start(f32[2,8,2048]{2,1,0:T(8,128)S(1)} %get-tuple-element.20), channel_id=1, source_target_pairs={{0,1},{1,0},{2,3},{3,2},{4,5},{5,4},{6,7},{7,6},{8,9},{9,8},{10,11... | collective-permute-start | bytes 393224 | tf_op jit(solution)/shard_map/ppermute | solution.py:301
  25.1 5.0 %collective-permute-start.7 = (f32[8,2048]{1,0:T(8,128)S(1)}, f32[8,2048]{1,0:T(8,128)S(1)}, u32[]{:S(2)}, u32[]{:S(2)}) collective-permute-start(f32[8,2048]{1,0:T(8,128)S(1)} %get-tuple-element.17), channel_id=1, source_target_pairs={{0,16},{4,20},{8,24},{12,28},{16,0},{20,4},{24,8},{28,12},{1,17},{... | collective-permute-start | bytes 196616 | tf_op jit(solution)/shard_map/ppermute | solution.py:301
  25.7 5.2 %collective-permute-start.8 = (f32[8,2048]{1,0:T(8,128)S(1)}, f32[8,2048]{1,0:T(8,128)S(1)}, u32[]{:S(2)}, u32[]{:S(2)}) collective-permute-start(f32[8,2048]{1,0:T(8,128)S(1)} %get-tuple-element.18), channel_id=1, source_target_pairs={{0,24},{4,28},{8,16},{12,20},{16,8},{20,12},{24,0},{28,4},{1,25},{... | collective-permute-start | bytes 196616 | tf_op jit(solution)/shard_map/ppermute | solution.py:301
  27.5 4.3 %collective-permute-start.6 = (f32[8,2048]{1,0:T(8,128)S(1)}, f32[8,2048]{1,0:T(8,128)S(1)}, u32[]{:S(2)}, u32[]{:S(2)}) collective-permute-start(f32[8,2048]{1,0:T(8,128)S(1)} %get-tuple-element.16.after_ref), channel_id=1, source_target_pairs={{0,8},{4,12},{8,0},{12,4},{16,24},{20,28},{24,16},{28,20},{1,9},{5... | collective-permute-start | bytes 196616 | tf_op jit(solution)/shard_map/ppermute | solution.py:301
  29.3 5.2 %collective-permute-start.11 = (f32[1,8,2048]{2,1,0:T(8,128)S(1)}, f32[1,8,2048]{2,1,0:T(8,128)S(1)}, u32[]{:S(2)}, u32[]{:S(2)}) collective-permute-start(f32[1,8,2048]{2,1,0:T(8,128)S(1)} %get-tuple-element.22), channel_id=1, source_target_pairs={{0,2},{1,3},{2,0},{3,1},{4,6},{5,7},{6,4},{7,5},{8,10},{9,11},{10,... | collective-permute-start | bytes 196616 | tf_op jit(solution)/shard_map/ppermute | solution.py:301

commit v3 on v2

--- a/solution.py
+++ b/solution.py
@@ -1,3 +1,5 @@
+import functools
+
 import jax
 import jax.numpy as jnp
 import numpy as np
@@ -63,10 +65,18 @@
     )(view)
 
 
+def doubled(size):
+    order, d = [0], size // 2
+    while d > 1:
+        order += [x ^ d for x in order]
+        d //= 2
+    return order
+
+
 def build_table(pieces, spread, table):
-    width, piece = pieces[0].shape
+    width, piece = pieces[0][1].shape
     pairs = piece // LANES
-    for n, ref in enumerate(pieces):
+    for n, ref in pieces:
         rows = jnp.concatenate([ref[:, p * LANES : (p + 1) * LANES] for p in range(pairs)], axis=0)
         wide = jnp.dot(rows, spread, preferred_element_type=F32)
         wide = wide.reshape(pairs, width, 4 * LANES)
@@ -78,12 +88,11 @@
                 table[n * 2 * pairs + 2 * p + q] = both[p]
 
 
-def backward_kernel(
-    rows_ref, cols_ref, count_ref, spread_ref, tiles_ref, seg_ref, after_ref, keep_ref, give_ref, table, acc
-):
-    pieces = [seg_ref.at[n] for n in range(seg_ref.shape[0])]
+def backward_kernel(n_in, rows_ref, cols_ref, count_ref, spread_ref, tiles_ref, *refs):
+    pieces = list(enumerate(refs[:n_in]))
+    _, keep_ref, give_ref, table, acc = refs[n_in:]
     n_out = 2 * keep_ref.shape[0]
-    width, piece = pieces[0].shape
+    width, piece = pieces[0][1].shape
     per_piece = piece // TILE
     slots = tiles_ref.shape[0]
     build_table(pieces, spread_ref[...], table)
@@ -117,13 +126,14 @@
             )
 
 
-def backward(segment, tiles, tile_rows, tile_cols, counts, n_out, after):
-    n_in, width, piece = segment.shape
+def backward(pieces, tiles, tile_rows, tile_cols, counts, n_out, after):
+    n_in = len(pieces)
+    width, piece = pieces[0].shape
     per_piece = piece // TILE
     half = jax.ShapeDtypeStruct((n_out // 2, width, piece), F32)
     return pl.pallas_call(
-        backward_kernel,
-        in_specs=[SMEM] * 3 + [VMEM] * 3 + [ANY],
+        functools.partial(backward_kernel, n_in),
+        in_specs=[SMEM] * 3 + [VMEM] * (2 + n_in) + [ANY],
         out_specs=[VMEM] * 2,
         out_shape=[half, half],
         scratch_shapes=[
@@ -132,10 +142,10 @@
         ],
         compiler_params=PARAMS,
         cost_estimate=pl.CostEstimate(
-            flops=2 * tiles.size * 64, bytes_accessed=4 * tiles.size, transcendentals=0
+            flops=2 * tiles.size * 64, bytes_accessed=12 * tiles.size, transcendentals=0
         ),
         name="transpose_product",
-    )(tile_rows, tile_cols, counts, row_spread(), tiles, segment, after)
+    )(tile_rows, tile_cols, counts, row_spread(), tiles, *pieces, after)
 
 
 def forward_kernel(
@@ -148,14 +158,14 @@
     same_ref,
     other_ref,
     after_ref,
-    keep_ref,
-    give_ref,
-    table,
-    acc,
+    *refs,
 ):
-    pieces = [ref.at[h] for h in range(same_ref.shape[0]) for ref in (same_ref, other_ref)]
-    n_out = 2 * keep_ref.shape[0]
-    width, piece = pieces[0].shape
+    outs, table, acc = refs[:-2], refs[-2], refs[-1]
+    pieces = []
+    for at, d in enumerate(doubled(2 * same_ref.shape[0])):
+        pieces += [(d, same_ref.at[at]), (d + 1, other_ref.at[at])]
+    n_out = len(outs)
+    width, piece = pieces[0][1].shape
     per_piece = piece // TILE
     slots = tiles_ref.shape[0]
     build_table(pieces, spread_ref[...], table)
@@ -194,35 +204,33 @@
         rest = (wide - first.astype(F32)).astype(BF16)
         out = jnp.dot(first, fold, preferred_element_type=F32)
         out = out + jnp.dot(rest, fold, preferred_element_type=F32)
-        dest = (keep_ref if n % 2 == 0 else give_ref).at[n // 2]
         for p in range(pairs):
-            dest[:, p * LANES : (p + 1) * LANES] = out[p * width : (p + 1) * width]
+            outs[n][:, p * LANES : (p + 1) * LANES] = out[p * width : (p + 1) * width]
 
 
 def forward(same, other, tiles, tile_rows, tile_cols, counts, n_out, after):
     n_chips, width, piece = same.shape
     per_piece = piece // TILE
-    half = jax.ShapeDtypeStruct((n_out // 2, width, piece), F32)
     return pl.pallas_call(
         forward_kernel,
         in_specs=[SMEM] * 3 + [VMEM] * 5 + [ANY],
-        out_specs=[VMEM] * 2,
-        out_shape=[half, half],
+        out_specs=[VMEM] * n_out,
+        out_shape=[jax.ShapeDtypeStruct((width, piece), F32)] * n_out,
         scratch_shapes=[
             pltpu.VMEM((2 * n_chips * per_piece, 2 * width, LANES), BF16),
             pltpu.VMEM((n_out * per_piece + 1, 2 * width, LANES), F32),
         ],
         compiler_params=PARAMS,
         cost_estimate=pl.CostEstimate(
-            flops=2 * tiles.size * 64, bytes_accessed=4 * tiles.size, transcendentals=0
+            flops=2 * tiles.size * 64, bytes_accessed=12 * tiles.size, transcendentals=0
         ),
         name="forward_product",
     )(tile_rows, tile_cols, counts, col_spread(), row_fold(), tiles, same, other, after)
 
 
-def stack_kernel(*refs):
+def stack_kernel(n_after, *refs):
     out_ref, at = refs[-1], 0
-    for ref in refs[:-2]:
+    for ref in refs[: -1 - n_after]:
         if len(ref.shape) == 2:
             out_ref[at] = ref[...]
             at += 1
@@ -231,33 +239,16 @@
             at += ref.shape[0]
 
 
-def stack(*parts, after):
+def stack(*parts, after=()):
     total = sum(x.shape[0] if x.ndim == 3 else 1 for x in parts)
     return pl.pallas_call(
-        stack_kernel,
-        in_specs=[VMEM] * len(parts) + [ANY],
+        functools.partial(stack_kernel, len(after)),
+        in_specs=[VMEM] * len(parts) + [ANY] * len(after),
         out_specs=VMEM,
         out_shape=jax.ShapeDtypeStruct((total,) + parts[0].shape[-2:], parts[0].dtype),
         compiler_params=PARAMS,
         name="stack_pieces",
-    )(*parts, after)
-
-
-def pair_sum_kernel(keep_ref, got_ref, *outs):
-    for h, out in enumerate(outs):
-        out[...] = keep_ref[h + 1] + got_ref[h + 1]
-
-
-def pair_sum(keep, got):
-    parts, width, piece = keep.shape
-    return pl.pallas_call(
-        pair_sum_kernel,
-        in_specs=[VMEM] * 2,
-        out_specs=[VMEM] * (parts - 1),
-        out_shape=[jax.ShapeDtypeStruct((width, piece), F32)] * (parts - 1),
-        compiler_params=PARAMS,
-        name="core_pair_sum",
-    )(keep, got)
+    )(*parts, *after)
 
 
 def split_sum_kernel(keep_ref, got_ref, after_ref, next_keep, next_give):
@@ -304,27 +295,26 @@
 def body(vectors, tiles, tile_rows, tile_cols, counts):
     n_rows = lax.axis_size("brow")
     n_cols = lax.axis_size("bcol")
-    chips = [swap(vectors, "brow", n_rows, 2 * h) for h in range(1, n_rows // 2)]
-    row_seg, d = vectors, 1
-    while d < n_cols:
-        row_seg = stack(row_seg, swap(row_seg, "bcol", n_cols, d), after=chips[0])
+    own = stack(vectors)
+    row_pieces = [own[0]] + [swap(vectors, "bcol", n_cols, d) for d in range(1, n_cols)]
+    blocks = prep(tiles)
+    same, got, d = own, swap(vectors, "brow", n_rows, n_rows // 2), n_rows // 2
+    while d > 1:
+        same = stack(same, got, after=(row_pieces[-1], blocks))
+        d //= 2
+        got = swap(same, "brow", n_rows, d)
+    other = got
+
+    keep, give = backward(row_pieces, blocks, tile_rows, tile_cols, counts, n_rows, other)
+    mine = forward(same, other, blocks, tile_rows, tile_cols, counts, n_cols, give)
+    got, d = swap(give, "brow", n_rows, 1), 2
+    while d < n_rows:
+        keep, give = split_sum(keep, got, mine[0])
+        got = swap(give, "brow", n_rows, d)
         d *= 2
-    blocks = prep(tiles)
-    same = stack(vectors, *chips, after=blocks)
-    other = swap(same, "brow", n_rows, 1)
-
-    col_keep, col_give = backward(row_seg, blocks, tile_rows, tile_cols, counts, n_rows, same)
-    row_keep, give = forward(same, other, blocks, tile_rows, tile_cols, counts, n_cols, col_give)
-    col_got = swap(col_give, "brow", n_rows, 1)
-    sums = pair_sum(col_keep, col_got)
-    from_chips = [swap(x, "brow", n_rows, 2 * (h + 1)) for h, x in enumerate(sums)]
-    row_got, d = swap(give, "bcol", n_cols, 1), 2
-    while d < n_cols:
-        row_keep, give = split_sum(row_keep, row_got, sums[0])
-        row_got = swap(give, "bcol", n_cols, d)
-        d *= 2
-    total = sum_pieces(col_keep[0] + col_got[0], *from_chips)
-    return total + (row_keep[0] + row_got[0])
+    from_rows = [swap(mine[d], "bcol", n_cols, d) for d in range(1, n_cols)]
+    total = sum_pieces(mine[0], *from_rows)
+    return total + (keep[0] + got[0])
 
 
 def solution(mesh):

time: 35.3 us -> 35.8 us (1.014)
  starting transfers between devices: 15.6 us -> 17.2 us
  waiting for transfers between devices: 9.61 us -> 8.61 us
  Pallas kernels: 7.05 us -> 6.13 us
  local copies, waits for them, and re-layouts: 1.44 us -> 2.23 us
    ppermute x12, starting transfers between devices: 15.6 us -> 17.2 us  [swap(): return lax.ppermute(x, axis, [(i, i ^ d) for i in range(size)])]
    pallas_call x5 -> x4, Pallas kernels: 3.66 us -> 2.49 us  [the longest x1 2.47 us: backward(): pl.pallas_call(functools.partial(backward_kernel, n_in), in_specs=[SMEM]...]
    ppermute x12, waiting for transfers between devices: 9.61 us -> 8.61 us  [swap(): return lax.ppermute(x, axis, [(i, i ^ d) for i in range(size)])]
    unnamed x12 -> x14, local copies, waits for them, and re-layouts: 1.44 us -> 2.23 us
  transfers between devices with their start and end apart: 12 -> 12, of which waited for: 8 -> 4; matrix products, arithmetic and copies ran while one was open for 0% -> 0% of each run, Pallas kernels for 18% -> 10%
where the time goes in v3:
time: 35.8 us; the launch traced here: 35.7 us
  starting transfers between devices  17.2 us (48%)
  waiting for transfers between devices  8.61 us (24%)
  Pallas kernels  6.13 us (17%)
  local copies, waits for them, and re-layouts  2.23 us (6%)
  between operations  0.83 us (2%)
  other arithmetic  0.64 us (2%)
    ppermute x12, starting transfers between devices, swap(): return lax.ppermute(x, axis, [(i, i ^ d) for i in range(size)])  17.2 us
    ppermute x12, waiting for transfers between devices, swap(): return lax.ppermute(x, axis, [(i, i ^ d) for i in range(size)])  8.61 us
    pallas_call x1, Pallas kernels, forward(): pl.pallas_call(forward_kernel, in_specs=[SMEM] * 3 + [VMEM] * 5 + [ANY],...  2.88 us
    pallas_call x1, Pallas kernels, backward(): pl.pallas_call(functools.partial(backward_kernel, n_in), in_specs=[SMEM]...  2.47 us
    unnamed x14, local copies, waits for them, and re-layouts  2.23 us
  transfers between devices with their start and end apart: 12, of which 4 were waited for; matrix products, arithmetic and copies ran while one was open for 0% of the time, Pallas kernels for 10%

profile of v3, /device:TPU:0, one launch (start us, length us, event | category | flops | bytes accessed | tf_op | source)
XLA Modules:
  0.0 35.7 jit_solution(17857145538500625479)
XLA Ops:
  0.0 5.0 %collective-permute-start.1 = (bf16[8,2048]{1,0:T(8,128)(2,1)}, bf16[8,2048]{1,0:T(8,128)(2,1)S(1)}, u32[]{:S(2)}, u32[]{:S(2)}) collective-permute-start(bf16[8,2048]{1,0:T(8,128)(2,1)} %refs_0_.1), channel_id=1, source_target_pairs={{0,3},{1,2},{2,1},{3,0},{4,7},{5,6},{6,5},{7,4},{8,11},{9,10},{10,... | collective-permute-start | bytes 98312 | tf_op jit(solution)/shard_map/ppermute | solution.py:292
  5.0 1.5 %collective-permute-start = (bf16[8,2048]{1,0:T(8,128)(2,1)}, bf16[8,2048]{1,0:T(8,128)(2,1)S(1)}, u32[]{:S(2)}, u32[]{:S(2)}) collective-permute-start(bf16[8,2048]{1,0:T(8,128)(2,1)} %refs_0_.1), channel_id=1, source_target_pairs={{0,16},{4,20},{8,24},{12,28},{16,0},{20,4},{24,8},{28,12},{1,17},{... | collective-permute-start | bytes 98312 | tf_op jit(solution)/shard_map/ppermute | solution.py:292
  6.6 0.8 %copy-done.4 = bf16[8,2048]{1,0:T(8,128)(2,1)S(1)} copy-done((bf16[8,2048]{1,0:T(8,128)(2,1)S(1)}, bf16[8,2048]{1,0:T(8,128)(2,1)}, u32[]{:S(2)}) %copy-start.4) | copy-done | bytes 32792
  7.4 1.4 %copy-done = bf16[192,4096]{1,0:T(8,128)(2,1)S(1)} copy-done((bf16[192,4096]{1,0:T(8,128)(2,1)S(1)}, bf16[192,4096]{1,0:T(8,128)(2,1)}, u32[]{:S(2)}) %copy-start) | copy-done | bytes 1572888
  8.8 0.7 %prep_tiles.1.refs_3_.tiles_ref = bf16[192,32,128]{2,1,0:T(8,128)(2,1)S(1)} custom-call(bf16[24,32,8,128]{3,2,1,0:T(8,128)(2,1)S(1)} %bitcast.6), custom_call_target="tpu_custom_call" | custom-call | bytes 3145728 | tf_op jit(solution)/shard_map/prep_tiles/pallas_call | solution.py:56
  9.5 0.0 copy-start.3
  9.5 0.0 copy-start.5
  9.5 0.0 copy-start.6
  9.5 0.0 collective-permute-done.1.refs_2_.refs_3_
  9.5 0.0 collective-permute-done.refs_1_
  9.5 0.0 copy-start.1
  9.6 0.0 copy-start.2
  9.6 1.6 %collective-permute-start.2 = (bf16[2,8,2048]{2,1,0:T(8,128)(2,1)S(1)}, bf16[2,8,2048]{2,1,0:T(8,128)(2,1)S(1)}, u32[]{:S(2)}, u32[]{:S(2)}) collective-permute-start(bf16[2,8,2048]{2,1,0:T(8,128)(2,1)S(1)} %stack_pieces.4.refs_0_), channel_id=1, source_target_pairs={{0,8},{4,12},{8,0},{12,4},{16,24},{20,28},{24,16},{28,20},{1,9},{5... | collective-permute-start | bytes 196616 | tf_op jit(solution)/shard_map/ppermute | solution.py:292
  11.1 2.8 %collective-permute-done.2.refs_1_ = bf16[2,8,2048]{2,1,0:T(8,128)(2,1)S(1)} collective-permute-done((bf16[2,8,2048]{2,1,0:T(8,128)(2,1)S(1)}, bf16[2,8,2048]{2,1,0:T(8,128)(2,1)S(1)}, u32[]{:S(2)}, u32[]{:S(2)}) %collective-permute-start.2) | collective-permute-done | bytes 65568 | tf_op jit(solution)/shard_map/ppermute | solution.py:292
  13.9 0.1 collective-permute-start.3
  14.0 0.1 collective-permute-start.5
  14.1 2.0 %collective-permute-start.4 = (bf16[8,2048]{1,0:T(8,128)(2,1)S(1)}, bf16[8,2048]{1,0:T(8,128)(2,1)S(1)}, u32[]{:S(2)}, u32[]{:S(2)}) collective-permute-start(bf16[8,2048]{1,0:T(8,128)(2,1)S(1)} %copy-done.4), channel_id=1, source_target_pairs={{0,1},{1,0},{2,3},{3,2},{4,5},{5,4},{6,7},{7,6},{8,9},{9,8},{10,11... | collective-permute-start | bytes 98312 | tf_op jit(solution)/shard_map/ppermute | solution.py:292
  16.7 2.2 %collective-permute-done.5.refs_2_ = bf16[8,2048]{1,0:T(8,128)(2,1)S(1)} collective-permute-done((bf16[8,2048]{1,0:T(8,128)(2,1)S(1)}, bf16[8,2048]{1,0:T(8,128)(2,1)S(1)}, u32[]{:S(2)}, u32[]{:S(2)}) %collective-permute-start.5) | collective-permute-done | bytes 32800 | tf_op jit(solution)/shard_map/ppermute | solution.py:292
  18.9 0.0 collective-permute-done.4.refs_1_
  18.9 0.0 collective-permute-done.3.refs_4_.other_ref
  18.9 2.5 %transpose_product.1 = (f32[4,8,2048]{2,1,0:T(8,128)S(1)}, f32[4,8,2048]{2,1,0:T(8,128)S(1)}) custom-call(s32[192]{0:T(256)S(1)} %copy-done.5, s32[192]{0:T(256)S(1)} %copy-done.6, s32[1,1]{1,0:T(1,128)S(6)} %copy.9.count_ref, bf16[128,512]{1,0:T(8,128)(2,1)S(1)} %copy-done.3, bf16[192,32,128]{2,1,0:T(8,128)(2,1)S(1)} %prep_tiles.1.refs_3_.tiles_ref, ...), custom_call_target="tpu_custom_call" | custom-call | flops 100663296 | bytes 9437184 | tf_op jit(solution)/shard_map/transpose_product/pallas_call | solution.py:134
  21.4 0.1 collective-permute-start.9
  21.5 2.9 %forward_product.1 = (f32[8,2048]{1,0:T(8,128)S(1)}, f32[8,2048]{1,0:T(8,128)S(1)}, f32[8,2048]{1,0:T(8,128)S(1)}, f32[8,2048]{1,0:T(8,128)S(1)}) custom-call(s32[192]{0:T(256)S(1)} %copy-done.5, s32[192]{0:T(256)S(1)} %copy-done.6, s32[1,1]{1,0:T(1,128)S(6)} %copy.9.count_ref, bf16[128,512]{1,0:T(8,128)(2,1)S(1)} %copy-done.2, ...), custom_call_target="tpu_custom_call" | custom-call | flops 100663296 | bytes 9437184 | tf_op jit(solution)/shard_map/forward_product/pallas_call | solution.py:214
  24.4 1.0 %collective-permute-start.10 = (f32[2,8,2048]{2,1,0:T(8,128)S(1)}, f32[2,8,2048]{2,1,0:T(8,128)S(1)}, u32[]{:S(2)}, u32[]{:S(2)}) collective-permute-start(f32[2,8,2048]{2,1,0:T(8,128)S(1)} %get-tuple-element.22), channel_id=1, source_target_pairs={{0,8},{4,12},{8,0},{12,4},{16,24},{20,28},{24,16},{28,20},{1,9},{5... | collective-permute-start | bytes 393224 | tf_op jit(solution)/shard_map/ppermute | solution.py:292
  25.4 1.4 %collective-permute-start.6 = (f32[8,2048]{1,0:T(8,128)S(1)}, f32[8,2048]{1,0:T(8,128)S(1)}, u32[]{:S(2)}, u32[]{:S(2)}) collective-permute-start(f32[8,2048]{1,0:T(8,128)S(1)} %get-tuple-element.17), channel_id=1, source_target_pairs={{0,1},{1,0},{2,3},{3,2},{4,5},{5,4},{6,7},{7,6},{8,9},{9,8},{10,11... | collective-permute-start | bytes 196616 | tf_op jit(solution)/shard_map/ppermute | solution.py:292
  26.8 1.8 %collective-permute-start.7 = (f32[8,2048]{1,0:T(8,128)S(1)}, f32[8,2048]{1,0:T(8,128)S(1)}, u32[]{:S(2)}, u32[]{:S(2)}) collective-permute-start(f32[8,2048]{1,0:T(8,128)S(1)} %get-tuple-element.18), channel_id=1, source_target_pairs={{0,2},{1,3},{2,0},{3,1},{4,6},{5,7},{6,4},{7,5},{8,10},{9,11},{10,... | collective-permute-start | bytes 196616 | tf_op jit(solution)/shard_map/ppermute | solution.py:292
  28.5 1.3 %collective-permute-start.8 = (f32[8,2048]{1,0:T(8,128)S(1)}, f32[8,2048]{1,0:T(8,128)S(1)}, u32[]{:S(2)}, u32[]{:S(2)}) collective-permute-start(f32[8,2048]{1,0:T(8,128)S(1)} %get-tuple-element.19), channel_id=1, source_target_pairs={{0,3},{1,2},{2,1},{3,0},{4,7},{5,6},{6,5},{7,4},{8,11},{9,10},{10,... | collective-permute-start | bytes 196616 | tf_op jit(solution)/shard_map/ppermute | solution.py:292
  29.8 0.4 %collective-permute-done.10.got_ref = f32[2,8,2048]{2,1,0:T(8,128)S(1)} collective-permute-done((f32[2,8,2048]{2,1,0:T(8,128)S(1)}, f32[2,8,2048]{2,1,0:T(8,128)S(1)}, u32[]{:S(2)}, u32[]{:S(2)}) %collective-permute-start.10) | collective-permute-done | bytes 131104 | tf_op jit(solution)/shard_map/ppermute | solution.py:292
  30.2 1.5 %collective-permute-start.11 = (f32[1,8,2048]{2,1,0:T(8,128)S(1)}, f32[1,8,2048]{2,1,0:T(8,128)S(1)}, u32[]{:S(2)}, u32[]{:S(2)}) collective-permute-start(f32[1,8,2048]{2,1,0:T(8,128)S(1)} %get-tuple-element.24), channel_id=1, source_target_pairs={{0,16},{4,20},{8,24},{12,28},{16,0},{20,4},{24,8},{28,12},{1,17},{... | collective-permute-start | bytes 196616 | tf_op jit(solution)/shard_map/ppermute | solution.py:292
  31.8 3.2 %collective-permute-done.7.refs_2_ = f32[8,2048]{1,0:T(8,128)S(1)} collective-permute-done((f32[8,2048]{1,0:T(8,128)S(1)}, f32[8,2048]{1,0:T(8,128)S(1)}, u32[]{:S(2)}, u32[]{:S(2)}) %collective-permute-start.7) | collective-permute-done | bytes 65568 | tf_op jit(solution)/shard_map/ppermute | solution.py:292
  35.0 0.0 collective-permute-done.11
  35.0 0.6 %bitcast_add_fusion = f32[8,2048]{1,0:T(8,128)} fusion(f32[8,2048]{1,0:T(8,128)S(1)} %sum_pieces.1, f32[1,8,2048]{2,1,0:T(8,128)S(1)} %get-tuple-element.23, f32[1,8,2048]{2,1,0:T(8,128)S(1)} %collective-permute-done.11), kind=kLoop, calls=%fused_computation | loop fusion | flops 32768 | bytes 262144 | tf_op jit(solution)/shard_map/add | solution.py:317
  (16 shorter events, 0.1 us)
Async XLA Ops:
  0.0 9.5 %collective-permute-start.1 = (bf16[8,2048]{1,0:T(8,128)(2,1)}, bf16[8,2048]{1,0:T(8,128)(2,1)S(1)}, u32[]{:S(2)}, u32[]{:S(2)}) collective-permute-start(bf16[8,2048]{1,0:T(8,128)(2,1)} %refs_0_.1), channel_id=1, source_target_pairs={{0,3},{1,2},{2,1},{3,0},{4,7},{5,6},{6,5},{7,4},{8,11},{9,10},{10,... | collective-permute-start | bytes 98312 | tf_op jit(solution)/shard_map/ppermute | solution.py:292
  5.0 4.5 %collective-permute-start = (bf16[8,2048]{1,0:T(8,128)(2,1)}, bf16[8,2048]{1,0:T(8,128)(2,1)S(1)}, u32[]{:S(2)}, u32[]{:S(2)}) collective-permute-start(bf16[8,2048]{1,0:T(8,128)(2,1)} %refs_0_.1), channel_id=1, source_target_pairs={{0,16},{4,20},{8,24},{12,28},{16,0},{20,4},{24,8},{28,12},{1,17},{... | collective-permute-start | bytes 98312 | tf_op jit(solution)/shard_map/ppermute | solution.py:292
  6.6 0.8 %copy-start.4 = (bf16[8,2048]{1,0:T(8,128)(2,1)S(1)}, bf16[8,2048]{1,0:T(8,128)(2,1)}, u32[]{:S(2)}) copy-start(bf16[8,2048]{1,0:T(8,128)(2,1)} %refs_0_.1) | copy-start | bytes 98308
  7.4 1.4 %copy-start = (bf16[192,4096]{1,0:T(8,128)(2,1)S(1)}, bf16[192,4096]{1,0:T(8,128)(2,1)}, u32[]{:S(2)}) copy-start(bf16[192,4096]{1,0:T(8,128)(2,1)} %param.9) | copy-start | bytes 4718596
  9.5 9.4 %copy-start.3 = (bf16[128,512]{1,0:T(8,128)(2,1)S(1)}, bf16[128,512]{1,0:T(8,128)(2,1)}, u32[]{:S(2)}) copy-start(bf16[128,512]{1,0:T(8,128)(2,1)} %constant.4.clone.spread_ref) | copy-start | bytes 393220
  9.5 9.4 %copy-start.5 = (s32[192]{0:T(256)S(1)}, s32[192]{0:T(256)}, u32[]{:S(2)}) copy-start(s32[192]{0:T(256)} %rows_ref.3) | copy-start | bytes 2308
  9.5 9.4 %copy-start.6 = (s32[192]{0:T(256)S(1)}, s32[192]{0:T(256)}, u32[]{:S(2)}) copy-start(s32[192]{0:T(256)} %cols_ref.3) | copy-start | bytes 2308
  9.5 11.9 %copy-start.1 = (bf16[512,128]{1,0:T(8,128)(2,1)S(1)}, bf16[512,128]{1,0:T(8,128)(2,1)}, u32[]{:S(2)}) copy-start(bf16[512,128]{1,0:T(8,128)(2,1)} %constant.7.fold_ref) | copy-start | bytes 393220
  9.6 11.9 %copy-start.2 = (bf16[128,512]{1,0:T(8,128)(2,1)S(1)}, bf16[128,512]{1,0:T(8,128)(2,1)}, u32[]{:S(2)}) copy-start(bf16[128,512]{1,0:T(8,128)(2,1)} %constant.5.clone.spread_ref) | copy-start | bytes 393220
  9.6 4.3 %collective-permute-start.2 = (bf16[2,8,2048]{2,1,0:T(8,128)(2,1)S(1)}, bf16[2,8,2048]{2,1,0:T(8,128)(2,1)S(1)}, u32[]{:S(2)}, u32[]{:S(2)}) collective-permute-start(bf16[2,8,2048]{2,1,0:T(8,128)(2,1)S(1)} %stack_pieces.4.refs_0_), channel_id=1, source_target_pairs={{0,8},{4,12},{8,0},{12,4},{16,24},{20,28},{24,16},{28,20},{1,9},{5... | collective-permute-start | bytes 196616 | tf_op jit(solution)/shard_map/ppermute | solution.py:292
  13.9 5.0 %collective-permute-start.3 = (bf16[4,8,2048]{2,1,0:T(8,128)(2,1)S(1)}, bf16[4,8,2048]{2,1,0:T(8,128)(2,1)S(1)}, u32[]{:S(2)}, u32[]{:S(2)}) collective-permute-start(bf16[4,8,2048]{2,1,0:T(8,128)(2,1)S(1)} %stack_pieces.5.same_ref), channel_id=1, source_target_pairs={{0,4},{4,0},{8,12},{12,8},{16,20},{20,16},{24,28},{28,24},{1,5},{5... | collective-permute-start | bytes 393224 | tf_op jit(solution)/shard_map/ppermute | solution.py:292
  14.0 4.9 %collective-permute-start.5 = (bf16[8,2048]{1,0:T(8,128)(2,1)S(1)}, bf16[8,2048]{1,0:T(8,128)(2,1)S(1)}, u32[]{:S(2)}, u32[]{:S(2)}) collective-permute-start(bf16[8,2048]{1,0:T(8,128)(2,1)S(1)} %copy-done.4), channel_id=1, source_target_pairs={{0,2},{1,3},{2,0},{3,1},{4,6},{5,7},{6,4},{7,5},{8,10},{9,11},{10,... | collective-permute-start | bytes 98312 | tf_op jit(solution)/shard_map/ppermute | solution.py:292
  14.1 4.8 %collective-permute-start.4 = (bf16[8,2048]{1,0:T(8,128)(2,1)S(1)}, bf16[8,2048]{1,0:T(8,128)(2,1)S(1)}, u32[]{:S(2)}, u32[]{:S(2)}) collective-permute-start(bf16[8,2048]{1,0:T(8,128)(2,1)S(1)} %copy-done.4), channel_id=1, source_target_pairs={{0,1},{1,0},{2,3},{3,2},{4,5},{5,4},{6,7},{7,6},{8,9},{9,8},{10,11... | collective-permute-start | bytes 98312 | tf_op jit(solution)/shard_map/ppermute | solution.py:292
  21.4 3.0 %collective-permute-start.9 = (f32[4,8,2048]{2,1,0:T(8,128)S(1)}, f32[4,8,2048]{2,1,0:T(8,128)S(1)}, u32[]{:S(2)}, u32[]{:S(2)}) collective-permute-start(f32[4,8,2048]{2,1,0:T(8,128)S(1)} %get-tuple-element.15.after_ref), channel_id=1, source_target_pairs={{0,4},{4,0},{8,12},{12,8},{16,20},{20,16},{24,28},{28,24},{1,5},{5... | collective-permute-start | bytes 786440 | tf_op jit(solution)/shard_map/ppermute | solution.py:292
  24.4 5.8 %collective-permute-start.10 = (f32[2,8,2048]{2,1,0:T(8,128)S(1)}, f32[2,8,2048]{2,1,0:T(8,128)S(1)}, u32[]{:S(2)}, u32[]{:S(2)}) collective-permute-start(f32[2,8,2048]{2,1,0:T(8,128)S(1)} %get-tuple-element.22), channel_id=1, source_target_pairs={{0,8},{4,12},{8,0},{12,4},{16,24},{20,28},{24,16},{28,20},{1,9},{5... | collective-permute-start | bytes 393224 | tf_op jit(solution)/shard_map/ppermute | solution.py:292
  25.4 6.3 %collective-permute-start.6 = (f32[8,2048]{1,0:T(8,128)S(1)}, f32[8,2048]{1,0:T(8,128)S(1)}, u32[]{:S(2)}, u32[]{:S(2)}) collective-permute-start(f32[8,2048]{1,0:T(8,128)S(1)} %get-tuple-element.17), channel_id=1, source_target_pairs={{0,1},{1,0},{2,3},{3,2},{4,5},{5,4},{6,7},{7,6},{8,9},{9,8},{10,11... | collective-permute-start | bytes 196616 | tf_op jit(solution)/shard_map/ppermute | solution.py:292
  26.8 8.2 %collective-permute-start.7 = (f32[8,2048]{1,0:T(8,128)S(1)}, f32[8,2048]{1,0:T(8,128)S(1)}, u32[]{:S(2)}, u32[]{:S(2)}) collective-permute-start(f32[8,2048]{1,0:T(8,128)S(1)} %get-tuple-element.18), channel_id=1, source_target_pairs={{0,2},{1,3},{2,0},{3,1},{4,6},{5,7},{6,4},{7,5},{8,10},{9,11},{10,... | collective-permute-start | bytes 196616 | tf_op jit(solution)/shard_map/ppermute | solution.py:292
  28.5 6.5 %collective-permute-start.8 = (f32[8,2048]{1,0:T(8,128)S(1)}, f32[8,2048]{1,0:T(8,128)S(1)}, u32[]{:S(2)}, u32[]{:S(2)}) collective-permute-start(f32[8,2048]{1,0:T(8,128)S(1)} %get-tuple-element.19), channel_id=1, source_target_pairs={{0,3},{1,2},{2,1},{3,0},{4,7},{5,6},{6,5},{7,4},{8,11},{9,10},{10,... | collective-permute-start | bytes 196616 | tf_op jit(solution)/shard_map/ppermute | solution.py:292
  30.2 4.8 %collective-permute-start.11 = (f32[1,8,2048]{2,1,0:T(8,128)S(1)}, f32[1,8,2048]{2,1,0:T(8,128)S(1)}, u32[]{:S(2)}, u32[]{:S(2)}) collective-permute-start(f32[1,8,2048]{2,1,0:T(8,128)S(1)} %get-tuple-element.24), channel_id=1, source_target_pairs={{0,16},{4,20},{8,24},{12,28},{16,0},{20,4},{24,8},{28,12},{1,17},{... | collective-permute-start | bytes 196616 | tf_op jit(solution)/shard_map/ppermute | solution.py:292

commit v4 on v2

--- a/solution.py
+++ b/solution.py
@@ -1,3 +1,5 @@
+import functools
+
 import jax
 import jax.numpy as jnp
 import numpy as np
@@ -78,10 +80,9 @@
                 table[n * 2 * pairs + 2 * p + q] = both[p]
 
 
-def backward_kernel(
-    rows_ref, cols_ref, count_ref, spread_ref, tiles_ref, seg_ref, after_ref, keep_ref, give_ref, table, acc
-):
-    pieces = [seg_ref.at[n] for n in range(seg_ref.shape[0])]
+def backward_kernel(n_in, rows_ref, cols_ref, count_ref, spread_ref, tiles_ref, *refs):
+    pieces = refs[:n_in]
+    _, keep_ref, give_ref, table, acc = refs[n_in:]
     n_out = 2 * keep_ref.shape[0]
     width, piece = pieces[0].shape
     per_piece = piece // TILE
@@ -117,13 +118,14 @@
             )
 
 
-def backward(segment, tiles, tile_rows, tile_cols, counts, n_out, after):
-    n_in, width, piece = segment.shape
+def backward(pieces, tiles, tile_rows, tile_cols, counts, n_out, after):
+    n_in = len(pieces)
+    width, piece = pieces[0].shape
     per_piece = piece // TILE
     half = jax.ShapeDtypeStruct((n_out // 2, width, piece), F32)
     return pl.pallas_call(
-        backward_kernel,
-        in_specs=[SMEM] * 3 + [VMEM] * 3 + [ANY],
+        functools.partial(backward_kernel, n_in),
+        in_specs=[SMEM] * 3 + [VMEM] * (2 + n_in) + [ANY],
         out_specs=[VMEM] * 2,
         out_shape=[half, half],
         scratch_shapes=[
@@ -135,7 +137,7 @@
             flops=2 * tiles.size * 64, bytes_accessed=4 * tiles.size, transcendentals=0
         ),
         name="transpose_product",
-    )(tile_rows, tile_cols, counts, row_spread(), tiles, segment, after)
+    )(tile_rows, tile_cols, counts, row_spread(), tiles, *pieces, after)
 
 
 def forward_kernel(
@@ -220,9 +222,9 @@
     )(tile_rows, tile_cols, counts, col_spread(), row_fold(), tiles, same, other, after)
 
 
-def stack_kernel(*refs):
+def stack_kernel(n_after, *refs):
     out_ref, at = refs[-1], 0
-    for ref in refs[:-2]:
+    for ref in refs[: -1 - n_after]:
         if len(ref.shape) == 2:
             out_ref[at] = ref[...]
             at += 1
@@ -231,16 +233,16 @@
             at += ref.shape[0]
 
 
-def stack(*parts, after):
+def stack(*parts, after=()):
     total = sum(x.shape[0] if x.ndim == 3 else 1 for x in parts)
     return pl.pallas_call(
-        stack_kernel,
-        in_specs=[VMEM] * len(parts) + [ANY],
+        functools.partial(stack_kernel, len(after)),
+        in_specs=[VMEM] * len(parts) + [ANY] * len(after),
         out_specs=VMEM,
         out_shape=jax.ShapeDtypeStruct((total,) + parts[0].shape[-2:], parts[0].dtype),
         compiler_params=PARAMS,
         name="stack_pieces",
-    )(*parts, after)
+    )(*parts, *after)
 
 
 def pair_sum_kernel(keep_ref, got_ref, *outs):
@@ -304,16 +306,14 @@
 def body(vectors, tiles, tile_rows, tile_cols, counts):
     n_rows = lax.axis_size("brow")
     n_cols = lax.axis_size("bcol")
+    own = stack(vectors)
     chips = [swap(vectors, "brow", n_rows, 2 * h) for h in range(1, n_rows // 2)]
-    row_seg, d = vectors, 1
-    while d < n_cols:
-        row_seg = stack(row_seg, swap(row_seg, "bcol", n_cols, d), after=chips[0])
-        d *= 2
+    row_pieces = [own[0]] + [swap(vectors, "bcol", n_cols, d) for d in range(1, n_cols)]
     blocks = prep(tiles)
-    same = stack(vectors, *chips, after=blocks)
+    same = stack(own, *chips, after=(blocks, *row_pieces[1:]))
     other = swap(same, "brow", n_rows, 1)
 
-    col_keep, col_give = backward(row_seg, blocks, tile_rows, tile_cols, counts, n_rows, same)
+    col_keep, col_give = backward(row_pieces, blocks, tile_rows, tile_cols, counts, n_rows, same)
     row_keep, give = forward(same, other, blocks, tile_rows, tile_cols, counts, n_cols, col_give)
     col_got = swap(col_give, "brow", n_rows, 1)
     sums = pair_sum(col_keep, col_got)

time: 35.3 us -> 32 us (0.907)
  waiting for transfers between devices: 9.61 us -> 4.76 us
  Pallas kernels: 7.05 us -> 5.56 us
  starting transfers between devices: 15.6 us -> 17 us
  local copies, waits for them, and re-layouts: 1.44 us -> 2.76 us
    ppermute x12 -> x13, waiting for transfers between devices: 9.61 us -> 4.76 us  [swap(): return lax.ppermute(x, axis, [(i, i ^ d) for i in range(size)])]
    pallas_call x4 -> x3, Pallas kernels: 3.64 us -> 2.13 us  [the longest x1 2.12 us: backward(): pl.pallas_call(functools.partial(backward_kernel, n_in), in_specs=[SMEM]...]
    ppermute x12 -> x13, starting transfers between devices: 15.6 us -> 17 us  [swap(): return lax.ppermute(x, axis, [(i, i ^ d) for i in range(size)])]
    unnamed x12 -> x14, local copies, waits for them, and re-layouts: 1.44 us -> 2.76 us
  transfers between devices with their start and end apart: 12 -> 13, of which waited for: 8 -> 4; matrix products, arithmetic and copies ran while one was open for 0% -> 0% of each run, Pallas kernels for 18% -> 18%
where the time goes in v4:
time: 32 us; the launch traced here: 31.6 us
  starting transfers between devices  17 us (53%)
  Pallas kernels  5.56 us (17%)
  waiting for transfers between devices  4.76 us (15%)
  local copies, waits for them, and re-layouts  2.76 us (9%)
  between operations  0.83 us (3%)
  other arithmetic  0.65 us (2%)
    ppermute x13, starting transfers between devices, swap(): return lax.ppermute(x, axis, [(i, i ^ d) for i in range(size)])  17 us
    ppermute x13, waiting for transfers between devices, swap(): return lax.ppermute(x, axis, [(i, i ^ d) for i in range(size)])  4.76 us
    unnamed x14, local copies, waits for them, and re-layouts  2.76 us
    pallas_call x1, Pallas kernels, forward(): pl.pallas_call(forward_kernel, in_specs=[SMEM] * 3 + [VMEM] * 5 + [ANY],...  2.68 us
    pallas_call x1, Pallas kernels, backward(): pl.pallas_call(functools.partial(backward_kernel, n_in), in_specs=[SMEM]...  2.12 us
    pallas_call x1, Pallas kernels, prep(): pl.pallas_call(prep_kernel, in_specs=[VMEM], out_specs=VMEM, out_shape=ja...  0.69 us
    add x1, other arithmetic, body(): return total + (row_keep[0] + row_got[0])  0.64 us
  transfers between devices with their start and end apart: 13, of which 4 were waited for; matrix products, arithmetic and copies ran while one was open for 0% of the time, Pallas kernels for 18%

profile of v4, /device:TPU:0, one launch (start us, length us, event | category | flops | bytes accessed | tf_op | source)
XLA Modules:
  0.0 31.6 jit_solution(12459719444137807078)
XLA Ops:
  0.0 2.9 %collective-permute-start.3 = (bf16[8,2048]{1,0:T(8,128)(2,1)}, bf16[8,2048]{1,0:T(8,128)(2,1)S(1)}, u32[]{:S(2)}, u32[]{:S(2)}) collective-permute-start(bf16[8,2048]{1,0:T(8,128)(2,1)} %refs_0_.1), channel_id=1, source_target_pairs={{0,8},{4,12},{8,0},{12,4},{16,24},{20,28},{24,16},{28,20},{1,9},{5... | collective-permute-start | bytes 98312 | tf_op jit(solution)/shard_map/ppermute | solution.py:303
  2.9 3.6 %collective-permute-start.2 = (bf16[8,2048]{1,0:T(8,128)(2,1)}, bf16[8,2048]{1,0:T(8,128)(2,1)S(1)}, u32[]{:S(2)}, u32[]{:S(2)}) collective-permute-start(bf16[8,2048]{1,0:T(8,128)(2,1)} %refs_0_.1), channel_id=1, source_target_pairs={{0,3},{1,2},{2,1},{3,0},{4,7},{5,6},{6,5},{7,4},{8,11},{9,10},{10,... | collective-permute-start | bytes 98312 | tf_op jit(solution)/shard_map/ppermute | solution.py:303
  6.5 0.0 collective-permute-start.1
  6.5 0.8 %collective-permute-start = (bf16[8,2048]{1,0:T(8,128)(2,1)}, bf16[8,2048]{1,0:T(8,128)(2,1)S(1)}, u32[]{:S(2)}, u32[]{:S(2)}) collective-permute-start(bf16[8,2048]{1,0:T(8,128)(2,1)} %refs_0_.1), channel_id=1, source_target_pairs={{0,1},{1,0},{2,3},{3,2},{4,5},{5,4},{6,7},{7,6},{8,9},{9,8},{10,11... | collective-permute-start | bytes 98312 | tf_op jit(solution)/shard_map/ppermute | solution.py:303
  7.3 1.5 %collective-permute-start.5 = (bf16[8,2048]{1,0:T(8,128)(2,1)}, bf16[8,2048]{1,0:T(8,128)(2,1)S(1)}, u32[]{:S(2)}, u32[]{:S(2)}) collective-permute-start(bf16[8,2048]{1,0:T(8,128)(2,1)} %refs_0_.1), channel_id=1, source_target_pairs={{0,24},{4,28},{8,16},{12,20},{16,8},{20,12},{24,0},{28,4},{1,25},{... | collective-permute-start | bytes 98312 | tf_op jit(solution)/shard_map/ppermute | solution.py:303
  8.8 0.3 collective-permute-start.4
  9.1 0.8 %copy-done.4 = bf16[8,2048]{1,0:T(8,128)(2,1)S(1)} copy-done((bf16[8,2048]{1,0:T(8,128)(2,1)S(1)}, bf16[8,2048]{1,0:T(8,128)(2,1)}, u32[]{:S(2)}) %copy-start.4) | copy-done | bytes 32792
  10.6 0.0 copy-start
  10.6 1.4 %copy-done = bf16[192,4096]{1,0:T(8,128)(2,1)S(1)} copy-done((bf16[192,4096]{1,0:T(8,128)(2,1)S(1)}, bf16[192,4096]{1,0:T(8,128)(2,1)}, u32[]{:S(2)}) %copy-start) | copy-done | bytes 1572888
  12.0 0.7 %prep_tiles.1.refs_4_.tiles_ref = bf16[192,32,128]{2,1,0:T(8,128)(2,1)S(1)} custom-call(bf16[24,32,8,128]{3,2,1,0:T(8,128)(2,1)S(1)} %bitcast.8), custom_call_target="tpu_custom_call" | custom-call | bytes 3145728 | tf_op jit(solution)/shard_map/prep_tiles/pallas_call | solution.py:56
  12.7 0.0 copy-start.3
  12.7 0.0 copy-start.5
  12.7 0.0 copy-start.6
  12.7 0.0 copy-start.1
  12.7 0.0 copy-start.2
  12.7 0.0 collective-permute-done.2.refs_7_.refs_3_
  12.7 0.0 collective-permute-done.1.refs_6_.refs_2_
  12.8 0.2 collective-permute-done.4.refs_2_
  13.0 0.1 collective-permute-start.10
  13.0 0.5 %copy-done.3 = bf16[128,512]{1,0:T(8,128)(2,1)S(1)} copy-done((bf16[128,512]{1,0:T(8,128)(2,1)S(1)}, bf16[128,512]{1,0:T(8,128)(2,1)}, u32[]{:S(2)}) %copy-start.3) | copy-done | bytes 131096
  13.6 2.1 %transpose_product.1 = (f32[4,8,2048]{2,1,0:T(8,128)S(1)}, f32[4,8,2048]{2,1,0:T(8,128)S(1)}) custom-call(s32[192]{0:T(256)S(1)} %copy-done.5, s32[192]{0:T(256)S(1)} %copy-done.6, s32[1,1]{1,0:T(1,128)S(6)} %copy.9.count_ref, bf16[128,512]{1,0:T(8,128)(2,1)S(1)} %copy-done.3, bf16[192,32,128]{2,1,0:T(8,128)(2,1)S(1)} %prep_tiles.1.refs_4_.tiles_ref, ...), custom_call_target="tpu_custom_call" | custom-call | flops 100663296 | bytes 3145728 | tf_op jit(solution)/shard_map/transpose_product/pallas_call | solution.py:126
  15.7 0.1 collective-permute-start.6
  15.8 2.7 %forward_product.1 = (f32[2,8,2048]{2,1,0:T(8,128)S(1)}, f32[2,8,2048]{2,1,0:T(8,128)S(1)}) custom-call(s32[192]{0:T(256)S(1)} %copy-done.5, s32[192]{0:T(256)S(1)} %copy-done.6, s32[1,1]{1,0:T(1,128)S(6)} %copy.9.count_ref, bf16[128,512]{1,0:T(8,128)(2,1)S(1)} %copy-done.2, bf16[512,128]{1,0:T(8,128)(2,1)S(1)} %copy-done.1, ...), custom_call_target="tpu_custom_call" | custom-call | flops 100663296 | bytes 3145728 | tf_op jit(solution)/shard_map/forward_product/pallas_call | solution.py:208
  18.5 1.5 %collective-permute-start.11 = (f32[2,8,2048]{2,1,0:T(8,128)S(1)}, f32[2,8,2048]{2,1,0:T(8,128)S(1)}, u32[]{:S(2)}, u32[]{:S(2)}) collective-permute-start(f32[2,8,2048]{2,1,0:T(8,128)S(1)} %get-tuple-element.20), channel_id=1, source_target_pairs={{0,1},{1,0},{2,3},{3,2},{4,5},{5,4},{6,7},{7,6},{8,9},{9,8},{10,11... | collective-permute-start | bytes 393224 | tf_op jit(solution)/shard_map/ppermute | solution.py:303
  20.1 1.8 %collective-permute-start.8 = (f32[8,2048]{1,0:T(8,128)S(1)}, f32[8,2048]{1,0:T(8,128)S(1)}, u32[]{:S(2)}, u32[]{:S(2)}) collective-permute-start(f32[8,2048]{1,0:T(8,128)S(1)} %get-tuple-element.17), channel_id=1, source_target_pairs={{0,16},{4,20},{8,24},{12,28},{16,0},{20,4},{24,8},{28,12},{1,17},{... | collective-permute-start | bytes 196616 | tf_op jit(solution)/shard_map/ppermute | solution.py:303
  21.9 1.4 %collective-permute-start.9 = (f32[8,2048]{1,0:T(8,128)S(1)}, f32[8,2048]{1,0:T(8,128)S(1)}, u32[]{:S(2)}, u32[]{:S(2)}) collective-permute-start(f32[8,2048]{1,0:T(8,128)S(1)} %get-tuple-element.18), channel_id=1, source_target_pairs={{0,24},{4,28},{8,16},{12,20},{16,8},{20,12},{24,0},{28,4},{1,25},{... | collective-permute-start | bytes 196616 | tf_op jit(solution)/shard_map/ppermute | solution.py:303
  23.4 0.3 collective-permute-start.7
  23.6 0.8 %collective-permute-done.11.got_ref = f32[2,8,2048]{2,1,0:T(8,128)S(1)} collective-permute-done((f32[2,8,2048]{2,1,0:T(8,128)S(1)}, f32[2,8,2048]{2,1,0:T(8,128)S(1)}, u32[]{:S(2)}, u32[]{:S(2)}) %collective-permute-start.11) | collective-permute-done | bytes 131104 | tf_op jit(solution)/shard_map/ppermute | solution.py:303
  24.4 2.7 %collective-permute-start.12 = (f32[1,8,2048]{2,1,0:T(8,128)S(1)}, f32[1,8,2048]{2,1,0:T(8,128)S(1)}, u32[]{:S(2)}, u32[]{:S(2)}) collective-permute-start(f32[1,8,2048]{2,1,0:T(8,128)S(1)} %get-tuple-element.22), channel_id=1, source_target_pairs={{0,2},{1,3},{2,0},{3,1},{4,6},{5,7},{6,4},{7,5},{8,10},{9,11},{10,... | collective-permute-start | bytes 196616 | tf_op jit(solution)/shard_map/ppermute | solution.py:303
  27.2 0.5 %collective-permute-done.9.refs_3_ = f32[8,2048]{1,0:T(8,128)S(1)} collective-permute-done((f32[8,2048]{1,0:T(8,128)S(1)}, f32[8,2048]{1,0:T(8,128)S(1)}, u32[]{:S(2)}, u32[]{:S(2)}) %collective-permute-start.9) | collective-permute-done | bytes 65568 | tf_op jit(solution)/shard_map/ppermute | solution.py:303
  27.7 3.3 %collective-permute-done.12 = f32[1,8,2048]{2,1,0:T(8,128)S(1)} collective-permute-done((f32[1,8,2048]{2,1,0:T(8,128)S(1)}, f32[1,8,2048]{2,1,0:T(8,128)S(1)}, u32[]{:S(2)}, u32[]{:S(2)}) %collective-permute-start.12) | collective-permute-done | bytes 65568 | tf_op jit(solution)/shard_map/ppermute | solution.py:303
  31.0 0.6 %bitcast_add_fusion = f32[8,2048]{1,0:T(8,128)} fusion(f32[8,2048]{1,0:T(8,128)S(1)} %sum_pieces.1, f32[1,8,2048]{2,1,0:T(8,128)S(1)} %get-tuple-element.21, f32[1,8,2048]{2,1,0:T(8,128)S(1)} %collective-permute-done.12), kind=kLoop, calls=%fused_computation.2 | loop fusion | flops 32768 | bytes 262144 | tf_op jit(solution)/shard_map/add | solution.py:327
  (18 shorter events, 0.1 us)
Async XLA Ops:
  0.0 8.8 %collective-permute-start.3 = (bf16[8,2048]{1,0:T(8,128)(2,1)}, bf16[8,2048]{1,0:T(8,128)(2,1)S(1)}, u32[]{:S(2)}, u32[]{:S(2)}) collective-permute-start(bf16[8,2048]{1,0:T(8,128)(2,1)} %refs_0_.1), channel_id=1, source_target_pairs={{0,8},{4,12},{8,0},{12,4},{16,24},{20,28},{24,16},{28,20},{1,9},{5... | collective-permute-start | bytes 98312 | tf_op jit(solution)/shard_map/ppermute | solution.py:303
  2.9 9.8 %collective-permute-start.2 = (bf16[8,2048]{1,0:T(8,128)(2,1)}, bf16[8,2048]{1,0:T(8,128)(2,1)S(1)}, u32[]{:S(2)}, u32[]{:S(2)}) collective-permute-start(bf16[8,2048]{1,0:T(8,128)(2,1)} %refs_0_.1), channel_id=1, source_target_pairs={{0,3},{1,2},{2,1},{3,0},{4,7},{5,6},{6,5},{7,4},{8,11},{9,10},{10,... | collective-permute-start | bytes 98312 | tf_op jit(solution)/shard_map/ppermute | solution.py:303
  6.5 6.2 %collective-permute-start.1 = (bf16[8,2048]{1,0:T(8,128)(2,1)}, bf16[8,2048]{1,0:T(8,128)(2,1)S(1)}, u32[]{:S(2)}, u32[]{:S(2)}) collective-permute-start(bf16[8,2048]{1,0:T(8,128)(2,1)} %refs_0_.1), channel_id=1, source_target_pairs={{0,2},{1,3},{2,0},{3,1},{4,6},{5,7},{6,4},{7,5},{8,10},{9,11},{10,... | collective-permute-start | bytes 98312 | tf_op jit(solution)/shard_map/ppermute | solution.py:303
  6.5 6.2 %collective-permute-start = (bf16[8,2048]{1,0:T(8,128)(2,1)}, bf16[8,2048]{1,0:T(8,128)(2,1)S(1)}, u32[]{:S(2)}, u32[]{:S(2)}) collective-permute-start(bf16[8,2048]{1,0:T(8,128)(2,1)} %refs_0_.1), channel_id=1, source_target_pairs={{0,1},{1,0},{2,3},{3,2},{4,5},{5,4},{6,7},{7,6},{8,9},{9,8},{10,11... | collective-permute-start | bytes 98312 | tf_op jit(solution)/shard_map/ppermute | solution.py:303
  7.3 5.4 %collective-permute-start.5 = (bf16[8,2048]{1,0:T(8,128)(2,1)}, bf16[8,2048]{1,0:T(8,128)(2,1)S(1)}, u32[]{:S(2)}, u32[]{:S(2)}) collective-permute-start(bf16[8,2048]{1,0:T(8,128)(2,1)} %refs_0_.1), channel_id=1, source_target_pairs={{0,24},{4,28},{8,16},{12,20},{16,8},{20,12},{24,0},{28,4},{1,25},{... | collective-permute-start | bytes 98312 | tf_op jit(solution)/shard_map/ppermute | solution.py:303
  8.8 4.1 %collective-permute-start.4 = (bf16[8,2048]{1,0:T(8,128)(2,1)}, bf16[8,2048]{1,0:T(8,128)(2,1)S(1)}, u32[]{:S(2)}, u32[]{:S(2)}) collective-permute-start(bf16[8,2048]{1,0:T(8,128)(2,1)} %refs_0_.1), channel_id=1, source_target_pairs={{0,16},{4,20},{8,24},{12,28},{16,0},{20,4},{24,8},{28,12},{1,17},{... | collective-permute-start | bytes 98312 | tf_op jit(solution)/shard_map/ppermute | solution.py:303
  9.1 0.8 %copy-start.4 = (bf16[8,2048]{1,0:T(8,128)(2,1)S(1)}, bf16[8,2048]{1,0:T(8,128)(2,1)}, u32[]{:S(2)}) copy-start(bf16[8,2048]{1,0:T(8,128)(2,1)} %refs_0_.1) | copy-start | bytes 98308
  10.6 1.4 %copy-start = (bf16[192,4096]{1,0:T(8,128)(2,1)S(1)}, bf16[192,4096]{1,0:T(8,128)(2,1)}, u32[]{:S(2)}) copy-start(bf16[192,4096]{1,0:T(8,128)(2,1)} %param.9) | copy-start | bytes 4718596
  12.7 0.9 %copy-start.3 = (bf16[128,512]{1,0:T(8,128)(2,1)S(1)}, bf16[128,512]{1,0:T(8,128)(2,1)}, u32[]{:S(2)}) copy-start(bf16[128,512]{1,0:T(8,128)(2,1)} %constant.4.clone.spread_ref) | copy-start | bytes 393220
  12.7 0.9 %copy-start.5 = (s32[192]{0:T(256)S(1)}, s32[192]{0:T(256)}, u32[]{:S(2)}) copy-start(s32[192]{0:T(256)} %rows_ref.3) | copy-start | bytes 2308
  12.7 0.9 %copy-start.6 = (s32[192]{0:T(256)S(1)}, s32[192]{0:T(256)}, u32[]{:S(2)}) copy-start(s32[192]{0:T(256)} %cols_ref.3) | copy-start | bytes 2308
  12.7 3.1 %copy-start.1 = (bf16[512,128]{1,0:T(8,128)(2,1)S(1)}, bf16[512,128]{1,0:T(8,128)(2,1)}, u32[]{:S(2)}) copy-start(bf16[512,128]{1,0:T(8,128)(2,1)} %constant.7.fold_ref) | copy-start | bytes 393220
  12.7 3.1 %copy-start.2 = (bf16[128,512]{1,0:T(8,128)(2,1)S(1)}, bf16[128,512]{1,0:T(8,128)(2,1)}, u32[]{:S(2)}) copy-start(bf16[128,512]{1,0:T(8,128)(2,1)} %constant.5.clone.spread_ref) | copy-start | bytes 393220
  13.0 2.8 %collective-permute-start.10 = (bf16[4,8,2048]{2,1,0:T(8,128)(2,1)S(1)}, bf16[4,8,2048]{2,1,0:T(8,128)(2,1)S(1)}, u32[]{:S(2)}, u32[]{:S(2)}) collective-permute-start(bf16[4,8,2048]{2,1,0:T(8,128)(2,1)S(1)} %stack_pieces.3.refs_4_.same_ref), channel_id=1, source_target_pairs={{0,4},{4,0},{8,12},{12,8},{16,20},{20,16},{24,28},{28,24},{1,5},{5... | collective-permute-start | bytes 393224 | tf_op jit(solution)/shard_map/ppermute | solution.py:303
  15.7 4.3 %collective-permute-start.6 = (f32[4,8,2048]{2,1,0:T(8,128)S(1)}, f32[4,8,2048]{2,1,0:T(8,128)S(1)}, u32[]{:S(2)}, u32[]{:S(2)}) collective-permute-start(f32[4,8,2048]{2,1,0:T(8,128)S(1)} %get-tuple-element.15.after_ref), channel_id=1, source_target_pairs={{0,4},{4,0},{8,12},{12,8},{16,20},{20,16},{24,28},{28,24},{1,5},{5... | collective-permute-start | bytes 786440 | tf_op jit(solution)/shard_map/ppermute | solution.py:303
  18.5 5.9 %collective-permute-start.11 = (f32[2,8,2048]{2,1,0:T(8,128)S(1)}, f32[2,8,2048]{2,1,0:T(8,128)S(1)}, u32[]{:S(2)}, u32[]{:S(2)}) collective-permute-start(f32[2,8,2048]{2,1,0:T(8,128)S(1)} %get-tuple-element.20), channel_id=1, source_target_pairs={{0,1},{1,0},{2,3},{3,2},{4,5},{5,4},{6,7},{7,6},{8,9},{9,8},{10,11... | collective-permute-start | bytes 393224 | tf_op jit(solution)/shard_map/ppermute | solution.py:303
  20.1 7.1 %collective-permute-start.8 = (f32[8,2048]{1,0:T(8,128)S(1)}, f32[8,2048]{1,0:T(8,128)S(1)}, u32[]{:S(2)}, u32[]{:S(2)}) collective-permute-start(f32[8,2048]{1,0:T(8,128)S(1)} %get-tuple-element.17), channel_id=1, source_target_pairs={{0,16},{4,20},{8,24},{12,28},{16,0},{20,4},{24,8},{28,12},{1,17},{... | collective-permute-start | bytes 196616 | tf_op jit(solution)/shard_map/ppermute | solution.py:303
  21.9 5.7 %collective-permute-start.9 = (f32[8,2048]{1,0:T(8,128)S(1)}, f32[8,2048]{1,0:T(8,128)S(1)}, u32[]{:S(2)}, u32[]{:S(2)}) collective-permute-start(f32[8,2048]{1,0:T(8,128)S(1)} %get-tuple-element.18), channel_id=1, source_target_pairs={{0,24},{4,28},{8,16},{12,20},{16,8},{20,12},{24,0},{28,4},{1,25},{... | collective-permute-start | bytes 196616 | tf_op jit(solution)/shard_map/ppermute | solution.py:303
  23.4 4.3 %collective-permute-start.7 = (f32[8,2048]{1,0:T(8,128)S(1)}, f32[8,2048]{1,0:T(8,128)S(1)}, u32[]{:S(2)}, u32[]{:S(2)}) collective-permute-start(f32[8,2048]{1,0:T(8,128)S(1)} %get-tuple-element.16.after_ref), channel_id=1, source_target_pairs={{0,8},{4,12},{8,0},{12,4},{16,24},{20,28},{24,16},{28,20},{1,9},{5... | collective-permute-start | bytes 196616 | tf_op jit(solution)/shard_map/ppermute | solution.py:303
  24.4 6.5 %collective-permute-start.12 = (f32[1,8,2048]{2,1,0:T(8,128)S(1)}, f32[1,8,2048]{2,1,0:T(8,128)S(1)}, u32[]{:S(2)}, u32[]{:S(2)}) collective-permute-start(f32[1,8,2048]{2,1,0:T(8,128)S(1)} %get-tuple-element.22), channel_id=1, source_target_pairs={{0,2},{1,3},{2,0},{3,1},{4,6},{5,7},{6,4},{7,5},{8,10},{9,11},{10,... | collective-permute-start | bytes 196616 | tf_op jit(solution)/shard_map/ppermute | solution.py:303

commit v5 on v4

--- a/solution.py
+++ b/solution.py
@@ -12,6 +12,7 @@
 LANES = 128
 HALF = TILE // 2
 GROUP = LANES // HALF
+STEPS = 32000.0
 F32 = jnp.float32
 BF16 = jnp.bfloat16
 VMEM = pl.BlockSpec(memory_space=pltpu.VMEM)
@@ -40,6 +41,29 @@
 
 def row_fold():
     return row_spread().T
+
+
+def encode(values, out_ref):
+    width, piece = values[0].shape[0], LANES * len(values)
+    lane = lax.broadcasted_iota(jnp.int32, (width, LANES), 1)
+    exponents = jnp.zeros((width, LANES), F32)
+    for n, value in enumerate(values):
+        top = jnp.max(jnp.abs(value), axis=1, keepdims=True)
+        e = jnp.clip(jnp.ceil(jnp.log2(top)), -100.0, 100.0)
+        exponents = jnp.where(lane == n, e, exponents)
+        scaled = jnp.floor(value * (STEPS * jnp.exp2(-e)) + 0.5)
+        out_ref[:, n * LANES : (n + 1) * LANES] = scaled.astype(jnp.int32).astype(jnp.int16)
+    out_ref[:, piece:] = exponents.astype(jnp.int32).astype(jnp.int16)
+
+
+def decode(ref):
+    chunks = ref.shape[1] // LANES - 1
+    exponents = ref[:, chunks * LANES :].astype(jnp.int32).astype(F32)
+    scales = jnp.exp2(exponents) * (1.0 / STEPS)
+    return [
+        ref[:, n * LANES : (n + 1) * LANES].astype(jnp.int32).astype(F32) * scales[:, n : n + 1]
+        for n in range(chunks)
+    ]
 
 
 def prep_kernel(tiles_ref, out_ref, wide):
@@ -196,20 +220,24 @@
         rest = (wide - first.astype(F32)).astype(BF16)
         out = jnp.dot(first, fold, preferred_element_type=F32)
         out = out + jnp.dot(rest, fold, preferred_element_type=F32)
-        dest = (keep_ref if n % 2 == 0 else give_ref).at[n // 2]
-        for p in range(pairs):
-            dest[:, p * LANES : (p + 1) * LANES] = out[p * width : (p + 1) * width]
+        parts = [out[p * width : (p + 1) * width] for p in range(pairs)]
+        if n % 2 == 0:
+            for p in range(pairs):
+                keep_ref[n // 2, :, p * LANES : (p + 1) * LANES] = parts[p]
+        else:
+            encode(parts, give_ref.at[n // 2])
 
 
 def forward(same, other, tiles, tile_rows, tile_cols, counts, n_out, after):
     n_chips, width, piece = same.shape
     per_piece = piece // TILE
     half = jax.ShapeDtypeStruct((n_out // 2, width, piece), F32)
+    coded = jax.ShapeDtypeStruct((n_out // 2, width, piece + LANES), jnp.int16)
     return pl.pallas_call(
         forward_kernel,
         in_specs=[SMEM] * 3 + [VMEM] * 5 + [ANY],
         out_specs=[VMEM] * 2,
-        out_shape=[half, half],
+        out_shape=[half, coded],
         scratch_shapes=[
             pltpu.VMEM((2 * n_chips * per_piece, 2 * width, LANES), BF16),
             pltpu.VMEM((n_out * per_piece + 1, 2 * width, LANES), F32),
@@ -264,39 +292,50 @@
 
 def split_sum_kernel(keep_ref, got_ref, after_ref, next_keep, next_give):
     for h in range(next_keep.shape[0]):
-        next_keep[h] = keep_ref[2 * h] + got_ref[2 * h]
-        next_give[h] = keep_ref[2 * h + 1] + got_ref[2 * h + 1]
+        for n, got in enumerate(decode(got_ref.at[2 * h])):
+            at = pl.ds(n * LANES, LANES)
+            next_keep[h, :, at] = keep_ref[2 * h, :, at] + got
+        sums = [
+            keep_ref[2 * h + 1, :, n * LANES : (n + 1) * LANES] + got
+            for n, got in enumerate(decode(got_ref.at[2 * h + 1]))
+        ]
+        encode(sums, next_give.at[h])
 
 
 def split_sum(keep, got, after):
     parts, width, piece = keep.shape
-    half = jax.ShapeDtypeStruct((parts // 2, width, piece), F32)
     return pl.pallas_call(
         split_sum_kernel,
         in_specs=[VMEM] * 2 + [ANY],
         out_specs=[VMEM] * 2,
-        out_shape=[half, half],
+        out_shape=[
+            jax.ShapeDtypeStruct((parts // 2, width, piece), F32),
+            jax.ShapeDtypeStruct((parts // 2,) + got.shape[1:], got.dtype),
+        ],
         compiler_params=PARAMS,
         name="halving_sum",
     )(keep, got, after)
 
 
-def sum_kernel(*refs):
-    total = refs[0][...]
-    for ref in refs[1:-1]:
-        total = total + ref[...]
-    refs[-1][...] = total
-
-
-def sum_pieces(*parts):
-    return pl.pallas_call(
-        sum_kernel,
-        in_specs=[VMEM] * len(parts),
+def last_sum_kernel(*refs):
+    chips, (brow_keep, brow_got, keep_ref, got_ref, out_ref) = refs[:-5], refs[-5:]
+    for n, got in enumerate(decode(got_ref.at[0])):
+        at = pl.ds(n * LANES, LANES)
+        total = brow_keep[0, :, at] + brow_got[0, :, at]
+        for ref in chips:
+            total = total + ref[:, at]
+        out_ref[:, at] = total + (keep_ref[0, :, at] + got)
+
+
+def last_sum(keep, got, brow_keep, brow_got, chips):
+    return pl.pallas_call(
+        last_sum_kernel,
+        in_specs=[VMEM] * (4 + len(chips)),
         out_specs=VMEM,
-        out_shape=jax.ShapeDtypeStruct(parts[0].shape, F32),
-        compiler_params=PARAMS,
-        name="sum_pieces",
-    )(*parts)
+        out_shape=jax.ShapeDtypeStruct(keep.shape[1:], F32),
+        compiler_params=PARAMS,
+        name="last_sum",
+    )(*chips, brow_keep, brow_got, keep, got)
 
 
 def swap(x, axis, size, d):
@@ -323,8 +362,7 @@
         row_keep, give = split_sum(row_keep, row_got, sums[0])
         row_got = swap(give, "bcol", n_cols, d)
         d *= 2
-    total = sum_pieces(col_keep[0] + col_got[0], *from_chips)
-    return total + (row_keep[0] + row_got[0])
+    return last_sum(row_keep, row_got, col_keep, col_got, from_chips)
 
 
 def solution(mesh):

time: 32 us -> 32.4 us (1.012)
  starting transfers between devices: 17 us -> 18.1 us
  Pallas kernels: 5.56 us -> 6.64 us
  waiting for transfers between devices: 4.76 us -> 3.7 us
  other arithmetic: 0.65 us -> 0 us
    ppermute x13, starting transfers between devices: 17 us -> 18.1 us  [swap(): return lax.ppermute(x, axis, [(i, i ^ d) for i in range(size)])]
    ppermute x13, waiting for transfers between devices: 4.76 us -> 3.7 us  [swap(): return lax.ppermute(x, axis, [(i, i ^ d) for i in range(size)])]
    pallas_call x1, Pallas kernels: 0.02 us -> 0.74 us  [last_sum(): pl.pallas_call(last_sum_kernel, in_specs=[VMEM] * (4 + len(chips)), out_s...]
    add x2 -> x0, other arithmetic: 0.65 us -> none  [the longest x1 0.64 us: body(): return total + (row_keep[0] + row_got[0])]
  transfers between devices with their start and end apart: 13 -> 13, of which waited for: 4 -> 3; matrix products, arithmetic and copies ran while one was open for 0% -> 0% of each run, Pallas kernels for 18% -> 12%
where the time goes in v5:
time: 32.4 us; the launch traced here: 32.1 us
  starting transfers between devices  18.1 us (56%)
  Pallas kernels  6.64 us (20%)
  waiting for transfers between devices  3.7 us (11%)
  local copies, waits for them, and re-layouts  2.84 us (9%)
  between operations  0.8 us (2%)
    ppermute x13, starting transfers between devices, swap(): return lax.ppermute(x, axis, [(i, i ^ d) for i in range(size)])  18.1 us
    ppermute x13, waiting for transfers between devices, swap(): return lax.ppermute(x, axis, [(i, i ^ d) for i in range(size)])  3.7 us
    unnamed x14, local copies, waits for them, and re-layouts  2.84 us
    pallas_call x1, Pallas kernels, forward(): pl.pallas_call(forward_kernel, in_specs=[SMEM] * 3 + [VMEM] * 5 + [ANY],...  2.8 us
    pallas_call x1, Pallas kernels, backward(): pl.pallas_call(functools.partial(backward_kernel, n_in), in_specs=[SMEM]...  2.17 us
    pallas_call x1, Pallas kernels, last_sum(): pl.pallas_call(last_sum_kernel, in_specs=[VMEM] * (4 + len(chips)), out_s...  0.74 us
    pallas_call x1, Pallas kernels, prep(): pl.pallas_call(prep_kernel, in_specs=[VMEM], out_specs=VMEM, out_shape=ja...  0.69 us
  transfers between devices with their start and end apart: 13, of which 3 were waited for; matrix products, arithmetic and copies ran while one was open for 0% of the time, Pallas kernels for 12%

profile of v5, /device:TPU:0, one launch (start us, length us, event | category | flops | bytes accessed | tf_op | source)
XLA Modules:
  0.0 32.1 jit_solution(4503720735074897189)
XLA Ops:
  0.0 2.9 %collective-permute-start.3 = (bf16[8,2048]{1,0:T(8,128)(2,1)}, bf16[8,2048]{1,0:T(8,128)(2,1)S(1)}, u32[]{:S(2)}, u32[]{:S(2)}) collective-permute-start(bf16[8,2048]{1,0:T(8,128)(2,1)} %refs_0_.1), channel_id=1, source_target_pairs={{0,8},{4,12},{8,0},{12,4},{16,24},{20,28},{24,16},{28,20},{1,9},{5... | collective-permute-start | bytes 98312 | tf_op jit(solution)/shard_map/ppermute | solution.py:342
  2.9 3.6 %collective-permute-start.2 = (bf16[8,2048]{1,0:T(8,128)(2,1)}, bf16[8,2048]{1,0:T(8,128)(2,1)S(1)}, u32[]{:S(2)}, u32[]{:S(2)}) collective-permute-start(bf16[8,2048]{1,0:T(8,128)(2,1)} %refs_0_.1), channel_id=1, source_target_pairs={{0,3},{1,2},{2,1},{3,0},{4,7},{5,6},{6,5},{7,4},{8,11},{9,10},{10,... | collective-permute-start | bytes 98312 | tf_op jit(solution)/shard_map/ppermute | solution.py:342
  6.5 0.8 %collective-permute-start = (bf16[8,2048]{1,0:T(8,128)(2,1)}, bf16[8,2048]{1,0:T(8,128)(2,1)S(1)}, u32[]{:S(2)}, u32[]{:S(2)}) collective-permute-start(bf16[8,2048]{1,0:T(8,128)(2,1)} %refs_0_.1), channel_id=1, source_target_pairs={{0,1},{1,0},{2,3},{3,2},{4,5},{5,4},{6,7},{7,6},{8,9},{9,8},{10,11... | collective-permute-start | bytes 98312 | tf_op jit(solution)/shard_map/ppermute | solution.py:342
  7.3 1.5 %collective-permute-start.5 = (bf16[8,2048]{1,0:T(8,128)(2,1)}, bf16[8,2048]{1,0:T(8,128)(2,1)S(1)}, u32[]{:S(2)}, u32[]{:S(2)}) collective-permute-start(bf16[8,2048]{1,0:T(8,128)(2,1)} %refs_0_.1), channel_id=1, source_target_pairs={{0,24},{4,28},{8,16},{12,20},{16,8},{20,12},{24,0},{28,4},{1,25},{... | collective-permute-start | bytes 98312 | tf_op jit(solution)/shard_map/ppermute | solution.py:342
  8.8 0.0 collective-permute-done.3.refs_1_
  8.8 0.3 collective-permute-start.4
  9.1 0.8 %copy-done.4 = bf16[8,2048]{1,0:T(8,128)(2,1)S(1)} copy-done((bf16[8,2048]{1,0:T(8,128)(2,1)S(1)}, bf16[8,2048]{1,0:T(8,128)(2,1)}, u32[]{:S(2)}) %copy-start.4) | copy-done | bytes 32792
  10.6 0.0 copy-start
  10.6 1.4 %copy-done = bf16[192,4096]{1,0:T(8,128)(2,1)S(1)} copy-done((bf16[192,4096]{1,0:T(8,128)(2,1)S(1)}, bf16[192,4096]{1,0:T(8,128)(2,1)}, u32[]{:S(2)}) %copy-start) | copy-done | bytes 1572888
  12.0 0.7 %prep_tiles.1.refs_4_.tiles_ref = bf16[192,32,128]{2,1,0:T(8,128)(2,1)S(1)} custom-call(bf16[24,32,8,128]{3,2,1,0:T(8,128)(2,1)S(1)} %bitcast.4), custom_call_target="tpu_custom_call" | custom-call | bytes 3145728 | tf_op jit(solution)/shard_map/prep_tiles/pallas_call | solution.py:80
  12.7 0.0 copy-start.3
  12.7 0.0 copy-start.5
  12.7 0.0 copy-start.6
  12.7 0.0 copy-start.1
  12.7 0.0 copy-start.2
  12.7 0.0 collective-permute-done.1.refs_6_.refs_2_
  12.8 0.0 collective-permute-done.refs_5_.refs_1_
  12.8 0.2 collective-permute-done.4.refs_2_
  13.0 0.6 %copy-done.3 = bf16[128,512]{1,0:T(8,128)(2,1)S(1)} copy-done((bf16[128,512]{1,0:T(8,128)(2,1)S(1)}, bf16[128,512]{1,0:T(8,128)(2,1)}, u32[]{:S(2)}) %copy-start.3) | copy-done | bytes 131096
  13.6 2.2 %transpose_product.1 = (f32[4,8,2048]{2,1,0:T(8,128)S(1)}, f32[4,8,2048]{2,1,0:T(8,128)S(1)}) custom-call(s32[192]{0:T(256)S(1)} %copy-done.5, s32[192]{0:T(256)S(1)} %copy-done.6, s32[1,1]{1,0:T(1,128)S(6)} %copy.9.count_ref, bf16[128,512]{1,0:T(8,128)(2,1)S(1)} %copy-done.3, bf16[192,32,128]{2,1,0:T(8,128)(2,1)S(1)} %prep_tiles.1.refs_4_.tiles_ref, ...), custom_call_target="tpu_custom_call" | custom-call | flops 100663296 | bytes 3145728 | tf_op jit(solution)/shard_map/transpose_product/pallas_call | solution.py:150
  15.8 0.1 collective-permute-start.6
  15.8 0.5 %collective-permute-start.10 = (bf16[4,8,2048]{2,1,0:T(8,128)(2,1)S(1)}, bf16[4,8,2048]{2,1,0:T(8,128)(2,1)S(1)}, u32[]{:S(2)}, u32[]{:S(2)}) collective-permute-start(bf16[4,8,2048]{2,1,0:T(8,128)(2,1)S(1)} %stack_pieces.3.refs_4_.same_ref), channel_id=1, source_target_pairs={{0,4},{4,0},{8,12},{12,8},{16,20},{20,16},{24,28},{28,24},{1,5},{5... | collective-permute-start | bytes 393224 | tf_op jit(solution)/shard_map/ppermute | solution.py:342
  16.3 1.2 %collective-permute-done.10.other_ref = bf16[4,8,2048]{2,1,0:T(8,128)(2,1)S(1)} collective-permute-done((bf16[4,8,2048]{2,1,0:T(8,128)(2,1)S(1)}, bf16[4,8,2048]{2,1,0:T(8,128)(2,1)S(1)}, u32[]{:S(2)}, u32[]{:S(2)}) %collective-permute-start.10) | collective-permute-done | bytes 131104 | tf_op jit(solution)/shard_map/ppermute | solution.py:342
  17.6 2.8 %forward_product.1 = (f32[2,8,2048]{2,1,0:T(8,128)S(1)}, s16[2,8,2176]{2,1,0:T(8,128)(2,1)S(1)}) custom-call(s32[192]{0:T(256)S(1)} %copy-done.5, s32[192]{0:T(256)S(1)} %copy-done.6, s32[1,1]{1,0:T(1,128)S(6)} %copy.9.count_ref, bf16[128,512]{1,0:T(8,128)(2,1)S(1)} %copy-done.2, bf16[512,128]{1,0:T(8,128)(2,1)S(1)} %copy-done.1, ...), custom_call_target="tpu_custom_call" | custom-call | flops 100663296 | bytes 3145728 | tf_op jit(solution)/shard_map/forward_product/pallas_call | solution.py:236
  20.4 1.4 %collective-permute-start.11 = (s16[2,8,2176]{2,1,0:T(8,128)(2,1)S(1)}, s16[2,8,2176]{2,1,0:T(8,128)(2,1)S(1)}, u32[]{:S(2)}, u32[]{:S(2)}) collective-permute-start(s16[2,8,2176]{2,1,0:T(8,128)(2,1)S(1)} %get-tuple-element.20), channel_id=1, source_target_pairs={{0,1},{1,0},{2,3},{3,2},{4,5},{5,4},{6,7},{7,6},{8,9},{9,8},{10,11... | collective-permute-start | bytes 208904 | tf_op jit(solution)/shard_map/ppermute | solution.py:342
  21.8 2.0 %collective-permute-start.8 = (f32[8,2048]{1,0:T(8,128)S(1)}, f32[8,2048]{1,0:T(8,128)S(1)}, u32[]{:S(2)}, u32[]{:S(2)}) collective-permute-start(f32[8,2048]{1,0:T(8,128)S(1)} %get-tuple-element.17), channel_id=1, source_target_pairs={{0,16},{4,20},{8,24},{12,28},{16,0},{20,4},{24,8},{28,12},{1,17},{... | collective-permute-start | bytes 196616 | tf_op jit(solution)/shard_map/ppermute | solution.py:342
  23.8 1.1 %collective-permute-start.9 = (f32[8,2048]{1,0:T(8,128)S(1)}, f32[8,2048]{1,0:T(8,128)S(1)}, u32[]{:S(2)}, u32[]{:S(2)}) collective-permute-start(f32[8,2048]{1,0:T(8,128)S(1)} %get-tuple-element.18), channel_id=1, source_target_pairs={{0,24},{4,28},{8,16},{12,20},{16,8},{20,12},{24,0},{28,4},{1,25},{... | collective-permute-start | bytes 196616 | tf_op jit(solution)/shard_map/ppermute | solution.py:342
  24.8 0.5 %collective-permute-start.7 = (f32[8,2048]{1,0:T(8,128)S(1)}, f32[8,2048]{1,0:T(8,128)S(1)}, u32[]{:S(2)}, u32[]{:S(2)}) collective-permute-start(f32[8,2048]{1,0:T(8,128)S(1)} %get-tuple-element.16.after_ref), channel_id=1, source_target_pairs={{0,8},{4,12},{8,0},{12,4},{16,24},{20,28},{24,16},{28,20},{1,9},{5... | collective-permute-start | bytes 196616 | tf_op jit(solution)/shard_map/ppermute | solution.py:342
  25.4 0.2 halving_sum.1
  25.6 3.5 %collective-permute-start.12 = (s16[1,8,2176]{2,1,0:T(8,128)(2,1)S(1)}, s16[1,8,2176]{2,1,0:T(8,128)(2,1)S(1)}, u32[]{:S(2)}, u32[]{:S(2)}) collective-permute-start(s16[1,8,2176]{2,1,0:T(8,128)(2,1)S(1)} %get-tuple-element.22), channel_id=1, source_target_pairs={{0,2},{1,3},{2,0},{3,1},{4,6},{5,7},{6,4},{7,5},{8,10},{9,11},{10,... | collective-permute-start | bytes 104456 | tf_op jit(solution)/shard_map/ppermute | solution.py:342
  29.1 2.3 %collective-permute-done.12.refs_6_ = s16[1,8,2176]{2,1,0:T(8,128)(2,1)S(1)} collective-permute-done((s16[1,8,2176]{2,1,0:T(8,128)(2,1)S(1)}, s16[1,8,2176]{2,1,0:T(8,128)(2,1)S(1)}, u32[]{:S(2)}, u32[]{:S(2)}) %collective-permute-start.12) | collective-permute-done | bytes 34848 | tf_op jit(solution)/shard_map/ppermute | solution.py:342
  31.4 0.7 %last_sum.1 = f32[8,2048]{1,0:T(8,128)} custom-call(f32[8,2048]{1,0:T(8,128)S(1)} %collective-permute-done.7.refs_0_, f32[8,2048]{1,0:T(8,128)S(1)} %collective-permute-done.8.refs_1_, f32[8,2048]{1,0:T(8,128)S(1)} %collective-permute-done.9.refs_2_, f32[4,8,2048]{2,1,0:T(8,128)S(1)} %get-tuple-element.14.keep_ref.refs_3_, ...), custom_call_target="tpu_custom_call" | custom-call | tf_op jit(solution)/shard_map/last_sum/pallas_call | solution.py:331
  (16 shorter events, 0.1 us)
Async XLA Ops:
  0.0 8.8 %collective-permute-start.3 = (bf16[8,2048]{1,0:T(8,128)(2,1)}, bf16[8,2048]{1,0:T(8,128)(2,1)S(1)}, u32[]{:S(2)}, u32[]{:S(2)}) collective-permute-start(bf16[8,2048]{1,0:T(8,128)(2,1)} %refs_0_.1), channel_id=1, source_target_pairs={{0,8},{4,12},{8,0},{12,4},{16,24},{20,28},{24,16},{28,20},{1,9},{5... | collective-permute-start | bytes 98312 | tf_op jit(solution)/shard_map/ppermute | solution.py:342
  2.9 9.8 %collective-permute-start.2 = (bf16[8,2048]{1,0:T(8,128)(2,1)}, bf16[8,2048]{1,0:T(8,128)(2,1)S(1)}, u32[]{:S(2)}, u32[]{:S(2)}) collective-permute-start(bf16[8,2048]{1,0:T(8,128)(2,1)} %refs_0_.1), channel_id=1, source_target_pairs={{0,3},{1,2},{2,1},{3,0},{4,7},{5,6},{6,5},{7,4},{8,11},{9,10},{10,... | collective-permute-start | bytes 98312 | tf_op jit(solution)/shard_map/ppermute | solution.py:342
  6.5 6.2 %collective-permute-start.1 = (bf16[8,2048]{1,0:T(8,128)(2,1)}, bf16[8,2048]{1,0:T(8,128)(2,1)S(1)}, u32[]{:S(2)}, u32[]{:S(2)}) collective-permute-start(bf16[8,2048]{1,0:T(8,128)(2,1)} %refs_0_.1), channel_id=1, source_target_pairs={{0,2},{1,3},{2,0},{3,1},{4,6},{5,7},{6,4},{7,5},{8,10},{9,11},{10,... | collective-permute-start | bytes 98312 | tf_op jit(solution)/shard_map/ppermute | solution.py:342
  6.5 6.2 %collective-permute-start = (bf16[8,2048]{1,0:T(8,128)(2,1)}, bf16[8,2048]{1,0:T(8,128)(2,1)S(1)}, u32[]{:S(2)}, u32[]{:S(2)}) collective-permute-start(bf16[8,2048]{1,0:T(8,128)(2,1)} %refs_0_.1), channel_id=1, source_target_pairs={{0,1},{1,0},{2,3},{3,2},{4,5},{5,4},{6,7},{7,6},{8,9},{9,8},{10,11... | collective-permute-start | bytes 98312 | tf_op jit(solution)/shard_map/ppermute | solution.py:342
  7.3 5.4 %collective-permute-start.5 = (bf16[8,2048]{1,0:T(8,128)(2,1)}, bf16[8,2048]{1,0:T(8,128)(2,1)S(1)}, u32[]{:S(2)}, u32[]{:S(2)}) collective-permute-start(bf16[8,2048]{1,0:T(8,128)(2,1)} %refs_0_.1), channel_id=1, source_target_pairs={{0,24},{4,28},{8,16},{12,20},{16,8},{20,12},{24,0},{28,4},{1,25},{... | collective-permute-start | bytes 98312 | tf_op jit(solution)/shard_map/ppermute | solution.py:342
  8.8 4.1 %collective-permute-start.4 = (bf16[8,2048]{1,0:T(8,128)(2,1)}, bf16[8,2048]{1,0:T(8,128)(2,1)S(1)}, u32[]{:S(2)}, u32[]{:S(2)}) collective-permute-start(bf16[8,2048]{1,0:T(8,128)(2,1)} %refs_0_.1), channel_id=1, source_target_pairs={{0,16},{4,20},{8,24},{12,28},{16,0},{20,4},{24,8},{28,12},{1,17},{... | collective-permute-start | bytes 98312 | tf_op jit(solution)/shard_map/ppermute | solution.py:342
  9.1 0.8 %copy-start.4 = (bf16[8,2048]{1,0:T(8,128)(2,1)S(1)}, bf16[8,2048]{1,0:T(8,128)(2,1)}, u32[]{:S(2)}) copy-start(bf16[8,2048]{1,0:T(8,128)(2,1)} %refs_0_.1) | copy-start | bytes 98308
  10.6 1.4 %copy-start = (bf16[192,4096]{1,0:T(8,128)(2,1)S(1)}, bf16[192,4096]{1,0:T(8,128)(2,1)}, u32[]{:S(2)}) copy-start(bf16[192,4096]{1,0:T(8,128)(2,1)} %param.9) | copy-start | bytes 4718596
  12.7 0.9 %copy-start.3 = (bf16[128,512]{1,0:T(8,128)(2,1)S(1)}, bf16[128,512]{1,0:T(8,128)(2,1)}, u32[]{:S(2)}) copy-start(bf16[128,512]{1,0:T(8,128)(2,1)} %constant.4.clone.spread_ref) | copy-start | bytes 393220
  12.7 0.9 %copy-start.5 = (s32[192]{0:T(256)S(1)}, s32[192]{0:T(256)}, u32[]{:S(2)}) copy-start(s32[192]{0:T(256)} %rows_ref.3) | copy-start | bytes 2308
  12.7 0.9 %copy-start.6 = (s32[192]{0:T(256)S(1)}, s32[192]{0:T(256)}, u32[]{:S(2)}) copy-start(s32[192]{0:T(256)} %cols_ref.3) | copy-start | bytes 2308
  12.7 4.8 %copy-start.1 = (bf16[512,128]{1,0:T(8,128)(2,1)S(1)}, bf16[512,128]{1,0:T(8,128)(2,1)}, u32[]{:S(2)}) copy-start(bf16[512,128]{1,0:T(8,128)(2,1)} %constant.7.fold_ref) | copy-start | bytes 393220
  12.7 4.8 %copy-start.2 = (bf16[128,512]{1,0:T(8,128)(2,1)S(1)}, bf16[128,512]{1,0:T(8,128)(2,1)}, u32[]{:S(2)}) copy-start(bf16[128,512]{1,0:T(8,128)(2,1)} %constant.5.clone.spread_ref) | copy-start | bytes 393220
  15.8 6.0 %collective-permute-start.6 = (f32[4,8,2048]{2,1,0:T(8,128)S(1)}, f32[4,8,2048]{2,1,0:T(8,128)S(1)}, u32[]{:S(2)}, u32[]{:S(2)}) collective-permute-start(f32[4,8,2048]{2,1,0:T(8,128)S(1)} %get-tuple-element.15.after_ref), channel_id=1, source_target_pairs={{0,4},{4,0},{8,12},{12,8},{16,20},{20,16},{24,28},{28,24},{1,5},{5... | collective-permute-start | bytes 786440 | tf_op jit(solution)/shard_map/ppermute | solution.py:342
  15.8 1.7 %collective-permute-start.10 = (bf16[4,8,2048]{2,1,0:T(8,128)(2,1)S(1)}, bf16[4,8,2048]{2,1,0:T(8,128)(2,1)S(1)}, u32[]{:S(2)}, u32[]{:S(2)}) collective-permute-start(bf16[4,8,2048]{2,1,0:T(8,128)(2,1)S(1)} %stack_pieces.3.refs_4_.same_ref), channel_id=1, source_target_pairs={{0,4},{4,0},{8,12},{12,8},{16,20},{20,16},{24,28},{28,24},{1,5},{5... | collective-permute-start | bytes 393224 | tf_op jit(solution)/shard_map/ppermute | solution.py:342
  20.4 5.0 %collective-permute-start.11 = (s16[2,8,2176]{2,1,0:T(8,128)(2,1)S(1)}, s16[2,8,2176]{2,1,0:T(8,128)(2,1)S(1)}, u32[]{:S(2)}, u32[]{:S(2)}) collective-permute-start(s16[2,8,2176]{2,1,0:T(8,128)(2,1)S(1)} %get-tuple-element.20), channel_id=1, source_target_pairs={{0,1},{1,0},{2,3},{3,2},{4,5},{5,4},{6,7},{7,6},{8,9},{9,8},{10,11... | collective-permute-start | bytes 208904 | tf_op jit(solution)/shard_map/ppermute | solution.py:342
  21.8 9.6 %collective-permute-start.8 = (f32[8,2048]{1,0:T(8,128)S(1)}, f32[8,2048]{1,0:T(8,128)S(1)}, u32[]{:S(2)}, u32[]{:S(2)}) collective-permute-start(f32[8,2048]{1,0:T(8,128)S(1)} %get-tuple-element.17), channel_id=1, source_target_pairs={{0,16},{4,20},{8,24},{12,28},{16,0},{20,4},{24,8},{28,12},{1,17},{... | collective-permute-start | bytes 196616 | tf_op jit(solution)/shard_map/ppermute | solution.py:342
  23.8 7.6 %collective-permute-start.9 = (f32[8,2048]{1,0:T(8,128)S(1)}, f32[8,2048]{1,0:T(8,128)S(1)}, u32[]{:S(2)}, u32[]{:S(2)}) collective-permute-start(f32[8,2048]{1,0:T(8,128)S(1)} %get-tuple-element.18), channel_id=1, source_target_pairs={{0,24},{4,28},{8,16},{12,20},{16,8},{20,12},{24,0},{28,4},{1,25},{... | collective-permute-start | bytes 196616 | tf_op jit(solution)/shard_map/ppermute | solution.py:342
  24.8 6.5 %collective-permute-start.7 = (f32[8,2048]{1,0:T(8,128)S(1)}, f32[8,2048]{1,0:T(8,128)S(1)}, u32[]{:S(2)}, u32[]{:S(2)}) collective-permute-start(f32[8,2048]{1,0:T(8,128)S(1)} %get-tuple-element.16.after_ref), channel_id=1, source_target_pairs={{0,8},{4,12},{8,0},{12,4},{16,24},{20,28},{24,16},{28,20},{1,9},{5... | collective-permute-start | bytes 196616 | tf_op jit(solution)/shard_map/ppermute | solution.py:342
  25.6 5.8 %collective-permute-start.12 = (s16[1,8,2176]{2,1,0:T(8,128)(2,1)S(1)}, s16[1,8,2176]{2,1,0:T(8,128)(2,1)S(1)}, u32[]{:S(2)}, u32[]{:S(2)}) collective-permute-start(s16[1,8,2176]{2,1,0:T(8,128)(2,1)S(1)} %get-tuple-element.22), channel_id=1, source_target_pairs={{0,2},{1,3},{2,0},{3,1},{4,6},{5,7},{6,4},{7,5},{8,10},{9,11},{10,... | collective-permute-start | bytes 104456 | tf_op jit(solution)/shard_map/ppermute | solution.py:342

commit v6 on v5

--- a/solution.py
+++ b/solution.py
@@ -106,7 +106,8 @@
 
 def backward_kernel(n_in, rows_ref, cols_ref, count_ref, spread_ref, tiles_ref, *refs):
     pieces = refs[:n_in]
-    _, keep_ref, give_ref, table, acc = refs[n_in:]
+    _, keep_ref, *give_refs, table, acc = refs[n_in:]
+    per_give = give_refs[0].shape[0]
     n_out = 2 * keep_ref.shape[0]
     width, piece = pieces[0].shape
     per_piece = piece // TILE
@@ -133,7 +134,8 @@
             acc[c] += part
 
     for n in range(n_out):
-        dest = (keep_ref if n % 2 == 0 else give_ref).at[n // 2]
+        h = n // 2
+        dest = keep_ref.at[h] if n % 2 == 0 else give_refs[h // per_give].at[h % per_give]
         for p in range(per_piece // 2):
             a = acc[n * per_piece + 2 * p]
             b = acc[n * per_piece + 2 * p + 1]
@@ -147,11 +149,12 @@
     width, piece = pieces[0].shape
     per_piece = piece // TILE
     half = jax.ShapeDtypeStruct((n_out // 2, width, piece), F32)
+    quarter = jax.ShapeDtypeStruct((n_out // 4, width, piece), F32)
     return pl.pallas_call(
         functools.partial(backward_kernel, n_in),
         in_specs=[SMEM] * 3 + [VMEM] * (2 + n_in) + [ANY],
-        out_specs=[VMEM] * 2,
-        out_shape=[half, half],
+        out_specs=[VMEM] * 3,
+        out_shape=[half, quarter, quarter],
         scratch_shapes=[
             pltpu.VMEM((n_in * per_piece, 2 * width, LANES), BF16),
             pltpu.VMEM((n_out * per_piece + 1, width, LANES), F32),
@@ -273,21 +276,24 @@
     )(*parts, *after)
 
 
-def pair_sum_kernel(keep_ref, got_ref, *outs):
+def pair_sum_kernel(keep_ref, *refs):
+    n_chips = keep_ref.shape[0]
+    gots, outs = refs[: 1 - n_chips], refs[1 - n_chips :]
+    got = [ref.at[h] for ref in gots for h in range(ref.shape[0])]
     for h, out in enumerate(outs):
-        out[...] = keep_ref[h + 1] + got_ref[h + 1]
-
-
-def pair_sum(keep, got):
+        out[...] = keep_ref[h + 1] + got[h + 1][...]
+
+
+def pair_sum(keep, gots):
     parts, width, piece = keep.shape
     return pl.pallas_call(
         pair_sum_kernel,
-        in_specs=[VMEM] * 2,
+        in_specs=[VMEM] * (1 + len(gots)),
         out_specs=[VMEM] * (parts - 1),
         out_shape=[jax.ShapeDtypeStruct((width, piece), F32)] * (parts - 1),
         compiler_params=PARAMS,
         name="core_pair_sum",
-    )(keep, got)
+    )(keep, *gots)
 
 
 def split_sum_kernel(keep_ref, got_ref, after_ref, next_keep, next_give):
@@ -352,9 +358,9 @@
     same = stack(own, *chips, after=(blocks, *row_pieces[1:]))
     other = swap(same, "brow", n_rows, 1)
 
-    col_keep, col_give = backward(row_pieces, blocks, tile_rows, tile_cols, counts, n_rows, same)
-    row_keep, give = forward(same, other, blocks, tile_rows, tile_cols, counts, n_cols, col_give)
-    col_got = swap(col_give, "brow", n_rows, 1)
+    col_keep, *col_give = backward(row_pieces, blocks, tile_rows, tile_cols, counts, n_rows, same)
+    row_keep, give = forward(same, other, blocks, tile_rows, tile_cols, counts, n_cols, col_give[0])
+    col_got = [swap(x, "brow", n_rows, 1) for x in col_give]
     sums = pair_sum(col_keep, col_got)
     from_chips = [swap(x, "brow", n_rows, 2 * (h + 1)) for h, x in enumerate(sums)]
     row_got, d = swap(give, "bcol", n_cols, 1), 2
@@ -362,7 +368,7 @@
         row_keep, give = split_sum(row_keep, row_got, sums[0])
         row_got = swap(give, "bcol", n_cols, d)
         d *= 2
-    return last_sum(row_keep, row_got, col_keep, col_got, from_chips)
+    return last_sum(row_keep, row_got, col_keep, col_got[0], from_chips)
 
 
 def solution(mesh):

time: 32.4 us -> 30.6 us (0.944)
  waiting for transfers between devices: 3.7 us -> 2.78 us
  local copies, waits for them, and re-layouts: 2.84 us -> 2.23 us
    ppermute x13 -> x14, waiting for transfers between devices: 3.7 us -> 2.78 us  [swap(): return lax.ppermute(x, axis, [(i, i ^ d) for i in range(size)])]
    unnamed x14, local copies, waits for them, and re-layouts: 2.84 us -> 2.23 us
    ppermute x13 -> x14, starting transfers between devices: 18.1 us -> 17.8 us  [swap(): return lax.ppermute(x, axis, [(i, i ^ d) for i in range(size)])]
  transfers between devices with their start and end apart: 13 -> 14, of which waited for: 3 -> 4; matrix products, arithmetic and copies ran while one was open for 0% -> 0% of each run, Pallas kernels for 12% -> 20%
where the time goes in v6:
time: 30.6 us; the launch traced here: 30.4 us
  starting transfers between devices  17.8 us (58%)
  Pallas kernels  6.7 us (22%)
  waiting for transfers between devices  2.78 us (9%)
  local copies, waits for them, and re-layouts  2.23 us (7%)
  between operations  0.8 us (3%)
    ppermute x14, starting transfers between devices, swap(): return lax.ppermute(x, axis, [(i, i ^ d) for i in range(size)])  17.8 us
    pallas_call x1, Pallas kernels, forward(): pl.pallas_call(forward_kernel, in_specs=[SMEM] * 3 + [VMEM] * 5 + [ANY],...  2.81 us
    ppermute x14, waiting for transfers between devices, swap(): return lax.ppermute(x, axis, [(i, i ^ d) for i in range(size)])  2.78 us
    unnamed x14, local copies, waits for them, and re-layouts  2.23 us
    pallas_call x1, Pallas kernels, backward(): pl.pallas_call(functools.partial(backward_kernel, n_in), in_specs=[SMEM]...  2.22 us
    pallas_call x1, Pallas kernels, last_sum(): pl.pallas_call(last_sum_kernel, in_specs=[VMEM] * (4 + len(chips)), out_s...  0.74 us
    pallas_call x1, Pallas kernels, prep(): pl.pallas_call(prep_kernel, in_specs=[VMEM], out_specs=VMEM, out_shape=ja...  0.69 us
  transfers between devices with their start and end apart: 14, of which 4 were waited for; matrix products, arithmetic and copies ran while one was open for 0% of the time, Pallas kernels for 20%

profile of v6, /device:TPU:0, one launch (start us, length us, event | category | flops | bytes accessed | tf_op | source)
XLA Modules:
  0.0 30.4 jit_solution(4930700103143243503)
XLA Ops:
  0.0 2.9 %collective-permute-start.3 = (bf16[8,2048]{1,0:T(8,128)(2,1)}, bf16[8,2048]{1,0:T(8,128)(2,1)S(1)}, u32[]{:S(2)}, u32[]{:S(2)}) collective-permute-start(bf16[8,2048]{1,0:T(8,128)(2,1)} %refs_0_.1), channel_id=1, source_target_pairs={{0,8},{4,12},{8,0},{12,4},{16,24},{20,28},{24,16},{28,20},{1,9},{5... | collective-permute-start | bytes 98312 | tf_op jit(solution)/shard_map/ppermute | solution.py:348
  2.9 3.6 %collective-permute-start.2 = (bf16[8,2048]{1,0:T(8,128)(2,1)}, bf16[8,2048]{1,0:T(8,128)(2,1)S(1)}, u32[]{:S(2)}, u32[]{:S(2)}) collective-permute-start(bf16[8,2048]{1,0:T(8,128)(2,1)} %refs_0_.1), channel_id=1, source_target_pairs={{0,3},{1,2},{2,1},{3,0},{4,7},{5,6},{6,5},{7,4},{8,11},{9,10},{10,... | collective-permute-start | bytes 98312 | tf_op jit(solution)/shard_map/ppermute | solution.py:348
  6.5 0.0 collective-permute-start.1
  6.5 0.8 %collective-permute-start = (bf16[8,2048]{1,0:T(8,128)(2,1)}, bf16[8,2048]{1,0:T(8,128)(2,1)S(1)}, u32[]{:S(2)}, u32[]{:S(2)}) collective-permute-start(bf16[8,2048]{1,0:T(8,128)(2,1)} %refs_0_.1), channel_id=1, source_target_pairs={{0,1},{1,0},{2,3},{3,2},{4,5},{5,4},{6,7},{7,6},{8,9},{9,8},{10,11... | collective-permute-start | bytes 98312 | tf_op jit(solution)/shard_map/ppermute | solution.py:348
  7.3 1.5 %collective-permute-start.5 = (bf16[8,2048]{1,0:T(8,128)(2,1)}, bf16[8,2048]{1,0:T(8,128)(2,1)S(1)}, u32[]{:S(2)}, u32[]{:S(2)}) collective-permute-start(bf16[8,2048]{1,0:T(8,128)(2,1)} %refs_0_.1), channel_id=1, source_target_pairs={{0,24},{4,28},{8,16},{12,20},{16,8},{20,12},{24,0},{28,4},{1,25},{... | collective-permute-start | bytes 98312 | tf_op jit(solution)/shard_map/ppermute | solution.py:348
  8.8 0.3 collective-permute-start.4
  9.1 0.8 %copy-done.4 = bf16[8,2048]{1,0:T(8,128)(2,1)S(1)} copy-done((bf16[8,2048]{1,0:T(8,128)(2,1)S(1)}, bf16[8,2048]{1,0:T(8,128)(2,1)}, u32[]{:S(2)}) %copy-start.4) | copy-done | bytes 32792
  9.9 1.4 %copy-done = bf16[192,4096]{1,0:T(8,128)(2,1)S(1)} copy-done((bf16[192,4096]{1,0:T(8,128)(2,1)S(1)}, bf16[192,4096]{1,0:T(8,128)(2,1)}, u32[]{:S(2)}) %copy-start) | copy-done | bytes 1572888
  11.3 0.7 %prep_tiles.1.refs_4_.tiles_ref = bf16[192,32,128]{2,1,0:T(8,128)(2,1)S(1)} custom-call(bf16[24,32,8,128]{3,2,1,0:T(8,128)(2,1)S(1)} %bitcast.4), custom_call_target="tpu_custom_call" | custom-call | bytes 3145728 | tf_op jit(solution)/shard_map/prep_tiles/pallas_call | solution.py:80
  12.0 0.0 copy-start.3
  12.0 0.0 copy-start.5
  12.0 0.0 copy-start.6
  12.1 0.0 copy-start.1
  12.1 0.0 copy-start.2
  12.1 0.0 collective-permute-done.2.refs_7_.refs_3_
  12.1 0.2 collective-permute-done.5.refs_3_
  12.4 0.6 %collective-permute-done.4.refs_2_ = bf16[8,2048]{1,0:T(8,128)(2,1)S(1)} collective-permute-done((bf16[8,2048]{1,0:T(8,128)(2,1)}, bf16[8,2048]{1,0:T(8,128)(2,1)S(1)}, u32[]{:S(2)}, u32[]{:S(2)}) %collective-permute-start.4) | collective-permute-done | bytes 32800 | tf_op jit(solution)/shard_map/ppermute | solution.py:348
  13.0 0.1 collective-permute-start.11
  13.7 2.2 %transpose_product.1 = (f32[4,8,2048]{2,1,0:T(8,128)S(1)}, f32[2,8,2048]{2,1,0:T(8,128)S(1)}, f32[2,8,2048]{2,1,0:T(8,128)S(1)}) custom-call(s32[192]{0:T(256)S(1)} %copy-done.5, s32[192]{0:T(256)S(1)} %copy-done.6, s32[1,1]{1,0:T(1,128)S(6)} %copy.9.count_ref, bf16[128,512]{1,0:T(8,128)(2,1)S(1)} %copy-done.3, ...), custom_call_target="tpu_custom_call" | custom-call | flops 100663296 | bytes 3145728 | tf_op jit(solution)/shard_map/transpose_product/pallas_call | solution.py:153
  15.9 0.8 %collective-permute-start.7 = (f32[2,8,2048]{2,1,0:T(8,128)S(1)}, f32[2,8,2048]{2,1,0:T(8,128)S(1)}, u32[]{:S(2)}, u32[]{:S(2)}) collective-permute-start(f32[2,8,2048]{2,1,0:T(8,128)S(1)} %get-tuple-element.17), channel_id=1, source_target_pairs={{0,4},{4,0},{8,12},{12,8},{16,20},{20,16},{24,28},{28,24},{1,5},{5... | collective-permute-start | bytes 393224 | tf_op jit(solution)/shard_map/ppermute | solution.py:348
  16.7 0.1 collective-permute-start.6
  16.8 2.8 %forward_product.1 = (f32[2,8,2048]{2,1,0:T(8,128)S(1)}, s16[2,8,2176]{2,1,0:T(8,128)(2,1)S(1)}) custom-call(s32[192]{0:T(256)S(1)} %copy-done.5, s32[192]{0:T(256)S(1)} %copy-done.6, s32[1,1]{1,0:T(1,128)S(6)} %copy.9.count_ref, bf16[128,512]{1,0:T(8,128)(2,1)S(1)} %copy-done.2, bf16[512,128]{1,0:T(8,128)(2,1)S(1)} %copy-done.1, ...), custom_call_target="tpu_custom_call" | custom-call | flops 100663296 | bytes 3145728 | tf_op jit(solution)/shard_map/forward_product/pallas_call | solution.py:239
  19.7 1.1 %collective-permute-start.12 = (s16[2,8,2176]{2,1,0:T(8,128)(2,1)S(1)}, s16[2,8,2176]{2,1,0:T(8,128)(2,1)S(1)}, u32[]{:S(2)}, u32[]{:S(2)}) collective-permute-start(s16[2,8,2176]{2,1,0:T(8,128)(2,1)S(1)} %get-tuple-element.22), channel_id=1, source_target_pairs={{0,1},{1,0},{2,3},{3,2},{4,5},{5,4},{6,7},{7,6},{8,9},{9,8},{10,11... | collective-permute-start | bytes 208904 | tf_op jit(solution)/shard_map/ppermute | solution.py:348
  20.8 1.1 %collective-permute-start.9 = (f32[8,2048]{1,0:T(8,128)S(1)}, f32[8,2048]{1,0:T(8,128)S(1)}, u32[]{:S(2)}, u32[]{:S(2)}) collective-permute-start(f32[8,2048]{1,0:T(8,128)S(1)} %get-tuple-element.19), channel_id=1, source_target_pairs={{0,16},{4,20},{8,24},{12,28},{16,0},{20,4},{24,8},{28,12},{1,17},{... | collective-permute-start | bytes 196616 | tf_op jit(solution)/shard_map/ppermute | solution.py:348
  21.9 1.8 %collective-permute-start.10 = (f32[8,2048]{1,0:T(8,128)S(1)}, f32[8,2048]{1,0:T(8,128)S(1)}, u32[]{:S(2)}, u32[]{:S(2)}) collective-permute-start(f32[8,2048]{1,0:T(8,128)S(1)} %get-tuple-element.20), channel_id=1, source_target_pairs={{0,24},{4,28},{8,16},{12,20},{16,8},{20,12},{24,0},{28,4},{1,25},{... | collective-permute-start | bytes 196616 | tf_op jit(solution)/shard_map/ppermute | solution.py:348
  23.7 0.7 %collective-permute-start.8 = (f32[8,2048]{1,0:T(8,128)S(1)}, f32[8,2048]{1,0:T(8,128)S(1)}, u32[]{:S(2)}, u32[]{:S(2)}) collective-permute-start(f32[8,2048]{1,0:T(8,128)S(1)} %get-tuple-element.18.after_ref), channel_id=1, source_target_pairs={{0,8},{4,12},{8,0},{12,4},{16,24},{20,28},{24,16},{28,20},{1,9},{5... | collective-permute-start | bytes 196616 | tf_op jit(solution)/shard_map/ppermute | solution.py:348
  24.3 0.0 collective-permute-done.12.got_ref
  24.4 0.2 halving_sum.1
  24.6 3.1 %collective-permute-start.13 = (s16[1,8,2176]{2,1,0:T(8,128)(2,1)S(1)}, s16[1,8,2176]{2,1,0:T(8,128)(2,1)S(1)}, u32[]{:S(2)}, u32[]{:S(2)}) collective-permute-start(s16[1,8,2176]{2,1,0:T(8,128)(2,1)S(1)} %get-tuple-element.24), channel_id=1, source_target_pairs={{0,2},{1,3},{2,0},{3,1},{4,6},{5,7},{6,4},{7,5},{8,10},{9,11},{10,... | collective-permute-start | bytes 104456 | tf_op jit(solution)/shard_map/ppermute | solution.py:348
  27.7 0.2 collective-permute-done.8.refs_0_
  27.9 1.7 %collective-permute-done.13.refs_6_ = s16[1,8,2176]{2,1,0:T(8,128)(2,1)S(1)} collective-permute-done((s16[1,8,2176]{2,1,0:T(8,128)(2,1)S(1)}, s16[1,8,2176]{2,1,0:T(8,128)(2,1)S(1)}, u32[]{:S(2)}, u32[]{:S(2)}) %collective-permute-start.13) | collective-permute-done | bytes 34848 | tf_op jit(solution)/shard_map/ppermute | solution.py:348
  29.6 0.7 %last_sum.1 = f32[8,2048]{1,0:T(8,128)} custom-call(f32[8,2048]{1,0:T(8,128)S(1)} %collective-permute-done.8.refs_0_, f32[8,2048]{1,0:T(8,128)S(1)} %collective-permute-done.9.refs_1_, f32[8,2048]{1,0:T(8,128)S(1)} %collective-permute-done.10.refs_2_, f32[4,8,2048]{2,1,0:T(8,128)S(1)} %get-tuple-element.15.keep_ref.refs_3_, ...), custom_call_target="tpu_custom_call" | custom-call | tf_op jit(solution)/shard_map/last_sum/pallas_call | solution.py:337
  (18 shorter events, 0.1 us)
Async XLA Ops:
  0.0 8.8 %collective-permute-start.3 = (bf16[8,2048]{1,0:T(8,128)(2,1)}, bf16[8,2048]{1,0:T(8,128)(2,1)S(1)}, u32[]{:S(2)}, u32[]{:S(2)}) collective-permute-start(bf16[8,2048]{1,0:T(8,128)(2,1)} %refs_0_.1), channel_id=1, source_target_pairs={{0,8},{4,12},{8,0},{12,4},{16,24},{20,28},{24,16},{28,20},{1,9},{5... | collective-permute-start | bytes 98312 | tf_op jit(solution)/shard_map/ppermute | solution.py:348
  2.9 9.1 %collective-permute-start.2 = (bf16[8,2048]{1,0:T(8,128)(2,1)}, bf16[8,2048]{1,0:T(8,128)(2,1)S(1)}, u32[]{:S(2)}, u32[]{:S(2)}) collective-permute-start(bf16[8,2048]{1,0:T(8,128)(2,1)} %refs_0_.1), channel_id=1, source_target_pairs={{0,3},{1,2},{2,1},{3,0},{4,7},{5,6},{6,5},{7,4},{8,11},{9,10},{10,... | collective-permute-start | bytes 98312 | tf_op jit(solution)/shard_map/ppermute | solution.py:348
  6.5 5.5 %collective-permute-start.1 = (bf16[8,2048]{1,0:T(8,128)(2,1)}, bf16[8,2048]{1,0:T(8,128)(2,1)S(1)}, u32[]{:S(2)}, u32[]{:S(2)}) collective-permute-start(bf16[8,2048]{1,0:T(8,128)(2,1)} %refs_0_.1), channel_id=1, source_target_pairs={{0,2},{1,3},{2,0},{3,1},{4,6},{5,7},{6,4},{7,5},{8,10},{9,11},{10,... | collective-permute-start | bytes 98312 | tf_op jit(solution)/shard_map/ppermute | solution.py:348
  6.5 5.6 %collective-permute-start = (bf16[8,2048]{1,0:T(8,128)(2,1)}, bf16[8,2048]{1,0:T(8,128)(2,1)S(1)}, u32[]{:S(2)}, u32[]{:S(2)}) collective-permute-start(bf16[8,2048]{1,0:T(8,128)(2,1)} %refs_0_.1), channel_id=1, source_target_pairs={{0,1},{1,0},{2,3},{3,2},{4,5},{5,4},{6,7},{7,6},{8,9},{9,8},{10,11... | collective-permute-start | bytes 98312 | tf_op jit(solution)/shard_map/ppermute | solution.py:348
  7.3 5.0 %collective-permute-start.5 = (bf16[8,2048]{1,0:T(8,128)(2,1)}, bf16[8,2048]{1,0:T(8,128)(2,1)S(1)}, u32[]{:S(2)}, u32[]{:S(2)}) collective-permute-start(bf16[8,2048]{1,0:T(8,128)(2,1)} %refs_0_.1), channel_id=1, source_target_pairs={{0,24},{4,28},{8,16},{12,20},{16,8},{20,12},{24,0},{28,4},{1,25},{... | collective-permute-start | bytes 98312 | tf_op jit(solution)/shard_map/ppermute | solution.py:348
  8.8 4.1 %collective-permute-start.4 = (bf16[8,2048]{1,0:T(8,128)(2,1)}, bf16[8,2048]{1,0:T(8,128)(2,1)S(1)}, u32[]{:S(2)}, u32[]{:S(2)}) collective-permute-start(bf16[8,2048]{1,0:T(8,128)(2,1)} %refs_0_.1), channel_id=1, source_target_pairs={{0,16},{4,20},{8,24},{12,28},{16,0},{20,4},{24,8},{28,12},{1,17},{... | collective-permute-start | bytes 98312 | tf_op jit(solution)/shard_map/ppermute | solution.py:348
  9.1 0.8 %copy-start.4 = (bf16[8,2048]{1,0:T(8,128)(2,1)S(1)}, bf16[8,2048]{1,0:T(8,128)(2,1)}, u32[]{:S(2)}) copy-start(bf16[8,2048]{1,0:T(8,128)(2,1)} %refs_0_.1) | copy-start | bytes 98308
  9.9 1.4 %copy-start = (bf16[192,4096]{1,0:T(8,128)(2,1)S(1)}, bf16[192,4096]{1,0:T(8,128)(2,1)}, u32[]{:S(2)}) copy-start(bf16[192,4096]{1,0:T(8,128)(2,1)} %param.9) | copy-start | bytes 4718596
  12.0 1.7 %copy-start.3 = (bf16[128,512]{1,0:T(8,128)(2,1)S(1)}, bf16[128,512]{1,0:T(8,128)(2,1)}, u32[]{:S(2)}) copy-start(bf16[128,512]{1,0:T(8,128)(2,1)} %constant.4.clone.spread_ref) | copy-start | bytes 393220
  12.0 1.7 %copy-start.5 = (s32[192]{0:T(256)S(1)}, s32[192]{0:T(256)}, u32[]{:S(2)}) copy-start(s32[192]{0:T(256)} %rows_ref.3) | copy-start | bytes 2308
  12.0 1.7 %copy-start.6 = (s32[192]{0:T(256)S(1)}, s32[192]{0:T(256)}, u32[]{:S(2)}) copy-start(s32[192]{0:T(256)} %cols_ref.3) | copy-start | bytes 2308
  12.1 4.8 %copy-start.1 = (bf16[512,128]{1,0:T(8,128)(2,1)S(1)}, bf16[512,128]{1,0:T(8,128)(2,1)}, u32[]{:S(2)}) copy-start(bf16[512,128]{1,0:T(8,128)(2,1)} %constant.7.fold_ref) | copy-start | bytes 393220
  12.1 4.8 %copy-start.2 = (bf16[128,512]{1,0:T(8,128)(2,1)S(1)}, bf16[128,512]{1,0:T(8,128)(2,1)}, u32[]{:S(2)}) copy-start(bf16[128,512]{1,0:T(8,128)(2,1)} %constant.5.clone.spread_ref) | copy-start | bytes 393220
  13.0 3.9 %collective-permute-start.11 = (bf16[4,8,2048]{2,1,0:T(8,128)(2,1)S(1)}, bf16[4,8,2048]{2,1,0:T(8,128)(2,1)S(1)}, u32[]{:S(2)}, u32[]{:S(2)}) collective-permute-start(bf16[4,8,2048]{2,1,0:T(8,128)(2,1)S(1)} %stack_pieces.3.refs_4_.same_ref), channel_id=1, source_target_pairs={{0,4},{4,0},{8,12},{12,8},{16,20},{20,16},{24,28},{28,24},{1,5},{5... | collective-permute-start | bytes 393224 | tf_op jit(solution)/shard_map/ppermute | solution.py:348
  15.9 4.8 %collective-permute-start.7 = (f32[2,8,2048]{2,1,0:T(8,128)S(1)}, f32[2,8,2048]{2,1,0:T(8,128)S(1)}, u32[]{:S(2)}, u32[]{:S(2)}) collective-permute-start(f32[2,8,2048]{2,1,0:T(8,128)S(1)} %get-tuple-element.17), channel_id=1, source_target_pairs={{0,4},{4,0},{8,12},{12,8},{16,20},{20,16},{24,28},{28,24},{1,5},{5... | collective-permute-start | bytes 393224 | tf_op jit(solution)/shard_map/ppermute | solution.py:348
  16.7 4.0 %collective-permute-start.6 = (f32[2,8,2048]{2,1,0:T(8,128)S(1)}, f32[2,8,2048]{2,1,0:T(8,128)S(1)}, u32[]{:S(2)}, u32[]{:S(2)}) collective-permute-start(f32[2,8,2048]{2,1,0:T(8,128)S(1)} %get-tuple-element.16.after_ref), channel_id=1, source_target_pairs={{0,4},{4,0},{8,12},{12,8},{16,20},{20,16},{24,28},{28,24},{1,5},{5... | collective-permute-start | bytes 393224 | tf_op jit(solution)/shard_map/ppermute | solution.py:348
  19.7 4.7 %collective-permute-start.12 = (s16[2,8,2176]{2,1,0:T(8,128)(2,1)S(1)}, s16[2,8,2176]{2,1,0:T(8,128)(2,1)S(1)}, u32[]{:S(2)}, u32[]{:S(2)}) collective-permute-start(s16[2,8,2176]{2,1,0:T(8,128)(2,1)S(1)} %get-tuple-element.22), channel_id=1, source_target_pairs={{0,1},{1,0},{2,3},{3,2},{4,5},{5,4},{6,7},{7,6},{8,9},{9,8},{10,11... | collective-permute-start | bytes 208904 | tf_op jit(solution)/shard_map/ppermute | solution.py:348
  20.8 6.9 %collective-permute-start.9 = (f32[8,2048]{1,0:T(8,128)S(1)}, f32[8,2048]{1,0:T(8,128)S(1)}, u32[]{:S(2)}, u32[]{:S(2)}) collective-permute-start(f32[8,2048]{1,0:T(8,128)S(1)} %get-tuple-element.19), channel_id=1, source_target_pairs={{0,16},{4,20},{8,24},{12,28},{16,0},{20,4},{24,8},{28,12},{1,17},{... | collective-permute-start | bytes 196616 | tf_op jit(solution)/shard_map/ppermute | solution.py:348
  21.9 5.8 %collective-permute-start.10 = (f32[8,2048]{1,0:T(8,128)S(1)}, f32[8,2048]{1,0:T(8,128)S(1)}, u32[]{:S(2)}, u32[]{:S(2)}) collective-permute-start(f32[8,2048]{1,0:T(8,128)S(1)} %get-tuple-element.20), channel_id=1, source_target_pairs={{0,24},{4,28},{8,16},{12,20},{16,8},{20,12},{24,0},{28,4},{1,25},{... | collective-permute-start | bytes 196616 | tf_op jit(solution)/shard_map/ppermute | solution.py:348
  23.7 4.3 %collective-permute-start.8 = (f32[8,2048]{1,0:T(8,128)S(1)}, f32[8,2048]{1,0:T(8,128)S(1)}, u32[]{:S(2)}, u32[]{:S(2)}) collective-permute-start(f32[8,2048]{1,0:T(8,128)S(1)} %get-tuple-element.18.after_ref), channel_id=1, source_target_pairs={{0,8},{4,12},{8,0},{12,4},{16,24},{20,28},{24,16},{28,20},{1,9},{5... | collective-permute-start | bytes 196616 | tf_op jit(solution)/shard_map/ppermute | solution.py:348
  24.6 5.1 %collective-permute-start.13 = (s16[1,8,2176]{2,1,0:T(8,128)(2,1)S(1)}, s16[1,8,2176]{2,1,0:T(8,128)(2,1)S(1)}, u32[]{:S(2)}, u32[]{:S(2)}) collective-permute-start(s16[1,8,2176]{2,1,0:T(8,128)(2,1)S(1)} %get-tuple-element.24), channel_id=1, source_target_pairs={{0,2},{1,3},{2,0},{3,1},{4,6},{5,7},{6,4},{7,5},{8,10},{9,11},{10,... | collective-permute-start | bytes 104456 | tf_op jit(solution)/shard_map/ppermute | solution.py:348

commit v7 on v6

--- a/solution.py
+++ b/solution.py
@@ -40,7 +40,13 @@
 
 
 def row_fold():
-    return row_spread().T
+    out = np.zeros((2, 2, 2, GROUP // 2, HALF, LANES), np.float32)
+    for q in range(2):
+        for e in range(2):
+            for m in range(HALF):
+                out[q, 0, e, :, m, q * TILE + 2 * m + e] = 1
+                out[q, 1, 1 - e, :, m, q * TILE + 2 * m + e] = 1
+    return jnp.asarray(out.reshape(4 * LANES, LANES), BF16)
 
 
 def encode(values, out_ref):
@@ -106,14 +112,15 @@
 
 def backward_kernel(n_in, rows_ref, cols_ref, count_ref, spread_ref, tiles_ref, *refs):
     pieces = refs[:n_in]
-    _, keep_ref, *give_refs, table, acc = refs[n_in:]
+    _, keep_ref, *give_refs, table, acc_a, acc_b = refs[n_in:]
     per_give = give_refs[0].shape[0]
     n_out = 2 * keep_ref.shape[0]
     width, piece = pieces[0].shape
     per_piece = piece // TILE
     slots = tiles_ref.shape[0]
     build_table(pieces, spread_ref[...], table)
-    acc[...] = jnp.zeros_like(acc)
+    for acc in (acc_a, acc_b):
+        acc[...] = jnp.zeros_like(acc)
     lane = lax.broadcasted_iota(jnp.int32, (2 * width, LANES), 1)
     masks = [(lane // HALF == s).astype(BF16) for s in range(GROUP)]
     low = lax.broadcasted_iota(jnp.int32, (width, LANES), 1) < TILE
@@ -131,14 +138,16 @@
             part = out[2 * width * s : 2 * width * (s + 1)]
             part = jnp.where(low, part[:width], part[width:])
             c = jnp.where(t < count, cols_ref[t] ^ col_flip, spare)
+            acc = acc_a if s % 2 == 0 else acc_b
             acc[c] += part
 
     for n in range(n_out):
         h = n // 2
         dest = keep_ref.at[h] if n % 2 == 0 else give_refs[h // per_give].at[h % per_give]
         for p in range(per_piece // 2):
-            a = acc[n * per_piece + 2 * p]
-            b = acc[n * per_piece + 2 * p + 1]
+            at = n * per_piece + 2 * p
+            a = acc_a[at] + acc_b[at]
+            b = acc_a[at + 1] + acc_b[at + 1]
             dest[:, p * LANES : (p + 1) * LANES] = jnp.where(low, a, b) + pltpu.roll(
                 jnp.where(low, b, a), TILE, 1
             )
@@ -157,6 +166,7 @@
         out_shape=[half, quarter, quarter],
         scratch_shapes=[
             pltpu.VMEM((n_in * per_piece, 2 * width, LANES), BF16),
+            pltpu.VMEM((n_out * per_piece + 1, width, LANES), F32),
             pltpu.VMEM((n_out * per_piece + 1, width, LANES), F32),
         ],
         compiler_params=PARAMS,
@@ -180,7 +190,8 @@
     keep_ref,
     give_ref,
     table,
-    acc,
+    acc_a,
+    acc_b,
 ):
     pieces = [ref.at[h] for h in range(same_ref.shape[0]) for ref in (same_ref, other_ref)]
     n_out = 2 * keep_ref.shape[0]
@@ -188,8 +199,9 @@
     per_piece = piece // TILE
     slots = tiles_ref.shape[0]
     build_table(pieces, spread_ref[...], table)
-    acc[...] = jnp.zeros_like(acc)
-    lane = lax.broadcasted_iota(jnp.int32, (2 * width, LANES), 1)
+    for acc in (acc_a, acc_b):
+        acc[...] = jnp.zeros_like(acc)
+    lane = lax.broadcasted_iota(jnp.int32, (width, LANES), 1)
     masks = [lane // HALF == s for s in range(GROUP)]
     count = count_ref[0, 0]
     row_flip = lax.axis_index("bcol") * per_piece
@@ -209,15 +221,22 @@
             t = g * GROUP + s
             part = out[2 * width * s : 2 * width * (s + 1)]
             r = jnp.where(t < count, rows_ref[t] ^ row_flip, spare)
-            acc[r] += jnp.where(masks[s], part, 0.0)
+            part = jnp.where(
+                masks[s],
+                part[:width],
+                jnp.where(masks[(s + 2) % GROUP], pltpu.roll(part[width:], TILE, 1), 0.0),
+            )
+            acc = acc_a if s < 2 else acc_b
+            acc[r] += part
 
     fold = fold_ref[...]
     pairs = per_piece // 2
     for n in range(n_out):
-        both = acc[n * per_piece : (n + 1) * per_piece].reshape(pairs, 4 * width, LANES)
-        blocks = [
-            both[:, x * width : (x + 1) * width, :].reshape(pairs * width, LANES) for x in range(4)
-        ]
+        blocks = []
+        for q in range(2):
+            for acc in (acc_a, acc_b):
+                both = acc[n * per_piece : (n + 1) * per_piece].reshape(pairs, 2 * width, LANES)
+                blocks.append(both[:, q * width : (q + 1) * width, :].reshape(pairs * width, LANES))
         wide = jnp.concatenate(blocks, axis=1)
         first = wide.astype(BF16)
         rest = (wide - first.astype(F32)).astype(BF16)
@@ -243,7 +262,8 @@
         out_shape=[half, coded],
         scratch_shapes=[
             pltpu.VMEM((2 * n_chips * per_piece, 2 * width, LANES), BF16),
-            pltpu.VMEM((n_out * per_piece + 1, 2 * width, LANES), F32),
+            pltpu.VMEM((n_out * per_piece + 1, width, LANES), F32),
+            pltpu.VMEM((n_out * per_piece + 1, width, LANES), F32),
         ],
         compiler_params=PARAMS,
         cost_estimate=pl.CostEstimate(

time: 30.6 us -> 30.1 us (0.984)
  Pallas kernels: 6.7 us -> 6.37 us
    pallas_call x1, Pallas kernels: 2.22 us -> 1.89 us  [backward(): pl.pallas_call(functools.partial(backward_kernel, n_in), in_specs=[SMEM]...]
    ppermute x14, starting transfers between devices: 17.8 us -> 17.5 us  [swap(): return lax.ppermute(x, axis, [(i, i ^ d) for i in range(size)])]
  transfers between devices with their start and end apart: 14 -> 14, of which waited for: 4 -> 5; matrix products, arithmetic and copies ran while one was open for 0% -> 0% of each run, Pallas kernels for 20% -> 19%
where the time goes in v7:
time: 30.1 us; the launch traced here: 29.8 us
  starting transfers between devices  17.5 us (58%)
  Pallas kernels  6.37 us (21%)
  waiting for transfers between devices  2.89 us (10%)
  local copies, waits for them, and re-layouts  2.23 us (7%)
  between operations  0.8 us (3%)
    ppermute x14, starting transfers between devices, swap(): return lax.ppermute(x, axis, [(i, i ^ d) for i in range(size)])  17.5 us
    ppermute x14, waiting for transfers between devices, swap(): return lax.ppermute(x, axis, [(i, i ^ d) for i in range(size)])  2.89 us
    pallas_call x1, Pallas kernels, forward(): pl.pallas_call(forward_kernel, in_specs=[SMEM] * 3 + [VMEM] * 5 + [ANY],...  2.81 us
    unnamed x14, local copies, waits for them, and re-layouts  2.23 us
    pallas_call x1, Pallas kernels, backward(): pl.pallas_call(functools.partial(backward_kernel, n_in), in_specs=[SMEM]...  1.89 us
    pallas_call x1, Pallas kernels, last_sum(): pl.pallas_call(last_sum_kernel, in_specs=[VMEM] * (4 + len(chips)), out_s...  0.74 us
    pallas_call x1, Pallas kernels, prep(): pl.pallas_call(prep_kernel, in_specs=[VMEM], out_specs=VMEM, out_shape=ja...  0.69 us
  transfers between devices with their start and end apart: 14, of which 5 were waited for; matrix products, arithmetic and copies ran while one was open for 0% of the time, Pallas kernels for 19%

profile of v7, /device:TPU:0, one launch (start us, length us, event | category | flops | bytes accessed | tf_op | source)
XLA Modules:
  0.0 29.8 jit_solution(15247117103991649574)
XLA Ops:
  0.0 2.9 %collective-permute-start.3 = (bf16[8,2048]{1,0:T(8,128)(2,1)}, bf16[8,2048]{1,0:T(8,128)(2,1)S(1)}, u32[]{:S(2)}, u32[]{:S(2)}) collective-permute-start(bf16[8,2048]{1,0:T(8,128)(2,1)} %refs_0_.1), channel_id=1, source_target_pairs={{0,8},{4,12},{8,0},{12,4},{16,24},{20,28},{24,16},{28,20},{1,9},{5... | collective-permute-start | bytes 98312 | tf_op jit(solution)/shard_map/ppermute | solution.py:368
  2.9 3.6 %collective-permute-start.2 = (bf16[8,2048]{1,0:T(8,128)(2,1)}, bf16[8,2048]{1,0:T(8,128)(2,1)S(1)}, u32[]{:S(2)}, u32[]{:S(2)}) collective-permute-start(bf16[8,2048]{1,0:T(8,128)(2,1)} %refs_0_.1), channel_id=1, source_target_pairs={{0,3},{1,2},{2,1},{3,0},{4,7},{5,6},{6,5},{7,4},{8,11},{9,10},{10,... | collective-permute-start | bytes 98312 | tf_op jit(solution)/shard_map/ppermute | solution.py:368
  6.5 0.8 %collective-permute-start = (bf16[8,2048]{1,0:T(8,128)(2,1)}, bf16[8,2048]{1,0:T(8,128)(2,1)S(1)}, u32[]{:S(2)}, u32[]{:S(2)}) collective-permute-start(bf16[8,2048]{1,0:T(8,128)(2,1)} %refs_0_.1), channel_id=1, source_target_pairs={{0,1},{1,0},{2,3},{3,2},{4,5},{5,4},{6,7},{7,6},{8,9},{9,8},{10,11... | collective-permute-start | bytes 98312 | tf_op jit(solution)/shard_map/ppermute | solution.py:368
  7.3 1.5 %collective-permute-start.5 = (bf16[8,2048]{1,0:T(8,128)(2,1)}, bf16[8,2048]{1,0:T(8,128)(2,1)S(1)}, u32[]{:S(2)}, u32[]{:S(2)}) collective-permute-start(bf16[8,2048]{1,0:T(8,128)(2,1)} %refs_0_.1), channel_id=1, source_target_pairs={{0,24},{4,28},{8,16},{12,20},{16,8},{20,12},{24,0},{28,4},{1,25},{... | collective-permute-start | bytes 98312 | tf_op jit(solution)/shard_map/ppermute | solution.py:368
  8.8 0.0 collective-permute-done.3.refs_1_
  8.8 0.3 collective-permute-start.4
  9.1 0.8 %copy-done.4 = bf16[8,2048]{1,0:T(8,128)(2,1)S(1)} copy-done((bf16[8,2048]{1,0:T(8,128)(2,1)S(1)}, bf16[8,2048]{1,0:T(8,128)(2,1)}, u32[]{:S(2)}) %copy-start.4) | copy-done | bytes 32792
  9.9 1.4 %copy-done = bf16[192,4096]{1,0:T(8,128)(2,1)S(1)} copy-done((bf16[192,4096]{1,0:T(8,128)(2,1)S(1)}, bf16[192,4096]{1,0:T(8,128)(2,1)}, u32[]{:S(2)}) %copy-start) | copy-done | bytes 1572888
  11.3 0.7 %prep_tiles.1.refs_4_.tiles_ref = bf16[192,32,128]{2,1,0:T(8,128)(2,1)S(1)} custom-call(bf16[24,32,8,128]{3,2,1,0:T(8,128)(2,1)S(1)} %bitcast.4), custom_call_target="tpu_custom_call" | custom-call | bytes 3145728 | tf_op jit(solution)/shard_map/prep_tiles/pallas_call | solution.py:86
  12.0 0.0 copy-start.3
  12.0 0.0 copy-start.5
  12.0 0.0 copy-start.6
  12.1 0.0 copy-start.1
  12.1 0.0 copy-start.2
  12.1 0.0 collective-permute-done.1.refs_6_.refs_2_
  12.1 0.2 collective-permute-done.5.refs_3_
  12.4 0.6 %collective-permute-done.4.refs_2_ = bf16[8,2048]{1,0:T(8,128)(2,1)S(1)} collective-permute-done((bf16[8,2048]{1,0:T(8,128)(2,1)}, bf16[8,2048]{1,0:T(8,128)(2,1)S(1)}, u32[]{:S(2)}, u32[]{:S(2)}) %collective-permute-start.4) | collective-permute-done | bytes 32800 | tf_op jit(solution)/shard_map/ppermute | solution.py:368
  13.0 0.1 collective-permute-start.11
  13.7 1.9 %transpose_product.1 = (f32[4,8,2048]{2,1,0:T(8,128)S(1)}, f32[2,8,2048]{2,1,0:T(8,128)S(1)}, f32[2,8,2048]{2,1,0:T(8,128)S(1)}) custom-call(s32[192]{0:T(256)S(1)} %copy-done.5, s32[192]{0:T(256)S(1)} %copy-done.6, s32[1,1]{1,0:T(1,128)S(6)} %copy.9.count_ref, bf16[128,512]{1,0:T(8,128)(2,1)S(1)} %copy-done.3, ...), custom_call_target="tpu_custom_call" | custom-call | flops 100663296 | bytes 3145728 | tf_op jit(solution)/shard_map/transpose_product/pallas_call | solution.py:162
  15.6 0.5 %collective-permute-start.7 = (f32[2,8,2048]{2,1,0:T(8,128)S(1)}, f32[2,8,2048]{2,1,0:T(8,128)S(1)}, u32[]{:S(2)}, u32[]{:S(2)}) collective-permute-start(f32[2,8,2048]{2,1,0:T(8,128)S(1)} %get-tuple-element.17), channel_id=1, source_target_pairs={{0,4},{4,0},{8,12},{12,8},{16,20},{20,16},{24,28},{28,24},{1,5},{5... | collective-permute-start | bytes 393224 | tf_op jit(solution)/shard_map/ppermute | solution.py:368
  16.2 0.1 collective-permute-start.6
  16.3 2.8 %forward_product.1 = (f32[2,8,2048]{2,1,0:T(8,128)S(1)}, s16[2,8,2176]{2,1,0:T(8,128)(2,1)S(1)}) custom-call(s32[192]{0:T(256)S(1)} %copy-done.5, s32[192]{0:T(256)S(1)} %copy-done.6, s32[1,1]{1,0:T(1,128)S(6)} %copy.9.count_ref, bf16[128,512]{1,0:T(8,128)(2,1)S(1)} %copy-done.2, bf16[512,128]{1,0:T(8,128)(2,1)S(1)} %copy-done.1, ...), custom_call_target="tpu_custom_call" | custom-call | flops 100663296 | bytes 3145728 | tf_op jit(solution)/shard_map/forward_product/pallas_call | solution.py:258
  19.1 1.3 %collective-permute-start.12 = (s16[2,8,2176]{2,1,0:T(8,128)(2,1)S(1)}, s16[2,8,2176]{2,1,0:T(8,128)(2,1)S(1)}, u32[]{:S(2)}, u32[]{:S(2)}) collective-permute-start(s16[2,8,2176]{2,1,0:T(8,128)(2,1)S(1)} %get-tuple-element.22), channel_id=1, source_target_pairs={{0,1},{1,0},{2,3},{3,2},{4,5},{5,4},{6,7},{7,6},{8,9},{9,8},{10,11... | collective-permute-start | bytes 208904 | tf_op jit(solution)/shard_map/ppermute | solution.py:368
  20.4 1.0 %collective-permute-start.9 = (f32[8,2048]{1,0:T(8,128)S(1)}, f32[8,2048]{1,0:T(8,128)S(1)}, u32[]{:S(2)}, u32[]{:S(2)}) collective-permute-start(f32[8,2048]{1,0:T(8,128)S(1)} %get-tuple-element.19), channel_id=1, source_target_pairs={{0,16},{4,20},{8,24},{12,28},{16,0},{20,4},{24,8},{28,12},{1,17},{... | collective-permute-start | bytes 196616 | tf_op jit(solution)/shard_map/ppermute | solution.py:368
  21.4 2.0 %collective-permute-start.10 = (f32[8,2048]{1,0:T(8,128)S(1)}, f32[8,2048]{1,0:T(8,128)S(1)}, u32[]{:S(2)}, u32[]{:S(2)}) collective-permute-start(f32[8,2048]{1,0:T(8,128)S(1)} %get-tuple-element.20), channel_id=1, source_target_pairs={{0,24},{4,28},{8,16},{12,20},{16,8},{20,12},{24,0},{28,4},{1,25},{... | collective-permute-start | bytes 196616 | tf_op jit(solution)/shard_map/ppermute | solution.py:368
  23.5 0.5 %collective-permute-start.8 = (f32[8,2048]{1,0:T(8,128)S(1)}, f32[8,2048]{1,0:T(8,128)S(1)}, u32[]{:S(2)}, u32[]{:S(2)}) collective-permute-start(f32[8,2048]{1,0:T(8,128)S(1)} %get-tuple-element.18.after_ref), channel_id=1, source_target_pairs={{0,8},{4,12},{8,0},{12,4},{16,24},{20,28},{24,16},{28,20},{1,9},{5... | collective-permute-start | bytes 196616 | tf_op jit(solution)/shard_map/ppermute | solution.py:368
  24.0 0.2 halving_sum.1
  24.2 2.9 %collective-permute-start.13 = (s16[1,8,2176]{2,1,0:T(8,128)(2,1)S(1)}, s16[1,8,2176]{2,1,0:T(8,128)(2,1)S(1)}, u32[]{:S(2)}, u32[]{:S(2)}) collective-permute-start(s16[1,8,2176]{2,1,0:T(8,128)(2,1)S(1)} %get-tuple-element.24), channel_id=1, source_target_pairs={{0,2},{1,3},{2,0},{3,1},{4,6},{5,7},{6,4},{7,5},{8,10},{9,11},{10,... | collective-permute-start | bytes 104456 | tf_op jit(solution)/shard_map/ppermute | solution.py:368
  27.1 0.1 collective-permute-done.10.refs_2_
  27.1 0.6 %collective-permute-done.8.refs_0_ = f32[8,2048]{1,0:T(8,128)S(1)} collective-permute-done((f32[8,2048]{1,0:T(8,128)S(1)}, f32[8,2048]{1,0:T(8,128)S(1)}, u32[]{:S(2)}, u32[]{:S(2)}) %collective-permute-start.8) | collective-permute-done | bytes 65568 | tf_op jit(solution)/shard_map/ppermute | solution.py:368
  27.7 1.4 %collective-permute-done.13.refs_6_ = s16[1,8,2176]{2,1,0:T(8,128)(2,1)S(1)} collective-permute-done((s16[1,8,2176]{2,1,0:T(8,128)(2,1)S(1)}, s16[1,8,2176]{2,1,0:T(8,128)(2,1)S(1)}, u32[]{:S(2)}, u32[]{:S(2)}) %collective-permute-start.13) | collective-permute-done | bytes 34848 | tf_op jit(solution)/shard_map/ppermute | solution.py:368
  29.1 0.7 %last_sum.1 = f32[8,2048]{1,0:T(8,128)} custom-call(f32[8,2048]{1,0:T(8,128)S(1)} %collective-permute-done.8.refs_0_, f32[8,2048]{1,0:T(8,128)S(1)} %collective-permute-done.9.refs_1_, f32[8,2048]{1,0:T(8,128)S(1)} %collective-permute-done.10.refs_2_, f32[4,8,2048]{2,1,0:T(8,128)S(1)} %get-tuple-element.15.keep_ref.refs_3_, ...), custom_call_target="tpu_custom_call" | custom-call | tf_op jit(solution)/shard_map/last_sum/pallas_call | solution.py:357
  (18 shorter events, 0.1 us)
Async XLA Ops:
  0.0 8.8 %collective-permute-start.3 = (bf16[8,2048]{1,0:T(8,128)(2,1)}, bf16[8,2048]{1,0:T(8,128)(2,1)S(1)}, u32[]{:S(2)}, u32[]{:S(2)}) collective-permute-start(bf16[8,2048]{1,0:T(8,128)(2,1)} %refs_0_.1), channel_id=1, source_target_pairs={{0,8},{4,12},{8,0},{12,4},{16,24},{20,28},{24,16},{28,20},{1,9},{5... | collective-permute-start | bytes 98312 | tf_op jit(solution)/shard_map/ppermute | solution.py:368
  2.9 9.1 %collective-permute-start.2 = (bf16[8,2048]{1,0:T(8,128)(2,1)}, bf16[8,2048]{1,0:T(8,128)(2,1)S(1)}, u32[]{:S(2)}, u32[]{:S(2)}) collective-permute-start(bf16[8,2048]{1,0:T(8,128)(2,1)} %refs_0_.1), channel_id=1, source_target_pairs={{0,3},{1,2},{2,1},{3,0},{4,7},{5,6},{6,5},{7,4},{8,11},{9,10},{10,... | collective-permute-start | bytes 98312 | tf_op jit(solution)/shard_map/ppermute | solution.py:368
  6.5 5.5 %collective-permute-start.1 = (bf16[8,2048]{1,0:T(8,128)(2,1)}, bf16[8,2048]{1,0:T(8,128)(2,1)S(1)}, u32[]{:S(2)}, u32[]{:S(2)}) collective-permute-start(bf16[8,2048]{1,0:T(8,128)(2,1)} %refs_0_.1), channel_id=1, source_target_pairs={{0,2},{1,3},{2,0},{3,1},{4,6},{5,7},{6,4},{7,5},{8,10},{9,11},{10,... | collective-permute-start | bytes 98312 | tf_op jit(solution)/shard_map/ppermute | solution.py:368
  6.5 5.6 %collective-permute-start = (bf16[8,2048]{1,0:T(8,128)(2,1)}, bf16[8,2048]{1,0:T(8,128)(2,1)S(1)}, u32[]{:S(2)}, u32[]{:S(2)}) collective-permute-start(bf16[8,2048]{1,0:T(8,128)(2,1)} %refs_0_.1), channel_id=1, source_target_pairs={{0,1},{1,0},{2,3},{3,2},{4,5},{5,4},{6,7},{7,6},{8,9},{9,8},{10,11... | collective-permute-start | bytes 98312 | tf_op jit(solution)/shard_map/ppermute | solution.py:368
  7.3 5.0 %collective-permute-start.5 = (bf16[8,2048]{1,0:T(8,128)(2,1)}, bf16[8,2048]{1,0:T(8,128)(2,1)S(1)}, u32[]{:S(2)}, u32[]{:S(2)}) collective-permute-start(bf16[8,2048]{1,0:T(8,128)(2,1)} %refs_0_.1), channel_id=1, source_target_pairs={{0,24},{4,28},{8,16},{12,20},{16,8},{20,12},{24,0},{28,4},{1,25},{... | collective-permute-start | bytes 98312 | tf_op jit(solution)/shard_map/ppermute | solution.py:368
  8.8 4.1 %collective-permute-start.4 = (bf16[8,2048]{1,0:T(8,128)(2,1)}, bf16[8,2048]{1,0:T(8,128)(2,1)S(1)}, u32[]{:S(2)}, u32[]{:S(2)}) collective-permute-start(bf16[8,2048]{1,0:T(8,128)(2,1)} %refs_0_.1), channel_id=1, source_target_pairs={{0,16},{4,20},{8,24},{12,28},{16,0},{20,4},{24,8},{28,12},{1,17},{... | collective-permute-start | bytes 98312 | tf_op jit(solution)/shard_map/ppermute | solution.py:368
  9.1 0.8 %copy-start.4 = (bf16[8,2048]{1,0:T(8,128)(2,1)S(1)}, bf16[8,2048]{1,0:T(8,128)(2,1)}, u32[]{:S(2)}) copy-start(bf16[8,2048]{1,0:T(8,128)(2,1)} %refs_0_.1) | copy-start | bytes 98308
  9.9 1.4 %copy-start = (bf16[192,4096]{1,0:T(8,128)(2,1)S(1)}, bf16[192,4096]{1,0:T(8,128)(2,1)}, u32[]{:S(2)}) copy-start(bf16[192,4096]{1,0:T(8,128)(2,1)} %param.9) | copy-start | bytes 4718596
  12.0 1.7 %copy-start.3 = (bf16[128,512]{1,0:T(8,128)(2,1)S(1)}, bf16[128,512]{1,0:T(8,128)(2,1)}, u32[]{:S(2)}) copy-start(bf16[128,512]{1,0:T(8,128)(2,1)} %constant.6.clone.spread_ref) | copy-start | bytes 393220
  12.0 1.7 %copy-start.5 = (s32[192]{0:T(256)S(1)}, s32[192]{0:T(256)}, u32[]{:S(2)}) copy-start(s32[192]{0:T(256)} %rows_ref.3) | copy-start | bytes 2308
  12.0 1.7 %copy-start.6 = (s32[192]{0:T(256)S(1)}, s32[192]{0:T(256)}, u32[]{:S(2)}) copy-start(s32[192]{0:T(256)} %cols_ref.3) | copy-start | bytes 2308
  12.1 4.2 %copy-start.1 = (bf16[512,128]{1,0:T(8,128)(2,1)S(1)}, bf16[512,128]{1,0:T(8,128)(2,1)}, u32[]{:S(2)}) copy-start(bf16[512,128]{1,0:T(8,128)(2,1)} %constant.8.clone.fold_ref) | copy-start | bytes 393220
  12.1 4.2 %copy-start.2 = (bf16[128,512]{1,0:T(8,128)(2,1)S(1)}, bf16[128,512]{1,0:T(8,128)(2,1)}, u32[]{:S(2)}) copy-start(bf16[128,512]{1,0:T(8,128)(2,1)} %constant.7.clone.spread_ref) | copy-start | bytes 393220
  13.0 3.3 %collective-permute-start.11 = (bf16[4,8,2048]{2,1,0:T(8,128)(2,1)S(1)}, bf16[4,8,2048]{2,1,0:T(8,128)(2,1)S(1)}, u32[]{:S(2)}, u32[]{:S(2)}) collective-permute-start(bf16[4,8,2048]{2,1,0:T(8,128)(2,1)S(1)} %stack_pieces.3.refs_4_.same_ref), channel_id=1, source_target_pairs={{0,4},{4,0},{8,12},{12,8},{16,20},{20,16},{24,28},{28,24},{1,5},{5... | collective-permute-start | bytes 393224 | tf_op jit(solution)/shard_map/ppermute | solution.py:368
  15.6 4.8 %collective-permute-start.7 = (f32[2,8,2048]{2,1,0:T(8,128)S(1)}, f32[2,8,2048]{2,1,0:T(8,128)S(1)}, u32[]{:S(2)}, u32[]{:S(2)}) collective-permute-start(f32[2,8,2048]{2,1,0:T(8,128)S(1)} %get-tuple-element.17), channel_id=1, source_target_pairs={{0,4},{4,0},{8,12},{12,8},{16,20},{20,16},{24,28},{28,24},{1,5},{5... | collective-permute-start | bytes 393224 | tf_op jit(solution)/shard_map/ppermute | solution.py:368
  16.2 4.2 %collective-permute-start.6 = (f32[2,8,2048]{2,1,0:T(8,128)S(1)}, f32[2,8,2048]{2,1,0:T(8,128)S(1)}, u32[]{:S(2)}, u32[]{:S(2)}) collective-permute-start(f32[2,8,2048]{2,1,0:T(8,128)S(1)} %get-tuple-element.16.after_ref), channel_id=1, source_target_pairs={{0,4},{4,0},{8,12},{12,8},{16,20},{20,16},{24,28},{28,24},{1,5},{5... | collective-permute-start | bytes 393224 | tf_op jit(solution)/shard_map/ppermute | solution.py:368
  19.1 4.9 %collective-permute-start.12 = (s16[2,8,2176]{2,1,0:T(8,128)(2,1)S(1)}, s16[2,8,2176]{2,1,0:T(8,128)(2,1)S(1)}, u32[]{:S(2)}, u32[]{:S(2)}) collective-permute-start(s16[2,8,2176]{2,1,0:T(8,128)(2,1)S(1)} %get-tuple-element.22), channel_id=1, source_target_pairs={{0,1},{1,0},{2,3},{3,2},{4,5},{5,4},{6,7},{7,6},{8,9},{9,8},{10,11... | collective-permute-start | bytes 208904 | tf_op jit(solution)/shard_map/ppermute | solution.py:368
  20.4 6.6 %collective-permute-start.9 = (f32[8,2048]{1,0:T(8,128)S(1)}, f32[8,2048]{1,0:T(8,128)S(1)}, u32[]{:S(2)}, u32[]{:S(2)}) collective-permute-start(f32[8,2048]{1,0:T(8,128)S(1)} %get-tuple-element.19), channel_id=1, source_target_pairs={{0,16},{4,20},{8,24},{12,28},{16,0},{20,4},{24,8},{28,12},{1,17},{... | collective-permute-start | bytes 196616 | tf_op jit(solution)/shard_map/ppermute | solution.py:368
  21.4 5.7 %collective-permute-start.10 = (f32[8,2048]{1,0:T(8,128)S(1)}, f32[8,2048]{1,0:T(8,128)S(1)}, u32[]{:S(2)}, u32[]{:S(2)}) collective-permute-start(f32[8,2048]{1,0:T(8,128)S(1)} %get-tuple-element.20), channel_id=1, source_target_pairs={{0,24},{4,28},{8,16},{12,20},{16,8},{20,12},{24,0},{28,4},{1,25},{... | collective-permute-start | bytes 196616 | tf_op jit(solution)/shard_map/ppermute | solution.py:368
  23.5 4.3 %collective-permute-start.8 = (f32[8,2048]{1,0:T(8,128)S(1)}, f32[8,2048]{1,0:T(8,128)S(1)}, u32[]{:S(2)}, u32[]{:S(2)}) collective-permute-start(f32[8,2048]{1,0:T(8,128)S(1)} %get-tuple-element.18.after_ref), channel_id=1, source_target_pairs={{0,8},{4,12},{8,0},{12,4},{16,24},{20,28},{24,16},{28,20},{1,9},{5... | collective-permute-start | bytes 196616 | tf_op jit(solution)/shard_map/ppermute | solution.py:368
  24.2 4.9 %collective-permute-start.13 = (s16[1,8,2176]{2,1,0:T(8,128)(2,1)S(1)}, s16[1,8,2176]{2,1,0:T(8,128)(2,1)S(1)}, u32[]{:S(2)}, u32[]{:S(2)}) collective-permute-start(s16[1,8,2176]{2,1,0:T(8,128)(2,1)S(1)} %get-tuple-element.24), channel_id=1, source_target_pairs={{0,2},{1,3},{2,0},{3,1},{4,6},{5,7},{6,4},{7,5},{8,10},{9,11},{10,... | collective-permute-start | bytes 104456 | tf_op jit(solution)/shard_map/ppermute | solution.py:368

commit v8 on v7

--- a/solution.py
+++ b/solution.py
@@ -27,15 +27,6 @@
         for e in range(2):
             for m in range(HALF):
                 out[q * TILE + 2 * m + e, q, e, :, m] = 1
-    return jnp.asarray(out.reshape(LANES, 4 * LANES), BF16)
-
-
-def col_spread():
-    out = np.zeros((LANES, 2, 2, 2, TILE), np.float32)
-    for q in range(2):
-        for e in range(2):
-            for j in range(TILE):
-                out[q * TILE + j, q, e, e, j] = 1
     return jnp.asarray(out.reshape(LANES, 4 * LANES), BF16)
 
 
@@ -177,11 +168,22 @@
     )(tile_rows, tile_cols, counts, row_spread(), tiles, *pieces, after)
 
 
+def double_table(pieces, table):
+    width, piece = pieces[0].shape
+    low = lax.broadcasted_iota(jnp.int32, (width, LANES), 1) < TILE
+    for n, ref in enumerate(pieces):
+        for p in range(piece // LANES):
+            pair = ref[:, p * LANES : (p + 1) * LANES].astype(F32)
+            turned = pltpu.roll(pair, TILE, 1)
+            at = (n * piece + p * LANES) // TILE
+            table[at] = jnp.where(low, pair, turned)
+            table[at + 1] = jnp.where(low, turned, pair)
+
+
 def forward_kernel(
     rows_ref,
     cols_ref,
     count_ref,
-    spread_ref,
     fold_ref,
     tiles_ref,
     same_ref,
@@ -198,11 +200,13 @@
     width, piece = pieces[0].shape
     per_piece = piece // TILE
     slots = tiles_ref.shape[0]
-    build_table(pieces, spread_ref[...], table)
+    double_table(pieces, table)
     for acc in (acc_a, acc_b):
         acc[...] = jnp.zeros_like(acc)
     lane = lax.broadcasted_iota(jnp.int32, (width, LANES), 1)
     masks = [lane // HALF == s for s in range(GROUP)]
+    wide_lane = lax.broadcasted_iota(jnp.int32, (LANES, LANES), 1)
+    parity = [(wide_lane // TILE == e).astype(BF16) for e in range(2)]
     count = count_ref[0, 0]
     row_flip = lax.axis_index("bcol") * per_piece
     col_flip = lax.axis_index("brow") * per_piece
@@ -211,20 +215,19 @@
     for g in range(slots // GROUP):
         at = [table[cols_ref[g * GROUP + s] ^ col_flip] for s in range(GROUP)]
         block = tiles_ref[g * GROUP : (g + 1) * GROUP].reshape(LANES, LANES)
+        turned = jnp.concatenate([block[LANES // 2 :], block[: LANES // 2]], axis=0)
         out = lax.dot_general(
-            jnp.concatenate(at, axis=0),
-            block,
+            jnp.concatenate(at, axis=0).astype(BF16),
+            jnp.concatenate([block * parity[0], turned * parity[1]], axis=0),
             (((1,), (1,)), ((), ())),
             preferred_element_type=F32,
         )
         for s in range(GROUP):
             t = g * GROUP + s
-            part = out[2 * width * s : 2 * width * (s + 1)]
+            part = out[width * s : width * (s + 1)]
             r = jnp.where(t < count, rows_ref[t] ^ row_flip, spare)
             part = jnp.where(
-                masks[s],
-                part[:width],
-                jnp.where(masks[(s + 2) % GROUP], pltpu.roll(part[width:], TILE, 1), 0.0),
+                masks[s], part[:, :LANES], jnp.where(masks[(s + 2) % GROUP], part[:, LANES:], 0.0)
             )
             acc = acc_a if s < 2 else acc_b
             acc[r] += part
@@ -257,11 +260,11 @@
     coded = jax.ShapeDtypeStruct((n_out // 2, width, piece + LANES), jnp.int16)
     return pl.pallas_call(
         forward_kernel,
-        in_specs=[SMEM] * 3 + [VMEM] * 5 + [ANY],
+        in_specs=[SMEM] * 3 + [VMEM] * 4 + [ANY],
         out_specs=[VMEM] * 2,
         out_shape=[half, coded],
         scratch_shapes=[
-            pltpu.VMEM((2 * n_chips * per_piece, 2 * width, LANES), BF16),
+            pltpu.VMEM((2 * n_chips * per_piece, width, LANES), F32),
             pltpu.VMEM((n_out * per_piece + 1, width, LANES), F32),
             pltpu.VMEM((n_out * per_piece + 1, width, LANES), F32),
         ],
@@ -270,7 +273,7 @@
             flops=2 * tiles.size * 64, bytes_accessed=4 * tiles.size, transcendentals=0
         ),
         name="forward_product",
-    )(tile_rows, tile_cols, counts, col_spread(), row_fold(), tiles, same, other, after)
+    )(tile_rows, tile_cols, counts, row_fold(), tiles, same, other, after)
 
 
 def stack_kernel(n_after, *refs):

time: 30.1 us -> 29.7 us (0.987)
  Pallas kernels: 6.37 us -> 5.96 us
    pallas_call x1, Pallas kernels: 2.81 us -> 2.47 us  [forward(): pl.pallas_call(forward_kernel, in_specs=[SMEM] * 3 + [VMEM] * 4 + [ANY],...]
    unnamed x14 -> x12, local copies, waits for them, and re-layouts: 2.23 us -> 2.22 us
  transfers between devices with their start and end apart: 14 -> 14, of which waited for: 5 -> 5; matrix products, arithmetic and copies ran while one was open for 0% -> 0% of each run, Pallas kernels for 19% -> 18%
where the time goes in v8:
time: 29.7 us; the launch traced here: 29.5 us
  starting transfers between devices  17.7 us (60%)
  Pallas kernels  5.96 us (20%)
  waiting for transfers between devices  2.79 us (9%)
  local copies, waits for them, and re-layouts  2.22 us (7%)
  between operations  0.79 us (3%)
    ppermute x14, starting transfers between devices, swap(): return lax.ppermute(x, axis, [(i, i ^ d) for i in range(size)])  17.7 us
    ppermute x14, waiting for transfers between devices, swap(): return lax.ppermute(x, axis, [(i, i ^ d) for i in range(size)])  2.79 us
    pallas_call x1, Pallas kernels, forward(): pl.pallas_call(forward_kernel, in_specs=[SMEM] * 3 + [VMEM] * 4 + [ANY],...  2.47 us
    unnamed x12, local copies, waits for them, and re-layouts  2.22 us
    pallas_call x1, Pallas kernels, backward(): pl.pallas_call(functools.partial(backward_kernel, n_in), in_specs=[SMEM]...  1.82 us
    pallas_call x1, Pallas kernels, last_sum(): pl.pallas_call(last_sum_kernel, in_specs=[VMEM] * (4 + len(chips)), out_s...  0.74 us
    pallas_call x1, Pallas kernels, prep(): pl.pallas_call(prep_kernel, in_specs=[VMEM], out_specs=VMEM, out_shape=ja...  0.69 us
  transfers between devices with their start and end apart: 14, of which 5 were waited for; matrix products, arithmetic and copies ran while one was open for 0% of the time, Pallas kernels for 18%

profile of v8, /device:TPU:0, one launch (start us, length us, event | category | flops | bytes accessed | tf_op | source)
XLA Modules:
  0.0 29.5 jit_solution(18002342155479630451)
XLA Ops:
  0.0 2.9 %collective-permute-start.3 = (bf16[8,2048]{1,0:T(8,128)(2,1)}, bf16[8,2048]{1,0:T(8,128)(2,1)S(1)}, u32[]{:S(2)}, u32[]{:S(2)}) collective-permute-start(bf16[8,2048]{1,0:T(8,128)(2,1)} %refs_0_.1), channel_id=1, source_target_pairs={{0,8},{4,12},{8,0},{12,4},{16,24},{20,28},{24,16},{28,20},{1,9},{5... | collective-permute-start | bytes 98312 | tf_op jit(solution)/shard_map/ppermute | solution.py:371
  2.9 3.6 %collective-permute-start.2 = (bf16[8,2048]{1,0:T(8,128)(2,1)}, bf16[8,2048]{1,0:T(8,128)(2,1)S(1)}, u32[]{:S(2)}, u32[]{:S(2)}) collective-permute-start(bf16[8,2048]{1,0:T(8,128)(2,1)} %refs_0_.1), channel_id=1, source_target_pairs={{0,3},{1,2},{2,1},{3,0},{4,7},{5,6},{6,5},{7,4},{8,11},{9,10},{10,... | collective-permute-start | bytes 98312 | tf_op jit(solution)/shard_map/ppermute | solution.py:371
  6.5 0.0 collective-permute-start.1
  6.5 0.8 %collective-permute-start = (bf16[8,2048]{1,0:T(8,128)(2,1)}, bf16[8,2048]{1,0:T(8,128)(2,1)S(1)}, u32[]{:S(2)}, u32[]{:S(2)}) collective-permute-start(bf16[8,2048]{1,0:T(8,128)(2,1)} %refs_0_.1), channel_id=1, source_target_pairs={{0,1},{1,0},{2,3},{3,2},{4,5},{5,4},{6,7},{7,6},{8,9},{9,8},{10,11... | collective-permute-start | bytes 98312 | tf_op jit(solution)/shard_map/ppermute | solution.py:371
  7.3 1.5 %collective-permute-start.5 = (bf16[8,2048]{1,0:T(8,128)(2,1)}, bf16[8,2048]{1,0:T(8,128)(2,1)S(1)}, u32[]{:S(2)}, u32[]{:S(2)}) collective-permute-start(bf16[8,2048]{1,0:T(8,128)(2,1)} %refs_0_.1), channel_id=1, source_target_pairs={{0,24},{4,28},{8,16},{12,20},{16,8},{20,12},{24,0},{28,4},{1,25},{... | collective-permute-start | bytes 98312 | tf_op jit(solution)/shard_map/ppermute | solution.py:371
  8.8 0.3 collective-permute-start.4
  9.1 0.8 %copy-done.3 = bf16[8,2048]{1,0:T(8,128)(2,1)S(1)} copy-done((bf16[8,2048]{1,0:T(8,128)(2,1)S(1)}, bf16[8,2048]{1,0:T(8,128)(2,1)}, u32[]{:S(2)}) %copy-start.3) | copy-done | bytes 32792
  9.9 1.4 %copy-done = bf16[192,4096]{1,0:T(8,128)(2,1)S(1)} copy-done((bf16[192,4096]{1,0:T(8,128)(2,1)S(1)}, bf16[192,4096]{1,0:T(8,128)(2,1)}, u32[]{:S(2)}) %copy-start) | copy-done | bytes 1572888
  11.3 0.7 %prep_tiles.1.refs_4_.tiles_ref = bf16[192,32,128]{2,1,0:T(8,128)(2,1)S(1)} custom-call(bf16[24,32,8,128]{3,2,1,0:T(8,128)(2,1)S(1)} %bitcast.4), custom_call_target="tpu_custom_call" | custom-call | bytes 3145728 | tf_op jit(solution)/shard_map/prep_tiles/pallas_call | solution.py:77
  12.0 0.0 copy-start.1
  12.0 0.0 copy-start.4
  12.0 0.0 copy-start.5
  12.1 0.0 copy-start.2
  12.1 0.0 collective-permute-done.refs_5_.refs_1_
  12.1 0.3 collective-permute-done.5.refs_3_
  12.4 0.6 %collective-permute-done.4.refs_2_ = bf16[8,2048]{1,0:T(8,128)(2,1)S(1)} collective-permute-done((bf16[8,2048]{1,0:T(8,128)(2,1)}, bf16[8,2048]{1,0:T(8,128)(2,1)S(1)}, u32[]{:S(2)}, u32[]{:S(2)}) %collective-permute-start.4) | collective-permute-done | bytes 32800 | tf_op jit(solution)/shard_map/ppermute | solution.py:371
  13.0 0.1 collective-permute-start.11
  13.7 1.8 %transpose_product.1 = (f32[4,8,2048]{2,1,0:T(8,128)S(1)}, f32[2,8,2048]{2,1,0:T(8,128)S(1)}, f32[2,8,2048]{2,1,0:T(8,128)S(1)}) custom-call(s32[192]{0:T(256)S(1)} %copy-done.4, s32[192]{0:T(256)S(1)} %copy-done.5, s32[1,1]{1,0:T(1,128)S(6)} %copy.8.count_ref, bf16[128,512]{1,0:T(8,128)(2,1)S(1)} %copy-done.1, ...), custom_call_target="tpu_custom_call" | custom-call | flops 100663296 | bytes 3145728 | tf_op jit(solution)/shard_map/transpose_product/pallas_call | solution.py:153
  15.5 0.7 %collective-permute-start.7 = (f32[2,8,2048]{2,1,0:T(8,128)S(1)}, f32[2,8,2048]{2,1,0:T(8,128)S(1)}, u32[]{:S(2)}, u32[]{:S(2)}) collective-permute-start(f32[2,8,2048]{2,1,0:T(8,128)S(1)} %get-tuple-element.17), channel_id=1, source_target_pairs={{0,4},{4,0},{8,12},{12,8},{16,20},{20,16},{24,28},{28,24},{1,5},{5... | collective-permute-start | bytes 393224 | tf_op jit(solution)/shard_map/ppermute | solution.py:371
  16.2 0.1 collective-permute-start.6
  16.3 2.5 %forward_product.1 = (f32[2,8,2048]{2,1,0:T(8,128)S(1)}, s16[2,8,2176]{2,1,0:T(8,128)(2,1)S(1)}) custom-call(s32[192]{0:T(256)S(1)} %copy-done.4, s32[192]{0:T(256)S(1)} %copy-done.5, s32[1,1]{1,0:T(1,128)S(6)} %copy.8.count_ref, bf16[512,128]{1,0:T(8,128)(2,1)S(1)} %copy-done.2, bf16[192,32,128]{2,1,0:T(8,128)(2,1)S(1)} %prep_tiles.1.refs_4_.tiles_ref, ...), custom_call_target="tpu_custom_call" | custom-call | flops 100663296 | bytes 3145728 | tf_op jit(solution)/shard_map/forward_product/pallas_call | solution.py:261
  18.7 1.3 %collective-permute-start.12 = (s16[2,8,2176]{2,1,0:T(8,128)(2,1)S(1)}, s16[2,8,2176]{2,1,0:T(8,128)(2,1)S(1)}, u32[]{:S(2)}, u32[]{:S(2)}) collective-permute-start(s16[2,8,2176]{2,1,0:T(8,128)(2,1)S(1)} %get-tuple-element.22), channel_id=1, source_target_pairs={{0,1},{1,0},{2,3},{3,2},{4,5},{5,4},{6,7},{7,6},{8,9},{9,8},{10,11... | collective-permute-start | bytes 208904 | tf_op jit(solution)/shard_map/ppermute | solution.py:371
  20.1 1.0 %collective-permute-start.9 = (f32[8,2048]{1,0:T(8,128)S(1)}, f32[8,2048]{1,0:T(8,128)S(1)}, u32[]{:S(2)}, u32[]{:S(2)}) collective-permute-start(f32[8,2048]{1,0:T(8,128)S(1)} %get-tuple-element.19), channel_id=1, source_target_pairs={{0,16},{4,20},{8,24},{12,28},{16,0},{20,4},{24,8},{28,12},{1,17},{... | collective-permute-start | bytes 196616 | tf_op jit(solution)/shard_map/ppermute | solution.py:371
  21.1 2.1 %collective-permute-start.10 = (f32[8,2048]{1,0:T(8,128)S(1)}, f32[8,2048]{1,0:T(8,128)S(1)}, u32[]{:S(2)}, u32[]{:S(2)}) collective-permute-start(f32[8,2048]{1,0:T(8,128)S(1)} %get-tuple-element.20), channel_id=1, source_target_pairs={{0,24},{4,28},{8,16},{12,20},{16,8},{20,12},{24,0},{28,4},{1,25},{... | collective-permute-start | bytes 196616 | tf_op jit(solution)/shard_map/ppermute | solution.py:371
  23.2 0.5 %collective-permute-start.8 = (f32[8,2048]{1,0:T(8,128)S(1)}, f32[8,2048]{1,0:T(8,128)S(1)}, u32[]{:S(2)}, u32[]{:S(2)}) collective-permute-start(f32[8,2048]{1,0:T(8,128)S(1)} %get-tuple-element.18.after_ref), channel_id=1, source_target_pairs={{0,8},{4,12},{8,0},{12,4},{16,24},{20,28},{24,16},{28,20},{1,9},{5... | collective-permute-start | bytes 196616 | tf_op jit(solution)/shard_map/ppermute | solution.py:371
  23.6 0.2 halving_sum.1
  23.8 3.0 %collective-permute-start.13 = (s16[1,8,2176]{2,1,0:T(8,128)(2,1)S(1)}, s16[1,8,2176]{2,1,0:T(8,128)(2,1)S(1)}, u32[]{:S(2)}, u32[]{:S(2)}) collective-permute-start(s16[1,8,2176]{2,1,0:T(8,128)(2,1)S(1)} %get-tuple-element.24), channel_id=1, source_target_pairs={{0,2},{1,3},{2,0},{3,1},{4,6},{5,7},{6,4},{7,5},{8,10},{9,11},{10,... | collective-permute-start | bytes 104456 | tf_op jit(solution)/shard_map/ppermute | solution.py:371
  26.8 0.0 collective-permute-done.9.refs_1_
  26.8 0.1 collective-permute-done.10.refs_2_
  26.9 0.5 %collective-permute-done.8.refs_0_ = f32[8,2048]{1,0:T(8,128)S(1)} collective-permute-done((f32[8,2048]{1,0:T(8,128)S(1)}, f32[8,2048]{1,0:T(8,128)S(1)}, u32[]{:S(2)}, u32[]{:S(2)}) %collective-permute-start.8) | collective-permute-done | bytes 65568 | tf_op jit(solution)/shard_map/ppermute | solution.py:371
  27.4 1.3 %collective-permute-done.13.refs_6_ = s16[1,8,2176]{2,1,0:T(8,128)(2,1)S(1)} collective-permute-done((s16[1,8,2176]{2,1,0:T(8,128)(2,1)S(1)}, s16[1,8,2176]{2,1,0:T(8,128)(2,1)S(1)}, u32[]{:S(2)}, u32[]{:S(2)}) %collective-permute-start.13) | collective-permute-done | bytes 34848 | tf_op jit(solution)/shard_map/ppermute | solution.py:371
  28.7 0.7 %last_sum.1 = f32[8,2048]{1,0:T(8,128)} custom-call(f32[8,2048]{1,0:T(8,128)S(1)} %collective-permute-done.8.refs_0_, f32[8,2048]{1,0:T(8,128)S(1)} %collective-permute-done.9.refs_1_, f32[8,2048]{1,0:T(8,128)S(1)} %collective-permute-done.10.refs_2_, f32[4,8,2048]{2,1,0:T(8,128)S(1)} %get-tuple-element.15.keep_ref.refs_3_, ...), custom_call_target="tpu_custom_call" | custom-call | tf_op jit(solution)/shard_map/last_sum/pallas_call | solution.py:360
  (16 shorter events, 0.1 us)
Async XLA Ops:
  0.0 8.8 %collective-permute-start.3 = (bf16[8,2048]{1,0:T(8,128)(2,1)}, bf16[8,2048]{1,0:T(8,128)(2,1)S(1)}, u32[]{:S(2)}, u32[]{:S(2)}) collective-permute-start(bf16[8,2048]{1,0:T(8,128)(2,1)} %refs_0_.1), channel_id=1, source_target_pairs={{0,8},{4,12},{8,0},{12,4},{16,24},{20,28},{24,16},{28,20},{1,9},{5... | collective-permute-start | bytes 98312 | tf_op jit(solution)/shard_map/ppermute | solution.py:371
  2.9 9.1 %collective-permute-start.2 = (bf16[8,2048]{1,0:T(8,128)(2,1)}, bf16[8,2048]{1,0:T(8,128)(2,1)S(1)}, u32[]{:S(2)}, u32[]{:S(2)}) collective-permute-start(bf16[8,2048]{1,0:T(8,128)(2,1)} %refs_0_.1), channel_id=1, source_target_pairs={{0,3},{1,2},{2,1},{3,0},{4,7},{5,6},{6,5},{7,4},{8,11},{9,10},{10,... | collective-permute-start | bytes 98312 | tf_op jit(solution)/shard_map/ppermute | solution.py:371
  6.5 5.5 %collective-permute-start.1 = (bf16[8,2048]{1,0:T(8,128)(2,1)}, bf16[8,2048]{1,0:T(8,128)(2,1)S(1)}, u32[]{:S(2)}, u32[]{:S(2)}) collective-permute-start(bf16[8,2048]{1,0:T(8,128)(2,1)} %refs_0_.1), channel_id=1, source_target_pairs={{0,2},{1,3},{2,0},{3,1},{4,6},{5,7},{6,4},{7,5},{8,10},{9,11},{10,... | collective-permute-start | bytes 98312 | tf_op jit(solution)/shard_map/ppermute | solution.py:371
  6.5 5.5 %collective-permute-start = (bf16[8,2048]{1,0:T(8,128)(2,1)}, bf16[8,2048]{1,0:T(8,128)(2,1)S(1)}, u32[]{:S(2)}, u32[]{:S(2)}) collective-permute-start(bf16[8,2048]{1,0:T(8,128)(2,1)} %refs_0_.1), channel_id=1, source_target_pairs={{0,1},{1,0},{2,3},{3,2},{4,5},{5,4},{6,7},{7,6},{8,9},{9,8},{10,11... | collective-permute-start | bytes 98312 | tf_op jit(solution)/shard_map/ppermute | solution.py:371
  7.3 5.0 %collective-permute-start.5 = (bf16[8,2048]{1,0:T(8,128)(2,1)}, bf16[8,2048]{1,0:T(8,128)(2,1)S(1)}, u32[]{:S(2)}, u32[]{:S(2)}) collective-permute-start(bf16[8,2048]{1,0:T(8,128)(2,1)} %refs_0_.1), channel_id=1, source_target_pairs={{0,24},{4,28},{8,16},{12,20},{16,8},{20,12},{24,0},{28,4},{1,25},{... | collective-permute-start | bytes 98312 | tf_op jit(solution)/shard_map/ppermute | solution.py:371
  8.8 4.1 %collective-permute-start.4 = (bf16[8,2048]{1,0:T(8,128)(2,1)}, bf16[8,2048]{1,0:T(8,128)(2,1)S(1)}, u32[]{:S(2)}, u32[]{:S(2)}) collective-permute-start(bf16[8,2048]{1,0:T(8,128)(2,1)} %refs_0_.1), channel_id=1, source_target_pairs={{0,16},{4,20},{8,24},{12,28},{16,0},{20,4},{24,8},{28,12},{1,17},{... | collective-permute-start | bytes 98312 | tf_op jit(solution)/shard_map/ppermute | solution.py:371
  9.1 0.8 %copy-start.3 = (bf16[8,2048]{1,0:T(8,128)(2,1)S(1)}, bf16[8,2048]{1,0:T(8,128)(2,1)}, u32[]{:S(2)}) copy-start(bf16[8,2048]{1,0:T(8,128)(2,1)} %refs_0_.1) | copy-start | bytes 98308
  9.9 1.4 %copy-start = (bf16[192,4096]{1,0:T(8,128)(2,1)S(1)}, bf16[192,4096]{1,0:T(8,128)(2,1)}, u32[]{:S(2)}) copy-start(bf16[192,4096]{1,0:T(8,128)(2,1)} %param.8) | copy-start | bytes 4718596
  12.0 1.7 %copy-start.1 = (bf16[128,512]{1,0:T(8,128)(2,1)S(1)}, bf16[128,512]{1,0:T(8,128)(2,1)}, u32[]{:S(2)}) copy-start(bf16[128,512]{1,0:T(8,128)(2,1)} %constant.4.clone.spread_ref) | copy-start | bytes 393220
  12.0 1.7 %copy-start.4 = (s32[192]{0:T(256)S(1)}, s32[192]{0:T(256)}, u32[]{:S(2)}) copy-start(s32[192]{0:T(256)} %rows_ref.3) | copy-start | bytes 2308
  12.0 1.7 %copy-start.5 = (s32[192]{0:T(256)S(1)}, s32[192]{0:T(256)}, u32[]{:S(2)}) copy-start(s32[192]{0:T(256)} %cols_ref.3) | copy-start | bytes 2308
  12.1 4.2 %copy-start.2 = (bf16[512,128]{1,0:T(8,128)(2,1)S(1)}, bf16[512,128]{1,0:T(8,128)(2,1)}, u32[]{:S(2)}) copy-start(bf16[512,128]{1,0:T(8,128)(2,1)} %constant.5.clone.fold_ref) | copy-start | bytes 393220
  13.0 3.3 %collective-permute-start.11 = (bf16[4,8,2048]{2,1,0:T(8,128)(2,1)S(1)}, bf16[4,8,2048]{2,1,0:T(8,128)(2,1)S(1)}, u32[]{:S(2)}, u32[]{:S(2)}) collective-permute-start(bf16[4,8,2048]{2,1,0:T(8,128)(2,1)S(1)} %stack_pieces.3.refs_4_.same_ref), channel_id=1, source_target_pairs={{0,4},{4,0},{8,12},{12,8},{16,20},{20,16},{24,28},{28,24},{1,5},{5... | collective-permute-start | bytes 393224 | tf_op jit(solution)/shard_map/ppermute | solution.py:371
  15.5 4.5 %collective-permute-start.7 = (f32[2,8,2048]{2,1,0:T(8,128)S(1)}, f32[2,8,2048]{2,1,0:T(8,128)S(1)}, u32[]{:S(2)}, u32[]{:S(2)}) collective-permute-start(f32[2,8,2048]{2,1,0:T(8,128)S(1)} %get-tuple-element.17), channel_id=1, source_target_pairs={{0,4},{4,0},{8,12},{12,8},{16,20},{20,16},{24,28},{28,24},{1,5},{5... | collective-permute-start | bytes 393224 | tf_op jit(solution)/shard_map/ppermute | solution.py:371
  16.2 3.9 %collective-permute-start.6 = (f32[2,8,2048]{2,1,0:T(8,128)S(1)}, f32[2,8,2048]{2,1,0:T(8,128)S(1)}, u32[]{:S(2)}, u32[]{:S(2)}) collective-permute-start(f32[2,8,2048]{2,1,0:T(8,128)S(1)} %get-tuple-element.16.after_ref), channel_id=1, source_target_pairs={{0,4},{4,0},{8,12},{12,8},{16,20},{20,16},{24,28},{28,24},{1,5},{5... | collective-permute-start | bytes 393224 | tf_op jit(solution)/shard_map/ppermute | solution.py:371
  18.7 4.9 %collective-permute-start.12 = (s16[2,8,2176]{2,1,0:T(8,128)(2,1)S(1)}, s16[2,8,2176]{2,1,0:T(8,128)(2,1)S(1)}, u32[]{:S(2)}, u32[]{:S(2)}) collective-permute-start(s16[2,8,2176]{2,1,0:T(8,128)(2,1)S(1)} %get-tuple-element.22), channel_id=1, source_target_pairs={{0,1},{1,0},{2,3},{3,2},{4,5},{5,4},{6,7},{7,6},{8,9},{9,8},{10,11... | collective-permute-start | bytes 208904 | tf_op jit(solution)/shard_map/ppermute | solution.py:371
  20.1 6.8 %collective-permute-start.9 = (f32[8,2048]{1,0:T(8,128)S(1)}, f32[8,2048]{1,0:T(8,128)S(1)}, u32[]{:S(2)}, u32[]{:S(2)}) collective-permute-start(f32[8,2048]{1,0:T(8,128)S(1)} %get-tuple-element.19), channel_id=1, source_target_pairs={{0,16},{4,20},{8,24},{12,28},{16,0},{20,4},{24,8},{28,12},{1,17},{... | collective-permute-start | bytes 196616 | tf_op jit(solution)/shard_map/ppermute | solution.py:371
  21.1 5.9 %collective-permute-start.10 = (f32[8,2048]{1,0:T(8,128)S(1)}, f32[8,2048]{1,0:T(8,128)S(1)}, u32[]{:S(2)}, u32[]{:S(2)}) collective-permute-start(f32[8,2048]{1,0:T(8,128)S(1)} %get-tuple-element.20), channel_id=1, source_target_pairs={{0,24},{4,28},{8,16},{12,20},{16,8},{20,12},{24,0},{28,4},{1,25},{... | collective-permute-start | bytes 196616 | tf_op jit(solution)/shard_map/ppermute | solution.py:371
  23.2 4.3 %collective-permute-start.8 = (f32[8,2048]{1,0:T(8,128)S(1)}, f32[8,2048]{1,0:T(8,128)S(1)}, u32[]{:S(2)}, u32[]{:S(2)}) collective-permute-start(f32[8,2048]{1,0:T(8,128)S(1)} %get-tuple-element.18.after_ref), channel_id=1, source_target_pairs={{0,8},{4,12},{8,0},{12,4},{16,24},{20,28},{24,16},{28,20},{1,9},{5... | collective-permute-start | bytes 196616 | tf_op jit(solution)/shard_map/ppermute | solution.py:371
  23.8 4.9 %collective-permute-start.13 = (s16[1,8,2176]{2,1,0:T(8,128)(2,1)S(1)}, s16[1,8,2176]{2,1,0:T(8,128)(2,1)S(1)}, u32[]{:S(2)}, u32[]{:S(2)}) collective-permute-start(s16[1,8,2176]{2,1,0:T(8,128)(2,1)S(1)} %get-tuple-element.24), channel_id=1, source_target_pairs={{0,2},{1,3},{2,0},{3,1},{4,6},{5,7},{6,4},{7,5},{8,10},{9,11},{10,... | collective-permute-start | bytes 104456 | tf_op jit(solution)/shard_map/ppermute | solution.py:371

commit v9 on v8

--- a/solution.py
+++ b/solution.py
@@ -299,7 +299,7 @@
     )(*parts, *after)
 
 
-def pair_sum_kernel(keep_ref, *refs):
+def pair_sum_kernel(after_ref, keep_ref, *refs):
     n_chips = keep_ref.shape[0]
     gots, outs = refs[: 1 - n_chips], refs[1 - n_chips :]
     got = [ref.at[h] for ref in gots for h in range(ref.shape[0])]
@@ -307,16 +307,16 @@
         out[...] = keep_ref[h + 1] + got[h + 1][...]
 
 
-def pair_sum(keep, gots):
+def pair_sum(keep, gots, after):
     parts, width, piece = keep.shape
     return pl.pallas_call(
         pair_sum_kernel,
-        in_specs=[VMEM] * (1 + len(gots)),
+        in_specs=[ANY] + [VMEM] * (1 + len(gots)),
         out_specs=[VMEM] * (parts - 1),
         out_shape=[jax.ShapeDtypeStruct((width, piece), F32)] * (parts - 1),
         compiler_params=PARAMS,
         name="core_pair_sum",
-    )(keep, *gots)
+    )(after, keep, *gots)
 
 
 def split_sum_kernel(keep_ref, got_ref, after_ref, next_keep, next_give):
@@ -376,15 +376,15 @@
     n_cols = lax.axis_size("bcol")
     own = stack(vectors)
     chips = [swap(vectors, "brow", n_rows, 2 * h) for h in range(1, n_rows // 2)]
+    blocks = prep(tiles)
+    same = stack(own, *chips, after=(blocks,))
+    other = swap(same, "brow", n_rows, 1)
     row_pieces = [own[0]] + [swap(vectors, "bcol", n_cols, d) for d in range(1, n_cols)]
-    blocks = prep(tiles)
-    same = stack(own, *chips, after=(blocks, *row_pieces[1:]))
-    other = swap(same, "brow", n_rows, 1)
-
-    col_keep, *col_give = backward(row_pieces, blocks, tile_rows, tile_cols, counts, n_rows, same)
-    row_keep, give = forward(same, other, blocks, tile_rows, tile_cols, counts, n_cols, col_give[0])
+
+    row_keep, give = forward(same, other, blocks, tile_rows, tile_cols, counts, n_cols, own)
+    col_keep, *col_give = backward(row_pieces, blocks, tile_rows, tile_cols, counts, n_rows, give)
     col_got = [swap(x, "brow", n_rows, 1) for x in col_give]
-    sums = pair_sum(col_keep, col_got)
+    sums = pair_sum(col_keep, col_got, give)
     from_chips = [swap(x, "brow", n_rows, 2 * (h + 1)) for h, x in enumerate(sums)]
     row_got, d = swap(give, "bcol", n_cols, 1), 2
     while d < n_cols:

time: 29.7 us -> 31.3 us (1.054)
  waiting for transfers between devices: 2.79 us -> 7.26 us
  starting transfers between devices: 17.7 us -> 14.7 us
  Pallas kernels: 5.96 us -> 6.93 us
  local copies, waits for them, and re-layouts: 2.22 us -> 1.43 us
    ppermute x14, waiting for transfers between devices: 2.79 us -> 7.26 us  [swap(): return lax.ppermute(x, axis, [(i, i ^ d) for i in range(size)])]
    ppermute x14, starting transfers between devices: 17.7 us -> 14.7 us  [swap(): return lax.ppermute(x, axis, [(i, i ^ d) for i in range(size)])]
    pallas_call x2, Pallas kernels: 0.01 us -> 0.82 us  [stack(): pl.pallas_call(functools.partial(stack_kernel, len(after)), in_specs=[VME...]
    unnamed x12 -> x10, local copies, waits for them, and re-layouts: 2.22 us -> 1.43 us
  transfers between devices with their start and end apart: 14 -> 14, of which waited for: 5 -> 7; matrix products, arithmetic and copies ran while one was open for 0% -> 0% of each run, Pallas kernels for 18% -> 14%
where the time goes in v9:
time: 31.3 us; the launch traced here: 31.1 us
  starting transfers between devices  14.7 us (47%)
  waiting for transfers between devices  7.26 us (23%)
  Pallas kernels  6.93 us (22%)
  local copies, waits for them, and re-layouts  1.43 us (5%)
  between operations  0.8 us (3%)
    ppermute x14, starting transfers between devices, swap(): return lax.ppermute(x, axis, [(i, i ^ d) for i in range(size)])  14.7 us
    ppermute x14, waiting for transfers between devices, swap(): return lax.ppermute(x, axis, [(i, i ^ d) for i in range(size)])  7.26 us
    pallas_call x1, Pallas kernels, forward(): pl.pallas_call(forward_kernel, in_specs=[SMEM] * 3 + [VMEM] * 4 + [ANY],...  2.54 us
    pallas_call x1, Pallas kernels, backward(): pl.pallas_call(functools.partial(backward_kernel, n_in), in_specs=[SMEM]...  1.91 us
    unnamed x10, local copies, waits for them, and re-layouts  1.43 us
    pallas_call x2, Pallas kernels, stack(): pl.pallas_call(functools.partial(stack_kernel, len(after)), in_specs=[VME...  0.82 us
    pallas_call x1, Pallas kernels, last_sum(): pl.pallas_call(last_sum_kernel, in_specs=[VMEM] * (4 + len(chips)), out_s...  0.74 us
    pallas_call x1, Pallas kernels, prep(): pl.pallas_call(prep_kernel, in_specs=[VMEM], out_specs=VMEM, out_shape=ja...  0.69 us
  transfers between devices with their start and end apart: 14, of which 7 were waited for; matrix products, arithmetic and copies ran while one was open for 0% of the time, Pallas kernels for 14%

profile of v9, /device:TPU:0, one launch (start us, length us, event | category | flops | bytes accessed | tf_op | source)
XLA Modules:
  0.0 31.1 jit_solution(10684781224195817249)
XLA Ops:
  0.0 3.9 %collective-permute-start.2 = (bf16[8,2048]{1,0:T(8,128)(2,1)}, bf16[8,2048]{1,0:T(8,128)(2,1)S(1)}, u32[]{:S(2)}, u32[]{:S(2)}) collective-permute-start(bf16[8,2048]{1,0:T(8,128)(2,1)} %refs_0_.1), channel_id=1, source_target_pairs={{0,24},{4,28},{8,16},{12,20},{16,8},{20,12},{24,0},{28,4},{1,25},{... | collective-permute-start | bytes 98312 | tf_op jit(solution)/shard_map/ppermute | solution.py:371
  3.9 0.5 %collective-permute-start.1 = (bf16[8,2048]{1,0:T(8,128)(2,1)}, bf16[8,2048]{1,0:T(8,128)(2,1)S(1)}, u32[]{:S(2)}, u32[]{:S(2)}) collective-permute-start(bf16[8,2048]{1,0:T(8,128)(2,1)} %refs_0_.1), channel_id=1, source_target_pairs={{0,16},{4,20},{8,24},{12,28},{16,0},{20,4},{24,8},{28,12},{1,17},{... | collective-permute-start | bytes 98312 | tf_op jit(solution)/shard_map/ppermute | solution.py:371
  4.4 0.1 collective-permute-start
  4.5 0.8 %stack_pieces.2.refs_0_.after_ref = bf16[1,8,2048]{2,1,0:T(8,128)(2,1)S(1)} custom-call(bf16[8,2048]{1,0:T(8,128)(2,1)} %refs_0_.1), custom_call_target="tpu_custom_call" | custom-call | tf_op jit(solution)/shard_map/stack_pieces/pallas_call | solution.py:292
  5.3 1.4 %copy-done = bf16[192,4096]{1,0:T(8,128)(2,1)S(1)} copy-done((bf16[192,4096]{1,0:T(8,128)(2,1)S(1)}, bf16[192,4096]{1,0:T(8,128)(2,1)}, u32[]{:S(2)}) %copy-start) | copy-done | bytes 1572888
  6.7 0.7 %prep_tiles.1.refs_4_.tiles_ref = bf16[192,32,128]{2,1,0:T(8,128)(2,1)S(1)} custom-call(bf16[24,32,8,128]{3,2,1,0:T(8,128)(2,1)S(1)} %bitcast.4), custom_call_target="tpu_custom_call" | custom-call | bytes 3145728 | tf_op jit(solution)/shard_map/prep_tiles/pallas_call | solution.py:77
  7.4 0.0 copy-start.2
  7.4 0.0 copy-start.3
  7.4 0.0 copy-start.4
  7.4 0.0 copy-start.1
  7.4 0.6 %collective-permute-done.1.refs_2_ = bf16[8,2048]{1,0:T(8,128)(2,1)S(1)} collective-permute-done((bf16[8,2048]{1,0:T(8,128)(2,1)}, bf16[8,2048]{1,0:T(8,128)(2,1)S(1)}, u32[]{:S(2)}, u32[]{:S(2)}) %collective-permute-start.1) | collective-permute-done | bytes 32800 | tf_op jit(solution)/shard_map/ppermute | solution.py:371
  8.0 0.5 %collective-permute-done.refs_1_ = bf16[8,2048]{1,0:T(8,128)(2,1)S(1)} collective-permute-done((bf16[8,2048]{1,0:T(8,128)(2,1)}, bf16[8,2048]{1,0:T(8,128)(2,1)S(1)}, u32[]{:S(2)}, u32[]{:S(2)}) %collective-permute-start) | collective-permute-done | bytes 32800 | tf_op jit(solution)/shard_map/ppermute | solution.py:371
  8.5 0.1 collective-permute-start.3
  8.6 1.6 %collective-permute-start.4 = (bf16[8,2048]{1,0:T(8,128)(2,1)}, bf16[8,2048]{1,0:T(8,128)(2,1)S(1)}, u32[]{:S(2)}, u32[]{:S(2)}) collective-permute-start(bf16[8,2048]{1,0:T(8,128)(2,1)} %refs_0_.1), channel_id=1, source_target_pairs={{0,1},{1,0},{2,3},{3,2},{4,5},{5,4},{6,7},{7,6},{8,9},{9,8},{10,11... | collective-permute-start | bytes 98312 | tf_op jit(solution)/shard_map/ppermute | solution.py:371
  10.3 2.5 %collective-permute-start.6 = (bf16[8,2048]{1,0:T(8,128)(2,1)}, bf16[8,2048]{1,0:T(8,128)(2,1)S(1)}, u32[]{:S(2)}, u32[]{:S(2)}) collective-permute-start(bf16[8,2048]{1,0:T(8,128)(2,1)} %refs_0_.1), channel_id=1, source_target_pairs={{0,3},{1,2},{2,1},{3,0},{4,7},{5,6},{6,5},{7,4},{8,11},{9,10},{10,... | collective-permute-start | bytes 98312 | tf_op jit(solution)/shard_map/ppermute | solution.py:371
  12.7 0.1 collective-permute-start.5
  13.5 2.5 %forward_product.1 = (f32[2,8,2048]{2,1,0:T(8,128)S(1)}, s16[2,8,2176]{2,1,0:T(8,128)(2,1)S(1)}) custom-call(s32[192]{0:T(256)S(1)} %copy-done.3, s32[192]{0:T(256)S(1)} %copy-done.4, s32[1,1]{1,0:T(1,128)S(6)} %copy.8.count_ref, bf16[512,128]{1,0:T(8,128)(2,1)S(1)} %copy-done.2, bf16[192,32,128]{2,1,0:T(8,128)(2,1)S(1)} %prep_tiles.1.refs_4_.tiles_ref, ...), custom_call_target="tpu_custom_call" | custom-call | flops 100663296 | bytes 3145728 | tf_op jit(solution)/shard_map/forward_product/pallas_call | solution.py:261
  16.1 0.1 collective-permute-done.6.refs_3_
  16.2 1.9 %collective-permute-done.5.refs_2_ = bf16[8,2048]{1,0:T(8,128)(2,1)S(1)} collective-permute-done((bf16[8,2048]{1,0:T(8,128)(2,1)}, bf16[8,2048]{1,0:T(8,128)(2,1)S(1)}, u32[]{:S(2)}, u32[]{:S(2)}) %collective-permute-start.5) | collective-permute-done | bytes 32800 | tf_op jit(solution)/shard_map/ppermute | solution.py:371
  18.1 1.9 %transpose_product.1 = (f32[4,8,2048]{2,1,0:T(8,128)S(1)}, f32[2,8,2048]{2,1,0:T(8,128)S(1)}, f32[2,8,2048]{2,1,0:T(8,128)S(1)}) custom-call(s32[192]{0:T(256)S(1)} %copy-done.3, s32[192]{0:T(256)S(1)} %copy-done.4, s32[1,1]{1,0:T(1,128)S(6)} %copy.8.count_ref, bf16[128,512]{1,0:T(8,128)(2,1)S(1)} %copy-done.1, ...), custom_call_target="tpu_custom_call" | custom-call | flops 100663296 | bytes 3145728 | tf_op jit(solution)/shard_map/transpose_product/pallas_call | solution.py:153
  20.0 0.1 collective-permute-start.7
  20.1 0.5 %collective-permute-start.8 = (f32[2,8,2048]{2,1,0:T(8,128)S(1)}, f32[2,8,2048]{2,1,0:T(8,128)S(1)}, u32[]{:S(2)}, u32[]{:S(2)}) collective-permute-start(f32[2,8,2048]{2,1,0:T(8,128)S(1)} %get-tuple-element.18), channel_id=1, source_target_pairs={{0,4},{4,0},{8,12},{12,8},{16,20},{20,16},{24,28},{28,24},{1,5},{5... | collective-permute-start | bytes 393224 | tf_op jit(solution)/shard_map/ppermute | solution.py:371
  20.6 0.4 %collective-permute-start.12 = (s16[2,8,2176]{2,1,0:T(8,128)(2,1)S(1)}, s16[2,8,2176]{2,1,0:T(8,128)(2,1)S(1)}, u32[]{:S(2)}, u32[]{:S(2)}) collective-permute-start(s16[2,8,2176]{2,1,0:T(8,128)(2,1)S(1)} %get-tuple-element.15.refs_4_.after_ref), channel_id=1, source_target_pairs={{0,1},{1,0},{2,3},{3,2},{4,5},{5,4},{6,7},{7,6},{8,9},{9,8},{10,11... | collective-permute-start | bytes 208904 | tf_op jit(solution)/shard_map/ppermute | solution.py:371
  21.0 0.4 %collective-permute-done.7.refs_0_.refs_4_ = f32[2,8,2048]{2,1,0:T(8,128)S(1)} collective-permute-done((f32[2,8,2048]{2,1,0:T(8,128)S(1)}, f32[2,8,2048]{2,1,0:T(8,128)S(1)}, u32[]{:S(2)}, u32[]{:S(2)}) %collective-permute-start.7) | collective-permute-done | bytes 131104 | tf_op jit(solution)/shard_map/ppermute | solution.py:371
  21.4 0.2 collective-permute-done.8.refs_1_
  21.7 1.6 %collective-permute-start.10 = (f32[8,2048]{1,0:T(8,128)S(1)}, f32[8,2048]{1,0:T(8,128)S(1)}, u32[]{:S(2)}, u32[]{:S(2)}) collective-permute-start(f32[8,2048]{1,0:T(8,128)S(1)} %get-tuple-element.20), channel_id=1, source_target_pairs={{0,16},{4,20},{8,24},{12,28},{16,0},{20,4},{24,8},{28,12},{1,17},{... | collective-permute-start | bytes 196616 | tf_op jit(solution)/shard_map/ppermute | solution.py:371
  23.2 0.8 %collective-permute-start.11 = (f32[8,2048]{1,0:T(8,128)S(1)}, f32[8,2048]{1,0:T(8,128)S(1)}, u32[]{:S(2)}, u32[]{:S(2)}) collective-permute-start(f32[8,2048]{1,0:T(8,128)S(1)} %get-tuple-element.21), channel_id=1, source_target_pairs={{0,24},{4,28},{8,16},{12,20},{16,8},{20,12},{24,0},{28,4},{1,25},{... | collective-permute-start | bytes 196616 | tf_op jit(solution)/shard_map/ppermute | solution.py:371
  24.0 1.2 %collective-permute-start.9 = (f32[8,2048]{1,0:T(8,128)S(1)}, f32[8,2048]{1,0:T(8,128)S(1)}, u32[]{:S(2)}, u32[]{:S(2)}) collective-permute-start(f32[8,2048]{1,0:T(8,128)S(1)} %get-tuple-element.19.after_ref), channel_id=1, source_target_pairs={{0,8},{4,12},{8,0},{12,4},{16,24},{20,28},{24,16},{28,20},{1,9},{5... | collective-permute-start | bytes 196616 | tf_op jit(solution)/shard_map/ppermute | solution.py:371
  25.2 0.2 halving_sum.1
  25.4 1.4 %collective-permute-start.13 = (s16[1,8,2176]{2,1,0:T(8,128)(2,1)S(1)}, s16[1,8,2176]{2,1,0:T(8,128)(2,1)S(1)}, u32[]{:S(2)}, u32[]{:S(2)}) collective-permute-start(s16[1,8,2176]{2,1,0:T(8,128)(2,1)S(1)} %get-tuple-element.24), channel_id=1, source_target_pairs={{0,2},{1,3},{2,0},{3,1},{4,6},{5,7},{6,4},{7,5},{8,10},{9,11},{10,... | collective-permute-start | bytes 104456 | tf_op jit(solution)/shard_map/ppermute | solution.py:371
  26.8 3.5 %collective-permute-done.13.refs_6_ = s16[1,8,2176]{2,1,0:T(8,128)(2,1)S(1)} collective-permute-done((s16[1,8,2176]{2,1,0:T(8,128)(2,1)S(1)}, s16[1,8,2176]{2,1,0:T(8,128)(2,1)S(1)}, u32[]{:S(2)}, u32[]{:S(2)}) %collective-permute-start.13) | collective-permute-done | bytes 34848 | tf_op jit(solution)/shard_map/ppermute | solution.py:371
  30.3 0.7 %last_sum.1 = f32[8,2048]{1,0:T(8,128)} custom-call(f32[8,2048]{1,0:T(8,128)S(1)} %collective-permute-done.9.refs_0_, f32[8,2048]{1,0:T(8,128)S(1)} %collective-permute-done.10.refs_1_, f32[8,2048]{1,0:T(8,128)S(1)} %collective-permute-done.11.refs_2_, f32[4,8,2048]{2,1,0:T(8,128)S(1)} %get-tuple-element.16.keep_ref.refs_3_, ...), custom_call_target="tpu_custom_call" | custom-call | tf_op jit(solution)/shard_map/last_sum/pallas_call | solution.py:360
  (14 shorter events, 0.1 us)
Async XLA Ops:
  0.0 7.4 %collective-permute-start.2 = (bf16[8,2048]{1,0:T(8,128)(2,1)}, bf16[8,2048]{1,0:T(8,128)(2,1)S(1)}, u32[]{:S(2)}, u32[]{:S(2)}) collective-permute-start(bf16[8,2048]{1,0:T(8,128)(2,1)} %refs_0_.1), channel_id=1, source_target_pairs={{0,24},{4,28},{8,16},{12,20},{16,8},{20,12},{24,0},{28,4},{1,25},{... | collective-permute-start | bytes 98312 | tf_op jit(solution)/shard_map/ppermute | solution.py:371
  3.9 4.1 %collective-permute-start.1 = (bf16[8,2048]{1,0:T(8,128)(2,1)}, bf16[8,2048]{1,0:T(8,128)(2,1)S(1)}, u32[]{:S(2)}, u32[]{:S(2)}) collective-permute-start(bf16[8,2048]{1,0:T(8,128)(2,1)} %refs_0_.1), channel_id=1, source_target_pairs={{0,16},{4,20},{8,24},{12,28},{16,0},{20,4},{24,8},{28,12},{1,17},{... | collective-permute-start | bytes 98312 | tf_op jit(solution)/shard_map/ppermute | solution.py:371
  4.4 4.1 %collective-permute-start = (bf16[8,2048]{1,0:T(8,128)(2,1)}, bf16[8,2048]{1,0:T(8,128)(2,1)S(1)}, u32[]{:S(2)}, u32[]{:S(2)}) collective-permute-start(bf16[8,2048]{1,0:T(8,128)(2,1)} %refs_0_.1), channel_id=1, source_target_pairs={{0,8},{4,12},{8,0},{12,4},{16,24},{20,28},{24,16},{28,20},{1,9},{5... | collective-permute-start | bytes 98312 | tf_op jit(solution)/shard_map/ppermute | solution.py:371
  5.3 1.4 %copy-start = (bf16[192,4096]{1,0:T(8,128)(2,1)S(1)}, bf16[192,4096]{1,0:T(8,128)(2,1)}, u32[]{:S(2)}) copy-start(bf16[192,4096]{1,0:T(8,128)(2,1)} %param.8) | copy-start | bytes 4718596
  7.4 6.1 %copy-start.2 = (bf16[512,128]{1,0:T(8,128)(2,1)S(1)}, bf16[512,128]{1,0:T(8,128)(2,1)}, u32[]{:S(2)}) copy-start(bf16[512,128]{1,0:T(8,128)(2,1)} %constant.4.clone.fold_ref) | copy-start | bytes 393220
  7.4 6.1 %copy-start.3 = (s32[192]{0:T(256)S(1)}, s32[192]{0:T(256)}, u32[]{:S(2)}) copy-start(s32[192]{0:T(256)} %rows_ref.3) | copy-start | bytes 2308
  7.4 6.1 %copy-start.4 = (s32[192]{0:T(256)S(1)}, s32[192]{0:T(256)}, u32[]{:S(2)}) copy-start(s32[192]{0:T(256)} %cols_ref.3) | copy-start | bytes 2308
  7.4 10.7 %copy-start.1 = (bf16[128,512]{1,0:T(8,128)(2,1)S(1)}, bf16[128,512]{1,0:T(8,128)(2,1)}, u32[]{:S(2)}) copy-start(bf16[128,512]{1,0:T(8,128)(2,1)} %constant.5.clone.spread_ref) | copy-start | bytes 393220
  8.5 5.0 %collective-permute-start.3 = (bf16[4,8,2048]{2,1,0:T(8,128)(2,1)S(1)}, bf16[4,8,2048]{2,1,0:T(8,128)(2,1)S(1)}, u32[]{:S(2)}, u32[]{:S(2)}) collective-permute-start(bf16[4,8,2048]{2,1,0:T(8,128)(2,1)S(1)} %stack_pieces.3.same_ref), channel_id=1, source_target_pairs={{0,4},{4,0},{8,12},{12,8},{16,20},{20,16},{24,28},{28,24},{1,5},{5... | collective-permute-start | bytes 393224 | tf_op jit(solution)/shard_map/ppermute | solution.py:371
  8.6 7.5 %collective-permute-start.4 = (bf16[8,2048]{1,0:T(8,128)(2,1)}, bf16[8,2048]{1,0:T(8,128)(2,1)S(1)}, u32[]{:S(2)}, u32[]{:S(2)}) collective-permute-start(bf16[8,2048]{1,0:T(8,128)(2,1)} %refs_0_.1), channel_id=1, source_target_pairs={{0,1},{1,0},{2,3},{3,2},{4,5},{5,4},{6,7},{7,6},{8,9},{9,8},{10,11... | collective-permute-start | bytes 98312 | tf_op jit(solution)/shard_map/ppermute | solution.py:371
  10.3 5.9 %collective-permute-start.6 = (bf16[8,2048]{1,0:T(8,128)(2,1)}, bf16[8,2048]{1,0:T(8,128)(2,1)S(1)}, u32[]{:S(2)}, u32[]{:S(2)}) collective-permute-start(bf16[8,2048]{1,0:T(8,128)(2,1)} %refs_0_.1), channel_id=1, source_target_pairs={{0,3},{1,2},{2,1},{3,0},{4,7},{5,6},{6,5},{7,4},{8,11},{9,10},{10,... | collective-permute-start | bytes 98312 | tf_op jit(solution)/shard_map/ppermute | solution.py:371
  12.7 5.4 %collective-permute-start.5 = (bf16[8,2048]{1,0:T(8,128)(2,1)}, bf16[8,2048]{1,0:T(8,128)(2,1)S(1)}, u32[]{:S(2)}, u32[]{:S(2)}) collective-permute-start(bf16[8,2048]{1,0:T(8,128)(2,1)} %refs_0_.1), channel_id=1, source_target_pairs={{0,2},{1,3},{2,0},{3,1},{4,6},{5,7},{6,4},{7,5},{8,10},{9,11},{10,... | collective-permute-start | bytes 98312 | tf_op jit(solution)/shard_map/ppermute | solution.py:371
  20.0 1.4 %collective-permute-start.7 = (f32[2,8,2048]{2,1,0:T(8,128)S(1)}, f32[2,8,2048]{2,1,0:T(8,128)S(1)}, u32[]{:S(2)}, u32[]{:S(2)}) collective-permute-start(f32[2,8,2048]{2,1,0:T(8,128)S(1)} %get-tuple-element.17), channel_id=1, source_target_pairs={{0,4},{4,0},{8,12},{12,8},{16,20},{20,16},{24,28},{28,24},{1,5},{5... | collective-permute-start | bytes 393224 | tf_op jit(solution)/shard_map/ppermute | solution.py:371
  20.1 1.5 %collective-permute-start.8 = (f32[2,8,2048]{2,1,0:T(8,128)S(1)}, f32[2,8,2048]{2,1,0:T(8,128)S(1)}, u32[]{:S(2)}, u32[]{:S(2)}) collective-permute-start(f32[2,8,2048]{2,1,0:T(8,128)S(1)} %get-tuple-element.18), channel_id=1, source_target_pairs={{0,4},{4,0},{8,12},{12,8},{16,20},{20,16},{24,28},{28,24},{1,5},{5... | collective-permute-start | bytes 393224 | tf_op jit(solution)/shard_map/ppermute | solution.py:371
  20.6 4.6 %collective-permute-start.12 = (s16[2,8,2176]{2,1,0:T(8,128)(2,1)S(1)}, s16[2,8,2176]{2,1,0:T(8,128)(2,1)S(1)}, u32[]{:S(2)}, u32[]{:S(2)}) collective-permute-start(s16[2,8,2176]{2,1,0:T(8,128)(2,1)S(1)} %get-tuple-element.15.refs_4_.after_ref), channel_id=1, source_target_pairs={{0,1},{1,0},{2,3},{3,2},{4,5},{5,4},{6,7},{7,6},{8,9},{9,8},{10,11... | collective-permute-start | bytes 208904 | tf_op jit(solution)/shard_map/ppermute | solution.py:371
  21.7 8.7 %collective-permute-start.10 = (f32[8,2048]{1,0:T(8,128)S(1)}, f32[8,2048]{1,0:T(8,128)S(1)}, u32[]{:S(2)}, u32[]{:S(2)}) collective-permute-start(f32[8,2048]{1,0:T(8,128)S(1)} %get-tuple-element.20), channel_id=1, source_target_pairs={{0,16},{4,20},{8,24},{12,28},{16,0},{20,4},{24,8},{28,12},{1,17},{... | collective-permute-start | bytes 196616 | tf_op jit(solution)/shard_map/ppermute | solution.py:371
  23.2 7.1 %collective-permute-start.11 = (f32[8,2048]{1,0:T(8,128)S(1)}, f32[8,2048]{1,0:T(8,128)S(1)}, u32[]{:S(2)}, u32[]{:S(2)}) collective-permute-start(f32[8,2048]{1,0:T(8,128)S(1)} %get-tuple-element.21), channel_id=1, source_target_pairs={{0,24},{4,28},{8,16},{12,20},{16,8},{20,12},{24,0},{28,4},{1,25},{... | collective-permute-start | bytes 196616 | tf_op jit(solution)/shard_map/ppermute | solution.py:371
  24.0 6.3 %collective-permute-start.9 = (f32[8,2048]{1,0:T(8,128)S(1)}, f32[8,2048]{1,0:T(8,128)S(1)}, u32[]{:S(2)}, u32[]{:S(2)}) collective-permute-start(f32[8,2048]{1,0:T(8,128)S(1)} %get-tuple-element.19.after_ref), channel_id=1, source_target_pairs={{0,8},{4,12},{8,0},{12,4},{16,24},{20,28},{24,16},{28,20},{1,9},{5... | collective-permute-start | bytes 196616 | tf_op jit(solution)/shard_map/ppermute | solution.py:371
  25.4 4.9 %collective-permute-start.13 = (s16[1,8,2176]{2,1,0:T(8,128)(2,1)S(1)}, s16[1,8,2176]{2,1,0:T(8,128)(2,1)S(1)}, u32[]{:S(2)}, u32[]{:S(2)}) collective-permute-start(s16[1,8,2176]{2,1,0:T(8,128)(2,1)S(1)} %get-tuple-element.24), channel_id=1, source_target_pairs={{0,2},{1,3},{2,0},{3,1},{4,6},{5,7},{6,4},{7,5},{8,10},{9,11},{10,... | collective-permute-start | bytes 104456 | tf_op jit(solution)/shard_map/ppermute | solution.py:371

commit v10 on v8

--- a/solution.py
+++ b/solution.py
@@ -101,9 +101,11 @@
                 table[n * 2 * pairs + 2 * p + q] = both[p]
 
 
-def backward_kernel(n_in, rows_ref, cols_ref, count_ref, spread_ref, tiles_ref, *refs):
-    pieces = refs[:n_in]
-    _, keep_ref, *give_refs, table, acc_a, acc_b = refs[n_in:]
+def backward_kernel(
+    rows_ref, cols_ref, count_ref, spread_ref, tiles_ref, seg_ref, after_ref, keep_ref, *refs
+):
+    pieces = [seg_ref.at[n] for n in range(seg_ref.shape[0])]
+    *give_refs, table, acc_a, acc_b = refs
     per_give = give_refs[0].shape[0]
     n_out = 2 * keep_ref.shape[0]
     width, piece = pieces[0].shape
@@ -144,15 +146,14 @@
             )
 
 
-def backward(pieces, tiles, tile_rows, tile_cols, counts, n_out, after):
-    n_in = len(pieces)
-    width, piece = pieces[0].shape
+def backward(segment, tiles, tile_rows, tile_cols, counts, n_out, after):
+    n_in, width, piece = segment.shape
     per_piece = piece // TILE
     half = jax.ShapeDtypeStruct((n_out // 2, width, piece), F32)
     quarter = jax.ShapeDtypeStruct((n_out // 4, width, piece), F32)
     return pl.pallas_call(
-        functools.partial(backward_kernel, n_in),
-        in_specs=[SMEM] * 3 + [VMEM] * (2 + n_in) + [ANY],
+        backward_kernel,
+        in_specs=[SMEM] * 3 + [VMEM] * 3 + [ANY],
         out_specs=[VMEM] * 3,
         out_shape=[half, quarter, quarter],
         scratch_shapes=[
@@ -165,7 +166,7 @@
             flops=2 * tiles.size * 64, bytes_accessed=4 * tiles.size, transcendentals=0
         ),
         name="transpose_product",
-    )(tile_rows, tile_cols, counts, row_spread(), tiles, *pieces, after)
+    )(tile_rows, tile_cols, counts, row_spread(), tiles, segment, after)
 
 
 def double_table(pieces, table):
@@ -376,12 +377,15 @@
     n_cols = lax.axis_size("bcol")
     own = stack(vectors)
     chips = [swap(vectors, "brow", n_rows, 2 * h) for h in range(1, n_rows // 2)]
-    row_pieces = [own[0]] + [swap(vectors, "bcol", n_cols, d) for d in range(1, n_cols)]
+    segment, d = own, 1
+    while d < n_cols:
+        segment = stack(segment, swap(segment if d > 1 else vectors[None], "bcol", n_cols, d))
+        d *= 2
     blocks = prep(tiles)
-    same = stack(own, *chips, after=(blocks, *row_pieces[1:]))
+    same = stack(own, *chips, after=(blocks,))
     other = swap(same, "brow", n_rows, 1)
 
-    col_keep, *col_give = backward(row_pieces, blocks, tile_rows, tile_cols, counts, n_rows, same)
+    col_keep, *col_give = backward(segment, blocks, tile_rows, tile_cols, counts, n_rows, same)
     row_keep, give = forward(same, other, blocks, tile_rows, tile_cols, counts, n_cols, col_give[0])
     col_got = [swap(x, "brow", n_rows, 1) for x in col_give]
     sums = pair_sum(col_keep, col_got)

time: 29.7 us -> 28.6 us (0.963)
  starting transfers between devices: 17.7 us -> 16.1 us
  waiting for transfers between devices: 2.79 us -> 3.27 us
    ppermute x14 -> x13, starting transfers between devices: 17.7 us -> 16.1 us  [swap(): return lax.ppermute(x, axis, [(i, i ^ d) for i in range(size)])]
    ppermute x14 -> x13, waiting for transfers between devices: 2.79 us -> 3.27 us  [swap(): return lax.ppermute(x, axis, [(i, i ^ d) for i in range(size)])]
  transfers between devices with their start and end apart: 14 -> 13, of which waited for: 5 -> 2; matrix products, arithmetic and copies ran while one was open for 0% -> 0% of each run, Pallas kernels for 18% -> 18%
where the time goes in v10:
time: 28.6 us; the launch traced here: 28.4 us
  starting transfers between devices  16.1 us (56%)
  Pallas kernels  5.99 us (21%)
  waiting for transfers between devices  3.27 us (11%)
  local copies, waits for them, and re-layouts  2.27 us (8%)
  between operations  0.79 us (3%)
    ppermute x13, starting transfers between devices, swap(): return lax.ppermute(x, axis, [(i, i ^ d) for i in range(size)])  16.1 us
    ppermute x13, waiting for transfers between devices, swap(): return lax.ppermute(x, axis, [(i, i ^ d) for i in range(size)])  3.27 us
    pallas_call x1, Pallas kernels, forward(): pl.pallas_call(forward_kernel, in_specs=[SMEM] * 3 + [VMEM] * 4 + [ANY],...  2.47 us
    unnamed x12, local copies, waits for them, and re-layouts  2.27 us
    pallas_call x1, Pallas kernels, backward(): pl.pallas_call(backward_kernel, in_specs=[SMEM] * 3 + [VMEM] * 3 + [ANY],...  1.83 us
    pallas_call x1, Pallas kernels, last_sum(): pl.pallas_call(last_sum_kernel, in_specs=[VMEM] * (4 + len(chips)), out_s...  0.74 us
    pallas_call x1, Pallas kernels, prep(): pl.pallas_call(prep_kernel, in_specs=[VMEM], out_specs=VMEM, out_shape=ja...  0.69 us
  transfers between devices with their start and end apart: 13, of which 2 were waited for; matrix products, arithmetic and copies ran while one was open for 0% of the time, Pallas kernels for 18%

profile of v10, /device:TPU:0, one launch (start us, length us, event | category | flops | bytes accessed | tf_op | source)
XLA Modules:
  0.0 28.4 jit_solution(1369809987058268694)
XLA Ops:
  0.0 3.0 %collective-permute-start = (bf16[1,8,2048]{2,1,0:T(8,128)(2,1)}, bf16[1,8,2048]{2,1,0:T(8,128)(2,1)S(1)}, u32[]{:S(2)}, u32[]{:S(2)}) collective-permute-start(bf16[1,8,2048]{2,1,0:T(8,128)(2,1)} %bitcast.5), channel_id=1, source_target_pairs={{0,1},{1,0},{2,3},{3,2},{4,5},{5,4},{6,7},{7,6},{8,9},{9,8},{10,11... | collective-permute-start | bytes 98312 | tf_op jit(solution)/shard_map/ppermute | solution.py:372
  3.0 1.5 %collective-permute-start.2 = (bf16[8,2048]{1,0:T(8,128)(2,1)}, bf16[8,2048]{1,0:T(8,128)(2,1)S(1)}, u32[]{:S(2)}, u32[]{:S(2)}) collective-permute-start(bf16[8,2048]{1,0:T(8,128)(2,1)} %refs_0_.1), channel_id=1, source_target_pairs={{0,8},{4,12},{8,0},{12,4},{16,24},{20,28},{24,16},{28,20},{1,9},{5... | collective-permute-start | bytes 98312 | tf_op jit(solution)/shard_map/ppermute | solution.py:372
  4.5 1.5 %collective-permute-start.4 = (bf16[8,2048]{1,0:T(8,128)(2,1)}, bf16[8,2048]{1,0:T(8,128)(2,1)S(1)}, u32[]{:S(2)}, u32[]{:S(2)}) collective-permute-start(bf16[8,2048]{1,0:T(8,128)(2,1)} %refs_0_.1), channel_id=1, source_target_pairs={{0,24},{4,28},{8,16},{12,20},{16,8},{20,12},{24,0},{28,4},{1,25},{... | collective-permute-start | bytes 98312 | tf_op jit(solution)/shard_map/ppermute | solution.py:372
  6.0 0.5 %collective-permute-start.3 = (bf16[8,2048]{1,0:T(8,128)(2,1)}, bf16[8,2048]{1,0:T(8,128)(2,1)S(1)}, u32[]{:S(2)}, u32[]{:S(2)}) collective-permute-start(bf16[8,2048]{1,0:T(8,128)(2,1)} %refs_0_.1), channel_id=1, source_target_pairs={{0,16},{4,20},{8,24},{12,28},{16,0},{20,4},{24,8},{28,12},{1,17},{... | collective-permute-start | bytes 98312 | tf_op jit(solution)/shard_map/ppermute | solution.py:372
  6.5 0.8 %copy-done.3 = bf16[8,2048]{1,0:T(8,128)(2,1)S(1)} copy-done((bf16[8,2048]{1,0:T(8,128)(2,1)S(1)}, bf16[8,2048]{1,0:T(8,128)(2,1)}, u32[]{:S(2)}) %copy-start.3) | copy-done | bytes 32792
  7.3 0.0 collective-permute-done.refs_1_
  7.3 2.7 %collective-permute-start.1 = (bf16[2,8,2048]{2,1,0:T(8,128)(2,1)S(1)}, bf16[2,8,2048]{2,1,0:T(8,128)(2,1)S(1)}, u32[]{:S(2)}, u32[]{:S(2)}) collective-permute-start(bf16[2,8,2048]{2,1,0:T(8,128)(2,1)S(1)} %stack_pieces.5.refs_0_), channel_id=1, source_target_pairs={{0,2},{1,3},{2,0},{3,1},{4,6},{5,7},{6,4},{7,5},{8,10},{9,11},{10,... | collective-permute-start | bytes 196616 | tf_op jit(solution)/shard_map/ppermute | solution.py:372
  10.0 1.4 %copy-done = bf16[192,4096]{1,0:T(8,128)(2,1)S(1)} copy-done((bf16[192,4096]{1,0:T(8,128)(2,1)S(1)}, bf16[192,4096]{1,0:T(8,128)(2,1)}, u32[]{:S(2)}) %copy-start) | copy-done | bytes 1572888
  11.4 0.7 %prep_tiles.1.refs_4_.tiles_ref = bf16[192,32,128]{2,1,0:T(8,128)(2,1)S(1)} custom-call(bf16[24,32,8,128]{3,2,1,0:T(8,128)(2,1)S(1)} %bitcast.4), custom_call_target="tpu_custom_call" | custom-call | bytes 3145728 | tf_op jit(solution)/shard_map/prep_tiles/pallas_call | solution.py:77
  12.1 0.0 copy-start.1
  12.1 0.0 copy-start.4
  12.1 0.0 copy-start.5
  12.1 0.0 collective-permute-done.4.refs_3_
  12.1 0.0 collective-permute-done.3.refs_2_
  12.2 0.0 copy-start.2
  12.2 0.1 collective-permute-start.10
  12.9 0.1 copy-done.1
  13.0 1.8 %transpose_product.1 = (f32[4,8,2048]{2,1,0:T(8,128)S(1)}, f32[2,8,2048]{2,1,0:T(8,128)S(1)}, f32[2,8,2048]{2,1,0:T(8,128)S(1)}) custom-call(s32[192]{0:T(256)S(1)} %copy-done.4, s32[192]{0:T(256)S(1)} %copy-done.5, s32[1,1]{1,0:T(1,128)S(6)} %copy.8.count_ref, bf16[128,512]{1,0:T(8,128)(2,1)S(1)} %copy-done.1, ...), custom_call_target="tpu_custom_call" | custom-call | flops 100663296 | bytes 3145728 | tf_op jit(solution)/shard_map/transpose_product/pallas_call | solution.py:154
  14.8 0.5 %collective-permute-start.6 = (f32[2,8,2048]{2,1,0:T(8,128)S(1)}, f32[2,8,2048]{2,1,0:T(8,128)S(1)}, u32[]{:S(2)}, u32[]{:S(2)}) collective-permute-start(f32[2,8,2048]{2,1,0:T(8,128)S(1)} %get-tuple-element.17), channel_id=1, source_target_pairs={{0,4},{4,0},{8,12},{12,8},{16,20},{20,16},{24,28},{28,24},{1,5},{5... | collective-permute-start | bytes 393224 | tf_op jit(solution)/shard_map/ppermute | solution.py:372
  15.4 0.1 collective-permute-start.5
  15.5 2.5 %forward_product.1 = (f32[2,8,2048]{2,1,0:T(8,128)S(1)}, s16[2,8,2176]{2,1,0:T(8,128)(2,1)S(1)}) custom-call(s32[192]{0:T(256)S(1)} %copy-done.4, s32[192]{0:T(256)S(1)} %copy-done.5, s32[1,1]{1,0:T(1,128)S(6)} %copy.8.count_ref, bf16[512,128]{1,0:T(8,128)(2,1)S(1)} %copy-done.2, bf16[192,32,128]{2,1,0:T(8,128)(2,1)S(1)} %prep_tiles.1.refs_4_.tiles_ref, ...), custom_call_target="tpu_custom_call" | custom-call | flops 100663296 | bytes 3145728 | tf_op jit(solution)/shard_map/forward_product/pallas_call | solution.py:262
  17.9 0.6 %collective-permute-start.11 = (s16[2,8,2176]{2,1,0:T(8,128)(2,1)S(1)}, s16[2,8,2176]{2,1,0:T(8,128)(2,1)S(1)}, u32[]{:S(2)}, u32[]{:S(2)}) collective-permute-start(s16[2,8,2176]{2,1,0:T(8,128)(2,1)S(1)} %get-tuple-element.22), channel_id=1, source_target_pairs={{0,1},{1,0},{2,3},{3,2},{4,5},{5,4},{6,7},{7,6},{8,9},{9,8},{10,11... | collective-permute-start | bytes 208904 | tf_op jit(solution)/shard_map/ppermute | solution.py:372
  18.6 0.0 collective-permute-done.6.refs_1_
  18.6 0.0 collective-permute-done.5.refs_0_.refs_4_
  18.6 1.5 %collective-permute-start.8 = (f32[8,2048]{1,0:T(8,128)S(1)}, f32[8,2048]{1,0:T(8,128)S(1)}, u32[]{:S(2)}, u32[]{:S(2)}) collective-permute-start(f32[8,2048]{1,0:T(8,128)S(1)} %get-tuple-element.19), channel_id=1, source_target_pairs={{0,16},{4,20},{8,24},{12,28},{16,0},{20,4},{24,8},{28,12},{1,17},{... | collective-permute-start | bytes 196616 | tf_op jit(solution)/shard_map/ppermute | solution.py:372
  20.1 1.5 %collective-permute-start.9 = (f32[8,2048]{1,0:T(8,128)S(1)}, f32[8,2048]{1,0:T(8,128)S(1)}, u32[]{:S(2)}, u32[]{:S(2)}) collective-permute-start(f32[8,2048]{1,0:T(8,128)S(1)} %get-tuple-element.20), channel_id=1, source_target_pairs={{0,24},{4,28},{8,16},{12,20},{16,8},{20,12},{24,0},{28,4},{1,25},{... | collective-permute-start | bytes 196616 | tf_op jit(solution)/shard_map/ppermute | solution.py:372
  21.6 0.6 %collective-permute-start.7 = (f32[8,2048]{1,0:T(8,128)S(1)}, f32[8,2048]{1,0:T(8,128)S(1)}, u32[]{:S(2)}, u32[]{:S(2)}) collective-permute-start(f32[8,2048]{1,0:T(8,128)S(1)} %get-tuple-element.18.after_ref), channel_id=1, source_target_pairs={{0,8},{4,12},{8,0},{12,4},{16,24},{20,28},{24,16},{28,20},{1,9},{5... | collective-permute-start | bytes 196616 | tf_op jit(solution)/shard_map/ppermute | solution.py:372
  22.1 0.4 %collective-permute-done.11.got_ref = s16[2,8,2176]{2,1,0:T(8,128)(2,1)S(1)} collective-permute-done((s16[2,8,2176]{2,1,0:T(8,128)(2,1)S(1)}, s16[2,8,2176]{2,1,0:T(8,128)(2,1)S(1)}, u32[]{:S(2)}, u32[]{:S(2)}) %collective-permute-start.11) | collective-permute-done | bytes 69664 | tf_op jit(solution)/shard_map/ppermute | solution.py:372
  22.5 0.2 halving_sum.1
  22.7 2.0 %collective-permute-start.12 = (s16[1,8,2176]{2,1,0:T(8,128)(2,1)S(1)}, s16[1,8,2176]{2,1,0:T(8,128)(2,1)S(1)}, u32[]{:S(2)}, u32[]{:S(2)}) collective-permute-start(s16[1,8,2176]{2,1,0:T(8,128)(2,1)S(1)} %get-tuple-element.24), channel_id=1, source_target_pairs={{0,2},{1,3},{2,0},{3,1},{4,6},{5,7},{6,4},{7,5},{8,10},{9,11},{10,... | collective-permute-start | bytes 104456 | tf_op jit(solution)/shard_map/ppermute | solution.py:372
  24.8 2.9 %collective-permute-done.12.refs_6_ = s16[1,8,2176]{2,1,0:T(8,128)(2,1)S(1)} collective-permute-done((s16[1,8,2176]{2,1,0:T(8,128)(2,1)S(1)}, s16[1,8,2176]{2,1,0:T(8,128)(2,1)S(1)}, u32[]{:S(2)}, u32[]{:S(2)}) %collective-permute-start.12) | collective-permute-done | bytes 34848 | tf_op jit(solution)/shard_map/ppermute | solution.py:372
  27.7 0.7 %last_sum.1 = f32[8,2048]{1,0:T(8,128)} custom-call(f32[8,2048]{1,0:T(8,128)S(1)} %collective-permute-done.7.refs_0_, f32[8,2048]{1,0:T(8,128)S(1)} %collective-permute-done.8.refs_1_, f32[8,2048]{1,0:T(8,128)S(1)} %collective-permute-done.9.refs_2_, f32[4,8,2048]{2,1,0:T(8,128)S(1)} %get-tuple-element.15.keep_ref.refs_3_, ...), custom_call_target="tpu_custom_call" | custom-call | tf_op jit(solution)/shard_map/last_sum/pallas_call | solution.py:361
  (16 shorter events, 0.1 us)
Async XLA Ops:
  0.0 7.3 %collective-permute-start = (bf16[1,8,2048]{2,1,0:T(8,128)(2,1)}, bf16[1,8,2048]{2,1,0:T(8,128)(2,1)S(1)}, u32[]{:S(2)}, u32[]{:S(2)}) collective-permute-start(bf16[1,8,2048]{2,1,0:T(8,128)(2,1)} %bitcast.5), channel_id=1, source_target_pairs={{0,1},{1,0},{2,3},{3,2},{4,5},{5,4},{6,7},{7,6},{8,9},{9,8},{10,11... | collective-permute-start | bytes 98312 | tf_op jit(solution)/shard_map/ppermute | solution.py:372
  3.0 9.1 %collective-permute-start.2 = (bf16[8,2048]{1,0:T(8,128)(2,1)}, bf16[8,2048]{1,0:T(8,128)(2,1)S(1)}, u32[]{:S(2)}, u32[]{:S(2)}) collective-permute-start(bf16[8,2048]{1,0:T(8,128)(2,1)} %refs_0_.1), channel_id=1, source_target_pairs={{0,8},{4,12},{8,0},{12,4},{16,24},{20,28},{24,16},{28,20},{1,9},{5... | collective-permute-start | bytes 98312 | tf_op jit(solution)/shard_map/ppermute | solution.py:372
  4.5 7.6 %collective-permute-start.4 = (bf16[8,2048]{1,0:T(8,128)(2,1)}, bf16[8,2048]{1,0:T(8,128)(2,1)S(1)}, u32[]{:S(2)}, u32[]{:S(2)}) collective-permute-start(bf16[8,2048]{1,0:T(8,128)(2,1)} %refs_0_.1), channel_id=1, source_target_pairs={{0,24},{4,28},{8,16},{12,20},{16,8},{20,12},{24,0},{28,4},{1,25},{... | collective-permute-start | bytes 98312 | tf_op jit(solution)/shard_map/ppermute | solution.py:372
  6.0 6.1 %collective-permute-start.3 = (bf16[8,2048]{1,0:T(8,128)(2,1)}, bf16[8,2048]{1,0:T(8,128)(2,1)S(1)}, u32[]{:S(2)}, u32[]{:S(2)}) collective-permute-start(bf16[8,2048]{1,0:T(8,128)(2,1)} %refs_0_.1), channel_id=1, source_target_pairs={{0,16},{4,20},{8,24},{12,28},{16,0},{20,4},{24,8},{28,12},{1,17},{... | collective-permute-start | bytes 98312 | tf_op jit(solution)/shard_map/ppermute | solution.py:372
  6.5 0.8 %copy-start.3 = (bf16[8,2048]{1,0:T(8,128)(2,1)S(1)}, bf16[8,2048]{1,0:T(8,128)(2,1)}, u32[]{:S(2)}) copy-start(bf16[8,2048]{1,0:T(8,128)(2,1)} %refs_0_.1) | copy-start | bytes 98308
  7.3 5.6 %collective-permute-start.1 = (bf16[2,8,2048]{2,1,0:T(8,128)(2,1)S(1)}, bf16[2,8,2048]{2,1,0:T(8,128)(2,1)S(1)}, u32[]{:S(2)}, u32[]{:S(2)}) collective-permute-start(bf16[2,8,2048]{2,1,0:T(8,128)(2,1)S(1)} %stack_pieces.5.refs_0_), channel_id=1, source_target_pairs={{0,2},{1,3},{2,0},{3,1},{4,6},{5,7},{6,4},{7,5},{8,10},{9,11},{10,... | collective-permute-start | bytes 196616 | tf_op jit(solution)/shard_map/ppermute | solution.py:372
  10.0 1.4 %copy-start = (bf16[192,4096]{1,0:T(8,128)(2,1)S(1)}, bf16[192,4096]{1,0:T(8,128)(2,1)}, u32[]{:S(2)}) copy-start(bf16[192,4096]{1,0:T(8,128)(2,1)} %param.8) | copy-start | bytes 4718596
  12.1 0.9 %copy-start.1 = (bf16[128,512]{1,0:T(8,128)(2,1)S(1)}, bf16[128,512]{1,0:T(8,128)(2,1)}, u32[]{:S(2)}) copy-start(bf16[128,512]{1,0:T(8,128)(2,1)} %constant.4.clone.spread_ref) | copy-start | bytes 393220
  12.1 0.9 %copy-start.4 = (s32[192]{0:T(256)S(1)}, s32[192]{0:T(256)}, u32[]{:S(2)}) copy-start(s32[192]{0:T(256)} %rows_ref.3) | copy-start | bytes 2308
  12.1 0.9 %copy-start.5 = (s32[192]{0:T(256)S(1)}, s32[192]{0:T(256)}, u32[]{:S(2)}) copy-start(s32[192]{0:T(256)} %cols_ref.3) | copy-start | bytes 2308
  12.2 3.3 %copy-start.2 = (bf16[512,128]{1,0:T(8,128)(2,1)S(1)}, bf16[512,128]{1,0:T(8,128)(2,1)}, u32[]{:S(2)}) copy-start(bf16[512,128]{1,0:T(8,128)(2,1)} %constant.5.clone.fold_ref) | copy-start | bytes 393220
  12.2 3.3 %collective-permute-start.10 = (bf16[4,8,2048]{2,1,0:T(8,128)(2,1)S(1)}, bf16[4,8,2048]{2,1,0:T(8,128)(2,1)S(1)}, u32[]{:S(2)}, u32[]{:S(2)}) collective-permute-start(bf16[4,8,2048]{2,1,0:T(8,128)(2,1)S(1)} %stack_pieces.7.after_ref.same_ref), channel_id=1, source_target_pairs={{0,4},{4,0},{8,12},{12,8},{16,20},{20,16},{24,28},{28,24},{1,5},{5... | collective-permute-start | bytes 393224 | tf_op jit(solution)/shard_map/ppermute | solution.py:372
  14.8 3.7 %collective-permute-start.6 = (f32[2,8,2048]{2,1,0:T(8,128)S(1)}, f32[2,8,2048]{2,1,0:T(8,128)S(1)}, u32[]{:S(2)}, u32[]{:S(2)}) collective-permute-start(f32[2,8,2048]{2,1,0:T(8,128)S(1)} %get-tuple-element.17), channel_id=1, source_target_pairs={{0,4},{4,0},{8,12},{12,8},{16,20},{20,16},{24,28},{28,24},{1,5},{5... | collective-permute-start | bytes 393224 | tf_op jit(solution)/shard_map/ppermute | solution.py:372
  15.4 3.2 %collective-permute-start.5 = (f32[2,8,2048]{2,1,0:T(8,128)S(1)}, f32[2,8,2048]{2,1,0:T(8,128)S(1)}, u32[]{:S(2)}, u32[]{:S(2)}) collective-permute-start(f32[2,8,2048]{2,1,0:T(8,128)S(1)} %get-tuple-element.16.after_ref), channel_id=1, source_target_pairs={{0,4},{4,0},{8,12},{12,8},{16,20},{20,16},{24,28},{28,24},{1,5},{5... | collective-permute-start | bytes 393224 | tf_op jit(solution)/shard_map/ppermute | solution.py:372
  17.9 4.6 %collective-permute-start.11 = (s16[2,8,2176]{2,1,0:T(8,128)(2,1)S(1)}, s16[2,8,2176]{2,1,0:T(8,128)(2,1)S(1)}, u32[]{:S(2)}, u32[]{:S(2)}) collective-permute-start(s16[2,8,2176]{2,1,0:T(8,128)(2,1)S(1)} %get-tuple-element.22), channel_id=1, source_target_pairs={{0,1},{1,0},{2,3},{3,2},{4,5},{5,4},{6,7},{7,6},{8,9},{9,8},{10,11... | collective-permute-start | bytes 208904 | tf_op jit(solution)/shard_map/ppermute | solution.py:372
  18.6 9.1 %collective-permute-start.8 = (f32[8,2048]{1,0:T(8,128)S(1)}, f32[8,2048]{1,0:T(8,128)S(1)}, u32[]{:S(2)}, u32[]{:S(2)}) collective-permute-start(f32[8,2048]{1,0:T(8,128)S(1)} %get-tuple-element.19), channel_id=1, source_target_pairs={{0,16},{4,20},{8,24},{12,28},{16,0},{20,4},{24,8},{28,12},{1,17},{... | collective-permute-start | bytes 196616 | tf_op jit(solution)/shard_map/ppermute | solution.py:372
  20.1 7.6 %collective-permute-start.9 = (f32[8,2048]{1,0:T(8,128)S(1)}, f32[8,2048]{1,0:T(8,128)S(1)}, u32[]{:S(2)}, u32[]{:S(2)}) collective-permute-start(f32[8,2048]{1,0:T(8,128)S(1)} %get-tuple-element.20), channel_id=1, source_target_pairs={{0,24},{4,28},{8,16},{12,20},{16,8},{20,12},{24,0},{28,4},{1,25},{... | collective-permute-start | bytes 196616 | tf_op jit(solution)/shard_map/ppermute | solution.py:372
  21.6 6.1 %collective-permute-start.7 = (f32[8,2048]{1,0:T(8,128)S(1)}, f32[8,2048]{1,0:T(8,128)S(1)}, u32[]{:S(2)}, u32[]{:S(2)}) collective-permute-start(f32[8,2048]{1,0:T(8,128)S(1)} %get-tuple-element.18.after_ref), channel_id=1, source_target_pairs={{0,8},{4,12},{8,0},{12,4},{16,24},{20,28},{24,16},{28,20},{1,9},{5... | collective-permute-start | bytes 196616 | tf_op jit(solution)/shard_map/ppermute | solution.py:372
  22.7 4.9 %collective-permute-start.12 = (s16[1,8,2176]{2,1,0:T(8,128)(2,1)S(1)}, s16[1,8,2176]{2,1,0:T(8,128)(2,1)S(1)}, u32[]{:S(2)}, u32[]{:S(2)}) collective-permute-start(s16[1,8,2176]{2,1,0:T(8,128)(2,1)S(1)} %get-tuple-element.24), channel_id=1, source_target_pairs={{0,2},{1,3},{2,0},{3,1},{4,6},{5,7},{6,4},{7,5},{8,10},{9,11},{10,... | collective-permute-start | bytes 104456 | tf_op jit(solution)/shard_map/ppermute | solution.py:372

commit v11 on v10

--- a/solution.py
+++ b/solution.py
@@ -379,10 +379,10 @@
     chips = [swap(vectors, "brow", n_rows, 2 * h) for h in range(1, n_rows // 2)]
     segment, d = own, 1
     while d < n_cols:
-        segment = stack(segment, swap(segment if d > 1 else vectors[None], "bcol", n_cols, d))
+        segment = stack(segment, swap(segment if d > 1 else vectors[None], "bcol", n_cols, d), after=tuple(chips[:1]))
         d *= 2
     blocks = prep(tiles)
-    same = stack(own, *chips, after=(blocks,))
+    same = stack(own, *chips, after=(blocks, segment))
     other = swap(same, "brow", n_rows, 1)
 
     col_keep, *col_give = backward(segment, blocks, tile_rows, tile_cols, counts, n_rows, same)

time: 28.6 us -> 32.7 us (1.14)
  waiting for transfers between devices: 3.27 us -> 8.28 us
  starting transfers between devices: 16.1 us -> 15.2 us
  Pallas kernels: 5.99 us -> 6.85 us
  local copies, waits for them, and re-layouts: 2.27 us -> 1.43 us
    ppermute x13, waiting for transfers between devices: 3.27 us -> 8.28 us  [swap(): return lax.ppermute(x, axis, [(i, i ^ d) for i in range(size)])]
    ppermute x13, starting transfers between devices: 16.1 us -> 15.2 us  [swap(): return lax.ppermute(x, axis, [(i, i ^ d) for i in range(size)])]
    unnamed x12 -> x10, local copies, waits for them, and re-layouts: 2.27 us -> 1.43 us
    pallas_call x4, Pallas kernels: 0.03 us -> 0.82 us  [stack(): pl.pallas_call(functools.partial(stack_kernel, len(after)), in_specs=[VME...]
  transfers between devices with their start and end apart: 13 -> 13, of which waited for: 2 -> 7; matrix products, arithmetic and copies ran while one was open for 0% -> 0% of each run, Pallas kernels for 18% -> 19%
where the time goes in v11:
time: 32.7 us; the launch traced here: 32.5 us
  starting transfers between devices  15.2 us (46%)
  waiting for transfers between devices  8.28 us (25%)
  Pallas kernels  6.85 us (21%)
  local copies, waits for them, and re-layouts  1.43 us (4%)
  between operations  0.79 us (2%)
    ppermute x13, starting transfers between devices, swap(): return lax.ppermute(x, axis, [(i, i ^ d) for i in range(size)])  15.2 us
    ppermute x13, waiting for transfers between devices, swap(): return lax.ppermute(x, axis, [(i, i ^ d) for i in range(size)])  8.28 us
    pallas_call x1, Pallas kernels, forward(): pl.pallas_call(forward_kernel, in_specs=[SMEM] * 3 + [VMEM] * 4 + [ANY],...  2.5 us
    pallas_call x1, Pallas kernels, backward(): pl.pallas_call(backward_kernel, in_specs=[SMEM] * 3 + [VMEM] * 3 + [ANY],...  1.87 us
    unnamed x10, local copies, waits for them, and re-layouts  1.43 us
    pallas_call x4, Pallas kernels, stack(): pl.pallas_call(functools.partial(stack_kernel, len(after)), in_specs=[VME...  0.82 us
    pallas_call x1, Pallas kernels, last_sum(): pl.pallas_call(last_sum_kernel, in_specs=[VMEM] * (4 + len(chips)), out_s...  0.74 us
    pallas_call x1, Pallas kernels, prep(): pl.pallas_call(prep_kernel, in_specs=[VMEM], out_specs=VMEM, out_shape=ja...  0.69 us
  transfers between devices with their start and end apart: 13, of which 7 were waited for; matrix products, arithmetic and copies ran while one was open for 0% of the time, Pallas kernels for 19%

profile of v11, /device:TPU:0, one launch (start us, length us, event | category | flops | bytes accessed | tf_op | source)
XLA Modules:
  0.0 32.5 jit_solution(2262733733372369657)
XLA Ops:
  0.0 3.0 %collective-permute-start = (bf16[1,8,2048]{2,1,0:T(8,128)(2,1)}, bf16[1,8,2048]{2,1,0:T(8,128)(2,1)S(1)}, u32[]{:S(2)}, u32[]{:S(2)}) collective-permute-start(bf16[1,8,2048]{2,1,0:T(8,128)(2,1)} %bitcast.2), channel_id=1, source_target_pairs={{0,1},{1,0},{2,3},{3,2},{4,5},{5,4},{6,7},{7,6},{8,9},{9,8},{10,11... | collective-permute-start | bytes 98312 | tf_op jit(solution)/shard_map/ppermute | solution.py:372
  3.0 1.5 %collective-permute-start.1 = (bf16[8,2048]{1,0:T(8,128)(2,1)}, bf16[8,2048]{1,0:T(8,128)(2,1)S(1)}, u32[]{:S(2)}, u32[]{:S(2)}) collective-permute-start(bf16[8,2048]{1,0:T(8,128)(2,1)} %refs_0_.1), channel_id=1, source_target_pairs={{0,8},{4,12},{8,0},{12,4},{16,24},{20,28},{24,16},{28,20},{1,9},{5... | collective-permute-start | bytes 98312 | tf_op jit(solution)/shard_map/ppermute | solution.py:372
  4.5 0.8 %stack_pieces.4.refs_0_ = bf16[1,8,2048]{2,1,0:T(8,128)(2,1)S(1)} custom-call(bf16[8,2048]{1,0:T(8,128)(2,1)} %refs_0_.1), custom_call_target="tpu_custom_call" | custom-call | tf_op jit(solution)/shard_map/stack_pieces/pallas_call | solution.py:293
  5.3 0.0 collective-permute-done.refs_1_
  5.3 1.8 %collective-permute-done.1.refs_2_.refs_1_ = bf16[8,2048]{1,0:T(8,128)(2,1)S(1)} collective-permute-done((bf16[8,2048]{1,0:T(8,128)(2,1)}, bf16[8,2048]{1,0:T(8,128)(2,1)S(1)}, u32[]{:S(2)}, u32[]{:S(2)}) %collective-permute-start.1) | collective-permute-done | bytes 32800 | tf_op jit(solution)/shard_map/ppermute | solution.py:372
  7.2 2.6 %collective-permute-start.2 = (bf16[2,8,2048]{2,1,0:T(8,128)(2,1)S(1)}, bf16[2,8,2048]{2,1,0:T(8,128)(2,1)S(1)}, u32[]{:S(2)}, u32[]{:S(2)}) collective-permute-start(bf16[2,8,2048]{2,1,0:T(8,128)(2,1)S(1)} %stack_pieces.5.refs_0_), channel_id=1, source_target_pairs={{0,2},{1,3},{2,0},{3,1},{4,6},{5,7},{6,4},{7,5},{8,10},{9,11},{10,... | collective-permute-start | bytes 196616 | tf_op jit(solution)/shard_map/ppermute | solution.py:372
  9.7 2.4 %collective-permute-start.4 = (bf16[8,2048]{1,0:T(8,128)(2,1)}, bf16[8,2048]{1,0:T(8,128)(2,1)S(1)}, u32[]{:S(2)}, u32[]{:S(2)}) collective-permute-start(bf16[8,2048]{1,0:T(8,128)(2,1)} %refs_0_.1), channel_id=1, source_target_pairs={{0,24},{4,28},{8,16},{12,20},{16,8},{20,12},{24,0},{28,4},{1,25},{... | collective-permute-start | bytes 98312 | tf_op jit(solution)/shard_map/ppermute | solution.py:372
  12.2 0.5 %collective-permute-start.3 = (bf16[8,2048]{1,0:T(8,128)(2,1)}, bf16[8,2048]{1,0:T(8,128)(2,1)S(1)}, u32[]{:S(2)}, u32[]{:S(2)}) collective-permute-start(bf16[8,2048]{1,0:T(8,128)(2,1)} %refs_0_.1), channel_id=1, source_target_pairs={{0,16},{4,20},{8,24},{12,28},{16,0},{20,4},{24,8},{28,12},{1,17},{... | collective-permute-start | bytes 98312 | tf_op jit(solution)/shard_map/ppermute | solution.py:372
  12.7 1.4 %copy-done = bf16[192,4096]{1,0:T(8,128)(2,1)S(1)} copy-done((bf16[192,4096]{1,0:T(8,128)(2,1)S(1)}, bf16[192,4096]{1,0:T(8,128)(2,1)}, u32[]{:S(2)}) %copy-start) | copy-done | bytes 1572888
  14.1 0.7 %prep_tiles.1.refs_4_.tiles_ref = bf16[192,32,128]{2,1,0:T(8,128)(2,1)S(1)} custom-call(bf16[24,32,8,128]{3,2,1,0:T(8,128)(2,1)S(1)} %bitcast.4), custom_call_target="tpu_custom_call" | custom-call | bytes 3145728 | tf_op jit(solution)/shard_map/prep_tiles/pallas_call | solution.py:77
  14.8 0.0 copy-start.1
  14.8 0.0 copy-start.3
  14.8 0.0 copy-start.4
  14.9 0.0 copy-start.2
  14.9 1.4 %collective-permute-done.3.refs_2_ = bf16[8,2048]{1,0:T(8,128)(2,1)S(1)} collective-permute-done((bf16[8,2048]{1,0:T(8,128)(2,1)}, bf16[8,2048]{1,0:T(8,128)(2,1)S(1)}, u32[]{:S(2)}, u32[]{:S(2)}) %collective-permute-start.3) | collective-permute-done | bytes 32800 | tf_op jit(solution)/shard_map/ppermute | solution.py:372
  16.3 0.1 collective-permute-start.10
  17.1 1.9 %transpose_product.1 = (f32[4,8,2048]{2,1,0:T(8,128)S(1)}, f32[2,8,2048]{2,1,0:T(8,128)S(1)}, f32[2,8,2048]{2,1,0:T(8,128)S(1)}) custom-call(s32[192]{0:T(256)S(1)} %copy-done.3, s32[192]{0:T(256)S(1)} %copy-done.4, s32[1,1]{1,0:T(1,128)S(6)} %copy.8.count_ref, bf16[128,512]{1,0:T(8,128)(2,1)S(1)} %copy-done.1, ...), custom_call_target="tpu_custom_call" | custom-call | flops 100663296 | bytes 3145728 | tf_op jit(solution)/shard_map/transpose_product/pallas_call | solution.py:154
  19.0 0.5 %collective-permute-start.6 = (f32[2,8,2048]{2,1,0:T(8,128)S(1)}, f32[2,8,2048]{2,1,0:T(8,128)S(1)}, u32[]{:S(2)}, u32[]{:S(2)}) collective-permute-start(f32[2,8,2048]{2,1,0:T(8,128)S(1)} %get-tuple-element.17), channel_id=1, source_target_pairs={{0,4},{4,0},{8,12},{12,8},{16,20},{20,16},{24,28},{28,24},{1,5},{5... | collective-permute-start | bytes 393224 | tf_op jit(solution)/shard_map/ppermute | solution.py:372
  19.5 0.1 collective-permute-start.5
  19.6 2.5 %forward_product.1 = (f32[2,8,2048]{2,1,0:T(8,128)S(1)}, s16[2,8,2176]{2,1,0:T(8,128)(2,1)S(1)}) custom-call(s32[192]{0:T(256)S(1)} %copy-done.3, s32[192]{0:T(256)S(1)} %copy-done.4, s32[1,1]{1,0:T(1,128)S(6)} %copy.8.count_ref, bf16[512,128]{1,0:T(8,128)(2,1)S(1)} %copy-done.2, bf16[192,32,128]{2,1,0:T(8,128)(2,1)S(1)} %prep_tiles.1.refs_4_.tiles_ref, ...), custom_call_target="tpu_custom_call" | custom-call | flops 100663296 | bytes 3145728 | tf_op jit(solution)/shard_map/forward_product/pallas_call | solution.py:262
  22.1 0.5 %collective-permute-start.11 = (s16[2,8,2176]{2,1,0:T(8,128)(2,1)S(1)}, s16[2,8,2176]{2,1,0:T(8,128)(2,1)S(1)}, u32[]{:S(2)}, u32[]{:S(2)}) collective-permute-start(s16[2,8,2176]{2,1,0:T(8,128)(2,1)S(1)} %get-tuple-element.22), channel_id=1, source_target_pairs={{0,1},{1,0},{2,3},{3,2},{4,5},{5,4},{6,7},{7,6},{8,9},{9,8},{10,11... | collective-permute-start | bytes 208904 | tf_op jit(solution)/shard_map/ppermute | solution.py:372
  22.6 0.7 %collective-permute-start.8 = (f32[8,2048]{1,0:T(8,128)S(1)}, f32[8,2048]{1,0:T(8,128)S(1)}, u32[]{:S(2)}, u32[]{:S(2)}) collective-permute-start(f32[8,2048]{1,0:T(8,128)S(1)} %get-tuple-element.19), channel_id=1, source_target_pairs={{0,16},{4,20},{8,24},{12,28},{16,0},{20,4},{24,8},{28,12},{1,17},{... | collective-permute-start | bytes 196616 | tf_op jit(solution)/shard_map/ppermute | solution.py:372
  23.3 1.5 %collective-permute-start.9 = (f32[8,2048]{1,0:T(8,128)S(1)}, f32[8,2048]{1,0:T(8,128)S(1)}, u32[]{:S(2)}, u32[]{:S(2)}) collective-permute-start(f32[8,2048]{1,0:T(8,128)S(1)} %get-tuple-element.20), channel_id=1, source_target_pairs={{0,24},{4,28},{8,16},{12,20},{16,8},{20,12},{24,0},{28,4},{1,25},{... | collective-permute-start | bytes 196616 | tf_op jit(solution)/shard_map/ppermute | solution.py:372
  24.8 1.4 %collective-permute-start.7 = (f32[8,2048]{1,0:T(8,128)S(1)}, f32[8,2048]{1,0:T(8,128)S(1)}, u32[]{:S(2)}, u32[]{:S(2)}) collective-permute-start(f32[8,2048]{1,0:T(8,128)S(1)} %get-tuple-element.18.after_ref), channel_id=1, source_target_pairs={{0,8},{4,12},{8,0},{12,4},{16,24},{20,28},{24,16},{28,20},{1,9},{5... | collective-permute-start | bytes 196616 | tf_op jit(solution)/shard_map/ppermute | solution.py:372
  26.1 0.5 %collective-permute-done.11.got_ref = s16[2,8,2176]{2,1,0:T(8,128)(2,1)S(1)} collective-permute-done((s16[2,8,2176]{2,1,0:T(8,128)(2,1)S(1)}, s16[2,8,2176]{2,1,0:T(8,128)(2,1)S(1)}, u32[]{:S(2)}, u32[]{:S(2)}) %collective-permute-start.11) | collective-permute-done | bytes 69664 | tf_op jit(solution)/shard_map/ppermute | solution.py:372
  26.7 0.2 halving_sum.1
  26.9 0.4 %collective-permute-start.12 = (s16[1,8,2176]{2,1,0:T(8,128)(2,1)S(1)}, s16[1,8,2176]{2,1,0:T(8,128)(2,1)S(1)}, u32[]{:S(2)}, u32[]{:S(2)}) collective-permute-start(s16[1,8,2176]{2,1,0:T(8,128)(2,1)S(1)} %get-tuple-element.24), channel_id=1, source_target_pairs={{0,2},{1,3},{2,0},{3,1},{4,6},{5,7},{6,4},{7,5},{8,10},{9,11},{10,... | collective-permute-start | bytes 104456 | tf_op jit(solution)/shard_map/ppermute | solution.py:372
  27.3 0.3 collective-permute-done.8.refs_1_
  27.6 1.1 %collective-permute-done.9.refs_2_ = f32[8,2048]{1,0:T(8,128)S(1)} collective-permute-done((f32[8,2048]{1,0:T(8,128)S(1)}, f32[8,2048]{1,0:T(8,128)S(1)}, u32[]{:S(2)}, u32[]{:S(2)}) %collective-permute-start.9) | collective-permute-done | bytes 65568 | tf_op jit(solution)/shard_map/ppermute | solution.py:372
  28.7 0.7 %collective-permute-done.7.refs_0_ = f32[8,2048]{1,0:T(8,128)S(1)} collective-permute-done((f32[8,2048]{1,0:T(8,128)S(1)}, f32[8,2048]{1,0:T(8,128)S(1)}, u32[]{:S(2)}, u32[]{:S(2)}) %collective-permute-start.7) | collective-permute-done | bytes 65568 | tf_op jit(solution)/shard_map/ppermute | solution.py:372
  29.4 2.4 %collective-permute-done.12.refs_6_ = s16[1,8,2176]{2,1,0:T(8,128)(2,1)S(1)} collective-permute-done((s16[1,8,2176]{2,1,0:T(8,128)(2,1)S(1)}, s16[1,8,2176]{2,1,0:T(8,128)(2,1)S(1)}, u32[]{:S(2)}, u32[]{:S(2)}) %collective-permute-start.12) | collective-permute-done | bytes 34848 | tf_op jit(solution)/shard_map/ppermute | solution.py:372
  31.8 0.7 %last_sum.1 = f32[8,2048]{1,0:T(8,128)} custom-call(f32[8,2048]{1,0:T(8,128)S(1)} %collective-permute-done.7.refs_0_, f32[8,2048]{1,0:T(8,128)S(1)} %collective-permute-done.8.refs_1_, f32[8,2048]{1,0:T(8,128)S(1)} %collective-permute-done.9.refs_2_, f32[4,8,2048]{2,1,0:T(8,128)S(1)} %get-tuple-element.15.keep_ref.refs_3_, ...), custom_call_target="tpu_custom_call" | custom-call | tf_op jit(solution)/shard_map/last_sum/pallas_call | solution.py:361
  (14 shorter events, 0.1 us)
Async XLA Ops:
  0.0 5.3 %collective-permute-start = (bf16[1,8,2048]{2,1,0:T(8,128)(2,1)}, bf16[1,8,2048]{2,1,0:T(8,128)(2,1)S(1)}, u32[]{:S(2)}, u32[]{:S(2)}) collective-permute-start(bf16[1,8,2048]{2,1,0:T(8,128)(2,1)} %bitcast.2), channel_id=1, source_target_pairs={{0,1},{1,0},{2,3},{3,2},{4,5},{5,4},{6,7},{7,6},{8,9},{9,8},{10,11... | collective-permute-start | bytes 98312 | tf_op jit(solution)/shard_map/ppermute | solution.py:372
  3.0 4.1 %collective-permute-start.1 = (bf16[8,2048]{1,0:T(8,128)(2,1)}, bf16[8,2048]{1,0:T(8,128)(2,1)S(1)}, u32[]{:S(2)}, u32[]{:S(2)}) collective-permute-start(bf16[8,2048]{1,0:T(8,128)(2,1)} %refs_0_.1), channel_id=1, source_target_pairs={{0,8},{4,12},{8,0},{12,4},{16,24},{20,28},{24,16},{28,20},{1,9},{5... | collective-permute-start | bytes 98312 | tf_op jit(solution)/shard_map/ppermute | solution.py:372
  7.2 7.7 %collective-permute-start.2 = (bf16[2,8,2048]{2,1,0:T(8,128)(2,1)S(1)}, bf16[2,8,2048]{2,1,0:T(8,128)(2,1)S(1)}, u32[]{:S(2)}, u32[]{:S(2)}) collective-permute-start(bf16[2,8,2048]{2,1,0:T(8,128)(2,1)S(1)} %stack_pieces.5.refs_0_), channel_id=1, source_target_pairs={{0,2},{1,3},{2,0},{3,1},{4,6},{5,7},{6,4},{7,5},{8,10},{9,11},{10,... | collective-permute-start | bytes 196616 | tf_op jit(solution)/shard_map/ppermute | solution.py:372
  9.7 5.1 %collective-permute-start.4 = (bf16[8,2048]{1,0:T(8,128)(2,1)}, bf16[8,2048]{1,0:T(8,128)(2,1)S(1)}, u32[]{:S(2)}, u32[]{:S(2)}) collective-permute-start(bf16[8,2048]{1,0:T(8,128)(2,1)} %refs_0_.1), channel_id=1, source_target_pairs={{0,24},{4,28},{8,16},{12,20},{16,8},{20,12},{24,0},{28,4},{1,25},{... | collective-permute-start | bytes 98312 | tf_op jit(solution)/shard_map/ppermute | solution.py:372
  12.2 4.1 %collective-permute-start.3 = (bf16[8,2048]{1,0:T(8,128)(2,1)}, bf16[8,2048]{1,0:T(8,128)(2,1)S(1)}, u32[]{:S(2)}, u32[]{:S(2)}) collective-permute-start(bf16[8,2048]{1,0:T(8,128)(2,1)} %refs_0_.1), channel_id=1, source_target_pairs={{0,16},{4,20},{8,24},{12,28},{16,0},{20,4},{24,8},{28,12},{1,17},{... | collective-permute-start | bytes 98312 | tf_op jit(solution)/shard_map/ppermute | solution.py:372
  12.7 1.4 %copy-start = (bf16[192,4096]{1,0:T(8,128)(2,1)S(1)}, bf16[192,4096]{1,0:T(8,128)(2,1)}, u32[]{:S(2)}) copy-start(bf16[192,4096]{1,0:T(8,128)(2,1)} %param.8) | copy-start | bytes 4718596
  14.8 2.3 %copy-start.1 = (bf16[128,512]{1,0:T(8,128)(2,1)S(1)}, bf16[128,512]{1,0:T(8,128)(2,1)}, u32[]{:S(2)}) copy-start(bf16[128,512]{1,0:T(8,128)(2,1)} %constant.4.clone.spread_ref) | copy-start | bytes 393220
  14.8 2.2 %copy-start.3 = (s32[192]{0:T(256)S(1)}, s32[192]{0:T(256)}, u32[]{:S(2)}) copy-start(s32[192]{0:T(256)} %rows_ref.3) | copy-start | bytes 2308
  14.8 2.2 %copy-start.4 = (s32[192]{0:T(256)S(1)}, s32[192]{0:T(256)}, u32[]{:S(2)}) copy-start(s32[192]{0:T(256)} %cols_ref.3) | copy-start | bytes 2308
  14.9 4.7 %copy-start.2 = (bf16[512,128]{1,0:T(8,128)(2,1)S(1)}, bf16[512,128]{1,0:T(8,128)(2,1)}, u32[]{:S(2)}) copy-start(bf16[512,128]{1,0:T(8,128)(2,1)} %constant.5.clone.fold_ref) | copy-start | bytes 393220
  16.3 3.3 %collective-permute-start.10 = (bf16[4,8,2048]{2,1,0:T(8,128)(2,1)S(1)}, bf16[4,8,2048]{2,1,0:T(8,128)(2,1)S(1)}, u32[]{:S(2)}, u32[]{:S(2)}) collective-permute-start(bf16[4,8,2048]{2,1,0:T(8,128)(2,1)S(1)} %stack_pieces.7.after_ref.same_ref), channel_id=1, source_target_pairs={{0,4},{4,0},{8,12},{12,8},{16,20},{20,16},{24,28},{28,24},{1,5},{5... | collective-permute-start | bytes 393224 | tf_op jit(solution)/shard_map/ppermute | solution.py:372
  19.0 3.6 %collective-permute-start.6 = (f32[2,8,2048]{2,1,0:T(8,128)S(1)}, f32[2,8,2048]{2,1,0:T(8,128)S(1)}, u32[]{:S(2)}, u32[]{:S(2)}) collective-permute-start(f32[2,8,2048]{2,1,0:T(8,128)S(1)} %get-tuple-element.17), channel_id=1, source_target_pairs={{0,4},{4,0},{8,12},{12,8},{16,20},{20,16},{24,28},{28,24},{1,5},{5... | collective-permute-start | bytes 393224 | tf_op jit(solution)/shard_map/ppermute | solution.py:372
  19.5 3.0 %collective-permute-start.5 = (f32[2,8,2048]{2,1,0:T(8,128)S(1)}, f32[2,8,2048]{2,1,0:T(8,128)S(1)}, u32[]{:S(2)}, u32[]{:S(2)}) collective-permute-start(f32[2,8,2048]{2,1,0:T(8,128)S(1)} %get-tuple-element.16.after_ref), channel_id=1, source_target_pairs={{0,4},{4,0},{8,12},{12,8},{16,20},{20,16},{24,28},{28,24},{1,5},{5... | collective-permute-start | bytes 393224 | tf_op jit(solution)/shard_map/ppermute | solution.py:372
  22.1 4.6 %collective-permute-start.11 = (s16[2,8,2176]{2,1,0:T(8,128)(2,1)S(1)}, s16[2,8,2176]{2,1,0:T(8,128)(2,1)S(1)}, u32[]{:S(2)}, u32[]{:S(2)}) collective-permute-start(s16[2,8,2176]{2,1,0:T(8,128)(2,1)S(1)} %get-tuple-element.22), channel_id=1, source_target_pairs={{0,1},{1,0},{2,3},{3,2},{4,5},{5,4},{6,7},{7,6},{8,9},{9,8},{10,11... | collective-permute-start | bytes 208904 | tf_op jit(solution)/shard_map/ppermute | solution.py:372
  22.6 5.0 %collective-permute-start.8 = (f32[8,2048]{1,0:T(8,128)S(1)}, f32[8,2048]{1,0:T(8,128)S(1)}, u32[]{:S(2)}, u32[]{:S(2)}) collective-permute-start(f32[8,2048]{1,0:T(8,128)S(1)} %get-tuple-element.19), channel_id=1, source_target_pairs={{0,16},{4,20},{8,24},{12,28},{16,0},{20,4},{24,8},{28,12},{1,17},{... | collective-permute-start | bytes 196616 | tf_op jit(solution)/shard_map/ppermute | solution.py:372
  23.3 5.5 %collective-permute-start.9 = (f32[8,2048]{1,0:T(8,128)S(1)}, f32[8,2048]{1,0:T(8,128)S(1)}, u32[]{:S(2)}, u32[]{:S(2)}) collective-permute-start(f32[8,2048]{1,0:T(8,128)S(1)} %get-tuple-element.20), channel_id=1, source_target_pairs={{0,24},{4,28},{8,16},{12,20},{16,8},{20,12},{24,0},{28,4},{1,25},{... | collective-permute-start | bytes 196616 | tf_op jit(solution)/shard_map/ppermute | solution.py:372
  24.8 4.6 %collective-permute-start.7 = (f32[8,2048]{1,0:T(8,128)S(1)}, f32[8,2048]{1,0:T(8,128)S(1)}, u32[]{:S(2)}, u32[]{:S(2)}) collective-permute-start(f32[8,2048]{1,0:T(8,128)S(1)} %get-tuple-element.18.after_ref), channel_id=1, source_target_pairs={{0,8},{4,12},{8,0},{12,4},{16,24},{20,28},{24,16},{28,20},{1,9},{5... | collective-permute-start | bytes 196616 | tf_op jit(solution)/shard_map/ppermute | solution.py:372
  26.9 4.9 %collective-permute-start.12 = (s16[1,8,2176]{2,1,0:T(8,128)(2,1)S(1)}, s16[1,8,2176]{2,1,0:T(8,128)(2,1)S(1)}, u32[]{:S(2)}, u32[]{:S(2)}) collective-permute-start(s16[1,8,2176]{2,1,0:T(8,128)(2,1)S(1)} %get-tuple-element.24), channel_id=1, source_target_pairs={{0,2},{1,3},{2,0},{3,1},{4,6},{5,7},{6,4},{7,5},{8,10},{9,11},{10,... | collective-permute-start | bytes 104456 | tf_op jit(solution)/shard_map/ppermute | solution.py:372

commit v12 on v10

--- a/solution.py
+++ b/solution.py
@@ -84,6 +84,14 @@
         cost_estimate=pl.CostEstimate(flops=0, bytes_accessed=4 * tiles.size, transcendentals=0),
         name="prep_tiles",
     )(view)
+
+
+def doubled(size):
+    order, d = [0], size // 2
+    while d > 0:
+        order += [x ^ d for x in order]
+        d //= 2
+    return order
 
 
 def build_table(pieces, spread, table):
@@ -104,7 +112,7 @@
 def backward_kernel(
     rows_ref, cols_ref, count_ref, spread_ref, tiles_ref, seg_ref, after_ref, keep_ref, *refs
 ):
-    pieces = [seg_ref.at[n] for n in range(seg_ref.shape[0])]
+    pieces = [seg_ref.at[at] for at in np.argsort(doubled(seg_ref.shape[0]))]
     *give_refs, table, acc_a, acc_b = refs
     per_give = give_refs[0].shape[0]
     n_out = 2 * keep_ref.shape[0]
@@ -247,11 +255,11 @@
         out = jnp.dot(first, fold, preferred_element_type=F32)
         out = out + jnp.dot(rest, fold, preferred_element_type=F32)
         parts = [out[p * width : (p + 1) * width] for p in range(pairs)]
-        if n % 2 == 0:
+        if n < n_out // 2:
             for p in range(pairs):
-                keep_ref[n // 2, :, p * LANES : (p + 1) * LANES] = parts[p]
+                keep_ref[n, :, p * LANES : (p + 1) * LANES] = parts[p]
         else:
-            encode(parts, give_ref.at[n // 2])
+            encode(parts, give_ref.at[n - n_out // 2])
 
 
 def forward(same, other, tiles, tile_rows, tile_cols, counts, n_out, after):
@@ -321,13 +329,14 @@
 
 
 def split_sum_kernel(keep_ref, got_ref, after_ref, next_keep, next_give):
-    for h in range(next_keep.shape[0]):
-        for n, got in enumerate(decode(got_ref.at[2 * h])):
+    half = next_keep.shape[0]
+    for h in range(half):
+        for n, got in enumerate(decode(got_ref.at[h])):
             at = pl.ds(n * LANES, LANES)
-            next_keep[h, :, at] = keep_ref[2 * h, :, at] + got
+            next_keep[h, :, at] = keep_ref[h, :, at] + got
         sums = [
-            keep_ref[2 * h + 1, :, n * LANES : (n + 1) * LANES] + got
-            for n, got in enumerate(decode(got_ref.at[2 * h + 1]))
+            keep_ref[half + h, :, n * LANES : (n + 1) * LANES] + got
+            for n, got in enumerate(decode(got_ref.at[half + h]))
         ]
         encode(sums, next_give.at[h])
 
@@ -377,10 +386,11 @@
     n_cols = lax.axis_size("bcol")
     own = stack(vectors)
     chips = [swap(vectors, "brow", n_rows, 2 * h) for h in range(1, n_rows // 2)]
-    segment, d = own, 1
-    while d < n_cols:
-        segment = stack(segment, swap(segment if d > 1 else vectors[None], "bcol", n_cols, d))
-        d *= 2
+    segment, d = own, n_cols // 2
+    while d > 0:
+        first = d == n_cols // 2
+        segment = stack(segment, swap(vectors[None] if first else segment, "bcol", n_cols, d))
+        d //= 2
     blocks = prep(tiles)
     same = stack(own, *chips, after=(blocks,))
     other = swap(same, "brow", n_rows, 1)
@@ -390,11 +400,11 @@
     col_got = [swap(x, "brow", n_rows, 1) for x in col_give]
     sums = pair_sum(col_keep, col_got)
     from_chips = [swap(x, "brow", n_rows, 2 * (h + 1)) for h, x in enumerate(sums)]
-    row_got, d = swap(give, "bcol", n_cols, 1), 2
-    while d < n_cols:
+    row_got, d = swap(give, "bcol", n_cols, n_cols // 2), n_cols // 4
+    while d > 0:
         row_keep, give = split_sum(row_keep, row_got, sums[0])
         row_got = swap(give, "bcol", n_cols, d)
-        d *= 2
+        d //= 2
     return last_sum(row_keep, row_got, col_keep, col_got[0], from_chips)
 
 

time: 28.6 us -> 30.2 us (1.056)
  waiting for transfers between devices: 3.27 us -> 6.33 us
  starting transfers between devices: 16.1 us -> 14.6 us
    ppermute x13, waiting for transfers between devices: 3.27 us -> 6.33 us  [swap(): return lax.ppermute(x, axis, [(i, i ^ d) for i in range(size)])]
    ppermute x13, starting transfers between devices: 16.1 us -> 14.6 us  [swap(): return lax.ppermute(x, axis, [(i, i ^ d) for i in range(size)])]
  transfers between devices with their start and end apart: 13 -> 13, of which waited for: 2 -> 2; matrix products, arithmetic and copies ran while one was open for 0% -> 0% of each run, Pallas kernels for 18% -> 17%
where the time goes in v12:
time: 30.2 us; the launch traced here: 29.9 us
  starting transfers between devices  14.6 us (48%)
  waiting for transfers between devices  6.33 us (21%)
  Pallas kernels  5.95 us (20%)
  local copies, waits for them, and re-layouts  2.27 us (8%)
  between operations  0.79 us (3%)
    ppermute x13, starting transfers between devices, swap(): return lax.ppermute(x, axis, [(i, i ^ d) for i in range(size)])  14.6 us
    ppermute x13, waiting for transfers between devices, swap(): return lax.ppermute(x, axis, [(i, i ^ d) for i in range(size)])  6.33 us
    pallas_call x1, Pallas kernels, forward(): pl.pallas_call(forward_kernel, in_specs=[SMEM] * 3 + [VMEM] * 4 + [ANY],...  2.46 us
    unnamed x12, local copies, waits for them, and re-layouts  2.27 us
    pallas_call x1, Pallas kernels, backward(): pl.pallas_call(backward_kernel, in_specs=[SMEM] * 3 + [VMEM] * 3 + [ANY],...  1.79 us
    pallas_call x1, Pallas kernels, last_sum(): pl.pallas_call(last_sum_kernel, in_specs=[VMEM] * (4 + len(chips)), out_s...  0.74 us
    pallas_call x1, Pallas kernels, prep(): pl.pallas_call(prep_kernel, in_specs=[VMEM], out_specs=VMEM, out_shape=ja...  0.69 us
  transfers between devices with their start and end apart: 13, of which 2 were waited for; matrix products, arithmetic and copies ran while one was open for 0% of the time, Pallas kernels for 17%

profile of v12, /device:TPU:0, one launch (start us, length us, event | category | flops | bytes accessed | tf_op | source)
XLA Modules:
  0.0 29.9 jit_solution(15742066211129821052)
XLA Ops:
  0.0 4.0 %collective-permute-start = (bf16[1,8,2048]{2,1,0:T(8,128)(2,1)}, bf16[1,8,2048]{2,1,0:T(8,128)(2,1)S(1)}, u32[]{:S(2)}, u32[]{:S(2)}) collective-permute-start(bf16[1,8,2048]{2,1,0:T(8,128)(2,1)} %bitcast.5), channel_id=1, source_target_pairs={{0,2},{1,3},{2,0},{3,1},{4,6},{5,7},{6,4},{7,5},{8,10},{9,11},{10,... | collective-permute-start | bytes 98312 | tf_op jit(solution)/shard_map/ppermute | solution.py:381
  4.0 1.5 %collective-permute-start.2 = (bf16[8,2048]{1,0:T(8,128)(2,1)}, bf16[8,2048]{1,0:T(8,128)(2,1)S(1)}, u32[]{:S(2)}, u32[]{:S(2)}) collective-permute-start(bf16[8,2048]{1,0:T(8,128)(2,1)} %refs_0_.1), channel_id=1, source_target_pairs={{0,8},{4,12},{8,0},{12,4},{16,24},{20,28},{24,16},{28,20},{1,9},{5... | collective-permute-start | bytes 98312 | tf_op jit(solution)/shard_map/ppermute | solution.py:381
  5.5 1.5 %collective-permute-start.4 = (bf16[8,2048]{1,0:T(8,128)(2,1)}, bf16[8,2048]{1,0:T(8,128)(2,1)S(1)}, u32[]{:S(2)}, u32[]{:S(2)}) collective-permute-start(bf16[8,2048]{1,0:T(8,128)(2,1)} %refs_0_.1), channel_id=1, source_target_pairs={{0,24},{4,28},{8,16},{12,20},{16,8},{20,12},{24,0},{28,4},{1,25},{... | collective-permute-start | bytes 98312 | tf_op jit(solution)/shard_map/ppermute | solution.py:381
  7.0 0.5 %collective-permute-start.3 = (bf16[8,2048]{1,0:T(8,128)(2,1)}, bf16[8,2048]{1,0:T(8,128)(2,1)S(1)}, u32[]{:S(2)}, u32[]{:S(2)}) collective-permute-start(bf16[8,2048]{1,0:T(8,128)(2,1)} %refs_0_.1), channel_id=1, source_target_pairs={{0,16},{4,20},{8,24},{12,28},{16,0},{20,4},{24,8},{28,12},{1,17},{... | collective-permute-start | bytes 98312 | tf_op jit(solution)/shard_map/ppermute | solution.py:381
  7.5 0.8 %copy-done.3 = bf16[8,2048]{1,0:T(8,128)(2,1)S(1)} copy-done((bf16[8,2048]{1,0:T(8,128)(2,1)S(1)}, bf16[8,2048]{1,0:T(8,128)(2,1)}, u32[]{:S(2)}) %copy-start.3) | copy-done | bytes 32792
  8.3 1.6 %collective-permute-start.1 = (bf16[2,8,2048]{2,1,0:T(8,128)(2,1)S(1)}, bf16[2,8,2048]{2,1,0:T(8,128)(2,1)S(1)}, u32[]{:S(2)}, u32[]{:S(2)}) collective-permute-start(bf16[2,8,2048]{2,1,0:T(8,128)(2,1)S(1)} %stack_pieces.5.refs_0_), channel_id=1, source_target_pairs={{0,1},{1,0},{2,3},{3,2},{4,5},{5,4},{6,7},{7,6},{8,9},{9,8},{10,11... | collective-permute-start | bytes 196616 | tf_op jit(solution)/shard_map/ppermute | solution.py:381
  10.0 1.4 %copy-done = bf16[192,4096]{1,0:T(8,128)(2,1)S(1)} copy-done((bf16[192,4096]{1,0:T(8,128)(2,1)S(1)}, bf16[192,4096]{1,0:T(8,128)(2,1)}, u32[]{:S(2)}) %copy-start) | copy-done | bytes 1572888
  11.4 0.7 %prep_tiles.1.refs_4_.tiles_ref = bf16[192,32,128]{2,1,0:T(8,128)(2,1)S(1)} custom-call(bf16[24,32,8,128]{3,2,1,0:T(8,128)(2,1)S(1)} %bitcast.4), custom_call_target="tpu_custom_call" | custom-call | bytes 3145728 | tf_op jit(solution)/shard_map/prep_tiles/pallas_call | solution.py:77
  12.1 0.0 copy-start.1
  12.1 0.0 copy-start.4
  12.1 0.0 copy-start.5
  12.1 0.0 collective-permute-done.2.refs_1_
  12.1 0.0 collective-permute-done.4.refs_3_
  12.2 0.0 copy-start.2
  12.2 0.1 collective-permute-start.10
  12.9 0.0 collective-permute-done.1.refs_1_
  12.9 0.1 copy-done.1
  13.0 1.8 %transpose_product.1 = (f32[4,8,2048]{2,1,0:T(8,128)S(1)}, f32[2,8,2048]{2,1,0:T(8,128)S(1)}, f32[2,8,2048]{2,1,0:T(8,128)S(1)}) custom-call(s32[192]{0:T(256)S(1)} %copy-done.4, s32[192]{0:T(256)S(1)} %copy-done.5, s32[1,1]{1,0:T(1,128)S(6)} %copy.8.count_ref, bf16[128,512]{1,0:T(8,128)(2,1)S(1)} %copy-done.1, ...), custom_call_target="tpu_custom_call" | custom-call | flops 100663296 | bytes 3145728 | tf_op jit(solution)/shard_map/transpose_product/pallas_call | solution.py:162
  14.8 0.6 %collective-permute-start.6 = (f32[2,8,2048]{2,1,0:T(8,128)S(1)}, f32[2,8,2048]{2,1,0:T(8,128)S(1)}, u32[]{:S(2)}, u32[]{:S(2)}) collective-permute-start(f32[2,8,2048]{2,1,0:T(8,128)S(1)} %get-tuple-element.17), channel_id=1, source_target_pairs={{0,4},{4,0},{8,12},{12,8},{16,20},{20,16},{24,28},{28,24},{1,5},{5... | collective-permute-start | bytes 393224 | tf_op jit(solution)/shard_map/ppermute | solution.py:381
  15.4 0.1 collective-permute-start.5
  15.5 0.0 collective-permute-done.10.other_ref
  15.5 2.5 %forward_product.1 = (f32[2,8,2048]{2,1,0:T(8,128)S(1)}, s16[2,8,2176]{2,1,0:T(8,128)(2,1)S(1)}) custom-call(s32[192]{0:T(256)S(1)} %copy-done.4, s32[192]{0:T(256)S(1)} %copy-done.5, s32[1,1]{1,0:T(1,128)S(6)} %copy.8.count_ref, bf16[512,128]{1,0:T(8,128)(2,1)S(1)} %copy-done.2, bf16[192,32,128]{2,1,0:T(8,128)(2,1)S(1)} %prep_tiles.1.refs_4_.tiles_ref, ...), custom_call_target="tpu_custom_call" | custom-call | flops 100663296 | bytes 3145728 | tf_op jit(solution)/shard_map/forward_product/pallas_call | solution.py:270
  18.0 1.0 %collective-permute-start.11 = (s16[2,8,2176]{2,1,0:T(8,128)(2,1)S(1)}, s16[2,8,2176]{2,1,0:T(8,128)(2,1)S(1)}, u32[]{:S(2)}, u32[]{:S(2)}) collective-permute-start(s16[2,8,2176]{2,1,0:T(8,128)(2,1)S(1)} %get-tuple-element.22), channel_id=1, source_target_pairs={{0,2},{1,3},{2,0},{3,1},{4,6},{5,7},{6,4},{7,5},{8,10},{9,11},{10,... | collective-permute-start | bytes 208904 | tf_op jit(solution)/shard_map/ppermute | solution.py:381
  19.0 1.6 %collective-permute-start.8 = (f32[8,2048]{1,0:T(8,128)S(1)}, f32[8,2048]{1,0:T(8,128)S(1)}, u32[]{:S(2)}, u32[]{:S(2)}) collective-permute-start(f32[8,2048]{1,0:T(8,128)S(1)} %get-tuple-element.19), channel_id=1, source_target_pairs={{0,16},{4,20},{8,24},{12,28},{16,0},{20,4},{24,8},{28,12},{1,17},{... | collective-permute-start | bytes 196616 | tf_op jit(solution)/shard_map/ppermute | solution.py:381
  20.6 1.5 %collective-permute-start.9 = (f32[8,2048]{1,0:T(8,128)S(1)}, f32[8,2048]{1,0:T(8,128)S(1)}, u32[]{:S(2)}, u32[]{:S(2)}) collective-permute-start(f32[8,2048]{1,0:T(8,128)S(1)} %get-tuple-element.20), channel_id=1, source_target_pairs={{0,24},{4,28},{8,16},{12,20},{16,8},{20,12},{24,0},{28,4},{1,25},{... | collective-permute-start | bytes 196616 | tf_op jit(solution)/shard_map/ppermute | solution.py:381
  22.1 0.5 %collective-permute-start.7 = (f32[8,2048]{1,0:T(8,128)S(1)}, f32[8,2048]{1,0:T(8,128)S(1)}, u32[]{:S(2)}, u32[]{:S(2)}) collective-permute-start(f32[8,2048]{1,0:T(8,128)S(1)} %get-tuple-element.18.after_ref), channel_id=1, source_target_pairs={{0,8},{4,12},{8,0},{12,4},{16,24},{20,28},{24,16},{28,20},{1,9},{5... | collective-permute-start | bytes 196616 | tf_op jit(solution)/shard_map/ppermute | solution.py:381
  22.6 2.4 %collective-permute-done.11.got_ref = s16[2,8,2176]{2,1,0:T(8,128)(2,1)S(1)} collective-permute-done((s16[2,8,2176]{2,1,0:T(8,128)(2,1)S(1)}, s16[2,8,2176]{2,1,0:T(8,128)(2,1)S(1)}, u32[]{:S(2)}, u32[]{:S(2)}) %collective-permute-start.11) | collective-permute-done | bytes 69664 | tf_op jit(solution)/shard_map/ppermute | solution.py:381
  25.0 0.2 halving_sum.1
  25.2 0.1 collective-permute-start.12
  25.3 3.9 %collective-permute-done.12.refs_6_ = s16[1,8,2176]{2,1,0:T(8,128)(2,1)S(1)} collective-permute-done((s16[1,8,2176]{2,1,0:T(8,128)(2,1)S(1)}, s16[1,8,2176]{2,1,0:T(8,128)(2,1)S(1)}, u32[]{:S(2)}, u32[]{:S(2)}) %collective-permute-start.12) | collective-permute-done | bytes 34848 | tf_op jit(solution)/shard_map/ppermute | solution.py:381
  29.2 0.0 collective-permute-done.8.refs_1_
  29.2 0.7 %last_sum.1 = f32[8,2048]{1,0:T(8,128)} custom-call(f32[8,2048]{1,0:T(8,128)S(1)} %collective-permute-done.7.refs_0_, f32[8,2048]{1,0:T(8,128)S(1)} %collective-permute-done.8.refs_1_, f32[8,2048]{1,0:T(8,128)S(1)} %collective-permute-done.9.refs_2_, f32[4,8,2048]{2,1,0:T(8,128)S(1)} %get-tuple-element.15.keep_ref.refs_3_, ...), custom_call_target="tpu_custom_call" | custom-call | tf_op jit(solution)/shard_map/last_sum/pallas_call | solution.py:370
  (16 shorter events, 0.1 us)
Async XLA Ops:
  0.0 8.3 %collective-permute-start = (bf16[1,8,2048]{2,1,0:T(8,128)(2,1)}, bf16[1,8,2048]{2,1,0:T(8,128)(2,1)S(1)}, u32[]{:S(2)}, u32[]{:S(2)}) collective-permute-start(bf16[1,8,2048]{2,1,0:T(8,128)(2,1)} %bitcast.5), channel_id=1, source_target_pairs={{0,2},{1,3},{2,0},{3,1},{4,6},{5,7},{6,4},{7,5},{8,10},{9,11},{10,... | collective-permute-start | bytes 98312 | tf_op jit(solution)/shard_map/ppermute | solution.py:381
  4.0 8.1 %collective-permute-start.2 = (bf16[8,2048]{1,0:T(8,128)(2,1)}, bf16[8,2048]{1,0:T(8,128)(2,1)S(1)}, u32[]{:S(2)}, u32[]{:S(2)}) collective-permute-start(bf16[8,2048]{1,0:T(8,128)(2,1)} %refs_0_.1), channel_id=1, source_target_pairs={{0,8},{4,12},{8,0},{12,4},{16,24},{20,28},{24,16},{28,20},{1,9},{5... | collective-permute-start | bytes 98312 | tf_op jit(solution)/shard_map/ppermute | solution.py:381
  5.5 6.6 %collective-permute-start.4 = (bf16[8,2048]{1,0:T(8,128)(2,1)}, bf16[8,2048]{1,0:T(8,128)(2,1)S(1)}, u32[]{:S(2)}, u32[]{:S(2)}) collective-permute-start(bf16[8,2048]{1,0:T(8,128)(2,1)} %refs_0_.1), channel_id=1, source_target_pairs={{0,24},{4,28},{8,16},{12,20},{16,8},{20,12},{24,0},{28,4},{1,25},{... | collective-permute-start | bytes 98312 | tf_op jit(solution)/shard_map/ppermute | solution.py:381
  7.0 5.1 %collective-permute-start.3 = (bf16[8,2048]{1,0:T(8,128)(2,1)}, bf16[8,2048]{1,0:T(8,128)(2,1)S(1)}, u32[]{:S(2)}, u32[]{:S(2)}) collective-permute-start(bf16[8,2048]{1,0:T(8,128)(2,1)} %refs_0_.1), channel_id=1, source_target_pairs={{0,16},{4,20},{8,24},{12,28},{16,0},{20,4},{24,8},{28,12},{1,17},{... | collective-permute-start | bytes 98312 | tf_op jit(solution)/shard_map/ppermute | solution.py:381
  7.5 0.8 %copy-start.3 = (bf16[8,2048]{1,0:T(8,128)(2,1)S(1)}, bf16[8,2048]{1,0:T(8,128)(2,1)}, u32[]{:S(2)}) copy-start(bf16[8,2048]{1,0:T(8,128)(2,1)} %refs_0_.1) | copy-start | bytes 98308
  8.3 4.6 %collective-permute-start.1 = (bf16[2,8,2048]{2,1,0:T(8,128)(2,1)S(1)}, bf16[2,8,2048]{2,1,0:T(8,128)(2,1)S(1)}, u32[]{:S(2)}, u32[]{:S(2)}) collective-permute-start(bf16[2,8,2048]{2,1,0:T(8,128)(2,1)S(1)} %stack_pieces.5.refs_0_), channel_id=1, source_target_pairs={{0,1},{1,0},{2,3},{3,2},{4,5},{5,4},{6,7},{7,6},{8,9},{9,8},{10,11... | collective-permute-start | bytes 196616 | tf_op jit(solution)/shard_map/ppermute | solution.py:381
  10.0 1.4 %copy-start = (bf16[192,4096]{1,0:T(8,128)(2,1)S(1)}, bf16[192,4096]{1,0:T(8,128)(2,1)}, u32[]{:S(2)}) copy-start(bf16[192,4096]{1,0:T(8,128)(2,1)} %param.8) | copy-start | bytes 4718596
  12.1 0.9 %copy-start.1 = (bf16[128,512]{1,0:T(8,128)(2,1)S(1)}, bf16[128,512]{1,0:T(8,128)(2,1)}, u32[]{:S(2)}) copy-start(bf16[128,512]{1,0:T(8,128)(2,1)} %constant.4.clone.spread_ref) | copy-start | bytes 393220
  12.1 0.9 %copy-start.4 = (s32[192]{0:T(256)S(1)}, s32[192]{0:T(256)}, u32[]{:S(2)}) copy-start(s32[192]{0:T(256)} %rows_ref.3) | copy-start | bytes 2308
  12.1 0.9 %copy-start.5 = (s32[192]{0:T(256)S(1)}, s32[192]{0:T(256)}, u32[]{:S(2)}) copy-start(s32[192]{0:T(256)} %cols_ref.3) | copy-start | bytes 2308
  12.2 3.3 %copy-start.2 = (bf16[512,128]{1,0:T(8,128)(2,1)S(1)}, bf16[512,128]{1,0:T(8,128)(2,1)}, u32[]{:S(2)}) copy-start(bf16[512,128]{1,0:T(8,128)(2,1)} %constant.5.clone.fold_ref) | copy-start | bytes 393220
  12.2 3.3 %collective-permute-start.10 = (bf16[4,8,2048]{2,1,0:T(8,128)(2,1)S(1)}, bf16[4,8,2048]{2,1,0:T(8,128)(2,1)S(1)}, u32[]{:S(2)}, u32[]{:S(2)}) collective-permute-start(bf16[4,8,2048]{2,1,0:T(8,128)(2,1)S(1)} %stack_pieces.7.after_ref.same_ref), channel_id=1, source_target_pairs={{0,4},{4,0},{8,12},{12,8},{16,20},{20,16},{24,28},{28,24},{1,5},{5... | collective-permute-start | bytes 393224 | tf_op jit(solution)/shard_map/ppermute | solution.py:381
  14.8 4.2 %collective-permute-start.6 = (f32[2,8,2048]{2,1,0:T(8,128)S(1)}, f32[2,8,2048]{2,1,0:T(8,128)S(1)}, u32[]{:S(2)}, u32[]{:S(2)}) collective-permute-start(f32[2,8,2048]{2,1,0:T(8,128)S(1)} %get-tuple-element.17), channel_id=1, source_target_pairs={{0,4},{4,0},{8,12},{12,8},{16,20},{20,16},{24,28},{28,24},{1,5},{5... | collective-permute-start | bytes 393224 | tf_op jit(solution)/shard_map/ppermute | solution.py:381
  15.4 3.6 %collective-permute-start.5 = (f32[2,8,2048]{2,1,0:T(8,128)S(1)}, f32[2,8,2048]{2,1,0:T(8,128)S(1)}, u32[]{:S(2)}, u32[]{:S(2)}) collective-permute-start(f32[2,8,2048]{2,1,0:T(8,128)S(1)} %get-tuple-element.16.after_ref), channel_id=1, source_target_pairs={{0,4},{4,0},{8,12},{12,8},{16,20},{20,16},{24,28},{28,24},{1,5},{5... | collective-permute-start | bytes 393224 | tf_op jit(solution)/shard_map/ppermute | solution.py:381
  18.0 7.0 %collective-permute-start.11 = (s16[2,8,2176]{2,1,0:T(8,128)(2,1)S(1)}, s16[2,8,2176]{2,1,0:T(8,128)(2,1)S(1)}, u32[]{:S(2)}, u32[]{:S(2)}) collective-permute-start(s16[2,8,2176]{2,1,0:T(8,128)(2,1)S(1)} %get-tuple-element.22), channel_id=1, source_target_pairs={{0,2},{1,3},{2,0},{3,1},{4,6},{5,7},{6,4},{7,5},{8,10},{9,11},{10,... | collective-permute-start | bytes 208904 | tf_op jit(solution)/shard_map/ppermute | solution.py:381
  19.0 10.2 %collective-permute-start.8 = (f32[8,2048]{1,0:T(8,128)S(1)}, f32[8,2048]{1,0:T(8,128)S(1)}, u32[]{:S(2)}, u32[]{:S(2)}) collective-permute-start(f32[8,2048]{1,0:T(8,128)S(1)} %get-tuple-element.19), channel_id=1, source_target_pairs={{0,16},{4,20},{8,24},{12,28},{16,0},{20,4},{24,8},{28,12},{1,17},{... | collective-permute-start | bytes 196616 | tf_op jit(solution)/shard_map/ppermute | solution.py:381
  20.6 8.6 %collective-permute-start.9 = (f32[8,2048]{1,0:T(8,128)S(1)}, f32[8,2048]{1,0:T(8,128)S(1)}, u32[]{:S(2)}, u32[]{:S(2)}) collective-permute-start(f32[8,2048]{1,0:T(8,128)S(1)} %get-tuple-element.20), channel_id=1, source_target_pairs={{0,24},{4,28},{8,16},{12,20},{16,8},{20,12},{24,0},{28,4},{1,25},{... | collective-permute-start | bytes 196616 | tf_op jit(solution)/shard_map/ppermute | solution.py:381
  22.1 7.1 %collective-permute-start.7 = (f32[8,2048]{1,0:T(8,128)S(1)}, f32[8,2048]{1,0:T(8,128)S(1)}, u32[]{:S(2)}, u32[]{:S(2)}) collective-permute-start(f32[8,2048]{1,0:T(8,128)S(1)} %get-tuple-element.18.after_ref), channel_id=1, source_target_pairs={{0,8},{4,12},{8,0},{12,4},{16,24},{20,28},{24,16},{28,20},{1,9},{5... | collective-permute-start | bytes 196616 | tf_op jit(solution)/shard_map/ppermute | solution.py:381
  25.2 4.0 %collective-permute-start.12 = (s16[1,8,2176]{2,1,0:T(8,128)(2,1)S(1)}, s16[1,8,2176]{2,1,0:T(8,128)(2,1)S(1)}, u32[]{:S(2)}, u32[]{:S(2)}) collective-permute-start(s16[1,8,2176]{2,1,0:T(8,128)(2,1)S(1)} %get-tuple-element.24), channel_id=1, source_target_pairs={{0,1},{1,0},{2,3},{3,2},{4,5},{5,4},{6,7},{7,6},{8,9},{9,8},{10,11... | collective-permute-start | bytes 104456 | tf_op jit(solution)/shard_map/ppermute | solution.py:381

commit v13 on v10

--- a/solution.py
+++ b/solution.py
@@ -84,6 +84,14 @@
         cost_estimate=pl.CostEstimate(flops=0, bytes_accessed=4 * tiles.size, transcendentals=0),
         name="prep_tiles",
     )(view)
+
+
+def doubled(size):
+    order, d = [0], size // 2
+    while d > 0:
+        order += [x ^ d for x in order]
+        d //= 2
+    return order
 
 
 def build_table(pieces, spread, table):
@@ -104,7 +112,7 @@
 def backward_kernel(
     rows_ref, cols_ref, count_ref, spread_ref, tiles_ref, seg_ref, after_ref, keep_ref, *refs
 ):
-    pieces = [seg_ref.at[n] for n in range(seg_ref.shape[0])]
+    pieces = [seg_ref.at[at] for at in np.argsort(doubled(seg_ref.shape[0]))]
     *give_refs, table, acc_a, acc_b = refs
     per_give = give_refs[0].shape[0]
     n_out = 2 * keep_ref.shape[0]
@@ -377,10 +385,11 @@
     n_cols = lax.axis_size("bcol")
     own = stack(vectors)
     chips = [swap(vectors, "brow", n_rows, 2 * h) for h in range(1, n_rows // 2)]
-    segment, d = own, 1
-    while d < n_cols:
-        segment = stack(segment, swap(segment if d > 1 else vectors[None], "bcol", n_cols, d))
-        d *= 2
+    segment, d = own, n_cols // 2
+    while d > 0:
+        first = d == n_cols // 2
+        segment = stack(segment, swap(vectors[None] if first else segment, "bcol", n_cols, d))
+        d //= 2
     blocks = prep(tiles)
     same = stack(own, *chips, after=(blocks,))
     other = swap(same, "brow", n_rows, 1)

time: 28.6 us -> 29.2 us (1.021); the launches traced: 28.4 us -> 28.7 us
  waiting for transfers between devices: 3.27 us -> 3.97 us
  starting transfers between devices: 16.1 us -> 15.7 us
    ppermute x13, waiting for transfers between devices: 3.27 us -> 3.97 us  [swap(): return lax.ppermute(x, axis, [(i, i ^ d) for i in range(size)])]
    ppermute x13, starting transfers between devices: 16.1 us -> 15.7 us  [swap(): return lax.ppermute(x, axis, [(i, i ^ d) for i in range(size)])]
  transfers between devices with their start and end apart: 13 -> 13, of which waited for: 2 -> 1; matrix products, arithmetic and copies ran while one was open for 0% -> 0% of each run, Pallas kernels for 18% -> 18%
where the time goes in v13:
time: 29.2 us; the launch traced here: 28.7 us
  starting transfers between devices  15.7 us (54%)
  Pallas kernels  6 us (21%)
  waiting for transfers between devices  3.97 us (14%)
  local copies, waits for them, and re-layouts  2.27 us (8%)
  between operations  0.79 us (3%)
    ppermute x13, starting transfers between devices, swap(): return lax.ppermute(x, axis, [(i, i ^ d) for i in range(size)])  15.7 us
    ppermute x13, waiting for transfers between devices, swap(): return lax.ppermute(x, axis, [(i, i ^ d) for i in range(size)])  3.97 us
    pallas_call x1, Pallas kernels, forward(): pl.pallas_call(forward_kernel, in_specs=[SMEM] * 3 + [VMEM] * 4 + [ANY],...  2.47 us
    unnamed x12, local copies, waits for them, and re-layouts  2.27 us
    pallas_call x1, Pallas kernels, backward(): pl.pallas_call(backward_kernel, in_specs=[SMEM] * 3 + [VMEM] * 3 + [ANY],...  1.83 us
    pallas_call x1, Pallas kernels, last_sum(): pl.pallas_call(last_sum_kernel, in_specs=[VMEM] * (4 + len(chips)), out_s...  0.74 us
    pallas_call x1, Pallas kernels, prep(): pl.pallas_call(prep_kernel, in_specs=[VMEM], out_specs=VMEM, out_shape=ja...  0.69 us
  transfers between devices with their start and end apart: 13, of which 1 were waited for; matrix products, arithmetic and copies ran while one was open for 0% of the time, Pallas kernels for 18%

profile of v13, /device:TPU:0, one launch (start us, length us, event | category | flops | bytes accessed | tf_op | source)
XLA Modules:
  0.0 28.7 jit_solution(6839890978969430320)
XLA Ops:
  0.0 4.0 %collective-permute-start = (bf16[1,8,2048]{2,1,0:T(8,128)(2,1)}, bf16[1,8,2048]{2,1,0:T(8,128)(2,1)S(1)}, u32[]{:S(2)}, u32[]{:S(2)}) collective-permute-start(bf16[1,8,2048]{2,1,0:T(8,128)(2,1)} %bitcast.5), channel_id=1, source_target_pairs={{0,2},{1,3},{2,0},{3,1},{4,6},{5,7},{6,4},{7,5},{8,10},{9,11},{10,... | collective-permute-start | bytes 98312 | tf_op jit(solution)/shard_map/ppermute | solution.py:380
  4.0 1.5 %collective-permute-start.2 = (bf16[8,2048]{1,0:T(8,128)(2,1)}, bf16[8,2048]{1,0:T(8,128)(2,1)S(1)}, u32[]{:S(2)}, u32[]{:S(2)}) collective-permute-start(bf16[8,2048]{1,0:T(8,128)(2,1)} %refs_0_.1), channel_id=1, source_target_pairs={{0,8},{4,12},{8,0},{12,4},{16,24},{20,28},{24,16},{28,20},{1,9},{5... | collective-permute-start | bytes 98312 | tf_op jit(solution)/shard_map/ppermute | solution.py:380
  5.5 1.5 %collective-permute-start.4 = (bf16[8,2048]{1,0:T(8,128)(2,1)}, bf16[8,2048]{1,0:T(8,128)(2,1)S(1)}, u32[]{:S(2)}, u32[]{:S(2)}) collective-permute-start(bf16[8,2048]{1,0:T(8,128)(2,1)} %refs_0_.1), channel_id=1, source_target_pairs={{0,24},{4,28},{8,16},{12,20},{16,8},{20,12},{24,0},{28,4},{1,25},{... | collective-permute-start | bytes 98312 | tf_op jit(solution)/shard_map/ppermute | solution.py:380
  7.0 0.5 %collective-permute-start.3 = (bf16[8,2048]{1,0:T(8,128)(2,1)}, bf16[8,2048]{1,0:T(8,128)(2,1)S(1)}, u32[]{:S(2)}, u32[]{:S(2)}) collective-permute-start(bf16[8,2048]{1,0:T(8,128)(2,1)} %refs_0_.1), channel_id=1, source_target_pairs={{0,16},{4,20},{8,24},{12,28},{16,0},{20,4},{24,8},{28,12},{1,17},{... | collective-permute-start | bytes 98312 | tf_op jit(solution)/shard_map/ppermute | solution.py:380
  7.5 0.8 %copy-done.3 = bf16[8,2048]{1,0:T(8,128)(2,1)S(1)} copy-done((bf16[8,2048]{1,0:T(8,128)(2,1)S(1)}, bf16[8,2048]{1,0:T(8,128)(2,1)}, u32[]{:S(2)}) %copy-start.3) | copy-done | bytes 32792
  8.3 0.0 collective-permute-done.refs_1_
  8.3 1.6 %collective-permute-start.1 = (bf16[2,8,2048]{2,1,0:T(8,128)(2,1)S(1)}, bf16[2,8,2048]{2,1,0:T(8,128)(2,1)S(1)}, u32[]{:S(2)}, u32[]{:S(2)}) collective-permute-start(bf16[2,8,2048]{2,1,0:T(8,128)(2,1)S(1)} %stack_pieces.5.refs_0_), channel_id=1, source_target_pairs={{0,1},{1,0},{2,3},{3,2},{4,5},{5,4},{6,7},{7,6},{8,9},{9,8},{10,11... | collective-permute-start | bytes 196616 | tf_op jit(solution)/shard_map/ppermute | solution.py:380
  10.0 1.4 %copy-done = bf16[192,4096]{1,0:T(8,128)(2,1)S(1)} copy-done((bf16[192,4096]{1,0:T(8,128)(2,1)S(1)}, bf16[192,4096]{1,0:T(8,128)(2,1)}, u32[]{:S(2)}) %copy-start) | copy-done | bytes 1572888
  11.4 0.7 %prep_tiles.1.refs_4_.tiles_ref = bf16[192,32,128]{2,1,0:T(8,128)(2,1)S(1)} custom-call(bf16[24,32,8,128]{3,2,1,0:T(8,128)(2,1)S(1)} %bitcast.4), custom_call_target="tpu_custom_call" | custom-call | bytes 3145728 | tf_op jit(solution)/shard_map/prep_tiles/pallas_call | solution.py:77
  12.1 0.0 copy-start.1
  12.1 0.0 copy-start.4
  12.1 0.0 copy-start.5
  12.1 0.0 collective-permute-done.2.refs_1_
  12.1 0.0 collective-permute-done.3.refs_2_
  12.2 0.0 copy-start.2
  12.2 0.1 collective-permute-start.10
  12.9 0.0 collective-permute-done.1.refs_1_
  12.9 0.1 copy-done.1
  13.0 1.8 %transpose_product.1 = (f32[4,8,2048]{2,1,0:T(8,128)S(1)}, f32[2,8,2048]{2,1,0:T(8,128)S(1)}, f32[2,8,2048]{2,1,0:T(8,128)S(1)}) custom-call(s32[192]{0:T(256)S(1)} %copy-done.4, s32[192]{0:T(256)S(1)} %copy-done.5, s32[1,1]{1,0:T(1,128)S(6)} %copy.8.count_ref, bf16[128,512]{1,0:T(8,128)(2,1)S(1)} %copy-done.1, ...), custom_call_target="tpu_custom_call" | custom-call | flops 100663296 | bytes 3145728 | tf_op jit(solution)/shard_map/transpose_product/pallas_call | solution.py:162
  14.8 0.6 %collective-permute-start.6 = (f32[2,8,2048]{2,1,0:T(8,128)S(1)}, f32[2,8,2048]{2,1,0:T(8,128)S(1)}, u32[]{:S(2)}, u32[]{:S(2)}) collective-permute-start(f32[2,8,2048]{2,1,0:T(8,128)S(1)} %get-tuple-element.17), channel_id=1, source_target_pairs={{0,4},{4,0},{8,12},{12,8},{16,20},{20,16},{24,28},{28,24},{1,5},{5... | collective-permute-start | bytes 393224 | tf_op jit(solution)/shard_map/ppermute | solution.py:380
  15.4 0.1 collective-permute-start.5
  15.5 0.0 collective-permute-done.10.other_ref
  15.5 2.5 %forward_product.1 = (f32[2,8,2048]{2,1,0:T(8,128)S(1)}, s16[2,8,2176]{2,1,0:T(8,128)(2,1)S(1)}) custom-call(s32[192]{0:T(256)S(1)} %copy-done.4, s32[192]{0:T(256)S(1)} %copy-done.5, s32[1,1]{1,0:T(1,128)S(6)} %copy.8.count_ref, bf16[512,128]{1,0:T(8,128)(2,1)S(1)} %copy-done.2, bf16[192,32,128]{2,1,0:T(8,128)(2,1)S(1)} %prep_tiles.1.refs_4_.tiles_ref, ...), custom_call_target="tpu_custom_call" | custom-call | flops 100663296 | bytes 3145728 | tf_op jit(solution)/shard_map/forward_product/pallas_call | solution.py:270
  18.0 1.2 %collective-permute-start.11 = (s16[2,8,2176]{2,1,0:T(8,128)(2,1)S(1)}, s16[2,8,2176]{2,1,0:T(8,128)(2,1)S(1)}, u32[]{:S(2)}, u32[]{:S(2)}) collective-permute-start(s16[2,8,2176]{2,1,0:T(8,128)(2,1)S(1)} %get-tuple-element.22), channel_id=1, source_target_pairs={{0,1},{1,0},{2,3},{3,2},{4,5},{5,4},{6,7},{7,6},{8,9},{9,8},{10,11... | collective-permute-start | bytes 208904 | tf_op jit(solution)/shard_map/ppermute | solution.py:380
  19.2 0.0 collective-permute-done.6.refs_1_
  19.3 1.6 %collective-permute-start.8 = (f32[8,2048]{1,0:T(8,128)S(1)}, f32[8,2048]{1,0:T(8,128)S(1)}, u32[]{:S(2)}, u32[]{:S(2)}) collective-permute-start(f32[8,2048]{1,0:T(8,128)S(1)} %get-tuple-element.19), channel_id=1, source_target_pairs={{0,16},{4,20},{8,24},{12,28},{16,0},{20,4},{24,8},{28,12},{1,17},{... | collective-permute-start | bytes 196616 | tf_op jit(solution)/shard_map/ppermute | solution.py:380
  20.8 1.6 %collective-permute-start.9 = (f32[8,2048]{1,0:T(8,128)S(1)}, f32[8,2048]{1,0:T(8,128)S(1)}, u32[]{:S(2)}, u32[]{:S(2)}) collective-permute-start(f32[8,2048]{1,0:T(8,128)S(1)} %get-tuple-element.20), channel_id=1, source_target_pairs={{0,24},{4,28},{8,16},{12,20},{16,8},{20,12},{24,0},{28,4},{1,25},{... | collective-permute-start | bytes 196616 | tf_op jit(solution)/shard_map/ppermute | solution.py:380
  22.5 0.4 %collective-permute-start.7 = (f32[8,2048]{1,0:T(8,128)S(1)}, f32[8,2048]{1,0:T(8,128)S(1)}, u32[]{:S(2)}, u32[]{:S(2)}) collective-permute-start(f32[8,2048]{1,0:T(8,128)S(1)} %get-tuple-element.18.after_ref), channel_id=1, source_target_pairs={{0,8},{4,12},{8,0},{12,4},{16,24},{20,28},{24,16},{28,20},{1,9},{5... | collective-permute-start | bytes 196616 | tf_op jit(solution)/shard_map/ppermute | solution.py:380
  22.8 0.2 halving_sum.1
  23.0 1.0 %collective-permute-start.12 = (s16[1,8,2176]{2,1,0:T(8,128)(2,1)S(1)}, s16[1,8,2176]{2,1,0:T(8,128)(2,1)S(1)}, u32[]{:S(2)}, u32[]{:S(2)}) collective-permute-start(s16[1,8,2176]{2,1,0:T(8,128)(2,1)S(1)} %get-tuple-element.24), channel_id=1, source_target_pairs={{0,2},{1,3},{2,0},{3,1},{4,6},{5,7},{6,4},{7,5},{8,10},{9,11},{10,... | collective-permute-start | bytes 104456 | tf_op jit(solution)/shard_map/ppermute | solution.py:380
  24.0 3.9 %collective-permute-done.12.refs_6_ = s16[1,8,2176]{2,1,0:T(8,128)(2,1)S(1)} collective-permute-done((s16[1,8,2176]{2,1,0:T(8,128)(2,1)S(1)}, s16[1,8,2176]{2,1,0:T(8,128)(2,1)S(1)}, u32[]{:S(2)}, u32[]{:S(2)}) %collective-permute-start.12) | collective-permute-done | bytes 34848 | tf_op jit(solution)/shard_map/ppermute | solution.py:380
  28.0 0.7 %last_sum.1 = f32[8,2048]{1,0:T(8,128)} custom-call(f32[8,2048]{1,0:T(8,128)S(1)} %collective-permute-done.7.refs_0_, f32[8,2048]{1,0:T(8,128)S(1)} %collective-permute-done.8.refs_1_, f32[8,2048]{1,0:T(8,128)S(1)} %collective-permute-done.9.refs_2_, f32[4,8,2048]{2,1,0:T(8,128)S(1)} %get-tuple-element.15.keep_ref.refs_3_, ...), custom_call_target="tpu_custom_call" | custom-call | tf_op jit(solution)/shard_map/last_sum/pallas_call | solution.py:369
  (16 shorter events, 0.1 us)
Async XLA Ops:
  0.0 8.3 %collective-permute-start = (bf16[1,8,2048]{2,1,0:T(8,128)(2,1)}, bf16[1,8,2048]{2,1,0:T(8,128)(2,1)S(1)}, u32[]{:S(2)}, u32[]{:S(2)}) collective-permute-start(bf16[1,8,2048]{2,1,0:T(8,128)(2,1)} %bitcast.5), channel_id=1, source_target_pairs={{0,2},{1,3},{2,0},{3,1},{4,6},{5,7},{6,4},{7,5},{8,10},{9,11},{10,... | collective-permute-start | bytes 98312 | tf_op jit(solution)/shard_map/ppermute | solution.py:380
  4.0 8.1 %collective-permute-start.2 = (bf16[8,2048]{1,0:T(8,128)(2,1)}, bf16[8,2048]{1,0:T(8,128)(2,1)S(1)}, u32[]{:S(2)}, u32[]{:S(2)}) collective-permute-start(bf16[8,2048]{1,0:T(8,128)(2,1)} %refs_0_.1), channel_id=1, source_target_pairs={{0,8},{4,12},{8,0},{12,4},{16,24},{20,28},{24,16},{28,20},{1,9},{5... | collective-permute-start | bytes 98312 | tf_op jit(solution)/shard_map/ppermute | solution.py:380
  5.5 6.6 %collective-permute-start.4 = (bf16[8,2048]{1,0:T(8,128)(2,1)}, bf16[8,2048]{1,0:T(8,128)(2,1)S(1)}, u32[]{:S(2)}, u32[]{:S(2)}) collective-permute-start(bf16[8,2048]{1,0:T(8,128)(2,1)} %refs_0_.1), channel_id=1, source_target_pairs={{0,24},{4,28},{8,16},{12,20},{16,8},{20,12},{24,0},{28,4},{1,25},{... | collective-permute-start | bytes 98312 | tf_op jit(solution)/shard_map/ppermute | solution.py:380
  7.0 5.1 %collective-permute-start.3 = (bf16[8,2048]{1,0:T(8,128)(2,1)}, bf16[8,2048]{1,0:T(8,128)(2,1)S(1)}, u32[]{:S(2)}, u32[]{:S(2)}) collective-permute-start(bf16[8,2048]{1,0:T(8,128)(2,1)} %refs_0_.1), channel_id=1, source_target_pairs={{0,16},{4,20},{8,24},{12,28},{16,0},{20,4},{24,8},{28,12},{1,17},{... | collective-permute-start | bytes 98312 | tf_op jit(solution)/shard_map/ppermute | solution.py:380
  7.5 0.8 %copy-start.3 = (bf16[8,2048]{1,0:T(8,128)(2,1)S(1)}, bf16[8,2048]{1,0:T(8,128)(2,1)}, u32[]{:S(2)}) copy-start(bf16[8,2048]{1,0:T(8,128)(2,1)} %refs_0_.1) | copy-start | bytes 98308
  8.3 4.6 %collective-permute-start.1 = (bf16[2,8,2048]{2,1,0:T(8,128)(2,1)S(1)}, bf16[2,8,2048]{2,1,0:T(8,128)(2,1)S(1)}, u32[]{:S(2)}, u32[]{:S(2)}) collective-permute-start(bf16[2,8,2048]{2,1,0:T(8,128)(2,1)S(1)} %stack_pieces.5.refs_0_), channel_id=1, source_target_pairs={{0,1},{1,0},{2,3},{3,2},{4,5},{5,4},{6,7},{7,6},{8,9},{9,8},{10,11... | collective-permute-start | bytes 196616 | tf_op jit(solution)/shard_map/ppermute | solution.py:380
  10.0 1.4 %copy-start = (bf16[192,4096]{1,0:T(8,128)(2,1)S(1)}, bf16[192,4096]{1,0:T(8,128)(2,1)}, u32[]{:S(2)}) copy-start(bf16[192,4096]{1,0:T(8,128)(2,1)} %param.8) | copy-start | bytes 4718596
  12.1 0.9 %copy-start.1 = (bf16[128,512]{1,0:T(8,128)(2,1)S(1)}, bf16[128,512]{1,0:T(8,128)(2,1)}, u32[]{:S(2)}) copy-start(bf16[128,512]{1,0:T(8,128)(2,1)} %constant.4.clone.spread_ref) | copy-start | bytes 393220
  12.1 0.9 %copy-start.4 = (s32[192]{0:T(256)S(1)}, s32[192]{0:T(256)}, u32[]{:S(2)}) copy-start(s32[192]{0:T(256)} %rows_ref.3) | copy-start | bytes 2308
  12.1 0.9 %copy-start.5 = (s32[192]{0:T(256)S(1)}, s32[192]{0:T(256)}, u32[]{:S(2)}) copy-start(s32[192]{0:T(256)} %cols_ref.3) | copy-start | bytes 2308
  12.2 3.3 %copy-start.2 = (bf16[512,128]{1,0:T(8,128)(2,1)S(1)}, bf16[512,128]{1,0:T(8,128)(2,1)}, u32[]{:S(2)}) copy-start(bf16[512,128]{1,0:T(8,128)(2,1)} %constant.5.clone.fold_ref) | copy-start | bytes 393220
  12.2 3.3 %collective-permute-start.10 = (bf16[4,8,2048]{2,1,0:T(8,128)(2,1)S(1)}, bf16[4,8,2048]{2,1,0:T(8,128)(2,1)S(1)}, u32[]{:S(2)}, u32[]{:S(2)}) collective-permute-start(bf16[4,8,2048]{2,1,0:T(8,128)(2,1)S(1)} %stack_pieces.7.after_ref.same_ref), channel_id=1, source_target_pairs={{0,4},{4,0},{8,12},{12,8},{16,20},{20,16},{24,28},{28,24},{1,5},{5... | collective-permute-start | bytes 393224 | tf_op jit(solution)/shard_map/ppermute | solution.py:380
  14.8 4.4 %collective-permute-start.6 = (f32[2,8,2048]{2,1,0:T(8,128)S(1)}, f32[2,8,2048]{2,1,0:T(8,128)S(1)}, u32[]{:S(2)}, u32[]{:S(2)}) collective-permute-start(f32[2,8,2048]{2,1,0:T(8,128)S(1)} %get-tuple-element.17), channel_id=1, source_target_pairs={{0,4},{4,0},{8,12},{12,8},{16,20},{20,16},{24,28},{28,24},{1,5},{5... | collective-permute-start | bytes 393224 | tf_op jit(solution)/shard_map/ppermute | solution.py:380
  15.4 3.8 %collective-permute-start.5 = (f32[2,8,2048]{2,1,0:T(8,128)S(1)}, f32[2,8,2048]{2,1,0:T(8,128)S(1)}, u32[]{:S(2)}, u32[]{:S(2)}) collective-permute-start(f32[2,8,2048]{2,1,0:T(8,128)S(1)} %get-tuple-element.16.after_ref), channel_id=1, source_target_pairs={{0,4},{4,0},{8,12},{12,8},{16,20},{20,16},{24,28},{28,24},{1,5},{5... | collective-permute-start | bytes 393224 | tf_op jit(solution)/shard_map/ppermute | solution.py:380
  18.0 4.8 %collective-permute-start.11 = (s16[2,8,2176]{2,1,0:T(8,128)(2,1)S(1)}, s16[2,8,2176]{2,1,0:T(8,128)(2,1)S(1)}, u32[]{:S(2)}, u32[]{:S(2)}) collective-permute-start(s16[2,8,2176]{2,1,0:T(8,128)(2,1)S(1)} %get-tuple-element.22), channel_id=1, source_target_pairs={{0,1},{1,0},{2,3},{3,2},{4,5},{5,4},{6,7},{7,6},{8,9},{9,8},{10,11... | collective-permute-start | bytes 208904 | tf_op jit(solution)/shard_map/ppermute | solution.py:380
  19.3 8.7 %collective-permute-start.8 = (f32[8,2048]{1,0:T(8,128)S(1)}, f32[8,2048]{1,0:T(8,128)S(1)}, u32[]{:S(2)}, u32[]{:S(2)}) collective-permute-start(f32[8,2048]{1,0:T(8,128)S(1)} %get-tuple-element.19), channel_id=1, source_target_pairs={{0,16},{4,20},{8,24},{12,28},{16,0},{20,4},{24,8},{28,12},{1,17},{... | collective-permute-start | bytes 196616 | tf_op jit(solution)/shard_map/ppermute | solution.py:380
  20.8 7.1 %collective-permute-start.9 = (f32[8,2048]{1,0:T(8,128)S(1)}, f32[8,2048]{1,0:T(8,128)S(1)}, u32[]{:S(2)}, u32[]{:S(2)}) collective-permute-start(f32[8,2048]{1,0:T(8,128)S(1)} %get-tuple-element.20), channel_id=1, source_target_pairs={{0,24},{4,28},{8,16},{12,20},{16,8},{20,12},{24,0},{28,4},{1,25},{... | collective-permute-start | bytes 196616 | tf_op jit(solution)/shard_map/ppermute | solution.py:380
  22.5 5.5 %collective-permute-start.7 = (f32[8,2048]{1,0:T(8,128)S(1)}, f32[8,2048]{1,0:T(8,128)S(1)}, u32[]{:S(2)}, u32[]{:S(2)}) collective-permute-start(f32[8,2048]{1,0:T(8,128)S(1)} %get-tuple-element.18.after_ref), channel_id=1, source_target_pairs={{0,8},{4,12},{8,0},{12,4},{16,24},{20,28},{24,16},{28,20},{1,9},{5... | collective-permute-start | bytes 196616 | tf_op jit(solution)/shard_map/ppermute | solution.py:380
  23.0 4.9 %collective-permute-start.12 = (s16[1,8,2176]{2,1,0:T(8,128)(2,1)S(1)}, s16[1,8,2176]{2,1,0:T(8,128)(2,1)S(1)}, u32[]{:S(2)}, u32[]{:S(2)}) collective-permute-start(s16[1,8,2176]{2,1,0:T(8,128)(2,1)S(1)} %get-tuple-element.24), channel_id=1, source_target_pairs={{0,2},{1,3},{2,0},{3,1},{4,6},{5,7},{6,4},{7,5},{8,10},{9,11},{10,... | collective-permute-start | bytes 104456 | tf_op jit(solution)/shard_map/ppermute | solution.py:380

commit v14 on v13

--- a/solution.py
+++ b/solution.py
@@ -63,27 +63,27 @@
     ]
 
 
-def prep_kernel(tiles_ref, out_ref, wide):
+def prep_kernel(tiles_ref, after_ref, out_ref, wide):
     for b in range(tiles_ref.shape[0]):
         wide[b] = tiles_ref[b].astype(F32).reshape(HALF * 8, LANES)
         for s in range(8):
             out_ref[8 * b + s] = wide[b, pl.ds(s, HALF, stride=8), :].astype(BF16)
 
 
-def prep(tiles):
+def prep(tiles, after):
     slots = tiles.shape[0]
     blocks = slots // 8
     view = tiles.reshape(blocks, 8, HALF, LANES).swapaxes(1, 2)
     return pl.pallas_call(
         prep_kernel,
-        in_specs=[VMEM],
+        in_specs=[VMEM, ANY],
         out_specs=VMEM,
         out_shape=jax.ShapeDtypeStruct((slots, HALF, LANES), BF16),
         scratch_shapes=[pltpu.VMEM((blocks, HALF * 8, LANES), F32)],
         compiler_params=PARAMS,
         cost_estimate=pl.CostEstimate(flops=0, bytes_accessed=4 * tiles.size, transcendentals=0),
         name="prep_tiles",
-    )(view)
+    )(view, after)
 
 
 def doubled(size):
@@ -308,24 +308,31 @@
     )(*parts, *after)
 
 
-def pair_sum_kernel(keep_ref, *refs):
-    n_chips = keep_ref.shape[0]
-    gots, outs = refs[: 1 - n_chips], refs[1 - n_chips :]
+def pair_sum_kernel(chips, keep_ref, *refs):
+    outs = refs[-len(chips) :]
+    gots = refs[: -1 - len(chips)]
     got = [ref.at[h] for ref in gots for h in range(ref.shape[0])]
-    for h, out in enumerate(outs):
-        out[...] = keep_ref[h + 1] + got[h + 1][...]
-
-
-def pair_sum(keep, gots):
-    parts, width, piece = keep.shape
-    return pl.pallas_call(
-        pair_sum_kernel,
-        in_specs=[VMEM] * (1 + len(gots)),
-        out_specs=[VMEM] * (parts - 1),
-        out_shape=[jax.ShapeDtypeStruct((width, piece), F32)] * (parts - 1),
+    for h, out in zip(chips, outs):
+        if out.dtype == F32:
+            out[...] = keep_ref[h] + got[h][...]
+        else:
+            total = keep_ref[h] + got[h][...]
+            encode([total[:, n : n + LANES] for n in range(0, total.shape[1], LANES)], out)
+
+
+def pair_sum(chips, keep, gots, after, coded=False):
+    _, width, piece = keep.shape
+    one = jax.ShapeDtypeStruct((width, piece), F32)
+    if coded:
+        one = jax.ShapeDtypeStruct((width, piece + LANES), jnp.int16)
+    return pl.pallas_call(
+        functools.partial(pair_sum_kernel, chips),
+        in_specs=[VMEM] * (1 + len(gots)) + [ANY],
+        out_specs=[VMEM] * len(chips),
+        out_shape=[one] * len(chips),
         compiler_params=PARAMS,
         name="core_pair_sum",
-    )(keep, *gots)
+    )(keep, *gots, after)
 
 
 def split_sum_kernel(keep_ref, got_ref, after_ref, next_keep, next_give):
@@ -355,8 +362,8 @@
     )(keep, got, after)
 
 
-def last_sum_kernel(*refs):
-    chips, (brow_keep, brow_got, keep_ref, got_ref, out_ref) = refs[:-5], refs[-5:]
+def last_sum_kernel(keep_ref, got_ref, brow_keep, brow_got, *refs):
+    chips, out_ref = refs[:-1], refs[-1]
     for n, got in enumerate(decode(got_ref.at[0])):
         at = pl.ds(n * LANES, LANES)
         total = brow_keep[0, :, at] + brow_got[0, :, at]
@@ -373,7 +380,24 @@
         out_shape=jax.ShapeDtypeStruct(keep.shape[1:], F32),
         compiler_params=PARAMS,
         name="last_sum",
-    )(*chips, brow_keep, brow_got, keep, got)
+    )(keep, got, brow_keep, brow_got, *chips)
+
+
+def add_kernel(x_ref, y_ref, out_ref):
+    for n, got in enumerate(decode(y_ref)):
+        at = pl.ds(n * LANES, LANES)
+        out_ref[:, at] = x_ref[:, at] + got
+
+
+def add(x, y):
+    return pl.pallas_call(
+        add_kernel,
+        in_specs=[VMEM] * 2,
+        out_specs=VMEM,
+        out_shape=jax.ShapeDtypeStruct(x.shape, x.dtype),
+        compiler_params=PARAMS,
+        name="add_last",
+    )(x, y)
 
 
 def swap(x, axis, size, d):
@@ -385,26 +409,28 @@
     n_cols = lax.axis_size("bcol")
     own = stack(vectors)
     chips = [swap(vectors, "brow", n_rows, 2 * h) for h in range(1, n_rows // 2)]
-    segment, d = own, n_cols // 2
+    far = swap(vectors[None], "bcol", n_cols, n_cols // 2)
+    segment, d = stack(own, far), n_cols // 4
+    blocks = prep(tiles, own)
     while d > 0:
-        first = d == n_cols // 2
-        segment = stack(segment, swap(vectors[None] if first else segment, "bcol", n_cols, d))
+        segment = stack(segment, swap(segment, "bcol", n_cols, d))
         d //= 2
-    blocks = prep(tiles)
     same = stack(own, *chips, after=(blocks,))
     other = swap(same, "brow", n_rows, 1)
 
     col_keep, *col_give = backward(segment, blocks, tile_rows, tile_cols, counts, n_rows, same)
     row_keep, give = forward(same, other, blocks, tile_rows, tile_cols, counts, n_cols, col_give[0])
     col_got = [swap(x, "brow", n_rows, 1) for x in col_give]
-    sums = pair_sum(col_keep, col_got)
-    from_chips = [swap(x, "brow", n_rows, 2 * (h + 1)) for h, x in enumerate(sums)]
+    sums = pair_sum(tuple(range(2, n_rows // 2)), col_keep, col_got, give)
+    from_chips = [swap(x, "brow", n_rows, 2 * (h + 2)) for h, x in enumerate(sums)]
     row_got, d = swap(give, "bcol", n_cols, 1), 2
     while d < n_cols:
         row_keep, give = split_sum(row_keep, row_got, sums[0])
         row_got = swap(give, "bcol", n_cols, d)
         d *= 2
-    return last_sum(row_keep, row_got, col_keep, col_got[0], from_chips)
+    (last,) = pair_sum((1,), col_keep, col_got, give, coded=True)
+    total = last_sum(row_keep, row_got, col_keep, col_got[0], from_chips)
+    return add(total, swap(last, "brow", n_rows, 2))
 
 
 def solution(mesh):

time: 29.2 us -> 28.9 us (0.990)
  waiting for transfers between devices: 3.97 us -> 2.31 us
  starting transfers between devices: 15.7 us -> 17 us
    ppermute x13, waiting for transfers between devices: 3.97 us -> 2.31 us  [swap(): return lax.ppermute(x, axis, [(i, i ^ d) for i in range(size)])]
    ppermute x13, starting transfers between devices: 15.7 us -> 17 us  [swap(): return lax.ppermute(x, axis, [(i, i ^ d) for i in range(size)])]
    pallas_call x2 -> x4, Pallas kernels: 0.72 us -> 1.56 us  [the longest x1 0.73 us: add(): pl.pallas_call(add_kernel, in_specs=[VMEM] * 2, out_specs=VMEM, out_shape...]
    pallas_call x1, Pallas kernels: 0.74 us -> 0.11 us  [last_sum(): pl.pallas_call(last_sum_kernel, in_specs=[VMEM] * (4 + len(chips)), out_s...]
  transfers between devices with their start and end apart: 13 -> 13, of which waited for: 1 -> 2; matrix products, arithmetic and copies ran while one was open for 0% -> 0% of each run, Pallas kernels for 18% -> 19%
where the time goes in v14:
time: 28.9 us; the launch traced here: 28.6 us
  starting transfers between devices  17 us (59%)
  Pallas kernels  6.18 us (21%)
  waiting for transfers between devices  2.31 us (8%)
  local copies, waits for them, and re-layouts  2.27 us (8%)
  between operations  0.81 us (3%)
    ppermute x13, starting transfers between devices, swap(): return lax.ppermute(x, axis, [(i, i ^ d) for i in range(size)])  17 us
    pallas_call x1, Pallas kernels, forward(): pl.pallas_call(forward_kernel, in_specs=[SMEM] * 3 + [VMEM] * 4 + [ANY],...  2.47 us
    ppermute x13, waiting for transfers between devices, swap(): return lax.ppermute(x, axis, [(i, i ^ d) for i in range(size)])  2.31 us
    unnamed x12, local copies, waits for them, and re-layouts  2.27 us
    pallas_call x1, Pallas kernels, backward(): pl.pallas_call(backward_kernel, in_specs=[SMEM] * 3 + [VMEM] * 3 + [ANY],...  1.8 us
    pallas_call x1, Pallas kernels, add(): pl.pallas_call(add_kernel, in_specs=[VMEM] * 2, out_specs=VMEM, out_shape...  0.73 us
    pallas_call x1, Pallas kernels, prep(): pl.pallas_call(prep_kernel, in_specs=[VMEM, ANY], out_specs=VMEM, out_sha...  0.69 us
  transfers between devices with their start and end apart: 13, of which 2 were waited for; matrix products, arithmetic and copies ran while one was open for 0% of the time, Pallas kernels for 19%

profile of v14, /device:TPU:0, one launch (start us, length us, event | category | flops | bytes accessed | tf_op | source)
XLA Modules:
  0.0 28.6 jit_solution(6710658598624838329)
XLA Ops:
  0.0 4.0 %collective-permute-start.4 = (bf16[1,8,2048]{2,1,0:T(8,128)(2,1)}, bf16[1,8,2048]{2,1,0:T(8,128)(2,1)S(1)}, u32[]{:S(2)}, u32[]{:S(2)}) collective-permute-start(bf16[1,8,2048]{2,1,0:T(8,128)(2,1)} %bitcast.5), channel_id=1, source_target_pairs={{0,2},{1,3},{2,0},{3,1},{4,6},{5,7},{6,4},{7,5},{8,10},{9,11},{10,... | collective-permute-start | bytes 98312 | tf_op jit(solution)/shard_map/ppermute | solution.py:404
  4.0 1.5 %collective-permute-start.1 = (bf16[8,2048]{1,0:T(8,128)(2,1)}, bf16[8,2048]{1,0:T(8,128)(2,1)S(1)}, u32[]{:S(2)}, u32[]{:S(2)}) collective-permute-start(bf16[8,2048]{1,0:T(8,128)(2,1)} %refs_0_.1), channel_id=1, source_target_pairs={{0,16},{4,20},{8,24},{12,28},{16,0},{20,4},{24,8},{28,12},{1,17},{... | collective-permute-start | bytes 98312 | tf_op jit(solution)/shard_map/ppermute | solution.py:404
  5.6 1.5 %collective-permute-start = (bf16[8,2048]{1,0:T(8,128)(2,1)}, bf16[8,2048]{1,0:T(8,128)(2,1)S(1)}, u32[]{:S(2)}, u32[]{:S(2)}) collective-permute-start(bf16[8,2048]{1,0:T(8,128)(2,1)} %refs_0_.1), channel_id=1, source_target_pairs={{0,8},{4,12},{8,0},{12,4},{16,24},{20,28},{24,16},{28,20},{1,9},{5... | collective-permute-start | bytes 98312 | tf_op jit(solution)/shard_map/ppermute | solution.py:404
  7.0 0.5 %collective-permute-start.2 = (bf16[8,2048]{1,0:T(8,128)(2,1)}, bf16[8,2048]{1,0:T(8,128)(2,1)S(1)}, u32[]{:S(2)}, u32[]{:S(2)}) collective-permute-start(bf16[8,2048]{1,0:T(8,128)(2,1)} %refs_0_.1), channel_id=1, source_target_pairs={{0,24},{4,28},{8,16},{12,20},{16,8},{20,12},{24,0},{28,4},{1,25},{... | collective-permute-start | bytes 98312 | tf_op jit(solution)/shard_map/ppermute | solution.py:404
  7.5 0.8 %copy-done.3 = bf16[8,2048]{1,0:T(8,128)(2,1)S(1)} copy-done((bf16[8,2048]{1,0:T(8,128)(2,1)S(1)}, bf16[8,2048]{1,0:T(8,128)(2,1)}, u32[]{:S(2)}) %copy-start.3) | copy-done | bytes 32792
  8.3 0.0 collective-permute-done.4.refs_1_
  8.3 1.6 %collective-permute-start.5 = (bf16[2,8,2048]{2,1,0:T(8,128)(2,1)S(1)}, bf16[2,8,2048]{2,1,0:T(8,128)(2,1)S(1)}, u32[]{:S(2)}, u32[]{:S(2)}) collective-permute-start(bf16[2,8,2048]{2,1,0:T(8,128)(2,1)S(1)} %stack_pieces.6.refs_0_), channel_id=1, source_target_pairs={{0,1},{1,0},{2,3},{3,2},{4,5},{5,4},{6,7},{7,6},{8,9},{9,8},{10,11... | collective-permute-start | bytes 196616 | tf_op jit(solution)/shard_map/ppermute | solution.py:404
  10.0 1.4 %copy-done = bf16[192,4096]{1,0:T(8,128)(2,1)S(1)} copy-done((bf16[192,4096]{1,0:T(8,128)(2,1)S(1)}, bf16[192,4096]{1,0:T(8,128)(2,1)}, u32[]{:S(2)}) %copy-start) | copy-done | bytes 1572888
  11.4 0.7 %prep_tiles.1.refs_4_.tiles_ref = bf16[192,32,128]{2,1,0:T(8,128)(2,1)S(1)} custom-call(bf16[24,32,8,128]{3,2,1,0:T(8,128)(2,1)S(1)} %bitcast.4, bf16[1,8,2048]{2,1,0:T(8,128)(2,1)S(1)} %stack_pieces.4.after_ref.refs_0_), custom_call_target="tpu_custom_call" | custom-call | bytes 3145728 | tf_op jit(solution)/shard_map/prep_tiles/pallas_call | solution.py:77
  12.1 0.0 copy-start.1
  12.1 0.0 copy-start.4
  12.1 0.0 copy-start.5
  12.1 0.0 collective-permute-done.refs_1_
  12.1 0.0 collective-permute-done.2.refs_3_
  12.2 0.0 copy-start.2
  12.2 0.1 collective-permute-start.3
  12.9 0.1 copy-done.1
  13.0 1.8 %transpose_product.1 = (f32[4,8,2048]{2,1,0:T(8,128)S(1)}, f32[2,8,2048]{2,1,0:T(8,128)S(1)}, f32[2,8,2048]{2,1,0:T(8,128)S(1)}) custom-call(s32[192]{0:T(256)S(1)} %copy-done.4, s32[192]{0:T(256)S(1)} %copy-done.5, s32[1,1]{1,0:T(1,128)S(6)} %copy.8.count_ref, bf16[128,512]{1,0:T(8,128)(2,1)S(1)} %copy-done.1, ...), custom_call_target="tpu_custom_call" | custom-call | flops 100663296 | bytes 3145728 | tf_op jit(solution)/shard_map/transpose_product/pallas_call | solution.py:162
  14.8 0.6 %collective-permute-start.8 = (f32[2,8,2048]{2,1,0:T(8,128)S(1)}, f32[2,8,2048]{2,1,0:T(8,128)S(1)}, u32[]{:S(2)}, u32[]{:S(2)}) collective-permute-start(f32[2,8,2048]{2,1,0:T(8,128)S(1)} %get-tuple-element.18), channel_id=1, source_target_pairs={{0,4},{4,0},{8,12},{12,8},{16,20},{20,16},{24,28},{28,24},{1,5},{5... | collective-permute-start | bytes 393224 | tf_op jit(solution)/shard_map/ppermute | solution.py:404
  15.4 0.1 collective-permute-start.7
  15.5 2.5 %forward_product.1 = (f32[2,8,2048]{2,1,0:T(8,128)S(1)}, s16[2,8,2176]{2,1,0:T(8,128)(2,1)S(1)}) custom-call(s32[192]{0:T(256)S(1)} %copy-done.4, s32[192]{0:T(256)S(1)} %copy-done.5, s32[1,1]{1,0:T(1,128)S(6)} %copy.8.count_ref, bf16[512,128]{1,0:T(8,128)(2,1)S(1)} %copy-done.2, bf16[192,32,128]{2,1,0:T(8,128)(2,1)S(1)} %prep_tiles.1.refs_4_.tiles_ref, ...), custom_call_target="tpu_custom_call" | custom-call | flops 100663296 | bytes 3145728 | tf_op jit(solution)/shard_map/forward_product/pallas_call | solution.py:270
  17.9 1.7 %collective-permute-start.6 = (s16[2,8,2176]{2,1,0:T(8,128)(2,1)S(1)}, s16[2,8,2176]{2,1,0:T(8,128)(2,1)S(1)}, u32[]{:S(2)}, u32[]{:S(2)}) collective-permute-start(s16[2,8,2176]{2,1,0:T(8,128)(2,1)S(1)} %get-tuple-element.16.refs_2_), channel_id=1, source_target_pairs={{0,1},{1,0},{2,3},{3,2},{4,5},{5,4},{6,7},{7,6},{8,9},{9,8},{10,11... | collective-permute-start | bytes 208904 | tf_op jit(solution)/shard_map/ppermute | solution.py:404
  19.6 2.3 %collective-permute-start.11 = (f32[8,2048]{1,0:T(8,128)S(1)}, f32[8,2048]{1,0:T(8,128)S(1)}, u32[]{:S(2)}, u32[]{:S(2)}) collective-permute-start(f32[8,2048]{1,0:T(8,128)S(1)} %get-tuple-element.22), channel_id=1, source_target_pairs={{0,24},{4,28},{8,16},{12,20},{16,8},{20,12},{24,0},{28,4},{1,25},{... | collective-permute-start | bytes 196616 | tf_op jit(solution)/shard_map/ppermute | solution.py:404
  21.9 0.5 %collective-permute-start.10 = (f32[8,2048]{1,0:T(8,128)S(1)}, f32[8,2048]{1,0:T(8,128)S(1)}, u32[]{:S(2)}, u32[]{:S(2)}) collective-permute-start(f32[8,2048]{1,0:T(8,128)S(1)} %get-tuple-element.19.after_ref), channel_id=1, source_target_pairs={{0,16},{4,20},{8,24},{12,28},{16,0},{20,4},{24,8},{28,12},{1,17},{... | collective-permute-start | bytes 196616 | tf_op jit(solution)/shard_map/ppermute | solution.py:404
  22.4 0.1 collective-permute-done.6.got_ref
  22.5 0.2 halving_sum.1
  22.7 0.9 %collective-permute-start.9 = (s16[1,8,2176]{2,1,0:T(8,128)(2,1)S(1)}, s16[1,8,2176]{2,1,0:T(8,128)(2,1)S(1)}, u32[]{:S(2)}, u32[]{:S(2)}) collective-permute-start(s16[1,8,2176]{2,1,0:T(8,128)(2,1)S(1)} %get-tuple-element.21.refs_2_), channel_id=1, source_target_pairs={{0,2},{1,3},{2,0},{3,1},{4,6},{5,7},{6,4},{7,5},{8,10},{9,11},{10,... | collective-permute-start | bytes 104456 | tf_op jit(solution)/shard_map/ppermute | solution.py:404
  23.7 0.1 core_pair_sum.3
  23.8 1.7 %collective-permute-start.12 = (s16[8,2176]{1,0:T(8,128)(2,1)S(1)}, s16[8,2176]{1,0:T(8,128)(2,1)S(1)}, u32[]{:S(2)}, u32[]{:S(2)}) collective-permute-start(s16[8,2176]{1,0:T(8,128)(2,1)S(1)} %core_pair_sum.3), channel_id=1, source_target_pairs={{0,8},{4,12},{8,0},{12,4},{16,24},{20,28},{24,16},{28,20},{1,9},{5... | collective-permute-start | bytes 104456 | tf_op jit(solution)/shard_map/ppermute | solution.py:404
  25.5 2.2 %collective-permute-done.9.got_ref = s16[1,8,2176]{2,1,0:T(8,128)(2,1)S(1)} collective-permute-done((s16[1,8,2176]{2,1,0:T(8,128)(2,1)S(1)}, s16[1,8,2176]{2,1,0:T(8,128)(2,1)S(1)}, u32[]{:S(2)}, u32[]{:S(2)}) %collective-permute-start.9) | collective-permute-done | bytes 34848 | tf_op jit(solution)/shard_map/ppermute | solution.py:404
  27.7 0.1 last_sum.1.x_ref
  27.8 0.7 %add_last.1 = f32[8,2048]{1,0:T(8,128)} custom-call(f32[8,2048]{1,0:T(8,128)S(1)} %last_sum.1.x_ref, s16[8,2176]{1,0:T(8,128)(2,1)S(1)} %collective-permute-done.12.y_ref), custom_call_target="tpu_custom_call" | custom-call | tf_op jit(solution)/shard_map/add_last/pallas_call | solution.py:393
  (18 shorter events, 0.1 us)
Async XLA Ops:
  0.0 8.3 %collective-permute-start.4 = (bf16[1,8,2048]{2,1,0:T(8,128)(2,1)}, bf16[1,8,2048]{2,1,0:T(8,128)(2,1)S(1)}, u32[]{:S(2)}, u32[]{:S(2)}) collective-permute-start(bf16[1,8,2048]{2,1,0:T(8,128)(2,1)} %bitcast.5), channel_id=1, source_target_pairs={{0,2},{1,3},{2,0},{3,1},{4,6},{5,7},{6,4},{7,5},{8,10},{9,11},{10,... | collective-permute-start | bytes 98312 | tf_op jit(solution)/shard_map/ppermute | solution.py:404
  4.0 8.1 %collective-permute-start.1 = (bf16[8,2048]{1,0:T(8,128)(2,1)}, bf16[8,2048]{1,0:T(8,128)(2,1)S(1)}, u32[]{:S(2)}, u32[]{:S(2)}) collective-permute-start(bf16[8,2048]{1,0:T(8,128)(2,1)} %refs_0_.1), channel_id=1, source_target_pairs={{0,16},{4,20},{8,24},{12,28},{16,0},{20,4},{24,8},{28,12},{1,17},{... | collective-permute-start | bytes 98312 | tf_op jit(solution)/shard_map/ppermute | solution.py:404
  5.6 6.6 %collective-permute-start = (bf16[8,2048]{1,0:T(8,128)(2,1)}, bf16[8,2048]{1,0:T(8,128)(2,1)S(1)}, u32[]{:S(2)}, u32[]{:S(2)}) collective-permute-start(bf16[8,2048]{1,0:T(8,128)(2,1)} %refs_0_.1), channel_id=1, source_target_pairs={{0,8},{4,12},{8,0},{12,4},{16,24},{20,28},{24,16},{28,20},{1,9},{5... | collective-permute-start | bytes 98312 | tf_op jit(solution)/shard_map/ppermute | solution.py:404
  7.0 5.1 %collective-permute-start.2 = (bf16[8,2048]{1,0:T(8,128)(2,1)}, bf16[8,2048]{1,0:T(8,128)(2,1)S(1)}, u32[]{:S(2)}, u32[]{:S(2)}) collective-permute-start(bf16[8,2048]{1,0:T(8,128)(2,1)} %refs_0_.1), channel_id=1, source_target_pairs={{0,24},{4,28},{8,16},{12,20},{16,8},{20,12},{24,0},{28,4},{1,25},{... | collective-permute-start | bytes 98312 | tf_op jit(solution)/shard_map/ppermute | solution.py:404
  7.5 0.8 %copy-start.3 = (bf16[8,2048]{1,0:T(8,128)(2,1)S(1)}, bf16[8,2048]{1,0:T(8,128)(2,1)}, u32[]{:S(2)}) copy-start(bf16[8,2048]{1,0:T(8,128)(2,1)} %refs_0_.1) | copy-start | bytes 98308
  8.3 4.6 %collective-permute-start.5 = (bf16[2,8,2048]{2,1,0:T(8,128)(2,1)S(1)}, bf16[2,8,2048]{2,1,0:T(8,128)(2,1)S(1)}, u32[]{:S(2)}, u32[]{:S(2)}) collective-permute-start(bf16[2,8,2048]{2,1,0:T(8,128)(2,1)S(1)} %stack_pieces.6.refs_0_), channel_id=1, source_target_pairs={{0,1},{1,0},{2,3},{3,2},{4,5},{5,4},{6,7},{7,6},{8,9},{9,8},{10,11... | collective-permute-start | bytes 196616 | tf_op jit(solution)/shard_map/ppermute | solution.py:404
  10.0 1.4 %copy-start = (bf16[192,4096]{1,0:T(8,128)(2,1)S(1)}, bf16[192,4096]{1,0:T(8,128)(2,1)}, u32[]{:S(2)}) copy-start(bf16[192,4096]{1,0:T(8,128)(2,1)} %param.8) | copy-start | bytes 4718596
  12.1 0.9 %copy-start.1 = (bf16[128,512]{1,0:T(8,128)(2,1)S(1)}, bf16[128,512]{1,0:T(8,128)(2,1)}, u32[]{:S(2)}) copy-start(bf16[128,512]{1,0:T(8,128)(2,1)} %constant.4.clone.spread_ref) | copy-start | bytes 393220
  12.1 0.9 %copy-start.4 = (s32[192]{0:T(256)S(1)}, s32[192]{0:T(256)}, u32[]{:S(2)}) copy-start(s32[192]{0:T(256)} %rows_ref.3) | copy-start | bytes 2308
  12.1 0.9 %copy-start.5 = (s32[192]{0:T(256)S(1)}, s32[192]{0:T(256)}, u32[]{:S(2)}) copy-start(s32[192]{0:T(256)} %cols_ref.3) | copy-start | bytes 2308
  12.2 3.3 %copy-start.2 = (bf16[512,128]{1,0:T(8,128)(2,1)S(1)}, bf16[512,128]{1,0:T(8,128)(2,1)}, u32[]{:S(2)}) copy-start(bf16[512,128]{1,0:T(8,128)(2,1)} %constant.5.clone.fold_ref) | copy-start | bytes 393220
  12.2 3.3 %collective-permute-start.3 = (bf16[4,8,2048]{2,1,0:T(8,128)(2,1)S(1)}, bf16[4,8,2048]{2,1,0:T(8,128)(2,1)S(1)}, u32[]{:S(2)}, u32[]{:S(2)}) collective-permute-start(bf16[4,8,2048]{2,1,0:T(8,128)(2,1)S(1)} %stack_pieces.5.after_ref.same_ref), channel_id=1, source_target_pairs={{0,4},{4,0},{8,12},{12,8},{16,20},{20,16},{24,28},{28,24},{1,5},{5... | collective-permute-start | bytes 393224 | tf_op jit(solution)/shard_map/ppermute | solution.py:404
  14.8 4.8 %collective-permute-start.8 = (f32[2,8,2048]{2,1,0:T(8,128)S(1)}, f32[2,8,2048]{2,1,0:T(8,128)S(1)}, u32[]{:S(2)}, u32[]{:S(2)}) collective-permute-start(f32[2,8,2048]{2,1,0:T(8,128)S(1)} %get-tuple-element.18), channel_id=1, source_target_pairs={{0,4},{4,0},{8,12},{12,8},{16,20},{20,16},{24,28},{28,24},{1,5},{5... | collective-permute-start | bytes 393224 | tf_op jit(solution)/shard_map/ppermute | solution.py:404
  15.4 4.2 %collective-permute-start.7 = (f32[2,8,2048]{2,1,0:T(8,128)S(1)}, f32[2,8,2048]{2,1,0:T(8,128)S(1)}, u32[]{:S(2)}, u32[]{:S(2)}) collective-permute-start(f32[2,8,2048]{2,1,0:T(8,128)S(1)} %get-tuple-element.14.after_ref), channel_id=1, source_target_pairs={{0,4},{4,0},{8,12},{12,8},{16,20},{20,16},{24,28},{28,24},{1,5},{5... | collective-permute-start | bytes 393224 | tf_op jit(solution)/shard_map/ppermute | solution.py:404
  17.9 4.6 %collective-permute-start.6 = (s16[2,8,2176]{2,1,0:T(8,128)(2,1)S(1)}, s16[2,8,2176]{2,1,0:T(8,128)(2,1)S(1)}, u32[]{:S(2)}, u32[]{:S(2)}) collective-permute-start(s16[2,8,2176]{2,1,0:T(8,128)(2,1)S(1)} %get-tuple-element.16.refs_2_), channel_id=1, source_target_pairs={{0,1},{1,0},{2,3},{3,2},{4,5},{5,4},{6,7},{7,6},{8,9},{9,8},{10,11... | collective-permute-start | bytes 208904 | tf_op jit(solution)/shard_map/ppermute | solution.py:404
  19.6 8.1 %collective-permute-start.11 = (f32[8,2048]{1,0:T(8,128)S(1)}, f32[8,2048]{1,0:T(8,128)S(1)}, u32[]{:S(2)}, u32[]{:S(2)}) collective-permute-start(f32[8,2048]{1,0:T(8,128)S(1)} %get-tuple-element.22), channel_id=1, source_target_pairs={{0,24},{4,28},{8,16},{12,20},{16,8},{20,12},{24,0},{28,4},{1,25},{... | collective-permute-start | bytes 196616 | tf_op jit(solution)/shard_map/ppermute | solution.py:404
  21.9 5.8 %collective-permute-start.10 = (f32[8,2048]{1,0:T(8,128)S(1)}, f32[8,2048]{1,0:T(8,128)S(1)}, u32[]{:S(2)}, u32[]{:S(2)}) collective-permute-start(f32[8,2048]{1,0:T(8,128)S(1)} %get-tuple-element.19.after_ref), channel_id=1, source_target_pairs={{0,16},{4,20},{8,24},{12,28},{16,0},{20,4},{24,8},{28,12},{1,17},{... | collective-permute-start | bytes 196616 | tf_op jit(solution)/shard_map/ppermute | solution.py:404
  22.7 5.0 %collective-permute-start.9 = (s16[1,8,2176]{2,1,0:T(8,128)(2,1)S(1)}, s16[1,8,2176]{2,1,0:T(8,128)(2,1)S(1)}, u32[]{:S(2)}, u32[]{:S(2)}) collective-permute-start(s16[1,8,2176]{2,1,0:T(8,128)(2,1)S(1)} %get-tuple-element.21.refs_2_), channel_id=1, source_target_pairs={{0,2},{1,3},{2,0},{3,1},{4,6},{5,7},{6,4},{7,5},{8,10},{9,11},{10,... | collective-permute-start | bytes 104456 | tf_op jit(solution)/shard_map/ppermute | solution.py:404
  23.8 4.0 %collective-permute-start.12 = (s16[8,2176]{1,0:T(8,128)(2,1)S(1)}, s16[8,2176]{1,0:T(8,128)(2,1)S(1)}, u32[]{:S(2)}, u32[]{:S(2)}) collective-permute-start(s16[8,2176]{1,0:T(8,128)(2,1)S(1)} %core_pair_sum.3), channel_id=1, source_target_pairs={{0,8},{4,12},{8,0},{12,4},{16,24},{20,28},{24,16},{28,20},{1,9},{5... | collective-permute-start | bytes 104456 | tf_op jit(solution)/shard_map/ppermute | solution.py:404

commit v15 on v13

--- a/solution.py
+++ b/solution.py
@@ -63,27 +63,27 @@
     ]
 
 
-def prep_kernel(tiles_ref, out_ref, wide):
+def prep_kernel(tiles_ref, after_ref, out_ref, wide):
     for b in range(tiles_ref.shape[0]):
         wide[b] = tiles_ref[b].astype(F32).reshape(HALF * 8, LANES)
         for s in range(8):
             out_ref[8 * b + s] = wide[b, pl.ds(s, HALF, stride=8), :].astype(BF16)
 
 
-def prep(tiles):
+def prep(tiles, after):
     slots = tiles.shape[0]
     blocks = slots // 8
     view = tiles.reshape(blocks, 8, HALF, LANES).swapaxes(1, 2)
     return pl.pallas_call(
         prep_kernel,
-        in_specs=[VMEM],
+        in_specs=[VMEM, ANY],
         out_specs=VMEM,
         out_shape=jax.ShapeDtypeStruct((slots, HALF, LANES), BF16),
         scratch_shapes=[pltpu.VMEM((blocks, HALF * 8, LANES), F32)],
         compiler_params=PARAMS,
         cost_estimate=pl.CostEstimate(flops=0, bytes_accessed=4 * tiles.size, transcendentals=0),
         name="prep_tiles",
-    )(view)
+    )(view, after)
 
 
 def doubled(size):
@@ -199,13 +199,11 @@
     other_ref,
     after_ref,
     keep_ref,
-    give_ref,
-    table,
-    acc_a,
-    acc_b,
+    *refs,
 ):
+    *give_refs, table, acc_a, acc_b = refs
     pieces = [ref.at[h] for h in range(same_ref.shape[0]) for ref in (same_ref, other_ref)]
-    n_out = 2 * keep_ref.shape[0]
+    n_out = 1 + len(give_refs)
     width, piece = pieces[0].shape
     per_piece = piece // TILE
     slots = tiles_ref.shape[0]
@@ -255,23 +253,23 @@
         out = jnp.dot(first, fold, preferred_element_type=F32)
         out = out + jnp.dot(rest, fold, preferred_element_type=F32)
         parts = [out[p * width : (p + 1) * width] for p in range(pairs)]
-        if n % 2 == 0:
+        if n == 0:
             for p in range(pairs):
-                keep_ref[n // 2, :, p * LANES : (p + 1) * LANES] = parts[p]
+                keep_ref[:, p * LANES : (p + 1) * LANES] = parts[p]
         else:
-            encode(parts, give_ref.at[n // 2])
+            encode(parts, give_refs[n - 1])
 
 
 def forward(same, other, tiles, tile_rows, tile_cols, counts, n_out, after):
     n_chips, width, piece = same.shape
     per_piece = piece // TILE
-    half = jax.ShapeDtypeStruct((n_out // 2, width, piece), F32)
-    coded = jax.ShapeDtypeStruct((n_out // 2, width, piece + LANES), jnp.int16)
+    own = jax.ShapeDtypeStruct((width, piece), F32)
+    coded = jax.ShapeDtypeStruct((width, piece + LANES), jnp.int16)
     return pl.pallas_call(
         forward_kernel,
         in_specs=[SMEM] * 3 + [VMEM] * 4 + [ANY],
-        out_specs=[VMEM] * 2,
-        out_shape=[half, coded],
+        out_specs=[VMEM] * n_out,
+        out_shape=[own] + [coded] * (n_out - 1),
         scratch_shapes=[
             pltpu.VMEM((2 * n_chips * per_piece, width, LANES), F32),
             pltpu.VMEM((n_out * per_piece + 1, width, LANES), F32),
@@ -289,7 +287,7 @@
     out_ref, at = refs[-1], 0
     for ref in refs[: -1 - n_after]:
         if len(ref.shape) == 2:
-            out_ref[at] = ref[...]
+            out_ref[at] = ref[...].astype(out_ref.dtype)
             at += 1
         else:
             out_ref[at : at + ref.shape[0]] = ref[...]
@@ -308,72 +306,89 @@
     )(*parts, *after)
 
 
-def pair_sum_kernel(keep_ref, *refs):
-    n_chips = keep_ref.shape[0]
-    gots, outs = refs[: 1 - n_chips], refs[1 - n_chips :]
+def split_sum_kernel(keep_ref, *refs):
+    gots, (next_keep, next_give) = refs[:-3], refs[-2:]
     got = [ref.at[h] for ref in gots for h in range(ref.shape[0])]
-    for h, out in enumerate(outs):
-        out[...] = keep_ref[h + 1] + got[h + 1][...]
-
-
-def pair_sum(keep, gots):
+    for h in range(next_keep.shape[0]):
+        next_keep[h] = keep_ref[2 * h] + got[2 * h][...]
+        odd = keep_ref[2 * h + 1] + got[2 * h + 1][...]
+        if next_give.dtype == F32:
+            next_give[h] = odd
+        else:
+            chunks = [odd[:, n : n + LANES] for n in range(0, odd.shape[1], LANES)]
+            encode(chunks, next_give.at[h])
+
+
+def split_sum(keep, gots, after):
     parts, width, piece = keep.shape
-    return pl.pallas_call(
-        pair_sum_kernel,
+    half = jax.ShapeDtypeStruct((parts // 2, width, piece), F32)
+    coded = jax.ShapeDtypeStruct((parts // 2, width, piece + LANES), jnp.int16)
+    return pl.pallas_call(
+        split_sum_kernel,
+        in_specs=[VMEM] * (1 + len(gots)) + [ANY],
+        out_specs=[VMEM] * 2,
+        out_shape=[half, half if parts > 2 else coded],
+        compiler_params=PARAMS,
+        name="halving_sum",
+    )(keep, *gots, after)
+
+
+def z_sum_kernel(mine_ref, *refs):
+    gots, out_ref = refs[:-1], refs[-1]
+    parts = [decode(ref) for ref in gots]
+    for n in range(mine_ref.shape[1] // LANES):
+        at = pl.ds(n * LANES, LANES)
+        total = mine_ref[:, at]
+        for part in parts:
+            total = total + part[n]
+        out_ref[:, at] = total
+
+
+def z_sum(mine, gots):
+    return pl.pallas_call(
+        z_sum_kernel,
         in_specs=[VMEM] * (1 + len(gots)),
-        out_specs=[VMEM] * (parts - 1),
-        out_shape=[jax.ShapeDtypeStruct((width, piece), F32)] * (parts - 1),
-        compiler_params=PARAMS,
-        name="core_pair_sum",
-    )(keep, *gots)
-
-
-def split_sum_kernel(keep_ref, got_ref, after_ref, next_keep, next_give):
-    for h in range(next_keep.shape[0]):
-        for n, got in enumerate(decode(got_ref.at[2 * h])):
-            at = pl.ds(n * LANES, LANES)
-            next_keep[h, :, at] = keep_ref[2 * h, :, at] + got
-        sums = [
-            keep_ref[2 * h + 1, :, n * LANES : (n + 1) * LANES] + got
-            for n, got in enumerate(decode(got_ref.at[2 * h + 1]))
-        ]
-        encode(sums, next_give.at[h])
-
-
-def split_sum(keep, got, after):
-    parts, width, piece = keep.shape
-    return pl.pallas_call(
-        split_sum_kernel,
-        in_specs=[VMEM] * 2 + [ANY],
+        out_specs=VMEM,
+        out_shape=jax.ShapeDtypeStruct(mine.shape, F32),
+        compiler_params=PARAMS,
+        name="z_sum",
+    )(mine, *gots)
+
+
+def last_sum_kernel(total_ref, keep_ref, got_ref, out_ref):
+    for n, got in enumerate(decode(got_ref.at[0])):
+        at = pl.ds(n * LANES, LANES)
+        out_ref[:, at] = total_ref[:, at] + (keep_ref[0, :, at] + got)
+
+
+def last_sum(total, keep, got):
+    return pl.pallas_call(
+        last_sum_kernel,
+        in_specs=[VMEM] * 3,
+        out_specs=VMEM,
+        out_shape=jax.ShapeDtypeStruct(total.shape, F32),
+        compiler_params=PARAMS,
+        name="last_sum",
+    )(total, keep, got)
+
+
+def take_kernel(x_ref, out_ref, wide_ref):
+    out_ref[0] = x_ref[...]
+    wide_ref[...] = x_ref[...].astype(F32)
+
+
+def take(x):
+    return pl.pallas_call(
+        take_kernel,
+        in_specs=[VMEM],
         out_specs=[VMEM] * 2,
         out_shape=[
-            jax.ShapeDtypeStruct((parts // 2, width, piece), F32),
-            jax.ShapeDtypeStruct((parts // 2,) + got.shape[1:], got.dtype),
+            jax.ShapeDtypeStruct((1,) + x.shape, x.dtype),
+            jax.ShapeDtypeStruct(x.shape, F32),
         ],
         compiler_params=PARAMS,
-        name="halving_sum",
-    )(keep, got, after)
-
-
-def last_sum_kernel(*refs):
-    chips, (brow_keep, brow_got, keep_ref, got_ref, out_ref) = refs[:-5], refs[-5:]
-    for n, got in enumerate(decode(got_ref.at[0])):
-        at = pl.ds(n * LANES, LANES)
-        total = brow_keep[0, :, at] + brow_got[0, :, at]
-        for ref in chips:
-            total = total + ref[:, at]
-        out_ref[:, at] = total + (keep_ref[0, :, at] + got)
-
-
-def last_sum(keep, got, brow_keep, brow_got, chips):
-    return pl.pallas_call(
-        last_sum_kernel,
-        in_specs=[VMEM] * (4 + len(chips)),
-        out_specs=VMEM,
-        out_shape=jax.ShapeDtypeStruct(keep.shape[1:], F32),
-        compiler_params=PARAMS,
-        name="last_sum",
-    )(*chips, brow_keep, brow_got, keep, got)
+        name="take_piece",
+    )(x)
 
 
 def swap(x, axis, size, d):
@@ -383,28 +398,26 @@
 def body(vectors, tiles, tile_rows, tile_cols, counts):
     n_rows = lax.axis_size("brow")
     n_cols = lax.axis_size("bcol")
-    own = stack(vectors)
-    chips = [swap(vectors, "brow", n_rows, 2 * h) for h in range(1, n_rows // 2)]
-    segment, d = own, n_cols // 2
+    own, wide = take(vectors)
+    chips = [swap(wide, "brow", n_rows, 2 * h) for h in range(1, n_rows // 2)]
+    far = swap(vectors[None], "bcol", n_cols, n_cols // 2)
+    segment, d = stack(own, far), n_cols // 4
+    blocks = prep(tiles, own)
     while d > 0:
-        first = d == n_cols // 2
-        segment = stack(segment, swap(vectors[None] if first else segment, "bcol", n_cols, d))
+        segment = stack(segment, swap(segment, "bcol", n_cols, d))
         d //= 2
-    blocks = prep(tiles)
     same = stack(own, *chips, after=(blocks,))
     other = swap(same, "brow", n_rows, 1)
 
     col_keep, *col_give = backward(segment, blocks, tile_rows, tile_cols, counts, n_rows, same)
-    row_keep, give = forward(same, other, blocks, tile_rows, tile_cols, counts, n_cols, col_give[0])
-    col_got = [swap(x, "brow", n_rows, 1) for x in col_give]
-    sums = pair_sum(col_keep, col_got)
-    from_chips = [swap(x, "brow", n_rows, 2 * (h + 1)) for h, x in enumerate(sums)]
-    row_got, d = swap(give, "bcol", n_cols, 1), 2
-    while d < n_cols:
-        row_keep, give = split_sum(row_keep, row_got, sums[0])
-        row_got = swap(give, "bcol", n_cols, d)
+    mine, *give = forward(same, other, blocks, tile_rows, tile_cols, counts, n_cols, col_give[0])
+    col_got, d = [swap(x, "brow", n_rows, 1) for x in col_give], 2
+    while d < n_rows:
+        col_keep, x = split_sum(col_keep, col_got, mine)
+        col_got = [swap(x, "brow", n_rows, d)]
         d *= 2
-    return last_sum(row_keep, row_got, col_keep, col_got[0], from_chips)
+    total = z_sum(mine, [swap(x, "bcol", n_cols, d + 1) for d, x in reversed(list(enumerate(give)))])
+    return last_sum(total, col_keep, col_got[0])
 
 
 def solution(mesh):

time: 29.2 us -> 29.8 us (1.021); the launches traced: 28.7 us -> 29.6 us
  starting transfers between devices: 15.7 us -> 17.4 us
  waiting for transfers between devices: 3.97 us -> 2.35 us
  local copies, waits for them, and re-layouts: 2.27 us -> 2.91 us
    ppermute x13, starting transfers between devices: 15.7 us -> 17.4 us  [swap(): return lax.ppermute(x, axis, [(i, i ^ d) for i in range(size)])]
    ppermute x13, waiting for transfers between devices: 3.97 us -> 2.35 us  [swap(): return lax.ppermute(x, axis, [(i, i ^ d) for i in range(size)])]
    unnamed x12, local copies, waits for them, and re-layouts: 2.27 us -> 2.91 us
    pallas_call x4 -> x6, Pallas kernels: 1.67 us -> 1.76 us  [the longest x1 0.73 us: last_sum(): pl.pallas_call(last_sum_kernel, in_specs=[VMEM] * 3, out_specs=VMEM, out_...]
  transfers between devices with their start and end apart: 13 -> 13, of which waited for: 1 -> 3; matrix products, arithmetic and copies ran while one was open for 0% -> 0% of each run, Pallas kernels for 18% -> 18%
where the time goes in v15:
time: 29.8 us; the launch traced here: 29.6 us
  starting transfers between devices  17.4 us (58%)
  Pallas kernels  6.1 us (20%)
  local copies, waits for them, and re-layouts  2.91 us (10%)
  waiting for transfers between devices  2.35 us (8%)
  between operations  0.81 us (3%)
    ppermute x13, starting transfers between devices, swap(): return lax.ppermute(x, axis, [(i, i ^ d) for i in range(size)])  17.4 us
    unnamed x12, local copies, waits for them, and re-layouts  2.91 us
    pallas_call x1, Pallas kernels, forward(): pl.pallas_call(forward_kernel, in_specs=[SMEM] * 3 + [VMEM] * 4 + [ANY],...  2.47 us
    ppermute x13, waiting for transfers between devices, swap(): return lax.ppermute(x, axis, [(i, i ^ d) for i in range(size)])  2.35 us
    pallas_call x1, Pallas kernels, backward(): pl.pallas_call(backward_kernel, in_specs=[SMEM] * 3 + [VMEM] * 3 + [ANY],...  1.84 us
    pallas_call x1, Pallas kernels, last_sum(): pl.pallas_call(last_sum_kernel, in_specs=[VMEM] * 3, out_specs=VMEM, out_...  0.73 us
    pallas_call x1, Pallas kernels, prep(): pl.pallas_call(prep_kernel, in_specs=[VMEM, ANY], out_specs=VMEM, out_sha...  0.69 us
  transfers between devices with their start and end apart: 13, of which 3 were waited for; matrix products, arithmetic and copies ran while one was open for 0% of the time, Pallas kernels for 18%

profile of v15, /device:TPU:0, one launch (start us, length us, event | category | flops | bytes accessed | tf_op | source)
XLA Modules:
  0.0 29.6 jit_solution(15231522145864863789)
XLA Ops:
  0.0 4.0 %collective-permute-start.4 = (bf16[1,8,2048]{2,1,0:T(8,128)(2,1)}, bf16[1,8,2048]{2,1,0:T(8,128)(2,1)S(1)}, u32[]{:S(2)}, u32[]{:S(2)}) collective-permute-start(bf16[1,8,2048]{2,1,0:T(8,128)(2,1)} %bitcast.5), channel_id=1, source_target_pairs={{0,2},{1,3},{2,0},{3,1},{4,6},{5,7},{6,4},{7,5},{8,10},{9,11},{10,... | collective-permute-start | bytes 98312 | tf_op jit(solution)/shard_map/ppermute | solution.py:395
  4.0 0.8 %copy-done.3 = bf16[8,2048]{1,0:T(8,128)(2,1)S(1)} copy-done((bf16[8,2048]{1,0:T(8,128)(2,1)S(1)}, bf16[8,2048]{1,0:T(8,128)(2,1)}, u32[]{:S(2)}) %copy-start.3) | copy-done | bytes 32792
  4.8 2.5 %collective-permute-start.2 = (f32[8,2048]{1,0:T(8,128)S(1)}, f32[8,2048]{1,0:T(8,128)S(1)}, u32[]{:S(2)}, u32[]{:S(2)}) collective-permute-start(f32[8,2048]{1,0:T(8,128)S(1)} %get-tuple-element.19), channel_id=1, source_target_pairs={{0,24},{4,28},{8,16},{12,20},{16,8},{20,12},{24,0},{28,4},{1,25},{... | collective-permute-start | bytes 196616 | tf_op jit(solution)/shard_map/ppermute | solution.py:395
  7.3 0.5 %collective-permute-start.1 = (f32[8,2048]{1,0:T(8,128)S(1)}, f32[8,2048]{1,0:T(8,128)S(1)}, u32[]{:S(2)}, u32[]{:S(2)}) collective-permute-start(f32[8,2048]{1,0:T(8,128)S(1)} %get-tuple-element.19), channel_id=1, source_target_pairs={{0,16},{4,20},{8,24},{12,28},{16,0},{20,4},{24,8},{28,12},{1,17},{... | collective-permute-start | bytes 196616 | tf_op jit(solution)/shard_map/ppermute | solution.py:395
  7.9 0.5 %collective-permute-start = (f32[8,2048]{1,0:T(8,128)S(1)}, f32[8,2048]{1,0:T(8,128)S(1)}, u32[]{:S(2)}, u32[]{:S(2)}) collective-permute-start(f32[8,2048]{1,0:T(8,128)S(1)} %get-tuple-element.19), channel_id=1, source_target_pairs={{0,8},{4,12},{8,0},{12,4},{16,24},{20,28},{24,16},{28,20},{1,9},{5... | collective-permute-start | bytes 196616 | tf_op jit(solution)/shard_map/ppermute | solution.py:395
  8.4 1.6 %collective-permute-start.5 = (bf16[2,8,2048]{2,1,0:T(8,128)(2,1)S(1)}, bf16[2,8,2048]{2,1,0:T(8,128)(2,1)S(1)}, u32[]{:S(2)}, u32[]{:S(2)}) collective-permute-start(bf16[2,8,2048]{2,1,0:T(8,128)(2,1)S(1)} %stack_pieces.4.refs_0_), channel_id=1, source_target_pairs={{0,1},{1,0},{2,3},{3,2},{4,5},{5,4},{6,7},{7,6},{8,9},{9,8},{10,11... | collective-permute-start | bytes 196616 | tf_op jit(solution)/shard_map/ppermute | solution.py:395
  10.7 0.0 copy-start
  10.7 1.4 %copy-done = bf16[192,4096]{1,0:T(8,128)(2,1)S(1)} copy-done((bf16[192,4096]{1,0:T(8,128)(2,1)S(1)}, bf16[192,4096]{1,0:T(8,128)(2,1)}, u32[]{:S(2)}) %copy-start) | copy-done | bytes 1572888
  12.1 0.7 %prep_tiles.1.refs_4_.tiles_ref = bf16[192,32,128]{2,1,0:T(8,128)(2,1)S(1)} custom-call(bf16[24,32,8,128]{3,2,1,0:T(8,128)(2,1)S(1)} %bitcast.4, bf16[1,8,2048]{2,1,0:T(8,128)(2,1)S(1)} %get-tuple-element.18.after_ref.refs_0_), custom_call_target="tpu_custom_call" | custom-call | bytes 3145728 | tf_op jit(solution)/shard_map/prep_tiles/pallas_call | solution.py:77
  12.8 0.0 copy-start.1
  12.8 0.0 copy-start.4
  12.8 0.0 copy-start.5
  12.8 0.0 collective-permute-done.2.refs_3_
  12.9 0.0 collective-permute-done.1.refs_2_
  12.9 0.0 copy-start.2
  12.9 0.1 collective-permute-start.3
  13.0 0.7 %copy-done.1 = bf16[128,512]{1,0:T(8,128)(2,1)S(1)} copy-done((bf16[128,512]{1,0:T(8,128)(2,1)S(1)}, bf16[128,512]{1,0:T(8,128)(2,1)}, u32[]{:S(2)}) %copy-start.1) | copy-done | bytes 131096
  13.7 1.8 %transpose_product.1 = (f32[4,8,2048]{2,1,0:T(8,128)S(1)}, f32[2,8,2048]{2,1,0:T(8,128)S(1)}, f32[2,8,2048]{2,1,0:T(8,128)S(1)}) custom-call(s32[192]{0:T(256)S(1)} %copy-done.4, s32[192]{0:T(256)S(1)} %copy-done.5, s32[1,1]{1,0:T(1,128)S(6)} %copy.8.count_ref, bf16[128,512]{1,0:T(8,128)(2,1)S(1)} %copy-done.1, ...), custom_call_target="tpu_custom_call" | custom-call | flops 100663296 | bytes 3145728 | tf_op jit(solution)/shard_map/transpose_product/pallas_call | solution.py:162
  15.6 0.1 collective-permute-start.10
  15.6 0.5 %collective-permute-start.9 = (f32[2,8,2048]{2,1,0:T(8,128)S(1)}, f32[2,8,2048]{2,1,0:T(8,128)S(1)}, u32[]{:S(2)}, u32[]{:S(2)}) collective-permute-start(f32[2,8,2048]{2,1,0:T(8,128)S(1)} %get-tuple-element.20.after_ref), channel_id=1, source_target_pairs={{0,4},{4,0},{8,12},{12,8},{16,20},{20,16},{24,28},{28,24},{1,5},{5... | collective-permute-start | bytes 393224 | tf_op jit(solution)/shard_map/ppermute | solution.py:395
  16.1 2.5 %forward_product.1 = (f32[8,2048]{1,0:T(8,128)S(1)}, s16[8,2176]{1,0:T(8,128)(2,1)S(1)}, s16[8,2176]{1,0:T(8,128)(2,1)S(1)}, s16[8,2176]{1,0:T(8,128)(2,1)S(1)}) custom-call(s32[192]{0:T(256)S(1)} %copy-done.4, s32[192]{0:T(256)S(1)} %copy-done.5, s32[1,1]{1,0:T(1,128)S(6)} %copy.8.count_ref, bf16[512,128]{1,0:T(8,128)(2,1)S(1)} %copy-done.2, ...), custom_call_target="tpu_custom_call" | custom-call | flops 100663296 | bytes 3145728 | tf_op jit(solution)/shard_map/forward_product/pallas_call | solution.py:268
  18.7 1.7 %collective-permute-start.11 = (f32[2,8,2048]{2,1,0:T(8,128)S(1)}, f32[2,8,2048]{2,1,0:T(8,128)S(1)}, u32[]{:S(2)}, u32[]{:S(2)}) collective-permute-start(f32[2,8,2048]{2,1,0:T(8,128)S(1)} %get-tuple-element.28), channel_id=1, source_target_pairs={{0,8},{4,12},{8,0},{12,4},{16,24},{20,28},{24,16},{28,20},{1,9},{5... | collective-permute-start | bytes 393224 | tf_op jit(solution)/shard_map/ppermute | solution.py:395
  20.3 0.8 %collective-permute-start.6 = (s16[8,2176]{1,0:T(8,128)(2,1)S(1)}, s16[8,2176]{1,0:T(8,128)(2,1)S(1)}, u32[]{:S(2)}, u32[]{:S(2)}) collective-permute-start(s16[8,2176]{1,0:T(8,128)(2,1)S(1)} %get-tuple-element.22), channel_id=1, source_target_pairs={{0,3},{1,2},{2,1},{3,0},{4,7},{5,6},{6,5},{7,4},{8,11},{9,10},{10,... | collective-permute-start | bytes 104456 | tf_op jit(solution)/shard_map/ppermute | solution.py:395
  21.2 1.3 %collective-permute-start.7 = (s16[8,2176]{1,0:T(8,128)(2,1)S(1)}, s16[8,2176]{1,0:T(8,128)(2,1)S(1)}, u32[]{:S(2)}, u32[]{:S(2)}) collective-permute-start(s16[8,2176]{1,0:T(8,128)(2,1)S(1)} %get-tuple-element.23), channel_id=1, source_target_pairs={{0,2},{1,3},{2,0},{3,1},{4,6},{5,7},{6,4},{7,5},{8,10},{9,11},{10,... | collective-permute-start | bytes 104456 | tf_op jit(solution)/shard_map/ppermute | solution.py:395
  22.4 2.3 %collective-permute-start.8 = (s16[8,2176]{1,0:T(8,128)(2,1)S(1)}, s16[8,2176]{1,0:T(8,128)(2,1)S(1)}, u32[]{:S(2)}, u32[]{:S(2)}) collective-permute-start(s16[8,2176]{1,0:T(8,128)(2,1)S(1)} %get-tuple-element.24), channel_id=1, source_target_pairs={{0,1},{1,0},{2,3},{3,2},{4,5},{5,4},{6,7},{7,6},{8,9},{9,8},{10,11... | collective-permute-start | bytes 104456 | tf_op jit(solution)/shard_map/ppermute | solution.py:395
  24.7 0.1 halving_sum.3
  24.9 1.5 %collective-permute-start.12 = (s16[1,8,2176]{2,1,0:T(8,128)(2,1)S(1)}, s16[1,8,2176]{2,1,0:T(8,128)(2,1)S(1)}, u32[]{:S(2)}, u32[]{:S(2)}) collective-permute-start(s16[1,8,2176]{2,1,0:T(8,128)(2,1)S(1)} %get-tuple-element.30), channel_id=1, source_target_pairs={{0,16},{4,20},{8,24},{12,28},{16,0},{20,4},{24,8},{28,12},{1,17},{... | collective-permute-start | bytes 104456 | tf_op jit(solution)/shard_map/ppermute | solution.py:395
  26.4 0.4 %collective-permute-done.7.refs_1_ = s16[8,2176]{1,0:T(8,128)(2,1)S(1)} collective-permute-done((s16[8,2176]{1,0:T(8,128)(2,1)S(1)}, s16[8,2176]{1,0:T(8,128)(2,1)S(1)}, u32[]{:S(2)}, u32[]{:S(2)}) %collective-permute-start.7) | collective-permute-done | bytes 34848 | tf_op jit(solution)/shard_map/ppermute | solution.py:395
  26.8 0.2 collective-permute-done.8.refs_2_
  26.9 0.2 z_sum.1.total_ref
  27.1 1.8 %collective-permute-done.12.got_ref = s16[1,8,2176]{2,1,0:T(8,128)(2,1)S(1)} collective-permute-done((s16[1,8,2176]{2,1,0:T(8,128)(2,1)S(1)}, s16[1,8,2176]{2,1,0:T(8,128)(2,1)S(1)}, u32[]{:S(2)}, u32[]{:S(2)}) %collective-permute-start.12) | collective-permute-done | bytes 34848 | tf_op jit(solution)/shard_map/ppermute | solution.py:395
  28.9 0.7 %last_sum.1 = f32[8,2048]{1,0:T(8,128)} custom-call(f32[8,2048]{1,0:T(8,128)S(1)} %z_sum.1.total_ref, f32[1,8,2048]{2,1,0:T(8,128)S(1)} %get-tuple-element.29.keep_ref, s16[1,8,2176]{2,1,0:T(8,128)(2,1)S(1)} %collective-permute-done.12.got_ref), custom_call_target="tpu_custom_call" | custom-call | tf_op jit(solution)/shard_map/last_sum/pallas_call | solution.py:365
  (17 shorter events, 0.1 us)
Async XLA Ops:
  0.0 8.4 %collective-permute-start.4 = (bf16[1,8,2048]{2,1,0:T(8,128)(2,1)}, bf16[1,8,2048]{2,1,0:T(8,128)(2,1)S(1)}, u32[]{:S(2)}, u32[]{:S(2)}) collective-permute-start(bf16[1,8,2048]{2,1,0:T(8,128)(2,1)} %bitcast.5), channel_id=1, source_target_pairs={{0,2},{1,3},{2,0},{3,1},{4,6},{5,7},{6,4},{7,5},{8,10},{9,11},{10,... | collective-permute-start | bytes 98312 | tf_op jit(solution)/shard_map/ppermute | solution.py:395
  4.0 0.8 %copy-start.3 = (bf16[8,2048]{1,0:T(8,128)(2,1)S(1)}, bf16[8,2048]{1,0:T(8,128)(2,1)}, u32[]{:S(2)}) copy-start(bf16[8,2048]{1,0:T(8,128)(2,1)} %x_ref.1) | copy-start | bytes 98308
  4.8 8.0 %collective-permute-start.2 = (f32[8,2048]{1,0:T(8,128)S(1)}, f32[8,2048]{1,0:T(8,128)S(1)}, u32[]{:S(2)}, u32[]{:S(2)}) collective-permute-start(f32[8,2048]{1,0:T(8,128)S(1)} %get-tuple-element.19), channel_id=1, source_target_pairs={{0,24},{4,28},{8,16},{12,20},{16,8},{20,12},{24,0},{28,4},{1,25},{... | collective-permute-start | bytes 196616 | tf_op jit(solution)/shard_map/ppermute | solution.py:395
  7.3 5.5 %collective-permute-start.1 = (f32[8,2048]{1,0:T(8,128)S(1)}, f32[8,2048]{1,0:T(8,128)S(1)}, u32[]{:S(2)}, u32[]{:S(2)}) collective-permute-start(f32[8,2048]{1,0:T(8,128)S(1)} %get-tuple-element.19), channel_id=1, source_target_pairs={{0,16},{4,20},{8,24},{12,28},{16,0},{20,4},{24,8},{28,12},{1,17},{... | collective-permute-start | bytes 196616 | tf_op jit(solution)/shard_map/ppermute | solution.py:395
  7.9 5.0 %collective-permute-start = (f32[8,2048]{1,0:T(8,128)S(1)}, f32[8,2048]{1,0:T(8,128)S(1)}, u32[]{:S(2)}, u32[]{:S(2)}) collective-permute-start(f32[8,2048]{1,0:T(8,128)S(1)} %get-tuple-element.19), channel_id=1, source_target_pairs={{0,8},{4,12},{8,0},{12,4},{16,24},{20,28},{24,16},{28,20},{1,9},{5... | collective-permute-start | bytes 196616 | tf_op jit(solution)/shard_map/ppermute | solution.py:395
  8.4 4.6 %collective-permute-start.5 = (bf16[2,8,2048]{2,1,0:T(8,128)(2,1)S(1)}, bf16[2,8,2048]{2,1,0:T(8,128)(2,1)S(1)}, u32[]{:S(2)}, u32[]{:S(2)}) collective-permute-start(bf16[2,8,2048]{2,1,0:T(8,128)(2,1)S(1)} %stack_pieces.4.refs_0_), channel_id=1, source_target_pairs={{0,1},{1,0},{2,3},{3,2},{4,5},{5,4},{6,7},{7,6},{8,9},{9,8},{10,11... | collective-permute-start | bytes 196616 | tf_op jit(solution)/shard_map/ppermute | solution.py:395
  10.7 1.4 %copy-start = (bf16[192,4096]{1,0:T(8,128)(2,1)S(1)}, bf16[192,4096]{1,0:T(8,128)(2,1)}, u32[]{:S(2)}) copy-start(bf16[192,4096]{1,0:T(8,128)(2,1)} %param.8) | copy-start | bytes 4718596
  12.8 0.9 %copy-start.1 = (bf16[128,512]{1,0:T(8,128)(2,1)S(1)}, bf16[128,512]{1,0:T(8,128)(2,1)}, u32[]{:S(2)}) copy-start(bf16[128,512]{1,0:T(8,128)(2,1)} %constant.4.clone.spread_ref) | copy-start | bytes 393220
  12.8 0.9 %copy-start.4 = (s32[192]{0:T(256)S(1)}, s32[192]{0:T(256)}, u32[]{:S(2)}) copy-start(s32[192]{0:T(256)} %rows_ref.3) | copy-start | bytes 2308
  12.8 0.9 %copy-start.5 = (s32[192]{0:T(256)S(1)}, s32[192]{0:T(256)}, u32[]{:S(2)}) copy-start(s32[192]{0:T(256)} %cols_ref.3) | copy-start | bytes 2308
  12.9 3.2 %copy-start.2 = (bf16[512,128]{1,0:T(8,128)(2,1)S(1)}, bf16[512,128]{1,0:T(8,128)(2,1)}, u32[]{:S(2)}) copy-start(bf16[512,128]{1,0:T(8,128)(2,1)} %constant.5.clone.fold_ref) | copy-start | bytes 393220
  12.9 3.2 %collective-permute-start.3 = (bf16[4,8,2048]{2,1,0:T(8,128)(2,1)S(1)}, bf16[4,8,2048]{2,1,0:T(8,128)(2,1)S(1)}, u32[]{:S(2)}, u32[]{:S(2)}) collective-permute-start(bf16[4,8,2048]{2,1,0:T(8,128)(2,1)S(1)} %stack_pieces.3.after_ref.same_ref), channel_id=1, source_target_pairs={{0,4},{4,0},{8,12},{12,8},{16,20},{20,16},{24,28},{28,24},{1,5},{5... | collective-permute-start | bytes 393224 | tf_op jit(solution)/shard_map/ppermute | solution.py:395
  15.6 3.1 %collective-permute-start.10 = (f32[2,8,2048]{2,1,0:T(8,128)S(1)}, f32[2,8,2048]{2,1,0:T(8,128)S(1)}, u32[]{:S(2)}, u32[]{:S(2)}) collective-permute-start(f32[2,8,2048]{2,1,0:T(8,128)S(1)} %get-tuple-element.26), channel_id=1, source_target_pairs={{0,4},{4,0},{8,12},{12,8},{16,20},{20,16},{24,28},{28,24},{1,5},{5... | collective-permute-start | bytes 393224 | tf_op jit(solution)/shard_map/ppermute | solution.py:395
  15.6 3.0 %collective-permute-start.9 = (f32[2,8,2048]{2,1,0:T(8,128)S(1)}, f32[2,8,2048]{2,1,0:T(8,128)S(1)}, u32[]{:S(2)}, u32[]{:S(2)}) collective-permute-start(f32[2,8,2048]{2,1,0:T(8,128)S(1)} %get-tuple-element.20.after_ref), channel_id=1, source_target_pairs={{0,4},{4,0},{8,12},{12,8},{16,20},{20,16},{24,28},{28,24},{1,5},{5... | collective-permute-start | bytes 393224 | tf_op jit(solution)/shard_map/ppermute | solution.py:395
  18.7 6.1 %collective-permute-start.11 = (f32[2,8,2048]{2,1,0:T(8,128)S(1)}, f32[2,8,2048]{2,1,0:T(8,128)S(1)}, u32[]{:S(2)}, u32[]{:S(2)}) collective-permute-start(f32[2,8,2048]{2,1,0:T(8,128)S(1)} %get-tuple-element.28), channel_id=1, source_target_pairs={{0,8},{4,12},{8,0},{12,4},{16,24},{20,28},{24,16},{28,20},{1,9},{5... | collective-permute-start | bytes 393224 | tf_op jit(solution)/shard_map/ppermute | solution.py:395
  20.3 6.0 %collective-permute-start.6 = (s16[8,2176]{1,0:T(8,128)(2,1)S(1)}, s16[8,2176]{1,0:T(8,128)(2,1)S(1)}, u32[]{:S(2)}, u32[]{:S(2)}) collective-permute-start(s16[8,2176]{1,0:T(8,128)(2,1)S(1)} %get-tuple-element.22), channel_id=1, source_target_pairs={{0,3},{1,2},{2,1},{3,0},{4,7},{5,6},{6,5},{7,4},{8,11},{9,10},{10,... | collective-permute-start | bytes 104456 | tf_op jit(solution)/shard_map/ppermute | solution.py:395
  21.2 5.6 %collective-permute-start.7 = (s16[8,2176]{1,0:T(8,128)(2,1)S(1)}, s16[8,2176]{1,0:T(8,128)(2,1)S(1)}, u32[]{:S(2)}, u32[]{:S(2)}) collective-permute-start(s16[8,2176]{1,0:T(8,128)(2,1)S(1)} %get-tuple-element.23), channel_id=1, source_target_pairs={{0,2},{1,3},{2,0},{3,1},{4,6},{5,7},{6,4},{7,5},{8,10},{9,11},{10,... | collective-permute-start | bytes 104456 | tf_op jit(solution)/shard_map/ppermute | solution.py:395
  22.4 4.5 %collective-permute-start.8 = (s16[8,2176]{1,0:T(8,128)(2,1)S(1)}, s16[8,2176]{1,0:T(8,128)(2,1)S(1)}, u32[]{:S(2)}, u32[]{:S(2)}) collective-permute-start(s16[8,2176]{1,0:T(8,128)(2,1)S(1)} %get-tuple-element.24), channel_id=1, source_target_pairs={{0,1},{1,0},{2,3},{3,2},{4,5},{5,4},{6,7},{7,6},{8,9},{9,8},{10,11... | collective-permute-start | bytes 104456 | tf_op jit(solution)/shard_map/ppermute | solution.py:395
  24.9 4.0 %collective-permute-start.12 = (s16[1,8,2176]{2,1,0:T(8,128)(2,1)S(1)}, s16[1,8,2176]{2,1,0:T(8,128)(2,1)S(1)}, u32[]{:S(2)}, u32[]{:S(2)}) collective-permute-start(s16[1,8,2176]{2,1,0:T(8,128)(2,1)S(1)} %get-tuple-element.30), channel_id=1, source_target_pairs={{0,16},{4,20},{8,24},{12,28},{16,0},{20,4},{24,8},{28,12},{1,17},{... | collective-permute-start | bytes 104456 | tf_op jit(solution)/shard_map/ppermute | solution.py:395

commit v16 on v10

--- a/solution.py
+++ b/solution.py
@@ -22,12 +22,10 @@
 
 
 def row_spread():
-    out = np.zeros((LANES, 2, 2, GROUP, HALF), np.float32)
-    for q in range(2):
-        for e in range(2):
-            for m in range(HALF):
-                out[q * TILE + 2 * m + e, q, e, :, m] = 1
-    return jnp.asarray(out.reshape(LANES, 4 * LANES), BF16)
+    source = lax.broadcasted_iota(jnp.int32, (LANES, LANES), 0)
+    m = lax.broadcasted_iota(jnp.int32, (LANES, LANES), 1) % HALF
+    blocks = [source == q * TILE + 2 * m + e for q in range(2) for e in range(2)]
+    return jnp.concatenate([block.astype(F32) for block in blocks], axis=1).astype(BF16)
 
 
 def row_fold():
@@ -102,7 +100,7 @@
 
 
 def backward_kernel(
-    rows_ref, cols_ref, count_ref, spread_ref, tiles_ref, seg_ref, after_ref, keep_ref, *refs
+    rows_ref, cols_ref, count_ref, tiles_ref, seg_ref, after_ref, keep_ref, *refs
 ):
     pieces = [seg_ref.at[n] for n in range(seg_ref.shape[0])]
     *give_refs, table, acc_a, acc_b = refs
@@ -111,7 +109,7 @@
     width, piece = pieces[0].shape
     per_piece = piece // TILE
     slots = tiles_ref.shape[0]
-    build_table(pieces, spread_ref[...], table)
+    build_table(pieces, row_spread(), table)
     for acc in (acc_a, acc_b):
         acc[...] = jnp.zeros_like(acc)
     lane = lax.broadcasted_iota(jnp.int32, (2 * width, LANES), 1)
@@ -153,7 +151,7 @@
     quarter = jax.ShapeDtypeStruct((n_out // 4, width, piece), F32)
     return pl.pallas_call(
         backward_kernel,
-        in_specs=[SMEM] * 3 + [VMEM] * 3 + [ANY],
+        in_specs=[SMEM] * 3 + [VMEM] * 2 + [ANY],
         out_specs=[VMEM] * 3,
         out_shape=[half, quarter, quarter],
         scratch_shapes=[
@@ -166,7 +164,7 @@
             flops=2 * tiles.size * 64, bytes_accessed=4 * tiles.size, transcendentals=0
         ),
         name="transpose_product",
-    )(tile_rows, tile_cols, counts, row_spread(), tiles, segment, after)
+    )(tile_rows, tile_cols, counts, tiles, segment, after)
 
 
 def double_table(pieces, table):
@@ -191,6 +189,7 @@
     other_ref,
     after_ref,
     keep_ref,
+    near_ref,
     give_ref,
     table,
     acc_a,
@@ -251,19 +250,20 @@
             for p in range(pairs):
                 keep_ref[n // 2, :, p * LANES : (p + 1) * LANES] = parts[p]
         else:
-            encode(parts, give_ref.at[n // 2])
+            encode(parts, near_ref.at[0] if n == 1 else give_ref.at[n // 2 - 1])
 
 
 def forward(same, other, tiles, tile_rows, tile_cols, counts, n_out, after):
     n_chips, width, piece = same.shape
     per_piece = piece // TILE
     half = jax.ShapeDtypeStruct((n_out // 2, width, piece), F32)
-    coded = jax.ShapeDtypeStruct((n_out // 2, width, piece + LANES), jnp.int16)
+    near = jax.ShapeDtypeStruct((1, width, piece + LANES), jnp.int16)
+    rest = jax.ShapeDtypeStruct((n_out // 2 - 1, width, piece + LANES), jnp.int16)
     return pl.pallas_call(
         forward_kernel,
         in_specs=[SMEM] * 3 + [VMEM] * 4 + [ANY],
-        out_specs=[VMEM] * 2,
-        out_shape=[half, coded],
+        out_specs=[VMEM] * 3,
+        out_shape=[half, near, rest],
         scratch_shapes=[
             pltpu.VMEM((2 * n_chips * per_piece, width, LANES), F32),
             pltpu.VMEM((n_out * per_piece + 1, width, LANES), F32),
@@ -281,7 +281,7 @@
     out_ref, at = refs[-1], 0
     for ref in refs[: -1 - n_after]:
         if len(ref.shape) == 2:
-            out_ref[at] = ref[...]
+            out_ref[at] = ref[...].astype(out_ref.dtype)
             at += 1
         else:
             out_ref[at : at + ref.shape[0]] = ref[...]
@@ -320,35 +320,40 @@
     )(keep, *gots)
 
 
-def split_sum_kernel(keep_ref, got_ref, after_ref, next_keep, next_give):
-    for h in range(next_keep.shape[0]):
-        for n, got in enumerate(decode(got_ref.at[2 * h])):
-            at = pl.ds(n * LANES, LANES)
-            next_keep[h, :, at] = keep_ref[2 * h, :, at] + got
-        sums = [
-            keep_ref[2 * h + 1, :, n * LANES : (n + 1) * LANES] + got
-            for n, got in enumerate(decode(got_ref.at[2 * h + 1]))
-        ]
-        encode(sums, next_give.at[h])
+def split_sum_kernel(keep_ref, got_ref, after_ref, next_keep, near_ref, *rest_refs):
+    spans = [pl.ds(n, LANES) for n in range(0, keep_ref.shape[2], LANES)]
+    for h in range(keep_ref.shape[0]):
+        sums = [keep_ref[h, :, at] for at in spans]
+        if h > 0:
+            sums = [x + got for x, got in zip(sums, decode(got_ref.at[h - 1]))]
+        if h % 2 == 0:
+            for at, x in zip(spans, sums):
+                next_keep[h // 2, :, at] = x
+        elif h == 1:
+            encode(sums, near_ref.at[0])
+        else:
+            encode(sums, rest_refs[0].at[h // 2 - 1])
 
 
 def split_sum(keep, got, after):
     parts, width, piece = keep.shape
-    return pl.pallas_call(
+    shapes = [jax.ShapeDtypeStruct((parts // 2, width, piece), F32)]
+    shapes += [
+        jax.ShapeDtypeStruct((n, width, piece + LANES), got.dtype) for n in (1, parts // 2 - 1) if n
+    ]
+    keep, near, *rest = pl.pallas_call(
         split_sum_kernel,
         in_specs=[VMEM] * 2 + [ANY],
-        out_specs=[VMEM] * 2,
-        out_shape=[
-            jax.ShapeDtypeStruct((parts // 2, width, piece), F32),
-            jax.ShapeDtypeStruct((parts // 2,) + got.shape[1:], got.dtype),
-        ],
+        out_specs=[VMEM] * len(shapes),
+        out_shape=shapes,
         compiler_params=PARAMS,
         name="halving_sum",
     )(keep, got, after)
-
-
-def last_sum_kernel(*refs):
-    chips, (brow_keep, brow_got, keep_ref, got_ref, out_ref) = refs[:-5], refs[-5:]
+    return keep, near, rest
+
+
+def part_sum_kernel(keep_ref, got_ref, brow_keep, brow_got, *refs):
+    chips, out_ref = refs[:-1], refs[-1]
     for n, got in enumerate(decode(got_ref.at[0])):
         at = pl.ds(n * LANES, LANES)
         total = brow_keep[0, :, at] + brow_got[0, :, at]
@@ -357,15 +362,56 @@
         out_ref[:, at] = total + (keep_ref[0, :, at] + got)
 
 
-def last_sum(keep, got, brow_keep, brow_got, chips):
-    return pl.pallas_call(
-        last_sum_kernel,
+def part_sum(keep, got, brow_keep, brow_got, chips):
+    return pl.pallas_call(
+        part_sum_kernel,
         in_specs=[VMEM] * (4 + len(chips)),
         out_specs=VMEM,
         out_shape=jax.ShapeDtypeStruct(keep.shape[1:], F32),
         compiler_params=PARAMS,
+        name="part_sum",
+    )(keep, got, brow_keep, brow_got, *chips)
+
+
+def last_sum_kernel(total_ref, *refs):
+    gots, out_ref = refs[:-1], refs[-1]
+    parts = [decode(ref.at[0]) for ref in gots]
+    for n in range(total_ref.shape[1] // LANES):
+        at = pl.ds(n * LANES, LANES)
+        total = total_ref[:, at]
+        for part in parts:
+            total = total + part[n]
+        out_ref[:, at] = total
+
+
+def last_sum(total, gots):
+    return pl.pallas_call(
+        last_sum_kernel,
+        in_specs=[VMEM] * (1 + len(gots)),
+        out_specs=VMEM,
+        out_shape=jax.ShapeDtypeStruct(total.shape, F32),
+        compiler_params=PARAMS,
         name="last_sum",
-    )(*chips, brow_keep, brow_got, keep, got)
+    )(total, *gots)
+
+
+def take_kernel(x_ref, out_ref, wide_ref):
+    out_ref[0] = x_ref[...]
+    wide_ref[...] = x_ref[...].astype(F32)
+
+
+def take(x):
+    return pl.pallas_call(
+        take_kernel,
+        in_specs=[VMEM],
+        out_specs=[VMEM] * 2,
+        out_shape=[
+            jax.ShapeDtypeStruct((1,) + x.shape, x.dtype),
+            jax.ShapeDtypeStruct(x.shape, F32),
+        ],
+        compiler_params=PARAMS,
+        name="take_piece",
+    )(x)
 
 
 def swap(x, axis, size, d):
@@ -375,8 +421,8 @@
 def body(vectors, tiles, tile_rows, tile_cols, counts):
     n_rows = lax.axis_size("brow")
     n_cols = lax.axis_size("bcol")
-    own = stack(vectors)
-    chips = [swap(vectors, "brow", n_rows, 2 * h) for h in range(1, n_rows // 2)]
+    own, wide = take(vectors)
+    chips = [swap(wide, "brow", n_rows, 2 * h) for h in range(1, n_rows // 2)]
     segment, d = own, 1
     while d < n_cols:
         segment = stack(segment, swap(segment if d > 1 else vectors[None], "bcol", n_cols, d))
@@ -386,16 +432,20 @@
     other = swap(same, "brow", n_rows, 1)
 
     col_keep, *col_give = backward(segment, blocks, tile_rows, tile_cols, counts, n_rows, same)
-    row_keep, give = forward(same, other, blocks, tile_rows, tile_cols, counts, n_cols, col_give[0])
+    row_keep, near, rest = forward(same, other, blocks, tile_rows, tile_cols, counts, n_cols, col_give[0])
     col_got = [swap(x, "brow", n_rows, 1) for x in col_give]
     sums = pair_sum(col_keep, col_got)
     from_chips = [swap(x, "brow", n_rows, 2 * (h + 1)) for h, x in enumerate(sums)]
-    row_got, d = swap(give, "bcol", n_cols, 1), 2
-    while d < n_cols:
-        row_keep, give = split_sum(row_keep, row_got, sums[0])
-        row_got = swap(give, "bcol", n_cols, d)
+    d, later = 1, []
+    while 2 * d < n_cols:
+        row_got = swap(rest, "bcol", n_cols, d)
+        later.append((near, d))
+        row_keep, near, rest = split_sum(row_keep, row_got, sums[0])
+        rest = rest[0] if rest else None
         d *= 2
-    return last_sum(row_keep, row_got, col_keep, col_got[0], from_chips)
+    far = swap(near, "bcol", n_cols, d)
+    total = part_sum(row_keep, far, col_keep, col_got[0], from_chips)
+    return last_sum(total, [swap(x, "bcol", n_cols, d) for x, d in later])
 
 
 def solution(mesh):

time: 28.6 us -> 29.6 us (1.035)
  starting transfers between devices: 16.1 us -> 17.7 us
  waiting for transfers between devices: 3.27 us -> 2.33 us
    ppermute x13 -> x14, starting transfers between devices: 16.1 us -> 17.7 us  [swap(): return lax.ppermute(x, axis, [(i, i ^ d) for i in range(size)])]
    ppermute x13 -> x14, waiting for transfers between devices: 3.27 us -> 2.33 us  [swap(): return lax.ppermute(x, axis, [(i, i ^ d) for i in range(size)])]
    pallas_call x2 -> x4, Pallas kernels: 2.57 us -> 2.77 us  [the longest x1 1.93 us: backward(): pl.pallas_call(backward_kernel, in_specs=[SMEM] * 3 + [VMEM] * 2 + [ANY],...]
    unnamed x12 -> x10, local copies, waits for them, and re-layouts: 2.27 us -> 2.22 us
  transfers between devices with their start and end apart: 13 -> 14, of which waited for: 2 -> 2; matrix products, arithmetic and copies ran while one was open for 0% -> 0% of each run, Pallas kernels for 18% -> 19%
where the time goes in v16:
time: 29.6 us; the launch traced here: 29.3 us
  starting transfers between devices  17.7 us (60%)
  Pallas kernels  6.22 us (21%)
  waiting for transfers between devices  2.33 us (8%)
  local copies, waits for them, and re-layouts  2.22 us (8%)
  between operations  0.8 us (3%)
    ppermute x14, starting transfers between devices, swap(): return lax.ppermute(x, axis, [(i, i ^ d) for i in range(size)])  17.7 us
    pallas_call x1, Pallas kernels, forward(): pl.pallas_call(forward_kernel, in_specs=[SMEM] * 3 + [VMEM] * 4 + [ANY],...  2.5 us
    ppermute x14, waiting for transfers between devices, swap(): return lax.ppermute(x, axis, [(i, i ^ d) for i in range(size)])  2.33 us
    unnamed x10, local copies, waits for them, and re-layouts  2.22 us
    pallas_call x1, Pallas kernels, backward(): pl.pallas_call(backward_kernel, in_specs=[SMEM] * 3 + [VMEM] * 2 + [ANY],...  1.93 us
    pallas_call x1, Pallas kernels, last_sum(): pl.pallas_call(last_sum_kernel, in_specs=[VMEM] * (1 + len(gots)), out_sp...  0.73 us
    pallas_call x1, Pallas kernels, prep(): pl.pallas_call(prep_kernel, in_specs=[VMEM], out_specs=VMEM, out_shape=ja...  0.69 us
  transfers between devices with their start and end apart: 14, of which 2 were waited for; matrix products, arithmetic and copies ran while one was open for 0% of the time, Pallas kernels for 19%

profile of v16, /device:TPU:0, one launch (start us, length us, event | category | flops | bytes accessed | tf_op | source)
XLA Modules:
  0.0 29.3 jit_solution(1683380052400513775)
XLA Ops:
  0.0 3.0 %collective-permute-start.4 = (bf16[1,8,2048]{2,1,0:T(8,128)(2,1)}, bf16[1,8,2048]{2,1,0:T(8,128)(2,1)S(1)}, u32[]{:S(2)}, u32[]{:S(2)}) collective-permute-start(bf16[1,8,2048]{2,1,0:T(8,128)(2,1)} %bitcast.5), channel_id=1, source_target_pairs={{0,1},{1,0},{2,3},{3,2},{4,5},{5,4},{6,7},{7,6},{8,9},{9,8},{10,11... | collective-permute-start | bytes 98312 | tf_op jit(solution)/shard_map/ppermute | solution.py:418
  3.0 0.8 %copy-done.2 = bf16[8,2048]{1,0:T(8,128)(2,1)S(1)} copy-done((bf16[8,2048]{1,0:T(8,128)(2,1)S(1)}, bf16[8,2048]{1,0:T(8,128)(2,1)}, u32[]{:S(2)}) %copy-start.2) | copy-done | bytes 32792
  3.8 2.5 %collective-permute-start.2 = (f32[8,2048]{1,0:T(8,128)S(1)}, f32[8,2048]{1,0:T(8,128)S(1)}, u32[]{:S(2)}, u32[]{:S(2)}) collective-permute-start(f32[8,2048]{1,0:T(8,128)S(1)} %get-tuple-element.19), channel_id=1, source_target_pairs={{0,24},{4,28},{8,16},{12,20},{16,8},{20,12},{24,0},{28,4},{1,25},{... | collective-permute-start | bytes 196616 | tf_op jit(solution)/shard_map/ppermute | solution.py:418
  6.3 0.5 %collective-permute-start.1 = (f32[8,2048]{1,0:T(8,128)S(1)}, f32[8,2048]{1,0:T(8,128)S(1)}, u32[]{:S(2)}, u32[]{:S(2)}) collective-permute-start(f32[8,2048]{1,0:T(8,128)S(1)} %get-tuple-element.19), channel_id=1, source_target_pairs={{0,16},{4,20},{8,24},{12,28},{16,0},{20,4},{24,8},{28,12},{1,17},{... | collective-permute-start | bytes 196616 | tf_op jit(solution)/shard_map/ppermute | solution.py:418
  6.8 0.5 %collective-permute-start = (f32[8,2048]{1,0:T(8,128)S(1)}, f32[8,2048]{1,0:T(8,128)S(1)}, u32[]{:S(2)}, u32[]{:S(2)}) collective-permute-start(f32[8,2048]{1,0:T(8,128)S(1)} %get-tuple-element.19), channel_id=1, source_target_pairs={{0,8},{4,12},{8,0},{12,4},{16,24},{20,28},{24,16},{28,20},{1,9},{5... | collective-permute-start | bytes 196616 | tf_op jit(solution)/shard_map/ppermute | solution.py:418
  7.4 0.0 collective-permute-done.4.refs_1_
  7.4 2.7 %collective-permute-start.5 = (bf16[2,8,2048]{2,1,0:T(8,128)(2,1)S(1)}, bf16[2,8,2048]{2,1,0:T(8,128)(2,1)S(1)}, u32[]{:S(2)}, u32[]{:S(2)}) collective-permute-start(bf16[2,8,2048]{2,1,0:T(8,128)(2,1)S(1)} %stack_pieces.4.refs_0_), channel_id=1, source_target_pairs={{0,2},{1,3},{2,0},{3,1},{4,6},{5,7},{6,4},{7,5},{8,10},{9,11},{10,... | collective-permute-start | bytes 196616 | tf_op jit(solution)/shard_map/ppermute | solution.py:418
  10.0 1.4 %copy-done = bf16[192,4096]{1,0:T(8,128)(2,1)S(1)} copy-done((bf16[192,4096]{1,0:T(8,128)(2,1)S(1)}, bf16[192,4096]{1,0:T(8,128)(2,1)}, u32[]{:S(2)}) %copy-start) | copy-done | bytes 1572888
  11.4 0.7 %prep_tiles.1.refs_4_.tiles_ref = bf16[192,32,128]{2,1,0:T(8,128)(2,1)S(1)} custom-call(bf16[24,32,8,128]{3,2,1,0:T(8,128)(2,1)S(1)} %bitcast.4), custom_call_target="tpu_custom_call" | custom-call | bytes 3145728 | tf_op jit(solution)/shard_map/prep_tiles/pallas_call | solution.py:75
  12.2 0.0 copy-start.3
  12.2 0.0 copy-start.4
  12.2 0.0 copy-start.1
  12.2 0.0 collective-permute-done.2.refs_3_
  12.2 0.0 collective-permute-done.1.refs_2_
  12.2 0.1 collective-permute-start.3
  13.0 0.0 collective-permute-done.5.refs_1_
  13.0 1.9 %transpose_product.1 = (f32[4,8,2048]{2,1,0:T(8,128)S(1)}, f32[2,8,2048]{2,1,0:T(8,128)S(1)}, f32[2,8,2048]{2,1,0:T(8,128)S(1)}) custom-call(s32[192]{0:T(256)S(1)} %copy-done.3, s32[192]{0:T(256)S(1)} %copy-done.4, s32[1,1]{1,0:T(1,128)S(6)} %copy.7.count_ref, bf16[192,32,128]{2,1,0:T(8,128)(2,1)S(1)} %prep_tiles.1.refs_4_.tiles_ref, ...), custom_call_target="tpu_custom_call" | custom-call | flops 100663296 | bytes 3145728 | tf_op jit(solution)/shard_map/transpose_product/pallas_call | solution.py:152
  14.9 0.6 %collective-permute-start.8 = (f32[2,8,2048]{2,1,0:T(8,128)S(1)}, f32[2,8,2048]{2,1,0:T(8,128)S(1)}, u32[]{:S(2)}, u32[]{:S(2)}) collective-permute-start(f32[2,8,2048]{2,1,0:T(8,128)S(1)} %get-tuple-element.24), channel_id=1, source_target_pairs={{0,4},{4,0},{8,12},{12,8},{16,20},{20,16},{24,28},{28,24},{1,5},{5... | collective-permute-start | bytes 393224 | tf_op jit(solution)/shard_map/ppermute | solution.py:418
  15.5 0.1 collective-permute-start.7
  15.6 0.0 collective-permute-done.3.other_ref
  15.6 2.5 %forward_product.1 = (f32[2,8,2048]{2,1,0:T(8,128)S(1)}, s16[1,8,2176]{2,1,0:T(8,128)(2,1)S(1)}, s16[1,8,2176]{2,1,0:T(8,128)(2,1)S(1)}) custom-call(s32[192]{0:T(256)S(1)} %copy-done.3, s32[192]{0:T(256)S(1)} %copy-done.4, s32[1,1]{1,0:T(1,128)S(6)} %copy.7.count_ref, bf16[512,128]{1,0:T(8,128)(2,1)S(1)} %copy-done.1, ...), custom_call_target="tpu_custom_call" | custom-call | flops 100663296 | bytes 3145728 | tf_op jit(solution)/shard_map/forward_product/pallas_call | solution.py:262
  18.1 0.5 %collective-permute-start.6 = (s16[1,8,2176]{2,1,0:T(8,128)(2,1)S(1)}, s16[1,8,2176]{2,1,0:T(8,128)(2,1)S(1)}, u32[]{:S(2)}, u32[]{:S(2)}) collective-permute-start(s16[1,8,2176]{2,1,0:T(8,128)(2,1)S(1)} %get-tuple-element.22), channel_id=1, source_target_pairs={{0,1},{1,0},{2,3},{3,2},{4,5},{5,4},{6,7},{7,6},{8,9},{9,8},{10,11... | collective-permute-start | bytes 104456 | tf_op jit(solution)/shard_map/ppermute | solution.py:418
  18.7 1.5 %collective-permute-start.11 = (f32[8,2048]{1,0:T(8,128)S(1)}, f32[8,2048]{1,0:T(8,128)S(1)}, u32[]{:S(2)}, u32[]{:S(2)}) collective-permute-start(f32[8,2048]{1,0:T(8,128)S(1)} %get-tuple-element.28), channel_id=1, source_target_pairs={{0,16},{4,20},{8,24},{12,28},{16,0},{20,4},{24,8},{28,12},{1,17},{... | collective-permute-start | bytes 196616 | tf_op jit(solution)/shard_map/ppermute | solution.py:418
  20.2 1.5 %collective-permute-start.12 = (f32[8,2048]{1,0:T(8,128)S(1)}, f32[8,2048]{1,0:T(8,128)S(1)}, u32[]{:S(2)}, u32[]{:S(2)}) collective-permute-start(f32[8,2048]{1,0:T(8,128)S(1)} %get-tuple-element.29), channel_id=1, source_target_pairs={{0,24},{4,28},{8,16},{12,20},{16,8},{20,12},{24,0},{28,4},{1,25},{... | collective-permute-start | bytes 196616 | tf_op jit(solution)/shard_map/ppermute | solution.py:418
  21.7 0.5 %collective-permute-start.10 = (f32[8,2048]{1,0:T(8,128)S(1)}, f32[8,2048]{1,0:T(8,128)S(1)}, u32[]{:S(2)}, u32[]{:S(2)}) collective-permute-start(f32[8,2048]{1,0:T(8,128)S(1)} %get-tuple-element.25.after_ref), channel_id=1, source_target_pairs={{0,8},{4,12},{8,0},{12,4},{16,24},{20,28},{24,16},{28,20},{1,9},{5... | collective-permute-start | bytes 196616 | tf_op jit(solution)/shard_map/ppermute | solution.py:418
  22.2 0.2 halving_sum.1
  22.4 2.2 %collective-permute-start.9 = (s16[1,8,2176]{2,1,0:T(8,128)(2,1)S(1)}, s16[1,8,2176]{2,1,0:T(8,128)(2,1)S(1)}, u32[]{:S(2)}, u32[]{:S(2)}) collective-permute-start(s16[1,8,2176]{2,1,0:T(8,128)(2,1)S(1)} %get-tuple-element.27), channel_id=1, source_target_pairs={{0,2},{1,3},{2,0},{3,1},{4,6},{5,7},{6,4},{7,5},{8,10},{9,11},{10,... | collective-permute-start | bytes 104456 | tf_op jit(solution)/shard_map/ppermute | solution.py:418
  24.6 1.5 %collective-permute-start.13 = (s16[1,8,2176]{2,1,0:T(8,128)(2,1)S(1)}, s16[1,8,2176]{2,1,0:T(8,128)(2,1)S(1)}, u32[]{:S(2)}, u32[]{:S(2)}) collective-permute-start(s16[1,8,2176]{2,1,0:T(8,128)(2,1)S(1)} %get-tuple-element.30), channel_id=1, source_target_pairs={{0,1},{1,0},{2,3},{3,2},{4,5},{5,4},{6,7},{7,6},{8,9},{9,8},{10,11... | collective-permute-start | bytes 104456 | tf_op jit(solution)/shard_map/ppermute | solution.py:418
  26.1 1.2 %collective-permute-done.9.got_ref = s16[1,8,2176]{2,1,0:T(8,128)(2,1)S(1)} collective-permute-done((s16[1,8,2176]{2,1,0:T(8,128)(2,1)S(1)}, s16[1,8,2176]{2,1,0:T(8,128)(2,1)S(1)}, u32[]{:S(2)}, u32[]{:S(2)}) %collective-permute-start.9) | collective-permute-done | bytes 34848 | tf_op jit(solution)/shard_map/ppermute | solution.py:418
  27.3 0.1 part_sum.1.total_ref
  27.4 1.1 %collective-permute-done.13.refs_0_ = s16[1,8,2176]{2,1,0:T(8,128)(2,1)S(1)} collective-permute-done((s16[1,8,2176]{2,1,0:T(8,128)(2,1)S(1)}, s16[1,8,2176]{2,1,0:T(8,128)(2,1)S(1)}, u32[]{:S(2)}, u32[]{:S(2)}) %collective-permute-start.13) | collective-permute-done | bytes 34848 | tf_op jit(solution)/shard_map/ppermute | solution.py:418
  28.6 0.7 %last_sum.1 = f32[8,2048]{1,0:T(8,128)} custom-call(f32[8,2048]{1,0:T(8,128)S(1)} %part_sum.1.total_ref, s16[1,8,2176]{2,1,0:T(8,128)(2,1)S(1)} %collective-permute-done.13.refs_0_), custom_call_target="tpu_custom_call" | custom-call | tf_op jit(solution)/shard_map/last_sum/pallas_call | solution.py:388
  (17 shorter events, 0.1 us)
Async XLA Ops:
  0.0 7.4 %collective-permute-start.4 = (bf16[1,8,2048]{2,1,0:T(8,128)(2,1)}, bf16[1,8,2048]{2,1,0:T(8,128)(2,1)S(1)}, u32[]{:S(2)}, u32[]{:S(2)}) collective-permute-start(bf16[1,8,2048]{2,1,0:T(8,128)(2,1)} %bitcast.5), channel_id=1, source_target_pairs={{0,1},{1,0},{2,3},{3,2},{4,5},{5,4},{6,7},{7,6},{8,9},{9,8},{10,11... | collective-permute-start | bytes 98312 | tf_op jit(solution)/shard_map/ppermute | solution.py:418
  3.0 0.8 %copy-start.2 = (bf16[8,2048]{1,0:T(8,128)(2,1)S(1)}, bf16[8,2048]{1,0:T(8,128)(2,1)}, u32[]{:S(2)}) copy-start(bf16[8,2048]{1,0:T(8,128)(2,1)} %x_ref.1) | copy-start | bytes 98308
  3.8 8.4 %collective-permute-start.2 = (f32[8,2048]{1,0:T(8,128)S(1)}, f32[8,2048]{1,0:T(8,128)S(1)}, u32[]{:S(2)}, u32[]{:S(2)}) collective-permute-start(f32[8,2048]{1,0:T(8,128)S(1)} %get-tuple-element.19), channel_id=1, source_target_pairs={{0,24},{4,28},{8,16},{12,20},{16,8},{20,12},{24,0},{28,4},{1,25},{... | collective-permute-start | bytes 196616 | tf_op jit(solution)/shard_map/ppermute | solution.py:418
  6.3 5.9 %collective-permute-start.1 = (f32[8,2048]{1,0:T(8,128)S(1)}, f32[8,2048]{1,0:T(8,128)S(1)}, u32[]{:S(2)}, u32[]{:S(2)}) collective-permute-start(f32[8,2048]{1,0:T(8,128)S(1)} %get-tuple-element.19), channel_id=1, source_target_pairs={{0,16},{4,20},{8,24},{12,28},{16,0},{20,4},{24,8},{28,12},{1,17},{... | collective-permute-start | bytes 196616 | tf_op jit(solution)/shard_map/ppermute | solution.py:418
  6.8 5.4 %collective-permute-start = (f32[8,2048]{1,0:T(8,128)S(1)}, f32[8,2048]{1,0:T(8,128)S(1)}, u32[]{:S(2)}, u32[]{:S(2)}) collective-permute-start(f32[8,2048]{1,0:T(8,128)S(1)} %get-tuple-element.19), channel_id=1, source_target_pairs={{0,8},{4,12},{8,0},{12,4},{16,24},{20,28},{24,16},{28,20},{1,9},{5... | collective-permute-start | bytes 196616 | tf_op jit(solution)/shard_map/ppermute | solution.py:418
  7.4 5.6 %collective-permute-start.5 = (bf16[2,8,2048]{2,1,0:T(8,128)(2,1)S(1)}, bf16[2,8,2048]{2,1,0:T(8,128)(2,1)S(1)}, u32[]{:S(2)}, u32[]{:S(2)}) collective-permute-start(bf16[2,8,2048]{2,1,0:T(8,128)(2,1)S(1)} %stack_pieces.4.refs_0_), channel_id=1, source_target_pairs={{0,2},{1,3},{2,0},{3,1},{4,6},{5,7},{6,4},{7,5},{8,10},{9,11},{10,... | collective-permute-start | bytes 196616 | tf_op jit(solution)/shard_map/ppermute | solution.py:418
  10.0 1.4 %copy-start = (bf16[192,4096]{1,0:T(8,128)(2,1)S(1)}, bf16[192,4096]{1,0:T(8,128)(2,1)}, u32[]{:S(2)}) copy-start(bf16[192,4096]{1,0:T(8,128)(2,1)} %param.7) | copy-start | bytes 4718596
  12.2 0.8 %copy-start.3 = (s32[192]{0:T(256)S(1)}, s32[192]{0:T(256)}, u32[]{:S(2)}) copy-start(s32[192]{0:T(256)} %rows_ref.3) | copy-start | bytes 2308
  12.2 0.8 %copy-start.4 = (s32[192]{0:T(256)S(1)}, s32[192]{0:T(256)}, u32[]{:S(2)}) copy-start(s32[192]{0:T(256)} %cols_ref.3) | copy-start | bytes 2308
  12.2 3.4 %copy-start.1 = (bf16[512,128]{1,0:T(8,128)(2,1)S(1)}, bf16[512,128]{1,0:T(8,128)(2,1)}, u32[]{:S(2)}) copy-start(bf16[512,128]{1,0:T(8,128)(2,1)} %constant.2.clone.fold_ref) | copy-start | bytes 393220
  12.2 3.4 %collective-permute-start.3 = (bf16[4,8,2048]{2,1,0:T(8,128)(2,1)S(1)}, bf16[4,8,2048]{2,1,0:T(8,128)(2,1)S(1)}, u32[]{:S(2)}, u32[]{:S(2)}) collective-permute-start(bf16[4,8,2048]{2,1,0:T(8,128)(2,1)S(1)} %stack_pieces.3.after_ref.same_ref), channel_id=1, source_target_pairs={{0,4},{4,0},{8,12},{12,8},{16,20},{20,16},{24,28},{28,24},{1,5},{5... | collective-permute-start | bytes 393224 | tf_op jit(solution)/shard_map/ppermute | solution.py:418
  14.9 3.7 %collective-permute-start.8 = (f32[2,8,2048]{2,1,0:T(8,128)S(1)}, f32[2,8,2048]{2,1,0:T(8,128)S(1)}, u32[]{:S(2)}, u32[]{:S(2)}) collective-permute-start(f32[2,8,2048]{2,1,0:T(8,128)S(1)} %get-tuple-element.24), channel_id=1, source_target_pairs={{0,4},{4,0},{8,12},{12,8},{16,20},{20,16},{24,28},{28,24},{1,5},{5... | collective-permute-start | bytes 393224 | tf_op jit(solution)/shard_map/ppermute | solution.py:418
  15.5 3.1 %collective-permute-start.7 = (f32[2,8,2048]{2,1,0:T(8,128)S(1)}, f32[2,8,2048]{2,1,0:T(8,128)S(1)}, u32[]{:S(2)}, u32[]{:S(2)}) collective-permute-start(f32[2,8,2048]{2,1,0:T(8,128)S(1)} %get-tuple-element.20.after_ref), channel_id=1, source_target_pairs={{0,4},{4,0},{8,12},{12,8},{16,20},{20,16},{24,28},{28,24},{1,5},{5... | collective-permute-start | bytes 393224 | tf_op jit(solution)/shard_map/ppermute | solution.py:418
  18.1 4.1 %collective-permute-start.6 = (s16[1,8,2176]{2,1,0:T(8,128)(2,1)S(1)}, s16[1,8,2176]{2,1,0:T(8,128)(2,1)S(1)}, u32[]{:S(2)}, u32[]{:S(2)}) collective-permute-start(s16[1,8,2176]{2,1,0:T(8,128)(2,1)S(1)} %get-tuple-element.22), channel_id=1, source_target_pairs={{0,1},{1,0},{2,3},{3,2},{4,5},{5,4},{6,7},{7,6},{8,9},{9,8},{10,11... | collective-permute-start | bytes 104456 | tf_op jit(solution)/shard_map/ppermute | solution.py:418
  18.7 8.7 %collective-permute-start.11 = (f32[8,2048]{1,0:T(8,128)S(1)}, f32[8,2048]{1,0:T(8,128)S(1)}, u32[]{:S(2)}, u32[]{:S(2)}) collective-permute-start(f32[8,2048]{1,0:T(8,128)S(1)} %get-tuple-element.28), channel_id=1, source_target_pairs={{0,16},{4,20},{8,24},{12,28},{16,0},{20,4},{24,8},{28,12},{1,17},{... | collective-permute-start | bytes 196616 | tf_op jit(solution)/shard_map/ppermute | solution.py:418
  20.2 7.2 %collective-permute-start.12 = (f32[8,2048]{1,0:T(8,128)S(1)}, f32[8,2048]{1,0:T(8,128)S(1)}, u32[]{:S(2)}, u32[]{:S(2)}) collective-permute-start(f32[8,2048]{1,0:T(8,128)S(1)} %get-tuple-element.29), channel_id=1, source_target_pairs={{0,24},{4,28},{8,16},{12,20},{16,8},{20,12},{24,0},{28,4},{1,25},{... | collective-permute-start | bytes 196616 | tf_op jit(solution)/shard_map/ppermute | solution.py:418
  21.7 5.7 %collective-permute-start.10 = (f32[8,2048]{1,0:T(8,128)S(1)}, f32[8,2048]{1,0:T(8,128)S(1)}, u32[]{:S(2)}, u32[]{:S(2)}) collective-permute-start(f32[8,2048]{1,0:T(8,128)S(1)} %get-tuple-element.25.after_ref), channel_id=1, source_target_pairs={{0,8},{4,12},{8,0},{12,4},{16,24},{20,28},{24,16},{28,20},{1,9},{5... | collective-permute-start | bytes 196616 | tf_op jit(solution)/shard_map/ppermute | solution.py:418
  22.4 4.9 %collective-permute-start.9 = (s16[1,8,2176]{2,1,0:T(8,128)(2,1)S(1)}, s16[1,8,2176]{2,1,0:T(8,128)(2,1)S(1)}, u32[]{:S(2)}, u32[]{:S(2)}) collective-permute-start(s16[1,8,2176]{2,1,0:T(8,128)(2,1)S(1)} %get-tuple-element.27), channel_id=1, source_target_pairs={{0,2},{1,3},{2,0},{3,1},{4,6},{5,7},{6,4},{7,5},{8,10},{9,11},{10,... | collective-permute-start | bytes 104456 | tf_op jit(solution)/shard_map/ppermute | solution.py:418
  24.6 3.9 %collective-permute-start.13 = (s16[1,8,2176]{2,1,0:T(8,128)(2,1)S(1)}, s16[1,8,2176]{2,1,0:T(8,128)(2,1)S(1)}, u32[]{:S(2)}, u32[]{:S(2)}) collective-permute-start(s16[1,8,2176]{2,1,0:T(8,128)(2,1)S(1)} %get-tuple-element.30), channel_id=1, source_target_pairs={{0,1},{1,0},{2,3},{3,2},{4,5},{5,4},{6,7},{7,6},{8,9},{9,8},{10,11... | collective-permute-start | bytes 104456 | tf_op jit(solution)/shard_map/ppermute | solution.py:418

commit v17 on v10

--- a/solution.py
+++ b/solution.py
@@ -375,13 +375,13 @@
 def body(vectors, tiles, tile_rows, tile_cols, counts):
     n_rows = lax.axis_size("brow")
     n_cols = lax.axis_size("bcol")
-    own = stack(vectors)
+    own = swap(vectors, "brow", n_rows, 0)[None]
     chips = [swap(vectors, "brow", n_rows, 2 * h) for h in range(1, n_rows // 2)]
     segment, d = own, 1
     while d < n_cols:
         segment = stack(segment, swap(segment if d > 1 else vectors[None], "bcol", n_cols, d))
         d *= 2
-    blocks = prep(tiles)
+    blocks = prep(swap(tiles, "brow", n_rows, 0))
     same = stack(own, *chips, after=(blocks,))
     other = swap(same, "brow", n_rows, 1)
 

time: 28.6 us -> 30.1 us (1.052)
  local copies, waits for them, and re-layouts: 2.27 us -> 0.03 us
  waiting for transfers between devices: 3.27 us -> 5.08 us
  starting transfers between devices: 16.1 us -> 17.9 us
    unnamed x12 -> x8, local copies, waits for them, and re-layouts: 2.27 us -> 0.03 us
    ppermute x13 -> x15, starting transfers between devices: 16.1 us -> 17.9 us  [swap(): return lax.ppermute(x, axis, [(i, i ^ d) for i in range(size)])]
    ppermute x13 -> x15, waiting for transfers between devices: 3.27 us -> 5.08 us  [swap(): return lax.ppermute(x, axis, [(i, i ^ d) for i in range(size)])]
  transfers between devices with their start and end apart: 13 -> 15, of which waited for: 2 -> 5; matrix products, arithmetic and copies ran while one was open for 0% -> 0% of each run, Pallas kernels for 18% -> 18%
where the time goes in v17:
time: 30.1 us; the launch traced here: 29.9 us
  starting transfers between devices  17.9 us (59%)
  Pallas kernels  6.11 us (20%)
  waiting for transfers between devices  5.08 us (17%)
  between operations  0.81 us (3%)
    ppermute x15, starting transfers between devices, swap(): return lax.ppermute(x, axis, [(i, i ^ d) for i in range(size)])  17.9 us
    ppermute x15, waiting for transfers between devices, swap(): return lax.ppermute(x, axis, [(i, i ^ d) for i in range(size)])  5.08 us
    pallas_call x1, Pallas kernels, forward(): pl.pallas_call(forward_kernel, in_specs=[SMEM] * 3 + [VMEM] * 4 + [ANY],...  2.53 us
    pallas_call x1, Pallas kernels, backward(): pl.pallas_call(backward_kernel, in_specs=[SMEM] * 3 + [VMEM] * 3 + [ANY],...  1.89 us
    pallas_call x1, Pallas kernels, last_sum(): pl.pallas_call(last_sum_kernel, in_specs=[VMEM] * (4 + len(chips)), out_s...  0.74 us
    pallas_call x1, Pallas kernels, prep(): pl.pallas_call(prep_kernel, in_specs=[VMEM], out_specs=VMEM, out_shape=ja...  0.69 us
  transfers between devices with their start and end apart: 15, of which 5 were waited for; matrix products, arithmetic and copies ran while one was open for 0% of the time, Pallas kernels for 18%

profile of v17, /device:TPU:0, one launch (start us, length us, event | category | flops | bytes accessed | tf_op | source)
XLA Modules:
  0.0 29.9 jit_solution(8333433382353034548)
XLA Ops:
  0.0 1.4 %collective-permute-start = (bf16[192,4096]{1,0:T(8,128)(2,1)}, bf16[192,4096]{1,0:T(8,128)(2,1)S(1)}, u32[]{:S(2)}, u32[]{:S(2)}) collective-permute-start(bf16[192,4096]{1,0:T(8,128)(2,1)} %param.8), channel_id=1, source_target_pairs={{0,0},{4,4},{8,8},{12,12},{16,16},{20,20},{24,24},{28,28},{1,1},{5... | collective-permute-start | bytes 4718600 | tf_op jit(solution)/shard_map/ppermute | solution.py:372
  1.4 0.8 %collective-permute-start.1 = (bf16[8,2048]{1,0:T(8,128)(2,1)}, bf16[8,2048]{1,0:T(8,128)(2,1)S(1)}, u32[]{:S(2)}, u32[]{:S(2)}) collective-permute-start(bf16[8,2048]{1,0:T(8,128)(2,1)} %param.7), channel_id=1, source_target_pairs={{0,0},{4,4},{8,8},{12,12},{16,16},{20,20},{24,24},{28,28},{1,1},{5... | collective-permute-start | bytes 98312 | tf_op jit(solution)/shard_map/ppermute | solution.py:372
  2.2 3.0 %collective-permute-start.2 = (bf16[1,8,2048]{2,1,0:T(8,128)(2,1)}, bf16[1,8,2048]{2,1,0:T(8,128)(2,1)S(1)}, u32[]{:S(2)}, u32[]{:S(2)}) collective-permute-start(bf16[1,8,2048]{2,1,0:T(8,128)(2,1)} %bitcast.8), channel_id=1, source_target_pairs={{0,1},{1,0},{2,3},{3,2},{4,5},{5,4},{6,7},{7,6},{8,9},{9,8},{10,11... | collective-permute-start | bytes 98312 | tf_op jit(solution)/shard_map/ppermute | solution.py:372
  5.2 1.5 %collective-permute-start.4 = (bf16[8,2048]{1,0:T(8,128)(2,1)}, bf16[8,2048]{1,0:T(8,128)(2,1)S(1)}, u32[]{:S(2)}, u32[]{:S(2)}) collective-permute-start(bf16[8,2048]{1,0:T(8,128)(2,1)} %param.7), channel_id=1, source_target_pairs={{0,8},{4,12},{8,0},{12,4},{16,24},{20,28},{24,16},{28,20},{1,9},{5... | collective-permute-start | bytes 98312 | tf_op jit(solution)/shard_map/ppermute | solution.py:372
  6.7 1.5 %collective-permute-start.5 = (bf16[8,2048]{1,0:T(8,128)(2,1)}, bf16[8,2048]{1,0:T(8,128)(2,1)S(1)}, u32[]{:S(2)}, u32[]{:S(2)}) collective-permute-start(bf16[8,2048]{1,0:T(8,128)(2,1)} %param.7), channel_id=1, source_target_pairs={{0,16},{4,20},{8,24},{12,28},{16,0},{20,4},{24,8},{28,12},{1,17},{... | collective-permute-start | bytes 98312 | tf_op jit(solution)/shard_map/ppermute | solution.py:372
  8.2 0.5 %collective-permute-start.6 = (bf16[8,2048]{1,0:T(8,128)(2,1)}, bf16[8,2048]{1,0:T(8,128)(2,1)S(1)}, u32[]{:S(2)}, u32[]{:S(2)}) collective-permute-start(bf16[8,2048]{1,0:T(8,128)(2,1)} %param.7), channel_id=1, source_target_pairs={{0,24},{4,28},{8,16},{12,20},{16,8},{20,12},{24,0},{28,4},{1,25},{... | collective-permute-start | bytes 98312 | tf_op jit(solution)/shard_map/ppermute | solution.py:372
  8.7 2.7 %collective-permute-start.3 = (bf16[2,8,2048]{2,1,0:T(8,128)(2,1)S(1)}, bf16[2,8,2048]{2,1,0:T(8,128)(2,1)S(1)}, u32[]{:S(2)}, u32[]{:S(2)}) collective-permute-start(bf16[2,8,2048]{2,1,0:T(8,128)(2,1)S(1)} %stack_pieces.3.refs_0_), channel_id=1, source_target_pairs={{0,2},{1,3},{2,0},{3,1},{4,6},{5,7},{6,4},{7,5},{8,10},{9,11},{10,... | collective-permute-start | bytes 196616 | tf_op jit(solution)/shard_map/ppermute | solution.py:372
  11.4 0.7 %prep_tiles.1.refs_4_.tiles_ref = bf16[192,32,128]{2,1,0:T(8,128)(2,1)S(1)} custom-call(bf16[24,32,8,128]{3,2,1,0:T(8,128)(2,1)S(1)} %bitcast.5), custom_call_target="tpu_custom_call" | custom-call | bytes 3145728 | tf_op jit(solution)/shard_map/prep_tiles/pallas_call | solution.py:77
  12.1 0.0 copy-start
  12.1 0.0 copy-start.2
  12.1 0.0 copy-start.3
  12.1 0.0 collective-permute-done.4.refs_1_
  12.1 1.1 %collective-permute-done.6.refs_3_ = bf16[8,2048]{1,0:T(8,128)(2,1)S(1)} collective-permute-done((bf16[8,2048]{1,0:T(8,128)(2,1)}, bf16[8,2048]{1,0:T(8,128)(2,1)S(1)}, u32[]{:S(2)}, u32[]{:S(2)}) %collective-permute-start.6) | collective-permute-done | bytes 32800 | tf_op jit(solution)/shard_map/ppermute | solution.py:372
  13.2 0.0 copy-start.1
  13.3 0.1 collective-permute-start.12
  14.0 0.6 %collective-permute-done.3.refs_1_ = bf16[2,8,2048]{2,1,0:T(8,128)(2,1)S(1)} collective-permute-done((bf16[2,8,2048]{2,1,0:T(8,128)(2,1)S(1)}, bf16[2,8,2048]{2,1,0:T(8,128)(2,1)S(1)}, u32[]{:S(2)}, u32[]{:S(2)}) %collective-permute-start.3) | collective-permute-done | bytes 65568 | tf_op jit(solution)/shard_map/ppermute | solution.py:372
  14.7 1.9 %transpose_product.1 = (f32[4,8,2048]{2,1,0:T(8,128)S(1)}, f32[2,8,2048]{2,1,0:T(8,128)S(1)}, f32[2,8,2048]{2,1,0:T(8,128)S(1)}) custom-call(s32[192]{0:T(256)S(1)} %copy-done.2, s32[192]{0:T(256)S(1)} %copy-done.3, s32[1,1]{1,0:T(1,128)S(6)} %copy.8.count_ref, bf16[128,512]{1,0:T(8,128)(2,1)S(1)} %copy-done, ...), custom_call_target="tpu_custom_call" | custom-call | flops 100663296 | bytes 3145728 | tf_op jit(solution)/shard_map/transpose_product/pallas_call | solution.py:154
  16.6 0.1 collective-permute-start.7
  16.7 0.5 %collective-permute-start.8 = (f32[2,8,2048]{2,1,0:T(8,128)S(1)}, f32[2,8,2048]{2,1,0:T(8,128)S(1)}, u32[]{:S(2)}, u32[]{:S(2)}) collective-permute-start(f32[2,8,2048]{2,1,0:T(8,128)S(1)} %get-tuple-element.17), channel_id=1, source_target_pairs={{0,4},{4,0},{8,12},{12,8},{16,20},{20,16},{24,28},{28,24},{1,5},{5... | collective-permute-start | bytes 393224 | tf_op jit(solution)/shard_map/ppermute | solution.py:372
  17.1 0.0 collective-permute-done.12.other_ref
  17.2 2.5 %forward_product.1 = (f32[2,8,2048]{2,1,0:T(8,128)S(1)}, s16[2,8,2176]{2,1,0:T(8,128)(2,1)S(1)}) custom-call(s32[192]{0:T(256)S(1)} %copy-done.2, s32[192]{0:T(256)S(1)} %copy-done.3, s32[1,1]{1,0:T(1,128)S(6)} %copy.8.count_ref, bf16[512,128]{1,0:T(8,128)(2,1)S(1)} %copy-done.1, bf16[192,32,128]{2,1,0:T(8,128)(2,1)S(1)} %prep_tiles.1.refs_4_.tiles_ref, ...), custom_call_target="tpu_custom_call" | custom-call | flops 100663296 | bytes 3145728 | tf_op jit(solution)/shard_map/forward_product/pallas_call | solution.py:262
  19.7 0.1 collective-permute-start.13
  19.8 0.0 collective-permute-done.8.refs_1_
  19.8 1.5 %collective-permute-start.9 = (f32[8,2048]{1,0:T(8,128)S(1)}, f32[8,2048]{1,0:T(8,128)S(1)}, u32[]{:S(2)}, u32[]{:S(2)}) collective-permute-start(f32[8,2048]{1,0:T(8,128)S(1)} %get-tuple-element.18.after_ref), channel_id=1, source_target_pairs={{0,8},{4,12},{8,0},{12,4},{16,24},{20,28},{24,16},{28,20},{1,9},{5... | collective-permute-start | bytes 196616 | tf_op jit(solution)/shard_map/ppermute | solution.py:372
  21.3 1.5 %collective-permute-start.10 = (f32[8,2048]{1,0:T(8,128)S(1)}, f32[8,2048]{1,0:T(8,128)S(1)}, u32[]{:S(2)}, u32[]{:S(2)}) collective-permute-start(f32[8,2048]{1,0:T(8,128)S(1)} %get-tuple-element.19), channel_id=1, source_target_pairs={{0,16},{4,20},{8,24},{12,28},{16,0},{20,4},{24,8},{28,12},{1,17},{... | collective-permute-start | bytes 196616 | tf_op jit(solution)/shard_map/ppermute | solution.py:372
  22.8 0.6 %collective-permute-start.11 = (f32[8,2048]{1,0:T(8,128)S(1)}, f32[8,2048]{1,0:T(8,128)S(1)}, u32[]{:S(2)}, u32[]{:S(2)}) collective-permute-start(f32[8,2048]{1,0:T(8,128)S(1)} %get-tuple-element.20), channel_id=1, source_target_pairs={{0,24},{4,28},{8,16},{12,20},{16,8},{20,12},{24,0},{28,4},{1,25},{... | collective-permute-start | bytes 196616 | tf_op jit(solution)/shard_map/ppermute | solution.py:372
  23.4 0.7 %collective-permute-done.13.got_ref = s16[2,8,2176]{2,1,0:T(8,128)(2,1)S(1)} collective-permute-done((s16[2,8,2176]{2,1,0:T(8,128)(2,1)S(1)}, s16[2,8,2176]{2,1,0:T(8,128)(2,1)S(1)}, u32[]{:S(2)}, u32[]{:S(2)}) %collective-permute-start.13) | collective-permute-done | bytes 69664 | tf_op jit(solution)/shard_map/ppermute | solution.py:372
  24.1 0.2 halving_sum.1
  24.3 2.3 %collective-permute-start.14 = (s16[1,8,2176]{2,1,0:T(8,128)(2,1)S(1)}, s16[1,8,2176]{2,1,0:T(8,128)(2,1)S(1)}, u32[]{:S(2)}, u32[]{:S(2)}) collective-permute-start(s16[1,8,2176]{2,1,0:T(8,128)(2,1)S(1)} %get-tuple-element.24), channel_id=1, source_target_pairs={{0,2},{1,3},{2,0},{3,1},{4,6},{5,7},{6,4},{7,5},{8,10},{9,11},{10,... | collective-permute-start | bytes 104456 | tf_op jit(solution)/shard_map/ppermute | solution.py:372
  26.6 1.4 %collective-permute-done.11.refs_2_ = f32[8,2048]{1,0:T(8,128)S(1)} collective-permute-done((f32[8,2048]{1,0:T(8,128)S(1)}, f32[8,2048]{1,0:T(8,128)S(1)}, u32[]{:S(2)}, u32[]{:S(2)}) %collective-permute-start.11) | collective-permute-done | bytes 65568 | tf_op jit(solution)/shard_map/ppermute | solution.py:372
  28.0 1.2 %collective-permute-done.14.refs_6_ = s16[1,8,2176]{2,1,0:T(8,128)(2,1)S(1)} collective-permute-done((s16[1,8,2176]{2,1,0:T(8,128)(2,1)S(1)}, s16[1,8,2176]{2,1,0:T(8,128)(2,1)S(1)}, u32[]{:S(2)}, u32[]{:S(2)}) %collective-permute-start.14) | collective-permute-done | bytes 34848 | tf_op jit(solution)/shard_map/ppermute | solution.py:372
  29.2 0.7 %last_sum.1 = f32[8,2048]{1,0:T(8,128)} custom-call(f32[8,2048]{1,0:T(8,128)S(1)} %collective-permute-done.9.refs_0_, f32[8,2048]{1,0:T(8,128)S(1)} %collective-permute-done.10.refs_1_, f32[8,2048]{1,0:T(8,128)S(1)} %collective-permute-done.11.refs_2_, f32[4,8,2048]{2,1,0:T(8,128)S(1)} %get-tuple-element.15.keep_ref.refs_3_, ...), custom_call_target="tpu_custom_call" | custom-call | tf_op jit(solution)/shard_map/last_sum/pallas_call | solution.py:361
  (15 shorter events, 0.1 us)
Async XLA Ops:
  0.0 11.4 %collective-permute-start = (bf16[192,4096]{1,0:T(8,128)(2,1)}, bf16[192,4096]{1,0:T(8,128)(2,1)S(1)}, u32[]{:S(2)}, u32[]{:S(2)}) collective-permute-start(bf16[192,4096]{1,0:T(8,128)(2,1)} %param.8), channel_id=1, source_target_pairs={{0,0},{4,4},{8,8},{12,12},{16,16},{20,20},{24,24},{28,28},{1,1},{5... | collective-permute-start | bytes 4718600 | tf_op jit(solution)/shard_map/ppermute | solution.py:372
  1.4 6.8 %collective-permute-start.1 = (bf16[8,2048]{1,0:T(8,128)(2,1)}, bf16[8,2048]{1,0:T(8,128)(2,1)S(1)}, u32[]{:S(2)}, u32[]{:S(2)}) collective-permute-start(bf16[8,2048]{1,0:T(8,128)(2,1)} %param.7), channel_id=1, source_target_pairs={{0,0},{4,4},{8,8},{12,12},{16,16},{20,20},{24,24},{28,28},{1,1},{5... | collective-permute-start | bytes 98312 | tf_op jit(solution)/shard_map/ppermute | solution.py:372
  2.2 6.5 %collective-permute-start.2 = (bf16[1,8,2048]{2,1,0:T(8,128)(2,1)}, bf16[1,8,2048]{2,1,0:T(8,128)(2,1)S(1)}, u32[]{:S(2)}, u32[]{:S(2)}) collective-permute-start(bf16[1,8,2048]{2,1,0:T(8,128)(2,1)} %bitcast.8), channel_id=1, source_target_pairs={{0,1},{1,0},{2,3},{3,2},{4,5},{5,4},{6,7},{7,6},{8,9},{9,8},{10,11... | collective-permute-start | bytes 98312 | tf_op jit(solution)/shard_map/ppermute | solution.py:372
  5.2 6.9 %collective-permute-start.4 = (bf16[8,2048]{1,0:T(8,128)(2,1)}, bf16[8,2048]{1,0:T(8,128)(2,1)S(1)}, u32[]{:S(2)}, u32[]{:S(2)}) collective-permute-start(bf16[8,2048]{1,0:T(8,128)(2,1)} %param.7), channel_id=1, source_target_pairs={{0,8},{4,12},{8,0},{12,4},{16,24},{20,28},{24,16},{28,20},{1,9},{5... | collective-permute-start | bytes 98312 | tf_op jit(solution)/shard_map/ppermute | solution.py:372
  6.7 5.4 %collective-permute-start.5 = (bf16[8,2048]{1,0:T(8,128)(2,1)}, bf16[8,2048]{1,0:T(8,128)(2,1)S(1)}, u32[]{:S(2)}, u32[]{:S(2)}) collective-permute-start(bf16[8,2048]{1,0:T(8,128)(2,1)} %param.7), channel_id=1, source_target_pairs={{0,16},{4,20},{8,24},{12,28},{16,0},{20,4},{24,8},{28,12},{1,17},{... | collective-permute-start | bytes 98312 | tf_op jit(solution)/shard_map/ppermute | solution.py:372
  8.2 5.0 %collective-permute-start.6 = (bf16[8,2048]{1,0:T(8,128)(2,1)}, bf16[8,2048]{1,0:T(8,128)(2,1)S(1)}, u32[]{:S(2)}, u32[]{:S(2)}) collective-permute-start(bf16[8,2048]{1,0:T(8,128)(2,1)} %param.7), channel_id=1, source_target_pairs={{0,24},{4,28},{8,16},{12,20},{16,8},{20,12},{24,0},{28,4},{1,25},{... | collective-permute-start | bytes 98312 | tf_op jit(solution)/shard_map/ppermute | solution.py:372
  8.7 5.9 %collective-permute-start.3 = (bf16[2,8,2048]{2,1,0:T(8,128)(2,1)S(1)}, bf16[2,8,2048]{2,1,0:T(8,128)(2,1)S(1)}, u32[]{:S(2)}, u32[]{:S(2)}) collective-permute-start(bf16[2,8,2048]{2,1,0:T(8,128)(2,1)S(1)} %stack_pieces.3.refs_0_), channel_id=1, source_target_pairs={{0,2},{1,3},{2,0},{3,1},{4,6},{5,7},{6,4},{7,5},{8,10},{9,11},{10,... | collective-permute-start | bytes 196616 | tf_op jit(solution)/shard_map/ppermute | solution.py:372
  12.1 2.6 %copy-start = (bf16[128,512]{1,0:T(8,128)(2,1)S(1)}, bf16[128,512]{1,0:T(8,128)(2,1)}, u32[]{:S(2)}) copy-start(bf16[128,512]{1,0:T(8,128)(2,1)} %constant.4.clone.spread_ref) | copy-start | bytes 393220
  12.1 2.6 %copy-start.2 = (s32[192]{0:T(256)S(1)}, s32[192]{0:T(256)}, u32[]{:S(2)}) copy-start(s32[192]{0:T(256)} %rows_ref.3) | copy-start | bytes 2308
  12.1 2.6 %copy-start.3 = (s32[192]{0:T(256)S(1)}, s32[192]{0:T(256)}, u32[]{:S(2)}) copy-start(s32[192]{0:T(256)} %cols_ref.3) | copy-start | bytes 2308
  13.2 3.9 %copy-start.1 = (bf16[512,128]{1,0:T(8,128)(2,1)S(1)}, bf16[512,128]{1,0:T(8,128)(2,1)}, u32[]{:S(2)}) copy-start(bf16[512,128]{1,0:T(8,128)(2,1)} %constant.5.clone.fold_ref) | copy-start | bytes 393220
  13.3 3.9 %collective-permute-start.12 = (bf16[4,8,2048]{2,1,0:T(8,128)(2,1)S(1)}, bf16[4,8,2048]{2,1,0:T(8,128)(2,1)S(1)}, u32[]{:S(2)}, u32[]{:S(2)}) collective-permute-start(bf16[4,8,2048]{2,1,0:T(8,128)(2,1)S(1)} %stack_pieces.5.after_ref.same_ref), channel_id=1, source_target_pairs={{0,4},{4,0},{8,12},{12,8},{16,20},{20,16},{24,28},{28,24},{1,5},{5... | collective-permute-start | bytes 393224 | tf_op jit(solution)/shard_map/ppermute | solution.py:372
  16.6 3.2 %collective-permute-start.7 = (f32[2,8,2048]{2,1,0:T(8,128)S(1)}, f32[2,8,2048]{2,1,0:T(8,128)S(1)}, u32[]{:S(2)}, u32[]{:S(2)}) collective-permute-start(f32[2,8,2048]{2,1,0:T(8,128)S(1)} %get-tuple-element.16.after_ref), channel_id=1, source_target_pairs={{0,4},{4,0},{8,12},{12,8},{16,20},{20,16},{24,28},{28,24},{1,5},{5... | collective-permute-start | bytes 393224 | tf_op jit(solution)/shard_map/ppermute | solution.py:372
  16.7 3.1 %collective-permute-start.8 = (f32[2,8,2048]{2,1,0:T(8,128)S(1)}, f32[2,8,2048]{2,1,0:T(8,128)S(1)}, u32[]{:S(2)}, u32[]{:S(2)}) collective-permute-start(f32[2,8,2048]{2,1,0:T(8,128)S(1)} %get-tuple-element.17), channel_id=1, source_target_pairs={{0,4},{4,0},{8,12},{12,8},{16,20},{20,16},{24,28},{28,24},{1,5},{5... | collective-permute-start | bytes 393224 | tf_op jit(solution)/shard_map/ppermute | solution.py:372
  19.7 4.4 %collective-permute-start.13 = (s16[2,8,2176]{2,1,0:T(8,128)(2,1)S(1)}, s16[2,8,2176]{2,1,0:T(8,128)(2,1)S(1)}, u32[]{:S(2)}, u32[]{:S(2)}) collective-permute-start(s16[2,8,2176]{2,1,0:T(8,128)(2,1)S(1)} %get-tuple-element.22), channel_id=1, source_target_pairs={{0,1},{1,0},{2,3},{3,2},{4,5},{5,4},{6,7},{7,6},{8,9},{9,8},{10,11... | collective-permute-start | bytes 208904 | tf_op jit(solution)/shard_map/ppermute | solution.py:372
  19.8 6.8 %collective-permute-start.9 = (f32[8,2048]{1,0:T(8,128)S(1)}, f32[8,2048]{1,0:T(8,128)S(1)}, u32[]{:S(2)}, u32[]{:S(2)}) collective-permute-start(f32[8,2048]{1,0:T(8,128)S(1)} %get-tuple-element.18.after_ref), channel_id=1, source_target_pairs={{0,8},{4,12},{8,0},{12,4},{16,24},{20,28},{24,16},{28,20},{1,9},{5... | collective-permute-start | bytes 196616 | tf_op jit(solution)/shard_map/ppermute | solution.py:372
  21.3 5.3 %collective-permute-start.10 = (f32[8,2048]{1,0:T(8,128)S(1)}, f32[8,2048]{1,0:T(8,128)S(1)}, u32[]{:S(2)}, u32[]{:S(2)}) collective-permute-start(f32[8,2048]{1,0:T(8,128)S(1)} %get-tuple-element.19), channel_id=1, source_target_pairs={{0,16},{4,20},{8,24},{12,28},{16,0},{20,4},{24,8},{28,12},{1,17},{... | collective-permute-start | bytes 196616 | tf_op jit(solution)/shard_map/ppermute | solution.py:372
  22.8 5.2 %collective-permute-start.11 = (f32[8,2048]{1,0:T(8,128)S(1)}, f32[8,2048]{1,0:T(8,128)S(1)}, u32[]{:S(2)}, u32[]{:S(2)}) collective-permute-start(f32[8,2048]{1,0:T(8,128)S(1)} %get-tuple-element.20), channel_id=1, source_target_pairs={{0,24},{4,28},{8,16},{12,20},{16,8},{20,12},{24,0},{28,4},{1,25},{... | collective-permute-start | bytes 196616 | tf_op jit(solution)/shard_map/ppermute | solution.py:372
  24.3 4.9 %collective-permute-start.14 = (s16[1,8,2176]{2,1,0:T(8,128)(2,1)S(1)}, s16[1,8,2176]{2,1,0:T(8,128)(2,1)S(1)}, u32[]{:S(2)}, u32[]{:S(2)}) collective-permute-start(s16[1,8,2176]{2,1,0:T(8,128)(2,1)S(1)} %get-tuple-element.24), channel_id=1, source_target_pairs={{0,2},{1,3},{2,0},{3,1},{4,6},{5,7},{6,4},{7,5},{8,10},{9,11},{10,... | collective-permute-start | bytes 104456 | tf_op jit(solution)/shard_map/ppermute | solution.py:372

commit v18 on v10

--- a/solution.py
+++ b/solution.py
@@ -136,7 +136,8 @@
 
     for n in range(n_out):
         h = n // 2
-        dest = keep_ref.at[h] if n % 2 == 0 else give_refs[h // per_give].at[h % per_give]
+        kept = (n % 2 == 0) == (h == 0)
+        dest = keep_ref.at[h] if kept else give_refs[h // per_give].at[h % per_give]
         for p in range(per_piece // 2):
             at = n * per_piece + 2 * p
             a = acc_a[at] + acc_b[at]
@@ -196,7 +197,10 @@
     acc_a,
     acc_b,
 ):
-    pieces = [ref.at[h] for h in range(same_ref.shape[0]) for ref in (same_ref, other_ref)]
+    pieces = []
+    for h in range(same_ref.shape[0]):
+        pair = [same_ref.at[h], other_ref.at[h]]
+        pieces += pair if h == 0 else pair[::-1]
     n_out = 2 * keep_ref.shape[0]
     width, piece = pieces[0].shape
     per_piece = piece // TILE
@@ -376,7 +380,7 @@
     n_rows = lax.axis_size("brow")
     n_cols = lax.axis_size("bcol")
     own = stack(vectors)
-    chips = [swap(vectors, "brow", n_rows, 2 * h) for h in range(1, n_rows // 2)]
+    chips = [swap(vectors, "brow", n_rows, 2 * h + 1) for h in range(1, n_rows // 2)]
     segment, d = own, 1
     while d < n_cols:
         segment = stack(segment, swap(segment if d > 1 else vectors[None], "bcol", n_cols, d))
@@ -389,7 +393,7 @@
     row_keep, give = forward(same, other, blocks, tile_rows, tile_cols, counts, n_cols, col_give[0])
     col_got = [swap(x, "brow", n_rows, 1) for x in col_give]
     sums = pair_sum(col_keep, col_got)
-    from_chips = [swap(x, "brow", n_rows, 2 * (h + 1)) for h, x in enumerate(sums)]
+    from_chips = [swap(x, "brow", n_rows, 2 * h + 3) for h, x in enumerate(sums)]
     row_got, d = swap(give, "bcol", n_cols, 1), 2
     while d < n_cols:
         row_keep, give = split_sum(row_keep, row_got, sums[0])

time: 28.6 us -> 29.2 us (1.021)
  waiting for transfers between devices: 3.27 us -> 5.6 us
  starting transfers between devices: 16.1 us -> 14.3 us
    ppermute x13, waiting for transfers between devices: 3.27 us -> 5.6 us  [swap(): return lax.ppermute(x, axis, [(i, i ^ d) for i in range(size)])]
    ppermute x13, starting transfers between devices: 16.1 us -> 14.3 us  [swap(): return lax.ppermute(x, axis, [(i, i ^ d) for i in range(size)])]
  transfers between devices with their start and end apart: 13 -> 13, of which waited for: 2 -> 3; matrix products, arithmetic and copies ran while one was open for 0% -> 0% of each run, Pallas kernels for 18% -> 18%
where the time goes in v18:
time: 29.2 us; the launch traced here: 29 us
  starting transfers between devices  14.3 us (49%)
  Pallas kernels  6.08 us (21%)
  waiting for transfers between devices  5.6 us (19%)
  local copies, waits for them, and re-layouts  2.23 us (8%)
  between operations  0.82 us (3%)
    ppermute x13, starting transfers between devices, swap(): return lax.ppermute(x, axis, [(i, i ^ d) for i in range(size)])  14.3 us
    ppermute x13, waiting for transfers between devices, swap(): return lax.ppermute(x, axis, [(i, i ^ d) for i in range(size)])  5.6 us
    pallas_call x1, Pallas kernels, forward(): pl.pallas_call(forward_kernel, in_specs=[SMEM] * 3 + [VMEM] * 4 + [ANY],...  2.51 us
    unnamed x12, local copies, waits for them, and re-layouts  2.23 us
    pallas_call x1, Pallas kernels, backward(): pl.pallas_call(backward_kernel, in_specs=[SMEM] * 3 + [VMEM] * 3 + [ANY],...  1.87 us
    pallas_call x1, Pallas kernels, last_sum(): pl.pallas_call(last_sum_kernel, in_specs=[VMEM] * (4 + len(chips)), out_s...  0.74 us
    pallas_call x1, Pallas kernels, prep(): pl.pallas_call(prep_kernel, in_specs=[VMEM], out_specs=VMEM, out_shape=ja...  0.69 us
  transfers between devices with their start and end apart: 13, of which 3 were waited for; matrix products, arithmetic and copies ran while one was open for 0% of the time, Pallas kernels for 18%

profile of v18, /device:TPU:0, one launch (start us, length us, event | category | flops | bytes accessed | tf_op | source)
XLA Modules:
  0.0 29.0 jit_solution(10142685329179245703)
XLA Ops:
  0.0 3.0 %collective-permute-start = (bf16[1,8,2048]{2,1,0:T(8,128)(2,1)}, bf16[1,8,2048]{2,1,0:T(8,128)(2,1)S(1)}, u32[]{:S(2)}, u32[]{:S(2)}) collective-permute-start(bf16[1,8,2048]{2,1,0:T(8,128)(2,1)} %bitcast.5), channel_id=1, source_target_pairs={{0,1},{1,0},{2,3},{3,2},{4,5},{5,4},{6,7},{7,6},{8,9},{9,8},{10,11... | collective-permute-start | bytes 98312 | tf_op jit(solution)/shard_map/ppermute | solution.py:376
  3.0 0.7 %collective-permute-start.2 = (bf16[8,2048]{1,0:T(8,128)(2,1)}, bf16[8,2048]{1,0:T(8,128)(2,1)S(1)}, u32[]{:S(2)}, u32[]{:S(2)}) collective-permute-start(bf16[8,2048]{1,0:T(8,128)(2,1)} %refs_0_.1), channel_id=1, source_target_pairs={{0,12},{4,8},{8,4},{12,0},{16,28},{20,24},{24,20},{28,16},{1,13},{... | collective-permute-start | bytes 98312 | tf_op jit(solution)/shard_map/ppermute | solution.py:376
  3.7 2.1 %collective-permute-start.4 = (bf16[8,2048]{1,0:T(8,128)(2,1)}, bf16[8,2048]{1,0:T(8,128)(2,1)S(1)}, u32[]{:S(2)}, u32[]{:S(2)}) collective-permute-start(bf16[8,2048]{1,0:T(8,128)(2,1)} %refs_0_.1), channel_id=1, source_target_pairs={{0,28},{4,24},{8,20},{12,16},{16,12},{20,8},{24,4},{28,0},{1,29},{... | collective-permute-start | bytes 98312 | tf_op jit(solution)/shard_map/ppermute | solution.py:376
  5.7 0.0 collective-permute-start.3
  5.8 0.8 %copy-done.3 = bf16[8,2048]{1,0:T(8,128)(2,1)S(1)} copy-done((bf16[8,2048]{1,0:T(8,128)(2,1)S(1)}, bf16[8,2048]{1,0:T(8,128)(2,1)}, u32[]{:S(2)}) %copy-start.3) | copy-done | bytes 32792
  6.6 0.0 collective-permute-done.refs_1_
  6.6 2.7 %collective-permute-start.1 = (bf16[2,8,2048]{2,1,0:T(8,128)(2,1)S(1)}, bf16[2,8,2048]{2,1,0:T(8,128)(2,1)S(1)}, u32[]{:S(2)}, u32[]{:S(2)}) collective-permute-start(bf16[2,8,2048]{2,1,0:T(8,128)(2,1)S(1)} %stack_pieces.5.refs_0_), channel_id=1, source_target_pairs={{0,2},{1,3},{2,0},{3,1},{4,6},{5,7},{6,4},{7,5},{8,10},{9,11},{10,... | collective-permute-start | bytes 196616 | tf_op jit(solution)/shard_map/ppermute | solution.py:376
  9.2 1.4 %copy-done = bf16[192,4096]{1,0:T(8,128)(2,1)S(1)} copy-done((bf16[192,4096]{1,0:T(8,128)(2,1)S(1)}, bf16[192,4096]{1,0:T(8,128)(2,1)}, u32[]{:S(2)}) %copy-start) | copy-done | bytes 1572888
  10.6 0.7 %prep_tiles.1.refs_4_.tiles_ref = bf16[192,32,128]{2,1,0:T(8,128)(2,1)S(1)} custom-call(bf16[24,32,8,128]{3,2,1,0:T(8,128)(2,1)S(1)} %bitcast.4), custom_call_target="tpu_custom_call" | custom-call | bytes 3145728 | tf_op jit(solution)/shard_map/prep_tiles/pallas_call | solution.py:77
  11.3 0.0 copy-start.1
  11.3 0.0 copy-start.4
  11.4 0.0 copy-start.5
  11.4 0.0 collective-permute-done.2.refs_1_
  11.4 0.0 collective-permute-done.4.refs_3_
  11.4 0.0 copy-start.2
  11.4 0.4 %collective-permute-start.10 = (bf16[4,8,2048]{2,1,0:T(8,128)(2,1)S(1)}, bf16[4,8,2048]{2,1,0:T(8,128)(2,1)S(1)}, u32[]{:S(2)}, u32[]{:S(2)}) collective-permute-start(bf16[4,8,2048]{2,1,0:T(8,128)(2,1)S(1)} %stack_pieces.7.after_ref.same_ref), channel_id=1, source_target_pairs={{0,4},{4,0},{8,12},{12,8},{16,20},{20,16},{24,28},{28,24},{1,5},{5... | collective-permute-start | bytes 393224 | tf_op jit(solution)/shard_map/ppermute | solution.py:376
  12.5 0.9 %collective-permute-done.1.refs_1_ = bf16[2,8,2048]{2,1,0:T(8,128)(2,1)S(1)} collective-permute-done((bf16[2,8,2048]{2,1,0:T(8,128)(2,1)S(1)}, bf16[2,8,2048]{2,1,0:T(8,128)(2,1)S(1)}, u32[]{:S(2)}, u32[]{:S(2)}) %collective-permute-start.1) | collective-permute-done | bytes 65568 | tf_op jit(solution)/shard_map/ppermute | solution.py:376
  13.4 1.9 %transpose_product.1 = (f32[4,8,2048]{2,1,0:T(8,128)S(1)}, f32[2,8,2048]{2,1,0:T(8,128)S(1)}, f32[2,8,2048]{2,1,0:T(8,128)S(1)}) custom-call(s32[192]{0:T(256)S(1)} %copy-done.4, s32[192]{0:T(256)S(1)} %copy-done.5, s32[1,1]{1,0:T(1,128)S(6)} %copy.8.count_ref, bf16[128,512]{1,0:T(8,128)(2,1)S(1)} %copy-done.1, ...), custom_call_target="tpu_custom_call" | custom-call | flops 100663296 | bytes 3145728 | tf_op jit(solution)/shard_map/transpose_product/pallas_call | solution.py:155
  15.3 0.1 collective-permute-start.6
  15.4 0.4 %collective-permute-start.5 = (f32[2,8,2048]{2,1,0:T(8,128)S(1)}, f32[2,8,2048]{2,1,0:T(8,128)S(1)}, u32[]{:S(2)}, u32[]{:S(2)}) collective-permute-start(f32[2,8,2048]{2,1,0:T(8,128)S(1)} %get-tuple-element.16.after_ref), channel_id=1, source_target_pairs={{0,4},{4,0},{8,12},{12,8},{16,20},{20,16},{24,28},{28,24},{1,5},{5... | collective-permute-start | bytes 393224 | tf_op jit(solution)/shard_map/ppermute | solution.py:376
  15.9 2.5 %forward_product.1 = (f32[2,8,2048]{2,1,0:T(8,128)S(1)}, s16[2,8,2176]{2,1,0:T(8,128)(2,1)S(1)}) custom-call(s32[192]{0:T(256)S(1)} %copy-done.4, s32[192]{0:T(256)S(1)} %copy-done.5, s32[1,1]{1,0:T(1,128)S(6)} %copy.8.count_ref, bf16[512,128]{1,0:T(8,128)(2,1)S(1)} %copy-done.2, bf16[192,32,128]{2,1,0:T(8,128)(2,1)S(1)} %prep_tiles.1.refs_4_.tiles_ref, ...), custom_call_target="tpu_custom_call" | custom-call | flops 100663296 | bytes 3145728 | tf_op jit(solution)/shard_map/forward_product/pallas_call | solution.py:266
  18.4 0.1 collective-permute-start.11
  18.5 0.0 collective-permute-done.6.refs_1_
  18.5 0.0 collective-permute-done.5.refs_0_.refs_4_
  18.5 1.3 %collective-permute-start.8 = (f32[8,2048]{1,0:T(8,128)S(1)}, f32[8,2048]{1,0:T(8,128)S(1)}, u32[]{:S(2)}, u32[]{:S(2)}) collective-permute-start(f32[8,2048]{1,0:T(8,128)S(1)} %get-tuple-element.19), channel_id=1, source_target_pairs={{0,20},{4,16},{8,28},{12,24},{16,4},{20,0},{24,12},{28,8},{1,21},{... | collective-permute-start | bytes 196616 | tf_op jit(solution)/shard_map/ppermute | solution.py:376
  19.8 1.5 %collective-permute-start.9 = (f32[8,2048]{1,0:T(8,128)S(1)}, f32[8,2048]{1,0:T(8,128)S(1)}, u32[]{:S(2)}, u32[]{:S(2)}) collective-permute-start(f32[8,2048]{1,0:T(8,128)S(1)} %get-tuple-element.20), channel_id=1, source_target_pairs={{0,28},{4,24},{8,20},{12,16},{16,12},{20,8},{24,4},{28,0},{1,29},{... | collective-permute-start | bytes 196616 | tf_op jit(solution)/shard_map/ppermute | solution.py:376
  21.3 0.1 collective-permute-start.7
  21.5 1.3 %collective-permute-done.11.got_ref = s16[2,8,2176]{2,1,0:T(8,128)(2,1)S(1)} collective-permute-done((s16[2,8,2176]{2,1,0:T(8,128)(2,1)S(1)}, s16[2,8,2176]{2,1,0:T(8,128)(2,1)S(1)}, u32[]{:S(2)}, u32[]{:S(2)}) %collective-permute-start.11) | collective-permute-done | bytes 69664 | tf_op jit(solution)/shard_map/ppermute | solution.py:376
  22.8 0.2 halving_sum.1
  23.0 1.9 %collective-permute-start.12 = (s16[1,8,2176]{2,1,0:T(8,128)(2,1)S(1)}, s16[1,8,2176]{2,1,0:T(8,128)(2,1)S(1)}, u32[]{:S(2)}, u32[]{:S(2)}) collective-permute-start(s16[1,8,2176]{2,1,0:T(8,128)(2,1)S(1)} %get-tuple-element.24), channel_id=1, source_target_pairs={{0,2},{1,3},{2,0},{3,1},{4,6},{5,7},{6,4},{7,5},{8,10},{9,11},{10,... | collective-permute-start | bytes 104456 | tf_op jit(solution)/shard_map/ppermute | solution.py:376
  24.9 3.4 %collective-permute-done.12.refs_6_ = s16[1,8,2176]{2,1,0:T(8,128)(2,1)S(1)} collective-permute-done((s16[1,8,2176]{2,1,0:T(8,128)(2,1)S(1)}, s16[1,8,2176]{2,1,0:T(8,128)(2,1)S(1)}, u32[]{:S(2)}, u32[]{:S(2)}) %collective-permute-start.12) | collective-permute-done | bytes 34848 | tf_op jit(solution)/shard_map/ppermute | solution.py:376
  28.3 0.7 %last_sum.1 = f32[8,2048]{1,0:T(8,128)} custom-call(f32[8,2048]{1,0:T(8,128)S(1)} %collective-permute-done.7.refs_0_, f32[8,2048]{1,0:T(8,128)S(1)} %collective-permute-done.8.refs_1_, f32[8,2048]{1,0:T(8,128)S(1)} %collective-permute-done.9.refs_2_, f32[4,8,2048]{2,1,0:T(8,128)S(1)} %get-tuple-element.15.keep_ref.refs_3_, ...), custom_call_target="tpu_custom_call" | custom-call | tf_op jit(solution)/shard_map/last_sum/pallas_call | solution.py:365
  (16 shorter events, 0.1 us)
Async XLA Ops:
  0.0 6.6 %collective-permute-start = (bf16[1,8,2048]{2,1,0:T(8,128)(2,1)}, bf16[1,8,2048]{2,1,0:T(8,128)(2,1)S(1)}, u32[]{:S(2)}, u32[]{:S(2)}) collective-permute-start(bf16[1,8,2048]{2,1,0:T(8,128)(2,1)} %bitcast.5), channel_id=1, source_target_pairs={{0,1},{1,0},{2,3},{3,2},{4,5},{5,4},{6,7},{7,6},{8,9},{9,8},{10,11... | collective-permute-start | bytes 98312 | tf_op jit(solution)/shard_map/ppermute | solution.py:376
  3.0 8.3 %collective-permute-start.2 = (bf16[8,2048]{1,0:T(8,128)(2,1)}, bf16[8,2048]{1,0:T(8,128)(2,1)S(1)}, u32[]{:S(2)}, u32[]{:S(2)}) collective-permute-start(bf16[8,2048]{1,0:T(8,128)(2,1)} %refs_0_.1), channel_id=1, source_target_pairs={{0,12},{4,8},{8,4},{12,0},{16,28},{20,24},{24,20},{28,16},{1,13},{... | collective-permute-start | bytes 98312 | tf_op jit(solution)/shard_map/ppermute | solution.py:376
  3.7 7.7 %collective-permute-start.4 = (bf16[8,2048]{1,0:T(8,128)(2,1)}, bf16[8,2048]{1,0:T(8,128)(2,1)S(1)}, u32[]{:S(2)}, u32[]{:S(2)}) collective-permute-start(bf16[8,2048]{1,0:T(8,128)(2,1)} %refs_0_.1), channel_id=1, source_target_pairs={{0,28},{4,24},{8,20},{12,16},{16,12},{20,8},{24,4},{28,0},{1,29},{... | collective-permute-start | bytes 98312 | tf_op jit(solution)/shard_map/ppermute | solution.py:376
  5.7 5.7 %collective-permute-start.3 = (bf16[8,2048]{1,0:T(8,128)(2,1)}, bf16[8,2048]{1,0:T(8,128)(2,1)S(1)}, u32[]{:S(2)}, u32[]{:S(2)}) collective-permute-start(bf16[8,2048]{1,0:T(8,128)(2,1)} %refs_0_.1), channel_id=1, source_target_pairs={{0,20},{4,16},{8,28},{12,24},{16,4},{20,0},{24,12},{28,8},{1,21},{... | collective-permute-start | bytes 98312 | tf_op jit(solution)/shard_map/ppermute | solution.py:376
  5.8 0.8 %copy-start.3 = (bf16[8,2048]{1,0:T(8,128)(2,1)S(1)}, bf16[8,2048]{1,0:T(8,128)(2,1)}, u32[]{:S(2)}) copy-start(bf16[8,2048]{1,0:T(8,128)(2,1)} %refs_0_.1) | copy-start | bytes 98308
  6.6 6.8 %collective-permute-start.1 = (bf16[2,8,2048]{2,1,0:T(8,128)(2,1)S(1)}, bf16[2,8,2048]{2,1,0:T(8,128)(2,1)S(1)}, u32[]{:S(2)}, u32[]{:S(2)}) collective-permute-start(bf16[2,8,2048]{2,1,0:T(8,128)(2,1)S(1)} %stack_pieces.5.refs_0_), channel_id=1, source_target_pairs={{0,2},{1,3},{2,0},{3,1},{4,6},{5,7},{6,4},{7,5},{8,10},{9,11},{10,... | collective-permute-start | bytes 196616 | tf_op jit(solution)/shard_map/ppermute | solution.py:376
  9.2 1.4 %copy-start = (bf16[192,4096]{1,0:T(8,128)(2,1)S(1)}, bf16[192,4096]{1,0:T(8,128)(2,1)}, u32[]{:S(2)}) copy-start(bf16[192,4096]{1,0:T(8,128)(2,1)} %param.8) | copy-start | bytes 4718596
  11.3 2.0 %copy-start.1 = (bf16[128,512]{1,0:T(8,128)(2,1)S(1)}, bf16[128,512]{1,0:T(8,128)(2,1)}, u32[]{:S(2)}) copy-start(bf16[128,512]{1,0:T(8,128)(2,1)} %constant.4.clone.spread_ref) | copy-start | bytes 393220
  11.3 2.0 %copy-start.4 = (s32[192]{0:T(256)S(1)}, s32[192]{0:T(256)}, u32[]{:S(2)}) copy-start(s32[192]{0:T(256)} %rows_ref.3) | copy-start | bytes 2308
  11.4 2.0 %copy-start.5 = (s32[192]{0:T(256)S(1)}, s32[192]{0:T(256)}, u32[]{:S(2)}) copy-start(s32[192]{0:T(256)} %cols_ref.3) | copy-start | bytes 2308
  11.4 4.4 %copy-start.2 = (bf16[512,128]{1,0:T(8,128)(2,1)S(1)}, bf16[512,128]{1,0:T(8,128)(2,1)}, u32[]{:S(2)}) copy-start(bf16[512,128]{1,0:T(8,128)(2,1)} %constant.5.clone.fold_ref) | copy-start | bytes 393220
  11.4 4.4 %collective-permute-start.10 = (bf16[4,8,2048]{2,1,0:T(8,128)(2,1)S(1)}, bf16[4,8,2048]{2,1,0:T(8,128)(2,1)S(1)}, u32[]{:S(2)}, u32[]{:S(2)}) collective-permute-start(bf16[4,8,2048]{2,1,0:T(8,128)(2,1)S(1)} %stack_pieces.7.after_ref.same_ref), channel_id=1, source_target_pairs={{0,4},{4,0},{8,12},{12,8},{16,20},{20,16},{24,28},{28,24},{1,5},{5... | collective-permute-start | bytes 393224 | tf_op jit(solution)/shard_map/ppermute | solution.py:376
  15.3 3.2 %collective-permute-start.6 = (f32[2,8,2048]{2,1,0:T(8,128)S(1)}, f32[2,8,2048]{2,1,0:T(8,128)S(1)}, u32[]{:S(2)}, u32[]{:S(2)}) collective-permute-start(f32[2,8,2048]{2,1,0:T(8,128)S(1)} %get-tuple-element.17), channel_id=1, source_target_pairs={{0,4},{4,0},{8,12},{12,8},{16,20},{20,16},{24,28},{28,24},{1,5},{5... | collective-permute-start | bytes 393224 | tf_op jit(solution)/shard_map/ppermute | solution.py:376
  15.4 3.0 %collective-permute-start.5 = (f32[2,8,2048]{2,1,0:T(8,128)S(1)}, f32[2,8,2048]{2,1,0:T(8,128)S(1)}, u32[]{:S(2)}, u32[]{:S(2)}) collective-permute-start(f32[2,8,2048]{2,1,0:T(8,128)S(1)} %get-tuple-element.16.after_ref), channel_id=1, source_target_pairs={{0,4},{4,0},{8,12},{12,8},{16,20},{20,16},{24,28},{28,24},{1,5},{5... | collective-permute-start | bytes 393224 | tf_op jit(solution)/shard_map/ppermute | solution.py:376
  18.4 4.4 %collective-permute-start.11 = (s16[2,8,2176]{2,1,0:T(8,128)(2,1)S(1)}, s16[2,8,2176]{2,1,0:T(8,128)(2,1)S(1)}, u32[]{:S(2)}, u32[]{:S(2)}) collective-permute-start(s16[2,8,2176]{2,1,0:T(8,128)(2,1)S(1)} %get-tuple-element.22), channel_id=1, source_target_pairs={{0,1},{1,0},{2,3},{3,2},{4,5},{5,4},{6,7},{7,6},{8,9},{9,8},{10,11... | collective-permute-start | bytes 208904 | tf_op jit(solution)/shard_map/ppermute | solution.py:376
  18.5 9.7 %collective-permute-start.8 = (f32[8,2048]{1,0:T(8,128)S(1)}, f32[8,2048]{1,0:T(8,128)S(1)}, u32[]{:S(2)}, u32[]{:S(2)}) collective-permute-start(f32[8,2048]{1,0:T(8,128)S(1)} %get-tuple-element.19), channel_id=1, source_target_pairs={{0,20},{4,16},{8,28},{12,24},{16,4},{20,0},{24,12},{28,8},{1,21},{... | collective-permute-start | bytes 196616 | tf_op jit(solution)/shard_map/ppermute | solution.py:376
  19.8 8.5 %collective-permute-start.9 = (f32[8,2048]{1,0:T(8,128)S(1)}, f32[8,2048]{1,0:T(8,128)S(1)}, u32[]{:S(2)}, u32[]{:S(2)}) collective-permute-start(f32[8,2048]{1,0:T(8,128)S(1)} %get-tuple-element.20), channel_id=1, source_target_pairs={{0,28},{4,24},{8,20},{12,16},{16,12},{20,8},{24,4},{28,0},{1,29},{... | collective-permute-start | bytes 196616 | tf_op jit(solution)/shard_map/ppermute | solution.py:376
  21.3 6.9 %collective-permute-start.7 = (f32[8,2048]{1,0:T(8,128)S(1)}, f32[8,2048]{1,0:T(8,128)S(1)}, u32[]{:S(2)}, u32[]{:S(2)}) collective-permute-start(f32[8,2048]{1,0:T(8,128)S(1)} %get-tuple-element.18.after_ref), channel_id=1, source_target_pairs={{0,12},{4,8},{8,4},{12,0},{16,28},{20,24},{24,20},{28,16},{1,13},{... | collective-permute-start | bytes 196616 | tf_op jit(solution)/shard_map/ppermute | solution.py:376
  23.0 5.3 %collective-permute-start.12 = (s16[1,8,2176]{2,1,0:T(8,128)(2,1)S(1)}, s16[1,8,2176]{2,1,0:T(8,128)(2,1)S(1)}, u32[]{:S(2)}, u32[]{:S(2)}) collective-permute-start(s16[1,8,2176]{2,1,0:T(8,128)(2,1)S(1)} %get-tuple-element.24), channel_id=1, source_target_pairs={{0,2},{1,3},{2,0},{3,1},{4,6},{5,7},{6,4},{7,5},{8,10},{9,11},{10,... | collective-permute-start | bytes 104456 | tf_op jit(solution)/shard_map/ppermute | solution.py:376

commit v19 on v13

--- a/solution.py
+++ b/solution.py
@@ -144,7 +144,8 @@
 
     for n in range(n_out):
         h = n // 2
-        dest = keep_ref.at[h] if n % 2 == 0 else give_refs[h // per_give].at[h % per_give]
+        kept = (n % 2 == 0) == (h == 0)
+        dest = keep_ref.at[h] if kept else give_refs[h // per_give].at[h % per_give]
         for p in range(per_piece // 2):
             at = n * per_piece + 2 * p
             a = acc_a[at] + acc_b[at]
@@ -204,7 +205,10 @@
     acc_a,
     acc_b,
 ):
-    pieces = [ref.at[h] for h in range(same_ref.shape[0]) for ref in (same_ref, other_ref)]
+    pieces = []
+    for h in range(same_ref.shape[0]):
+        pair = [same_ref.at[h], other_ref.at[h]]
+        pieces += pair if h == 0 else pair[::-1]
     n_out = 2 * keep_ref.shape[0]
     width, piece = pieces[0].shape
     per_piece = piece // TILE
@@ -384,7 +388,7 @@
     n_rows = lax.axis_size("brow")
     n_cols = lax.axis_size("bcol")
     own = stack(vectors)
-    chips = [swap(vectors, "brow", n_rows, 2 * h) for h in range(1, n_rows // 2)]
+    chips = [swap(vectors, "brow", n_rows, 2 * h + 1) for h in range(1, n_rows // 2)]
     segment, d = own, n_cols // 2
     while d > 0:
         first = d == n_cols // 2
@@ -398,7 +402,7 @@
     row_keep, give = forward(same, other, blocks, tile_rows, tile_cols, counts, n_cols, col_give[0])
     col_got = [swap(x, "brow", n_rows, 1) for x in col_give]
     sums = pair_sum(col_keep, col_got)
-    from_chips = [swap(x, "brow", n_rows, 2 * (h + 1)) for h, x in enumerate(sums)]
+    from_chips = [swap(x, "brow", n_rows, 2 * h + 3) for h, x in enumerate(sums)]
     row_got, d = swap(give, "bcol", n_cols, 1), 2
     while d < n_cols:
         row_keep, give = split_sum(row_keep, row_got, sums[0])

time: 29.2 us -> 28.1 us (0.962)
  waiting for transfers between devices: 3.97 us -> 3.57 us
  starting transfers between devices: 15.7 us -> 15.3 us
    ppermute x13, starting transfers between devices: 15.7 us -> 15.3 us  [swap(): return lax.ppermute(x, axis, [(i, i ^ d) for i in range(size)])]
    ppermute x13, waiting for transfers between devices: 3.97 us -> 3.57 us  [swap(): return lax.ppermute(x, axis, [(i, i ^ d) for i in range(size)])]
  transfers between devices with their start and end apart: 13 -> 13, of which waited for: 1 -> 2; matrix products, arithmetic and copies ran while one was open for 0% -> 0% of each run, Pallas kernels for 18% -> 19%
where the time goes in v19:
time: 28.1 us; the launch traced here: 27.9 us
  starting transfers between devices  15.3 us (54%)
  Pallas kernels  6.02 us (21%)
  waiting for transfers between devices  3.57 us (13%)
  local copies, waits for them, and re-layouts  2.23 us (8%)
  between operations  0.81 us (3%)
    ppermute x13, starting transfers between devices, swap(): return lax.ppermute(x, axis, [(i, i ^ d) for i in range(size)])  15.3 us
    ppermute x13, waiting for transfers between devices, swap(): return lax.ppermute(x, axis, [(i, i ^ d) for i in range(size)])  3.57 us
    pallas_call x1, Pallas kernels, forward(): pl.pallas_call(forward_kernel, in_specs=[SMEM] * 3 + [VMEM] * 4 + [ANY],...  2.48 us
    unnamed x12, local copies, waits for them, and re-layouts  2.23 us
    pallas_call x1, Pallas kernels, backward(): pl.pallas_call(backward_kernel, in_specs=[SMEM] * 3 + [VMEM] * 3 + [ANY],...  1.84 us
    pallas_call x1, Pallas kernels, last_sum(): pl.pallas_call(last_sum_kernel, in_specs=[VMEM] * (4 + len(chips)), out_s...  0.74 us
    pallas_call x1, Pallas kernels, prep(): pl.pallas_call(prep_kernel, in_specs=[VMEM], out_specs=VMEM, out_shape=ja...  0.69 us
  transfers between devices with their start and end apart: 13, of which 2 were waited for; matrix products, arithmetic and copies ran while one was open for 0% of the time, Pallas kernels for 19%

profile of v19, /device:TPU:0, one launch (start us, length us, event | category | flops | bytes accessed | tf_op | source)
XLA Modules:
  0.0 27.9 jit_solution(815298857647329487)
XLA Ops:
  0.0 4.0 %collective-permute-start = (bf16[1,8,2048]{2,1,0:T(8,128)(2,1)}, bf16[1,8,2048]{2,1,0:T(8,128)(2,1)S(1)}, u32[]{:S(2)}, u32[]{:S(2)}) collective-permute-start(bf16[1,8,2048]{2,1,0:T(8,128)(2,1)} %bitcast.5), channel_id=1, source_target_pairs={{0,2},{1,3},{2,0},{3,1},{4,6},{5,7},{6,4},{7,5},{8,10},{9,11},{10,... | collective-permute-start | bytes 98312 | tf_op jit(solution)/shard_map/ppermute | solution.py:384
  4.0 0.7 %collective-permute-start.2 = (bf16[8,2048]{1,0:T(8,128)(2,1)}, bf16[8,2048]{1,0:T(8,128)(2,1)S(1)}, u32[]{:S(2)}, u32[]{:S(2)}) collective-permute-start(bf16[8,2048]{1,0:T(8,128)(2,1)} %refs_0_.1), channel_id=1, source_target_pairs={{0,12},{4,8},{8,4},{12,0},{16,28},{20,24},{24,20},{28,16},{1,13},{... | collective-permute-start | bytes 98312 | tf_op jit(solution)/shard_map/ppermute | solution.py:384
  4.7 2.1 %collective-permute-start.4 = (bf16[8,2048]{1,0:T(8,128)(2,1)}, bf16[8,2048]{1,0:T(8,128)(2,1)S(1)}, u32[]{:S(2)}, u32[]{:S(2)}) collective-permute-start(bf16[8,2048]{1,0:T(8,128)(2,1)} %refs_0_.1), channel_id=1, source_target_pairs={{0,28},{4,24},{8,20},{12,16},{16,12},{20,8},{24,4},{28,0},{1,29},{... | collective-permute-start | bytes 98312 | tf_op jit(solution)/shard_map/ppermute | solution.py:384
  6.7 0.0 collective-permute-start.3
  6.8 0.8 %copy-done.3 = bf16[8,2048]{1,0:T(8,128)(2,1)S(1)} copy-done((bf16[8,2048]{1,0:T(8,128)(2,1)S(1)}, bf16[8,2048]{1,0:T(8,128)(2,1)}, u32[]{:S(2)}) %copy-start.3) | copy-done | bytes 32792
  7.6 0.0 collective-permute-done.refs_1_
  7.6 1.6 %collective-permute-start.1 = (bf16[2,8,2048]{2,1,0:T(8,128)(2,1)S(1)}, bf16[2,8,2048]{2,1,0:T(8,128)(2,1)S(1)}, u32[]{:S(2)}, u32[]{:S(2)}) collective-permute-start(bf16[2,8,2048]{2,1,0:T(8,128)(2,1)S(1)} %stack_pieces.5.refs_0_), channel_id=1, source_target_pairs={{0,1},{1,0},{2,3},{3,2},{4,5},{5,4},{6,7},{7,6},{8,9},{9,8},{10,11... | collective-permute-start | bytes 196616 | tf_op jit(solution)/shard_map/ppermute | solution.py:384
  9.2 1.4 %copy-done = bf16[192,4096]{1,0:T(8,128)(2,1)S(1)} copy-done((bf16[192,4096]{1,0:T(8,128)(2,1)S(1)}, bf16[192,4096]{1,0:T(8,128)(2,1)}, u32[]{:S(2)}) %copy-start) | copy-done | bytes 1572888
  10.6 0.7 %prep_tiles.1.refs_4_.tiles_ref = bf16[192,32,128]{2,1,0:T(8,128)(2,1)S(1)} custom-call(bf16[24,32,8,128]{3,2,1,0:T(8,128)(2,1)S(1)} %bitcast.4), custom_call_target="tpu_custom_call" | custom-call | bytes 3145728 | tf_op jit(solution)/shard_map/prep_tiles/pallas_call | solution.py:77
  11.3 0.0 copy-start.1
  11.3 0.0 copy-start.4
  11.4 0.0 copy-start.5
  11.4 0.0 collective-permute-done.2.refs_1_
  11.4 0.0 collective-permute-done.4.refs_3_
  11.4 0.0 collective-permute-done.3.refs_2_
  11.4 0.0 copy-start.2
  11.4 0.4 %collective-permute-start.10 = (bf16[4,8,2048]{2,1,0:T(8,128)(2,1)S(1)}, bf16[4,8,2048]{2,1,0:T(8,128)(2,1)S(1)}, u32[]{:S(2)}, u32[]{:S(2)}) collective-permute-start(bf16[4,8,2048]{2,1,0:T(8,128)(2,1)S(1)} %stack_pieces.7.after_ref.same_ref), channel_id=1, source_target_pairs={{0,4},{4,0},{8,12},{12,8},{16,20},{20,16},{24,28},{28,24},{1,5},{5... | collective-permute-start | bytes 393224 | tf_op jit(solution)/shard_map/ppermute | solution.py:384
  12.5 1.8 %transpose_product.1 = (f32[4,8,2048]{2,1,0:T(8,128)S(1)}, f32[2,8,2048]{2,1,0:T(8,128)S(1)}, f32[2,8,2048]{2,1,0:T(8,128)S(1)}) custom-call(s32[192]{0:T(256)S(1)} %copy-done.4, s32[192]{0:T(256)S(1)} %copy-done.5, s32[1,1]{1,0:T(1,128)S(6)} %copy.8.count_ref, bf16[128,512]{1,0:T(8,128)(2,1)S(1)} %copy-done.1, ...), custom_call_target="tpu_custom_call" | custom-call | flops 100663296 | bytes 3145728 | tf_op jit(solution)/shard_map/transpose_product/pallas_call | solution.py:163
  14.4 0.2 collective-permute-start.6
  14.6 0.3 %collective-permute-start.5 = (f32[2,8,2048]{2,1,0:T(8,128)S(1)}, f32[2,8,2048]{2,1,0:T(8,128)S(1)}, u32[]{:S(2)}, u32[]{:S(2)}) collective-permute-start(f32[2,8,2048]{2,1,0:T(8,128)S(1)} %get-tuple-element.16.after_ref), channel_id=1, source_target_pairs={{0,4},{4,0},{8,12},{12,8},{16,20},{20,16},{24,28},{28,24},{1,5},{5... | collective-permute-start | bytes 393224 | tf_op jit(solution)/shard_map/ppermute | solution.py:384
  14.9 0.0 collective-permute-done.10.other_ref
  14.9 2.5 %forward_product.1 = (f32[2,8,2048]{2,1,0:T(8,128)S(1)}, s16[2,8,2176]{2,1,0:T(8,128)(2,1)S(1)}) custom-call(s32[192]{0:T(256)S(1)} %copy-done.4, s32[192]{0:T(256)S(1)} %copy-done.5, s32[1,1]{1,0:T(1,128)S(6)} %copy.8.count_ref, bf16[512,128]{1,0:T(8,128)(2,1)S(1)} %copy-done.2, bf16[192,32,128]{2,1,0:T(8,128)(2,1)S(1)} %prep_tiles.1.refs_4_.tiles_ref, ...), custom_call_target="tpu_custom_call" | custom-call | flops 100663296 | bytes 3145728 | tf_op jit(solution)/shard_map/forward_product/pallas_call | solution.py:274
  17.4 1.3 %collective-permute-start.11 = (s16[2,8,2176]{2,1,0:T(8,128)(2,1)S(1)}, s16[2,8,2176]{2,1,0:T(8,128)(2,1)S(1)}, u32[]{:S(2)}, u32[]{:S(2)}) collective-permute-start(s16[2,8,2176]{2,1,0:T(8,128)(2,1)S(1)} %get-tuple-element.22), channel_id=1, source_target_pairs={{0,1},{1,0},{2,3},{3,2},{4,5},{5,4},{6,7},{7,6},{8,9},{9,8},{10,11... | collective-permute-start | bytes 208904 | tf_op jit(solution)/shard_map/ppermute | solution.py:384
  18.8 1.0 %collective-permute-start.8 = (f32[8,2048]{1,0:T(8,128)S(1)}, f32[8,2048]{1,0:T(8,128)S(1)}, u32[]{:S(2)}, u32[]{:S(2)}) collective-permute-start(f32[8,2048]{1,0:T(8,128)S(1)} %get-tuple-element.19), channel_id=1, source_target_pairs={{0,20},{4,16},{8,28},{12,24},{16,4},{20,0},{24,12},{28,8},{1,21},{... | collective-permute-start | bytes 196616 | tf_op jit(solution)/shard_map/ppermute | solution.py:384
  19.8 1.8 %collective-permute-start.9 = (f32[8,2048]{1,0:T(8,128)S(1)}, f32[8,2048]{1,0:T(8,128)S(1)}, u32[]{:S(2)}, u32[]{:S(2)}) collective-permute-start(f32[8,2048]{1,0:T(8,128)S(1)} %get-tuple-element.20), channel_id=1, source_target_pairs={{0,28},{4,24},{8,20},{12,16},{16,12},{20,8},{24,4},{28,0},{1,29},{... | collective-permute-start | bytes 196616 | tf_op jit(solution)/shard_map/ppermute | solution.py:384
  21.7 0.1 collective-permute-start.7
  21.7 0.1 collective-permute-done.11.got_ref
  21.8 0.2 halving_sum.1
  22.0 1.6 %collective-permute-start.12 = (s16[1,8,2176]{2,1,0:T(8,128)(2,1)S(1)}, s16[1,8,2176]{2,1,0:T(8,128)(2,1)S(1)}, u32[]{:S(2)}, u32[]{:S(2)}) collective-permute-start(s16[1,8,2176]{2,1,0:T(8,128)(2,1)S(1)} %get-tuple-element.24), channel_id=1, source_target_pairs={{0,2},{1,3},{2,0},{3,1},{4,6},{5,7},{6,4},{7,5},{8,10},{9,11},{10,... | collective-permute-start | bytes 104456 | tf_op jit(solution)/shard_map/ppermute | solution.py:384
  23.7 3.5 %collective-permute-done.12.refs_6_ = s16[1,8,2176]{2,1,0:T(8,128)(2,1)S(1)} collective-permute-done((s16[1,8,2176]{2,1,0:T(8,128)(2,1)S(1)}, s16[1,8,2176]{2,1,0:T(8,128)(2,1)S(1)}, u32[]{:S(2)}, u32[]{:S(2)}) %collective-permute-start.12) | collective-permute-done | bytes 34848 | tf_op jit(solution)/shard_map/ppermute | solution.py:384
  27.1 0.0 collective-permute-done.8.refs_1_
  27.1 0.7 %last_sum.1 = f32[8,2048]{1,0:T(8,128)} custom-call(f32[8,2048]{1,0:T(8,128)S(1)} %collective-permute-done.7.refs_0_, f32[8,2048]{1,0:T(8,128)S(1)} %collective-permute-done.8.refs_1_, f32[8,2048]{1,0:T(8,128)S(1)} %collective-permute-done.9.refs_2_, f32[4,8,2048]{2,1,0:T(8,128)S(1)} %get-tuple-element.15.keep_ref.refs_3_, ...), custom_call_target="tpu_custom_call" | custom-call | tf_op jit(solution)/shard_map/last_sum/pallas_call | solution.py:373
  (16 shorter events, 0.1 us)
Async XLA Ops:
  0.0 7.6 %collective-permute-start = (bf16[1,8,2048]{2,1,0:T(8,128)(2,1)}, bf16[1,8,2048]{2,1,0:T(8,128)(2,1)S(1)}, u32[]{:S(2)}, u32[]{:S(2)}) collective-permute-start(bf16[1,8,2048]{2,1,0:T(8,128)(2,1)} %bitcast.5), channel_id=1, source_target_pairs={{0,2},{1,3},{2,0},{3,1},{4,6},{5,7},{6,4},{7,5},{8,10},{9,11},{10,... | collective-permute-start | bytes 98312 | tf_op jit(solution)/shard_map/ppermute | solution.py:384
  4.0 7.3 %collective-permute-start.2 = (bf16[8,2048]{1,0:T(8,128)(2,1)}, bf16[8,2048]{1,0:T(8,128)(2,1)S(1)}, u32[]{:S(2)}, u32[]{:S(2)}) collective-permute-start(bf16[8,2048]{1,0:T(8,128)(2,1)} %refs_0_.1), channel_id=1, source_target_pairs={{0,12},{4,8},{8,4},{12,0},{16,28},{20,24},{24,20},{28,16},{1,13},{... | collective-permute-start | bytes 98312 | tf_op jit(solution)/shard_map/ppermute | solution.py:384
  4.7 6.7 %collective-permute-start.4 = (bf16[8,2048]{1,0:T(8,128)(2,1)}, bf16[8,2048]{1,0:T(8,128)(2,1)S(1)}, u32[]{:S(2)}, u32[]{:S(2)}) collective-permute-start(bf16[8,2048]{1,0:T(8,128)(2,1)} %refs_0_.1), channel_id=1, source_target_pairs={{0,28},{4,24},{8,20},{12,16},{16,12},{20,8},{24,4},{28,0},{1,29},{... | collective-permute-start | bytes 98312 | tf_op jit(solution)/shard_map/ppermute | solution.py:384
  6.7 4.7 %collective-permute-start.3 = (bf16[8,2048]{1,0:T(8,128)(2,1)}, bf16[8,2048]{1,0:T(8,128)(2,1)S(1)}, u32[]{:S(2)}, u32[]{:S(2)}) collective-permute-start(bf16[8,2048]{1,0:T(8,128)(2,1)} %refs_0_.1), channel_id=1, source_target_pairs={{0,20},{4,16},{8,28},{12,24},{16,4},{20,0},{24,12},{28,8},{1,21},{... | collective-permute-start | bytes 98312 | tf_op jit(solution)/shard_map/ppermute | solution.py:384
  6.8 0.8 %copy-start.3 = (bf16[8,2048]{1,0:T(8,128)(2,1)S(1)}, bf16[8,2048]{1,0:T(8,128)(2,1)}, u32[]{:S(2)}) copy-start(bf16[8,2048]{1,0:T(8,128)(2,1)} %refs_0_.1) | copy-start | bytes 98308
  7.6 4.9 %collective-permute-start.1 = (bf16[2,8,2048]{2,1,0:T(8,128)(2,1)S(1)}, bf16[2,8,2048]{2,1,0:T(8,128)(2,1)S(1)}, u32[]{:S(2)}, u32[]{:S(2)}) collective-permute-start(bf16[2,8,2048]{2,1,0:T(8,128)(2,1)S(1)} %stack_pieces.5.refs_0_), channel_id=1, source_target_pairs={{0,1},{1,0},{2,3},{3,2},{4,5},{5,4},{6,7},{7,6},{8,9},{9,8},{10,11... | collective-permute-start | bytes 196616 | tf_op jit(solution)/shard_map/ppermute | solution.py:384
  9.2 1.4 %copy-start = (bf16[192,4096]{1,0:T(8,128)(2,1)S(1)}, bf16[192,4096]{1,0:T(8,128)(2,1)}, u32[]{:S(2)}) copy-start(bf16[192,4096]{1,0:T(8,128)(2,1)} %param.8) | copy-start | bytes 4718596
  11.3 1.2 %copy-start.1 = (bf16[128,512]{1,0:T(8,128)(2,1)S(1)}, bf16[128,512]{1,0:T(8,128)(2,1)}, u32[]{:S(2)}) copy-start(bf16[128,512]{1,0:T(8,128)(2,1)} %constant.4.clone.spread_ref) | copy-start | bytes 393220
  11.3 1.2 %copy-start.4 = (s32[192]{0:T(256)S(1)}, s32[192]{0:T(256)}, u32[]{:S(2)}) copy-start(s32[192]{0:T(256)} %rows_ref.3) | copy-start | bytes 2308
  11.4 1.2 %copy-start.5 = (s32[192]{0:T(256)S(1)}, s32[192]{0:T(256)}, u32[]{:S(2)}) copy-start(s32[192]{0:T(256)} %cols_ref.3) | copy-start | bytes 2308
  11.4 3.5 %copy-start.2 = (bf16[512,128]{1,0:T(8,128)(2,1)S(1)}, bf16[512,128]{1,0:T(8,128)(2,1)}, u32[]{:S(2)}) copy-start(bf16[512,128]{1,0:T(8,128)(2,1)} %constant.5.clone.fold_ref) | copy-start | bytes 393220
  11.4 3.5 %collective-permute-start.10 = (bf16[4,8,2048]{2,1,0:T(8,128)(2,1)S(1)}, bf16[4,8,2048]{2,1,0:T(8,128)(2,1)S(1)}, u32[]{:S(2)}, u32[]{:S(2)}) collective-permute-start(bf16[4,8,2048]{2,1,0:T(8,128)(2,1)S(1)} %stack_pieces.7.after_ref.same_ref), channel_id=1, source_target_pairs={{0,4},{4,0},{8,12},{12,8},{16,20},{20,16},{24,28},{28,24},{1,5},{5... | collective-permute-start | bytes 393224 | tf_op jit(solution)/shard_map/ppermute | solution.py:384
  14.4 4.4 %collective-permute-start.6 = (f32[2,8,2048]{2,1,0:T(8,128)S(1)}, f32[2,8,2048]{2,1,0:T(8,128)S(1)}, u32[]{:S(2)}, u32[]{:S(2)}) collective-permute-start(f32[2,8,2048]{2,1,0:T(8,128)S(1)} %get-tuple-element.17), channel_id=1, source_target_pairs={{0,4},{4,0},{8,12},{12,8},{16,20},{20,16},{24,28},{28,24},{1,5},{5... | collective-permute-start | bytes 393224 | tf_op jit(solution)/shard_map/ppermute | solution.py:384
  14.6 4.2 %collective-permute-start.5 = (f32[2,8,2048]{2,1,0:T(8,128)S(1)}, f32[2,8,2048]{2,1,0:T(8,128)S(1)}, u32[]{:S(2)}, u32[]{:S(2)}) collective-permute-start(f32[2,8,2048]{2,1,0:T(8,128)S(1)} %get-tuple-element.16.after_ref), channel_id=1, source_target_pairs={{0,4},{4,0},{8,12},{12,8},{16,20},{20,16},{24,28},{28,24},{1,5},{5... | collective-permute-start | bytes 393224 | tf_op jit(solution)/shard_map/ppermute | solution.py:384
  17.4 4.4 %collective-permute-start.11 = (s16[2,8,2176]{2,1,0:T(8,128)(2,1)S(1)}, s16[2,8,2176]{2,1,0:T(8,128)(2,1)S(1)}, u32[]{:S(2)}, u32[]{:S(2)}) collective-permute-start(s16[2,8,2176]{2,1,0:T(8,128)(2,1)S(1)} %get-tuple-element.22), channel_id=1, source_target_pairs={{0,1},{1,0},{2,3},{3,2},{4,5},{5,4},{6,7},{7,6},{8,9},{9,8},{10,11... | collective-permute-start | bytes 208904 | tf_op jit(solution)/shard_map/ppermute | solution.py:384
  18.8 8.3 %collective-permute-start.8 = (f32[8,2048]{1,0:T(8,128)S(1)}, f32[8,2048]{1,0:T(8,128)S(1)}, u32[]{:S(2)}, u32[]{:S(2)}) collective-permute-start(f32[8,2048]{1,0:T(8,128)S(1)} %get-tuple-element.19), channel_id=1, source_target_pairs={{0,20},{4,16},{8,28},{12,24},{16,4},{20,0},{24,12},{28,8},{1,21},{... | collective-permute-start | bytes 196616 | tf_op jit(solution)/shard_map/ppermute | solution.py:384
  19.8 7.3 %collective-permute-start.9 = (f32[8,2048]{1,0:T(8,128)S(1)}, f32[8,2048]{1,0:T(8,128)S(1)}, u32[]{:S(2)}, u32[]{:S(2)}) collective-permute-start(f32[8,2048]{1,0:T(8,128)S(1)} %get-tuple-element.20), channel_id=1, source_target_pairs={{0,28},{4,24},{8,20},{12,16},{16,12},{20,8},{24,4},{28,0},{1,29},{... | collective-permute-start | bytes 196616 | tf_op jit(solution)/shard_map/ppermute | solution.py:384
  21.7 5.5 %collective-permute-start.7 = (f32[8,2048]{1,0:T(8,128)S(1)}, f32[8,2048]{1,0:T(8,128)S(1)}, u32[]{:S(2)}, u32[]{:S(2)}) collective-permute-start(f32[8,2048]{1,0:T(8,128)S(1)} %get-tuple-element.18.after_ref), channel_id=1, source_target_pairs={{0,12},{4,8},{8,4},{12,0},{16,28},{20,24},{24,20},{28,16},{1,13},{... | collective-permute-start | bytes 196616 | tf_op jit(solution)/shard_map/ppermute | solution.py:384
  22.0 5.1 %collective-permute-start.12 = (s16[1,8,2176]{2,1,0:T(8,128)(2,1)S(1)}, s16[1,8,2176]{2,1,0:T(8,128)(2,1)S(1)}, u32[]{:S(2)}, u32[]{:S(2)}) collective-permute-start(s16[1,8,2176]{2,1,0:T(8,128)(2,1)S(1)} %get-tuple-element.24), channel_id=1, source_target_pairs={{0,2},{1,3},{2,0},{3,1},{4,6},{5,7},{6,4},{7,5},{8,10},{9,11},{10,... | collective-permute-start | bytes 104456 | tf_op jit(solution)/shard_map/ppermute | solution.py:384

commit v20 on v16

--- a/solution.py
+++ b/solution.py
@@ -82,6 +82,14 @@
         cost_estimate=pl.CostEstimate(flops=0, bytes_accessed=4 * tiles.size, transcendentals=0),
         name="prep_tiles",
     )(view)
+
+
+def doubled(size):
+    order, d = [0], size // 2
+    while d > 0:
+        order += [x ^ d for x in order]
+        d //= 2
+    return order
 
 
 def build_table(pieces, spread, table):
@@ -102,7 +110,7 @@
 def backward_kernel(
     rows_ref, cols_ref, count_ref, tiles_ref, seg_ref, after_ref, keep_ref, *refs
 ):
-    pieces = [seg_ref.at[n] for n in range(seg_ref.shape[0])]
+    pieces = [seg_ref.at[at] for at in np.argsort(doubled(seg_ref.shape[0]))]
     *give_refs, table, acc_a, acc_b = refs
     per_give = give_refs[0].shape[0]
     n_out = 2 * keep_ref.shape[0]
@@ -134,7 +142,8 @@
 
     for n in range(n_out):
         h = n // 2
-        dest = keep_ref.at[h] if n % 2 == 0 else give_refs[h // per_give].at[h % per_give]
+        kept = (n % 2 == 0) == (h == 0)
+        dest = keep_ref.at[h] if kept else give_refs[h // per_give].at[h % per_give]
         for p in range(per_piece // 2):
             at = n * per_piece + 2 * p
             a = acc_a[at] + acc_b[at]
@@ -195,7 +204,10 @@
     acc_a,
     acc_b,
 ):
-    pieces = [ref.at[h] for h in range(same_ref.shape[0]) for ref in (same_ref, other_ref)]
+    pieces = []
+    for h in range(same_ref.shape[0]):
+        pair = [same_ref.at[h], other_ref.at[h]]
+        pieces += pair if h == 0 else pair[::-1]
     n_out = 2 * keep_ref.shape[0]
     width, piece = pieces[0].shape
     per_piece = piece // TILE
@@ -422,11 +434,12 @@
     n_rows = lax.axis_size("brow")
     n_cols = lax.axis_size("bcol")
     own, wide = take(vectors)
-    chips = [swap(wide, "brow", n_rows, 2 * h) for h in range(1, n_rows // 2)]
-    segment, d = own, 1
-    while d < n_cols:
-        segment = stack(segment, swap(segment if d > 1 else vectors[None], "bcol", n_cols, d))
-        d *= 2
+    chips = [swap(wide, "brow", n_rows, 2 * h + 1) for h in range(1, n_rows // 2)]
+    segment, d = own, n_cols // 2
+    while d > 0:
+        first = d == n_cols // 2
+        segment = stack(segment, swap(vectors[None] if first else segment, "bcol", n_cols, d))
+        d //= 2
     blocks = prep(tiles)
     same = stack(own, *chips, after=(blocks,))
     other = swap(same, "brow", n_rows, 1)
@@ -435,7 +448,7 @@
     row_keep, near, rest = forward(same, other, blocks, tile_rows, tile_cols, counts, n_cols, col_give[0])
     col_got = [swap(x, "brow", n_rows, 1) for x in col_give]
     sums = pair_sum(col_keep, col_got)
-    from_chips = [swap(x, "brow", n_rows, 2 * (h + 1)) for h, x in enumerate(sums)]
+    from_chips = [swap(x, "brow", n_rows, 2 * h + 3) for h, x in enumerate(sums)]
     d, later = 1, []
     while 2 * d < n_cols:
         row_got = swap(rest, "bcol", n_cols, d)

time: 29.6 us -> 29.1 us (0.983)
  starting transfers between devices: 17.7 us -> 15.8 us
  waiting for transfers between devices: 2.33 us -> 3.83 us
    ppermute x14, starting transfers between devices: 17.7 us -> 15.8 us  [swap(): return lax.ppermute(x, axis, [(i, i ^ d) for i in range(size)])]
    ppermute x14, waiting for transfers between devices: 2.33 us -> 3.83 us  [swap(): return lax.ppermute(x, axis, [(i, i ^ d) for i in range(size)])]
  transfers between devices with their start and end apart: 14 -> 14, of which waited for: 2 -> 3; matrix products, arithmetic and copies ran while one was open for 0% -> 0% of each run, Pallas kernels for 19% -> 19%
where the time goes in v20:
time: 29.1 us; the launch traced here: 28.8 us
  starting transfers between devices  15.8 us (54%)
  Pallas kernels  6.16 us (21%)
  waiting for transfers between devices  3.83 us (13%)
  local copies, waits for them, and re-layouts  2.22 us (8%)
  between operations  0.79 us (3%)
    ppermute x14, starting transfers between devices, swap(): return lax.ppermute(x, axis, [(i, i ^ d) for i in range(size)])  15.8 us
    ppermute x14, waiting for transfers between devices, swap(): return lax.ppermute(x, axis, [(i, i ^ d) for i in range(size)])  3.83 us
    pallas_call x1, Pallas kernels, forward(): pl.pallas_call(forward_kernel, in_specs=[SMEM] * 3 + [VMEM] * 4 + [ANY],...  2.47 us
    unnamed x10, local copies, waits for them, and re-layouts  2.22 us
    pallas_call x1, Pallas kernels, backward(): pl.pallas_call(backward_kernel, in_specs=[SMEM] * 3 + [VMEM] * 2 + [ANY],...  1.89 us
    pallas_call x1, Pallas kernels, last_sum(): pl.pallas_call(last_sum_kernel, in_specs=[VMEM] * (1 + len(gots)), out_sp...  0.73 us
    pallas_call x1, Pallas kernels, prep(): pl.pallas_call(prep_kernel, in_specs=[VMEM], out_specs=VMEM, out_shape=ja...  0.69 us
  transfers between devices with their start and end apart: 14, of which 3 were waited for; matrix products, arithmetic and copies ran while one was open for 0% of the time, Pallas kernels for 19%

profile of v20, /device:TPU:0, one launch (start us, length us, event | category | flops | bytes accessed | tf_op | source)
XLA Modules:
  0.0 28.8 jit_solution(13893288667810028483)
XLA Ops:
  0.0 4.0 %collective-permute-start.4 = (bf16[1,8,2048]{2,1,0:T(8,128)(2,1)}, bf16[1,8,2048]{2,1,0:T(8,128)(2,1)S(1)}, u32[]{:S(2)}, u32[]{:S(2)}) collective-permute-start(bf16[1,8,2048]{2,1,0:T(8,128)(2,1)} %bitcast.5), channel_id=1, source_target_pairs={{0,2},{1,3},{2,0},{3,1},{4,6},{5,7},{6,4},{7,5},{8,10},{9,11},{10,... | collective-permute-start | bytes 98312 | tf_op jit(solution)/shard_map/ppermute | solution.py:430
  4.0 0.8 %copy-done.2 = bf16[8,2048]{1,0:T(8,128)(2,1)S(1)} copy-done((bf16[8,2048]{1,0:T(8,128)(2,1)S(1)}, bf16[8,2048]{1,0:T(8,128)(2,1)}, u32[]{:S(2)}) %copy-start.2) | copy-done | bytes 32792
  4.8 1.7 %collective-permute-start.2 = (f32[8,2048]{1,0:T(8,128)S(1)}, f32[8,2048]{1,0:T(8,128)S(1)}, u32[]{:S(2)}, u32[]{:S(2)}) collective-permute-start(f32[8,2048]{1,0:T(8,128)S(1)} %get-tuple-element.19), channel_id=1, source_target_pairs={{0,28},{4,24},{8,20},{12,16},{16,12},{20,8},{24,4},{28,0},{1,29},{... | collective-permute-start | bytes 196616 | tf_op jit(solution)/shard_map/ppermute | solution.py:430
  6.5 1.1 %collective-permute-start.1 = (f32[8,2048]{1,0:T(8,128)S(1)}, f32[8,2048]{1,0:T(8,128)S(1)}, u32[]{:S(2)}, u32[]{:S(2)}) collective-permute-start(f32[8,2048]{1,0:T(8,128)S(1)} %get-tuple-element.19), channel_id=1, source_target_pairs={{0,20},{4,16},{8,28},{12,24},{16,4},{20,0},{24,12},{28,8},{1,21},{... | collective-permute-start | bytes 196616 | tf_op jit(solution)/shard_map/ppermute | solution.py:430
  7.6 0.1 collective-permute-start
  7.7 0.0 collective-permute-done.4.refs_1_
  7.7 1.6 %collective-permute-start.5 = (bf16[2,8,2048]{2,1,0:T(8,128)(2,1)S(1)}, bf16[2,8,2048]{2,1,0:T(8,128)(2,1)S(1)}, u32[]{:S(2)}, u32[]{:S(2)}) collective-permute-start(bf16[2,8,2048]{2,1,0:T(8,128)(2,1)S(1)} %stack_pieces.4.refs_0_), channel_id=1, source_target_pairs={{0,1},{1,0},{2,3},{3,2},{4,5},{5,4},{6,7},{7,6},{8,9},{9,8},{10,11... | collective-permute-start | bytes 196616 | tf_op jit(solution)/shard_map/ppermute | solution.py:430
  9.4 1.4 %copy-done = bf16[192,4096]{1,0:T(8,128)(2,1)S(1)} copy-done((bf16[192,4096]{1,0:T(8,128)(2,1)S(1)}, bf16[192,4096]{1,0:T(8,128)(2,1)}, u32[]{:S(2)}) %copy-start) | copy-done | bytes 1572888
  10.8 0.7 %prep_tiles.1.refs_4_.tiles_ref = bf16[192,32,128]{2,1,0:T(8,128)(2,1)S(1)} custom-call(bf16[24,32,8,128]{3,2,1,0:T(8,128)(2,1)S(1)} %bitcast.4), custom_call_target="tpu_custom_call" | custom-call | bytes 3145728 | tf_op jit(solution)/shard_map/prep_tiles/pallas_call | solution.py:75
  11.5 0.0 copy-start.3
  11.5 0.0 copy-start.4
  11.5 0.0 copy-start.1
  11.5 0.0 collective-permute-done.2.refs_3_
  11.5 0.4 %collective-permute-done.refs_1_ = f32[8,2048]{1,0:T(8,128)S(1)} collective-permute-done((f32[8,2048]{1,0:T(8,128)S(1)}, f32[8,2048]{1,0:T(8,128)S(1)}, u32[]{:S(2)}, u32[]{:S(2)}) %collective-permute-start) | collective-permute-done | bytes 65568 | tf_op jit(solution)/shard_map/ppermute | solution.py:430
  11.9 0.3 collective-permute-start.3
  12.8 0.0 collective-permute-done.5.refs_1_
  12.9 1.9 %transpose_product.1 = (f32[4,8,2048]{2,1,0:T(8,128)S(1)}, f32[2,8,2048]{2,1,0:T(8,128)S(1)}, f32[2,8,2048]{2,1,0:T(8,128)S(1)}) custom-call(s32[192]{0:T(256)S(1)} %copy-done.3, s32[192]{0:T(256)S(1)} %copy-done.4, s32[1,1]{1,0:T(1,128)S(6)} %copy.7.count_ref, bf16[192,32,128]{2,1,0:T(8,128)(2,1)S(1)} %prep_tiles.1.refs_4_.tiles_ref, ...), custom_call_target="tpu_custom_call" | custom-call | flops 100663296 | bytes 3145728 | tf_op jit(solution)/shard_map/transpose_product/pallas_call | solution.py:161
  14.8 0.4 %collective-permute-start.8 = (f32[2,8,2048]{2,1,0:T(8,128)S(1)}, f32[2,8,2048]{2,1,0:T(8,128)S(1)}, u32[]{:S(2)}, u32[]{:S(2)}) collective-permute-start(f32[2,8,2048]{2,1,0:T(8,128)S(1)} %get-tuple-element.24), channel_id=1, source_target_pairs={{0,4},{4,0},{8,12},{12,8},{16,20},{20,16},{24,28},{28,24},{1,5},{5... | collective-permute-start | bytes 393224 | tf_op jit(solution)/shard_map/ppermute | solution.py:430
  15.2 0.2 collective-permute-start.7
  15.3 0.0 collective-permute-done.3.other_ref
  15.3 2.5 %forward_product.1 = (f32[2,8,2048]{2,1,0:T(8,128)S(1)}, s16[1,8,2176]{2,1,0:T(8,128)(2,1)S(1)}, s16[1,8,2176]{2,1,0:T(8,128)(2,1)S(1)}) custom-call(s32[192]{0:T(256)S(1)} %copy-done.3, s32[192]{0:T(256)S(1)} %copy-done.4, s32[1,1]{1,0:T(1,128)S(6)} %copy.7.count_ref, bf16[512,128]{1,0:T(8,128)(2,1)S(1)} %copy-done.1, ...), custom_call_target="tpu_custom_call" | custom-call | flops 100663296 | bytes 3145728 | tf_op jit(solution)/shard_map/forward_product/pallas_call | solution.py:274
  17.8 1.7 %collective-permute-start.6 = (s16[1,8,2176]{2,1,0:T(8,128)(2,1)S(1)}, s16[1,8,2176]{2,1,0:T(8,128)(2,1)S(1)}, u32[]{:S(2)}, u32[]{:S(2)}) collective-permute-start(s16[1,8,2176]{2,1,0:T(8,128)(2,1)S(1)} %get-tuple-element.22), channel_id=1, source_target_pairs={{0,1},{1,0},{2,3},{3,2},{4,5},{5,4},{6,7},{7,6},{8,9},{9,8},{10,11... | collective-permute-start | bytes 104456 | tf_op jit(solution)/shard_map/ppermute | solution.py:430
  19.5 1.1 %collective-permute-start.11 = (f32[8,2048]{1,0:T(8,128)S(1)}, f32[8,2048]{1,0:T(8,128)S(1)}, u32[]{:S(2)}, u32[]{:S(2)}) collective-permute-start(f32[8,2048]{1,0:T(8,128)S(1)} %get-tuple-element.28), channel_id=1, source_target_pairs={{0,20},{4,16},{8,28},{12,24},{16,4},{20,0},{24,12},{28,8},{1,21},{... | collective-permute-start | bytes 196616 | tf_op jit(solution)/shard_map/ppermute | solution.py:430
  20.6 1.1 %collective-permute-start.12 = (f32[8,2048]{1,0:T(8,128)S(1)}, f32[8,2048]{1,0:T(8,128)S(1)}, u32[]{:S(2)}, u32[]{:S(2)}) collective-permute-start(f32[8,2048]{1,0:T(8,128)S(1)} %get-tuple-element.29), channel_id=1, source_target_pairs={{0,28},{4,24},{8,20},{12,16},{16,12},{20,8},{24,4},{28,0},{1,29},{... | collective-permute-start | bytes 196616 | tf_op jit(solution)/shard_map/ppermute | solution.py:430
  21.7 0.7 %collective-permute-start.10 = (f32[8,2048]{1,0:T(8,128)S(1)}, f32[8,2048]{1,0:T(8,128)S(1)}, u32[]{:S(2)}, u32[]{:S(2)}) collective-permute-start(f32[8,2048]{1,0:T(8,128)S(1)} %get-tuple-element.25.after_ref), channel_id=1, source_target_pairs={{0,12},{4,8},{8,4},{12,0},{16,28},{20,24},{24,20},{28,16},{1,13},{... | collective-permute-start | bytes 196616 | tf_op jit(solution)/shard_map/ppermute | solution.py:430
  22.4 0.2 halving_sum.1
  22.6 0.9 %collective-permute-start.9 = (s16[1,8,2176]{2,1,0:T(8,128)(2,1)S(1)}, s16[1,8,2176]{2,1,0:T(8,128)(2,1)S(1)}, u32[]{:S(2)}, u32[]{:S(2)}) collective-permute-start(s16[1,8,2176]{2,1,0:T(8,128)(2,1)S(1)} %get-tuple-element.27), channel_id=1, source_target_pairs={{0,2},{1,3},{2,0},{3,1},{4,6},{5,7},{6,4},{7,5},{8,10},{9,11},{10,... | collective-permute-start | bytes 104456 | tf_op jit(solution)/shard_map/ppermute | solution.py:430
  23.5 1.0 %collective-permute-start.13 = (s16[1,8,2176]{2,1,0:T(8,128)(2,1)S(1)}, s16[1,8,2176]{2,1,0:T(8,128)(2,1)S(1)}, u32[]{:S(2)}, u32[]{:S(2)}) collective-permute-start(s16[1,8,2176]{2,1,0:T(8,128)(2,1)S(1)} %get-tuple-element.30), channel_id=1, source_target_pairs={{0,1},{1,0},{2,3},{3,2},{4,5},{5,4},{6,7},{7,6},{8,9},{9,8},{10,11... | collective-permute-start | bytes 104456 | tf_op jit(solution)/shard_map/ppermute | solution.py:430
  24.5 3.3 %collective-permute-done.9.got_ref = s16[1,8,2176]{2,1,0:T(8,128)(2,1)S(1)} collective-permute-done((s16[1,8,2176]{2,1,0:T(8,128)(2,1)S(1)}, s16[1,8,2176]{2,1,0:T(8,128)(2,1)S(1)}, u32[]{:S(2)}, u32[]{:S(2)}) %collective-permute-start.9) | collective-permute-done | bytes 34848 | tf_op jit(solution)/shard_map/ppermute | solution.py:430
  27.8 0.1 part_sum.1.total_ref
  27.9 0.2 collective-permute-done.13.refs_0_
  28.1 0.7 %last_sum.1 = f32[8,2048]{1,0:T(8,128)} custom-call(f32[8,2048]{1,0:T(8,128)S(1)} %part_sum.1.total_ref, s16[1,8,2176]{2,1,0:T(8,128)(2,1)S(1)} %collective-permute-done.13.refs_0_), custom_call_target="tpu_custom_call" | custom-call | tf_op jit(solution)/shard_map/last_sum/pallas_call | solution.py:400
  (17 shorter events, 0.1 us)
Async XLA Ops:
  0.0 7.7 %collective-permute-start.4 = (bf16[1,8,2048]{2,1,0:T(8,128)(2,1)}, bf16[1,8,2048]{2,1,0:T(8,128)(2,1)S(1)}, u32[]{:S(2)}, u32[]{:S(2)}) collective-permute-start(bf16[1,8,2048]{2,1,0:T(8,128)(2,1)} %bitcast.5), channel_id=1, source_target_pairs={{0,2},{1,3},{2,0},{3,1},{4,6},{5,7},{6,4},{7,5},{8,10},{9,11},{10,... | collective-permute-start | bytes 98312 | tf_op jit(solution)/shard_map/ppermute | solution.py:430
  4.0 0.8 %copy-start.2 = (bf16[8,2048]{1,0:T(8,128)(2,1)S(1)}, bf16[8,2048]{1,0:T(8,128)(2,1)}, u32[]{:S(2)}) copy-start(bf16[8,2048]{1,0:T(8,128)(2,1)} %x_ref.1) | copy-start | bytes 98308
  4.8 6.7 %collective-permute-start.2 = (f32[8,2048]{1,0:T(8,128)S(1)}, f32[8,2048]{1,0:T(8,128)S(1)}, u32[]{:S(2)}, u32[]{:S(2)}) collective-permute-start(f32[8,2048]{1,0:T(8,128)S(1)} %get-tuple-element.19), channel_id=1, source_target_pairs={{0,28},{4,24},{8,20},{12,16},{16,12},{20,8},{24,4},{28,0},{1,29},{... | collective-permute-start | bytes 196616 | tf_op jit(solution)/shard_map/ppermute | solution.py:430
  6.5 5.0 %collective-permute-start.1 = (f32[8,2048]{1,0:T(8,128)S(1)}, f32[8,2048]{1,0:T(8,128)S(1)}, u32[]{:S(2)}, u32[]{:S(2)}) collective-permute-start(f32[8,2048]{1,0:T(8,128)S(1)} %get-tuple-element.19), channel_id=1, source_target_pairs={{0,20},{4,16},{8,28},{12,24},{16,4},{20,0},{24,12},{28,8},{1,21},{... | collective-permute-start | bytes 196616 | tf_op jit(solution)/shard_map/ppermute | solution.py:430
  7.6 4.3 %collective-permute-start = (f32[8,2048]{1,0:T(8,128)S(1)}, f32[8,2048]{1,0:T(8,128)S(1)}, u32[]{:S(2)}, u32[]{:S(2)}) collective-permute-start(f32[8,2048]{1,0:T(8,128)S(1)} %get-tuple-element.19), channel_id=1, source_target_pairs={{0,12},{4,8},{8,4},{12,0},{16,28},{20,24},{24,20},{28,16},{1,13},{... | collective-permute-start | bytes 196616 | tf_op jit(solution)/shard_map/ppermute | solution.py:430
  7.7 5.1 %collective-permute-start.5 = (bf16[2,8,2048]{2,1,0:T(8,128)(2,1)S(1)}, bf16[2,8,2048]{2,1,0:T(8,128)(2,1)S(1)}, u32[]{:S(2)}, u32[]{:S(2)}) collective-permute-start(bf16[2,8,2048]{2,1,0:T(8,128)(2,1)S(1)} %stack_pieces.4.refs_0_), channel_id=1, source_target_pairs={{0,1},{1,0},{2,3},{3,2},{4,5},{5,4},{6,7},{7,6},{8,9},{9,8},{10,11... | collective-permute-start | bytes 196616 | tf_op jit(solution)/shard_map/ppermute | solution.py:430
  9.4 1.4 %copy-start = (bf16[192,4096]{1,0:T(8,128)(2,1)S(1)}, bf16[192,4096]{1,0:T(8,128)(2,1)}, u32[]{:S(2)}) copy-start(bf16[192,4096]{1,0:T(8,128)(2,1)} %param.7) | copy-start | bytes 4718596
  11.5 1.4 %copy-start.3 = (s32[192]{0:T(256)S(1)}, s32[192]{0:T(256)}, u32[]{:S(2)}) copy-start(s32[192]{0:T(256)} %rows_ref.3) | copy-start | bytes 2308
  11.5 1.4 %copy-start.4 = (s32[192]{0:T(256)S(1)}, s32[192]{0:T(256)}, u32[]{:S(2)}) copy-start(s32[192]{0:T(256)} %cols_ref.3) | copy-start | bytes 2308
  11.5 3.9 %copy-start.1 = (bf16[512,128]{1,0:T(8,128)(2,1)S(1)}, bf16[512,128]{1,0:T(8,128)(2,1)}, u32[]{:S(2)}) copy-start(bf16[512,128]{1,0:T(8,128)(2,1)} %constant.2.clone.fold_ref) | copy-start | bytes 393220
  11.9 3.4 %collective-permute-start.3 = (bf16[4,8,2048]{2,1,0:T(8,128)(2,1)S(1)}, bf16[4,8,2048]{2,1,0:T(8,128)(2,1)S(1)}, u32[]{:S(2)}, u32[]{:S(2)}) collective-permute-start(bf16[4,8,2048]{2,1,0:T(8,128)(2,1)S(1)} %stack_pieces.3.after_ref.same_ref), channel_id=1, source_target_pairs={{0,4},{4,0},{8,12},{12,8},{16,20},{20,16},{24,28},{28,24},{1,5},{5... | collective-permute-start | bytes 393224 | tf_op jit(solution)/shard_map/ppermute | solution.py:430
  14.8 4.7 %collective-permute-start.8 = (f32[2,8,2048]{2,1,0:T(8,128)S(1)}, f32[2,8,2048]{2,1,0:T(8,128)S(1)}, u32[]{:S(2)}, u32[]{:S(2)}) collective-permute-start(f32[2,8,2048]{2,1,0:T(8,128)S(1)} %get-tuple-element.24), channel_id=1, source_target_pairs={{0,4},{4,0},{8,12},{12,8},{16,20},{20,16},{24,28},{28,24},{1,5},{5... | collective-permute-start | bytes 393224 | tf_op jit(solution)/shard_map/ppermute | solution.py:430
  15.2 4.3 %collective-permute-start.7 = (f32[2,8,2048]{2,1,0:T(8,128)S(1)}, f32[2,8,2048]{2,1,0:T(8,128)S(1)}, u32[]{:S(2)}, u32[]{:S(2)}) collective-permute-start(f32[2,8,2048]{2,1,0:T(8,128)S(1)} %get-tuple-element.20.after_ref), channel_id=1, source_target_pairs={{0,4},{4,0},{8,12},{12,8},{16,20},{20,16},{24,28},{28,24},{1,5},{5... | collective-permute-start | bytes 393224 | tf_op jit(solution)/shard_map/ppermute | solution.py:430
  17.8 4.5 %collective-permute-start.6 = (s16[1,8,2176]{2,1,0:T(8,128)(2,1)S(1)}, s16[1,8,2176]{2,1,0:T(8,128)(2,1)S(1)}, u32[]{:S(2)}, u32[]{:S(2)}) collective-permute-start(s16[1,8,2176]{2,1,0:T(8,128)(2,1)S(1)} %get-tuple-element.22), channel_id=1, source_target_pairs={{0,1},{1,0},{2,3},{3,2},{4,5},{5,4},{6,7},{7,6},{8,9},{9,8},{10,11... | collective-permute-start | bytes 104456 | tf_op jit(solution)/shard_map/ppermute | solution.py:430
  19.5 8.2 %collective-permute-start.11 = (f32[8,2048]{1,0:T(8,128)S(1)}, f32[8,2048]{1,0:T(8,128)S(1)}, u32[]{:S(2)}, u32[]{:S(2)}) collective-permute-start(f32[8,2048]{1,0:T(8,128)S(1)} %get-tuple-element.28), channel_id=1, source_target_pairs={{0,20},{4,16},{8,28},{12,24},{16,4},{20,0},{24,12},{28,8},{1,21},{... | collective-permute-start | bytes 196616 | tf_op jit(solution)/shard_map/ppermute | solution.py:430
  20.6 7.2 %collective-permute-start.12 = (f32[8,2048]{1,0:T(8,128)S(1)}, f32[8,2048]{1,0:T(8,128)S(1)}, u32[]{:S(2)}, u32[]{:S(2)}) collective-permute-start(f32[8,2048]{1,0:T(8,128)S(1)} %get-tuple-element.29), channel_id=1, source_target_pairs={{0,28},{4,24},{8,20},{12,16},{16,12},{20,8},{24,4},{28,0},{1,29},{... | collective-permute-start | bytes 196616 | tf_op jit(solution)/shard_map/ppermute | solution.py:430
  21.7 6.1 %collective-permute-start.10 = (f32[8,2048]{1,0:T(8,128)S(1)}, f32[8,2048]{1,0:T(8,128)S(1)}, u32[]{:S(2)}, u32[]{:S(2)}) collective-permute-start(f32[8,2048]{1,0:T(8,128)S(1)} %get-tuple-element.25.after_ref), channel_id=1, source_target_pairs={{0,12},{4,8},{8,4},{12,0},{16,28},{20,24},{24,20},{28,16},{1,13},{... | collective-permute-start | bytes 196616 | tf_op jit(solution)/shard_map/ppermute | solution.py:430
  22.6 5.2 %collective-permute-start.9 = (s16[1,8,2176]{2,1,0:T(8,128)(2,1)S(1)}, s16[1,8,2176]{2,1,0:T(8,128)(2,1)S(1)}, u32[]{:S(2)}, u32[]{:S(2)}) collective-permute-start(s16[1,8,2176]{2,1,0:T(8,128)(2,1)S(1)} %get-tuple-element.27), channel_id=1, source_target_pairs={{0,2},{1,3},{2,0},{3,1},{4,6},{5,7},{6,4},{7,5},{8,10},{9,11},{10,... | collective-permute-start | bytes 104456 | tf_op jit(solution)/shard_map/ppermute | solution.py:430
  23.5 4.6 %collective-permute-start.13 = (s16[1,8,2176]{2,1,0:T(8,128)(2,1)S(1)}, s16[1,8,2176]{2,1,0:T(8,128)(2,1)S(1)}, u32[]{:S(2)}, u32[]{:S(2)}) collective-permute-start(s16[1,8,2176]{2,1,0:T(8,128)(2,1)S(1)} %get-tuple-element.30), channel_id=1, source_target_pairs={{0,1},{1,0},{2,3},{3,2},{4,5},{5,4},{6,7},{7,6},{8,9},{9,8},{10,11... | collective-permute-start | bytes 104456 | tf_op jit(solution)/shard_map/ppermute | solution.py:430

commit v21 on v19

--- a/solution.py
+++ b/solution.py
@@ -43,12 +43,13 @@
 def encode(values, out_ref):
     width, piece = values[0].shape[0], LANES * len(values)
     lane = lax.broadcasted_iota(jnp.int32, (width, LANES), 1)
-    exponents = jnp.zeros((width, LANES), F32)
+    tops = jnp.zeros((width, LANES), F32)
     for n, value in enumerate(values):
-        top = jnp.max(jnp.abs(value), axis=1, keepdims=True)
-        e = jnp.clip(jnp.ceil(jnp.log2(top)), -100.0, 100.0)
-        exponents = jnp.where(lane == n, e, exponents)
-        scaled = jnp.floor(value * (STEPS * jnp.exp2(-e)) + 0.5)
+        tops = jnp.where(lane == n, jnp.max(jnp.abs(value), axis=1, keepdims=True), tops)
+    exponents = jnp.clip(jnp.ceil(jnp.log2(tops)), -100.0, 100.0)
+    scales = STEPS * jnp.exp2(-exponents)
+    for n, value in enumerate(values):
+        scaled = jnp.floor(value * scales[:, n : n + 1] + 0.5)
         out_ref[:, n * LANES : (n + 1) * LANES] = scaled.astype(jnp.int32).astype(jnp.int16)
     out_ref[:, piece:] = exponents.astype(jnp.int32).astype(jnp.int16)
 

time: 28.1 us -> 28.3 us (level)
  no operation moved by 1% of the time
where the time goes in v21:
time: 28.3 us; the launch traced here: 28.1 us
  starting transfers between devices  15.4 us (54%)
  Pallas kernels  6.16 us (22%)
  waiting for transfers between devices  3.52 us (12%)
  local copies, waits for them, and re-layouts  2.23 us (8%)
  between operations  0.8 us (3%)
    ppermute x13, starting transfers between devices, swap(): return lax.ppermute(x, axis, [(i, i ^ d) for i in range(size)])  15.4 us
    ppermute x13, waiting for transfers between devices, swap(): return lax.ppermute(x, axis, [(i, i ^ d) for i in range(size)])  3.52 us
    pallas_call x1, Pallas kernels, forward(): pl.pallas_call(forward_kernel, in_specs=[SMEM] * 3 + [VMEM] * 4 + [ANY],...  2.55 us
    unnamed x12, local copies, waits for them, and re-layouts  2.23 us
    pallas_call x1, Pallas kernels, backward(): pl.pallas_call(backward_kernel, in_specs=[SMEM] * 3 + [VMEM] * 3 + [ANY],...  1.8 us
    pallas_call x1, Pallas kernels, last_sum(): pl.pallas_call(last_sum_kernel, in_specs=[VMEM] * (4 + len(chips)), out_s...  0.74 us
    pallas_call x1, Pallas kernels, prep(): pl.pallas_call(prep_kernel, in_specs=[VMEM], out_specs=VMEM, out_shape=ja...  0.69 us
  transfers between devices with their start and end apart: 13, of which 2 were waited for; matrix products, arithmetic and copies ran while one was open for 0% of the time, Pallas kernels for 19%

profile of v21, /device:TPU:0, one launch (start us, length us, event | category | flops | bytes accessed | tf_op | source)
XLA Modules:
  0.0 28.1 jit_solution(2380270622619121975)
XLA Ops:
  0.0 4.0 %collective-permute-start = (bf16[1,8,2048]{2,1,0:T(8,128)(2,1)}, bf16[1,8,2048]{2,1,0:T(8,128)(2,1)S(1)}, u32[]{:S(2)}, u32[]{:S(2)}) collective-permute-start(bf16[1,8,2048]{2,1,0:T(8,128)(2,1)} %bitcast.5), channel_id=1, source_target_pairs={{0,2},{1,3},{2,0},{3,1},{4,6},{5,7},{6,4},{7,5},{8,10},{9,11},{10,... | collective-permute-start | bytes 98312 | tf_op jit(solution)/shard_map/ppermute | solution.py:385
  4.0 0.7 %collective-permute-start.2 = (bf16[8,2048]{1,0:T(8,128)(2,1)}, bf16[8,2048]{1,0:T(8,128)(2,1)S(1)}, u32[]{:S(2)}, u32[]{:S(2)}) collective-permute-start(bf16[8,2048]{1,0:T(8,128)(2,1)} %refs_0_.1), channel_id=1, source_target_pairs={{0,12},{4,8},{8,4},{12,0},{16,28},{20,24},{24,20},{28,16},{1,13},{... | collective-permute-start | bytes 98312 | tf_op jit(solution)/shard_map/ppermute | solution.py:385
  4.7 2.1 %collective-permute-start.4 = (bf16[8,2048]{1,0:T(8,128)(2,1)}, bf16[8,2048]{1,0:T(8,128)(2,1)S(1)}, u32[]{:S(2)}, u32[]{:S(2)}) collective-permute-start(bf16[8,2048]{1,0:T(8,128)(2,1)} %refs_0_.1), channel_id=1, source_target_pairs={{0,28},{4,24},{8,20},{12,16},{16,12},{20,8},{24,4},{28,0},{1,29},{... | collective-permute-start | bytes 98312 | tf_op jit(solution)/shard_map/ppermute | solution.py:385
  6.7 0.0 collective-permute-start.3
  6.8 0.8 %copy-done.3 = bf16[8,2048]{1,0:T(8,128)(2,1)S(1)} copy-done((bf16[8,2048]{1,0:T(8,128)(2,1)S(1)}, bf16[8,2048]{1,0:T(8,128)(2,1)}, u32[]{:S(2)}) %copy-start.3) | copy-done | bytes 32792
  7.6 0.0 collective-permute-done.refs_1_
  7.6 1.6 %collective-permute-start.1 = (bf16[2,8,2048]{2,1,0:T(8,128)(2,1)S(1)}, bf16[2,8,2048]{2,1,0:T(8,128)(2,1)S(1)}, u32[]{:S(2)}, u32[]{:S(2)}) collective-permute-start(bf16[2,8,2048]{2,1,0:T(8,128)(2,1)S(1)} %stack_pieces.5.refs_0_), channel_id=1, source_target_pairs={{0,1},{1,0},{2,3},{3,2},{4,5},{5,4},{6,7},{7,6},{8,9},{9,8},{10,11... | collective-permute-start | bytes 196616 | tf_op jit(solution)/shard_map/ppermute | solution.py:385
  9.2 1.4 %copy-done = bf16[192,4096]{1,0:T(8,128)(2,1)S(1)} copy-done((bf16[192,4096]{1,0:T(8,128)(2,1)S(1)}, bf16[192,4096]{1,0:T(8,128)(2,1)}, u32[]{:S(2)}) %copy-start) | copy-done | bytes 1572888
  10.6 0.7 %prep_tiles.1.refs_4_.tiles_ref = bf16[192,32,128]{2,1,0:T(8,128)(2,1)S(1)} custom-call(bf16[24,32,8,128]{3,2,1,0:T(8,128)(2,1)S(1)} %bitcast.4), custom_call_target="tpu_custom_call" | custom-call | bytes 3145728 | tf_op jit(solution)/shard_map/prep_tiles/pallas_call | solution.py:78
  11.3 0.0 copy-start.1
  11.3 0.0 copy-start.4
  11.4 0.0 copy-start.5
  11.4 0.0 collective-permute-done.2.refs_1_
  11.4 0.0 collective-permute-done.3.refs_2_
  11.4 0.0 copy-start.2
  11.4 0.4 %collective-permute-start.10 = (bf16[4,8,2048]{2,1,0:T(8,128)(2,1)S(1)}, bf16[4,8,2048]{2,1,0:T(8,128)(2,1)S(1)}, u32[]{:S(2)}, u32[]{:S(2)}) collective-permute-start(bf16[4,8,2048]{2,1,0:T(8,128)(2,1)S(1)} %stack_pieces.7.after_ref.same_ref), channel_id=1, source_target_pairs={{0,4},{4,0},{8,12},{12,8},{16,20},{20,16},{24,28},{28,24},{1,5},{5... | collective-permute-start | bytes 393224 | tf_op jit(solution)/shard_map/ppermute | solution.py:385
  12.5 0.0 collective-permute-done.1.refs_1_
  12.5 1.8 %transpose_product.1 = (f32[4,8,2048]{2,1,0:T(8,128)S(1)}, f32[2,8,2048]{2,1,0:T(8,128)S(1)}, f32[2,8,2048]{2,1,0:T(8,128)S(1)}) custom-call(s32[192]{0:T(256)S(1)} %copy-done.4, s32[192]{0:T(256)S(1)} %copy-done.5, s32[1,1]{1,0:T(1,128)S(6)} %copy.8.count_ref, bf16[128,512]{1,0:T(8,128)(2,1)S(1)} %copy-done.1, ...), custom_call_target="tpu_custom_call" | custom-call | flops 100663296 | bytes 3145728 | tf_op jit(solution)/shard_map/transpose_product/pallas_call | solution.py:164
  14.3 0.4 %collective-permute-start.6 = (f32[2,8,2048]{2,1,0:T(8,128)S(1)}, f32[2,8,2048]{2,1,0:T(8,128)S(1)}, u32[]{:S(2)}, u32[]{:S(2)}) collective-permute-start(f32[2,8,2048]{2,1,0:T(8,128)S(1)} %get-tuple-element.17), channel_id=1, source_target_pairs={{0,4},{4,0},{8,12},{12,8},{16,20},{20,16},{24,28},{28,24},{1,5},{5... | collective-permute-start | bytes 393224 | tf_op jit(solution)/shard_map/ppermute | solution.py:385
  14.7 0.2 collective-permute-start.5
  14.9 0.0 collective-permute-done.10.other_ref
  14.9 2.6 %forward_product.1 = (f32[2,8,2048]{2,1,0:T(8,128)S(1)}, s16[2,8,2176]{2,1,0:T(8,128)(2,1)S(1)}) custom-call(s32[192]{0:T(256)S(1)} %copy-done.4, s32[192]{0:T(256)S(1)} %copy-done.5, s32[1,1]{1,0:T(1,128)S(6)} %copy.8.count_ref, bf16[512,128]{1,0:T(8,128)(2,1)S(1)} %copy-done.2, bf16[192,32,128]{2,1,0:T(8,128)(2,1)S(1)} %prep_tiles.1.refs_4_.tiles_ref, ...), custom_call_target="tpu_custom_call" | custom-call | flops 100663296 | bytes 3145728 | tf_op jit(solution)/shard_map/forward_product/pallas_call | solution.py:275
  17.5 1.4 %collective-permute-start.11 = (s16[2,8,2176]{2,1,0:T(8,128)(2,1)S(1)}, s16[2,8,2176]{2,1,0:T(8,128)(2,1)S(1)}, u32[]{:S(2)}, u32[]{:S(2)}) collective-permute-start(s16[2,8,2176]{2,1,0:T(8,128)(2,1)S(1)} %get-tuple-element.22), channel_id=1, source_target_pairs={{0,1},{1,0},{2,3},{3,2},{4,5},{5,4},{6,7},{7,6},{8,9},{9,8},{10,11... | collective-permute-start | bytes 208904 | tf_op jit(solution)/shard_map/ppermute | solution.py:385
  18.9 1.1 %collective-permute-start.8 = (f32[8,2048]{1,0:T(8,128)S(1)}, f32[8,2048]{1,0:T(8,128)S(1)}, u32[]{:S(2)}, u32[]{:S(2)}) collective-permute-start(f32[8,2048]{1,0:T(8,128)S(1)} %get-tuple-element.19), channel_id=1, source_target_pairs={{0,20},{4,16},{8,28},{12,24},{16,4},{20,0},{24,12},{28,8},{1,21},{... | collective-permute-start | bytes 196616 | tf_op jit(solution)/shard_map/ppermute | solution.py:385
  20.0 1.7 %collective-permute-start.9 = (f32[8,2048]{1,0:T(8,128)S(1)}, f32[8,2048]{1,0:T(8,128)S(1)}, u32[]{:S(2)}, u32[]{:S(2)}) collective-permute-start(f32[8,2048]{1,0:T(8,128)S(1)} %get-tuple-element.20), channel_id=1, source_target_pairs={{0,28},{4,24},{8,20},{12,16},{16,12},{20,8},{24,4},{28,0},{1,29},{... | collective-permute-start | bytes 196616 | tf_op jit(solution)/shard_map/ppermute | solution.py:385
  21.7 0.1 collective-permute-start.7
  21.9 0.1 collective-permute-done.11.got_ref
  22.0 0.3 %halving_sum.1 = (f32[1,8,2048]{2,1,0:T(8,128)S(1)}, s16[1,8,2176]{2,1,0:T(8,128)(2,1)S(1)}) custom-call(f32[2,8,2048]{2,1,0:T(8,128)S(1)} %get-tuple-element.21.keep_ref, s16[2,8,2176]{2,1,0:T(8,128)(2,1)S(1)} %collective-permute-done.11.got_ref, f32[8,2048]{1,0:T(8,128)S(1)} %get-tuple-element.18.after_ref), custom_call_target="tpu_custom_call" | custom-call | tf_op jit(solution)/shard_map/halving_sum/pallas_call | solution.py:350
  22.3 1.7 %collective-permute-start.12 = (s16[1,8,2176]{2,1,0:T(8,128)(2,1)S(1)}, s16[1,8,2176]{2,1,0:T(8,128)(2,1)S(1)}, u32[]{:S(2)}, u32[]{:S(2)}) collective-permute-start(s16[1,8,2176]{2,1,0:T(8,128)(2,1)S(1)} %get-tuple-element.24), channel_id=1, source_target_pairs={{0,2},{1,3},{2,0},{3,1},{4,6},{5,7},{6,4},{7,5},{8,10},{9,11},{10,... | collective-permute-start | bytes 104456 | tf_op jit(solution)/shard_map/ppermute | solution.py:385
  23.9 3.4 %collective-permute-done.12.refs_6_ = s16[1,8,2176]{2,1,0:T(8,128)(2,1)S(1)} collective-permute-done((s16[1,8,2176]{2,1,0:T(8,128)(2,1)S(1)}, s16[1,8,2176]{2,1,0:T(8,128)(2,1)S(1)}, u32[]{:S(2)}, u32[]{:S(2)}) %collective-permute-start.12) | collective-permute-done | bytes 34848 | tf_op jit(solution)/shard_map/ppermute | solution.py:385
  27.3 0.0 collective-permute-done.8.refs_1_
  27.4 0.7 %last_sum.1 = f32[8,2048]{1,0:T(8,128)} custom-call(f32[8,2048]{1,0:T(8,128)S(1)} %collective-permute-done.7.refs_0_, f32[8,2048]{1,0:T(8,128)S(1)} %collective-permute-done.8.refs_1_, f32[8,2048]{1,0:T(8,128)S(1)} %collective-permute-done.9.refs_2_, f32[4,8,2048]{2,1,0:T(8,128)S(1)} %get-tuple-element.15.keep_ref.refs_3_, ...), custom_call_target="tpu_custom_call" | custom-call | tf_op jit(solution)/shard_map/last_sum/pallas_call | solution.py:374
  (16 shorter events, 0.1 us)
Async XLA Ops:
  0.0 7.6 %collective-permute-start = (bf16[1,8,2048]{2,1,0:T(8,128)(2,1)}, bf16[1,8,2048]{2,1,0:T(8,128)(2,1)S(1)}, u32[]{:S(2)}, u32[]{:S(2)}) collective-permute-start(bf16[1,8,2048]{2,1,0:T(8,128)(2,1)} %bitcast.5), channel_id=1, source_target_pairs={{0,2},{1,3},{2,0},{3,1},{4,6},{5,7},{6,4},{7,5},{8,10},{9,11},{10,... | collective-permute-start | bytes 98312 | tf_op jit(solution)/shard_map/ppermute | solution.py:385
  4.0 7.3 %collective-permute-start.2 = (bf16[8,2048]{1,0:T(8,128)(2,1)}, bf16[8,2048]{1,0:T(8,128)(2,1)S(1)}, u32[]{:S(2)}, u32[]{:S(2)}) collective-permute-start(bf16[8,2048]{1,0:T(8,128)(2,1)} %refs_0_.1), channel_id=1, source_target_pairs={{0,12},{4,8},{8,4},{12,0},{16,28},{20,24},{24,20},{28,16},{1,13},{... | collective-permute-start | bytes 98312 | tf_op jit(solution)/shard_map/ppermute | solution.py:385
  4.7 6.7 %collective-permute-start.4 = (bf16[8,2048]{1,0:T(8,128)(2,1)}, bf16[8,2048]{1,0:T(8,128)(2,1)S(1)}, u32[]{:S(2)}, u32[]{:S(2)}) collective-permute-start(bf16[8,2048]{1,0:T(8,128)(2,1)} %refs_0_.1), channel_id=1, source_target_pairs={{0,28},{4,24},{8,20},{12,16},{16,12},{20,8},{24,4},{28,0},{1,29},{... | collective-permute-start | bytes 98312 | tf_op jit(solution)/shard_map/ppermute | solution.py:385
  6.7 4.7 %collective-permute-start.3 = (bf16[8,2048]{1,0:T(8,128)(2,1)}, bf16[8,2048]{1,0:T(8,128)(2,1)S(1)}, u32[]{:S(2)}, u32[]{:S(2)}) collective-permute-start(bf16[8,2048]{1,0:T(8,128)(2,1)} %refs_0_.1), channel_id=1, source_target_pairs={{0,20},{4,16},{8,28},{12,24},{16,4},{20,0},{24,12},{28,8},{1,21},{... | collective-permute-start | bytes 98312 | tf_op jit(solution)/shard_map/ppermute | solution.py:385
  6.8 0.8 %copy-start.3 = (bf16[8,2048]{1,0:T(8,128)(2,1)S(1)}, bf16[8,2048]{1,0:T(8,128)(2,1)}, u32[]{:S(2)}) copy-start(bf16[8,2048]{1,0:T(8,128)(2,1)} %refs_0_.1) | copy-start | bytes 98308
  7.6 4.9 %collective-permute-start.1 = (bf16[2,8,2048]{2,1,0:T(8,128)(2,1)S(1)}, bf16[2,8,2048]{2,1,0:T(8,128)(2,1)S(1)}, u32[]{:S(2)}, u32[]{:S(2)}) collective-permute-start(bf16[2,8,2048]{2,1,0:T(8,128)(2,1)S(1)} %stack_pieces.5.refs_0_), channel_id=1, source_target_pairs={{0,1},{1,0},{2,3},{3,2},{4,5},{5,4},{6,7},{7,6},{8,9},{9,8},{10,11... | collective-permute-start | bytes 196616 | tf_op jit(solution)/shard_map/ppermute | solution.py:385
  9.2 1.4 %copy-start = (bf16[192,4096]{1,0:T(8,128)(2,1)S(1)}, bf16[192,4096]{1,0:T(8,128)(2,1)}, u32[]{:S(2)}) copy-start(bf16[192,4096]{1,0:T(8,128)(2,1)} %param.8) | copy-start | bytes 4718596
  11.3 1.2 %copy-start.1 = (bf16[128,512]{1,0:T(8,128)(2,1)S(1)}, bf16[128,512]{1,0:T(8,128)(2,1)}, u32[]{:S(2)}) copy-start(bf16[128,512]{1,0:T(8,128)(2,1)} %constant.4.clone.spread_ref) | copy-start | bytes 393220
  11.3 1.2 %copy-start.4 = (s32[192]{0:T(256)S(1)}, s32[192]{0:T(256)}, u32[]{:S(2)}) copy-start(s32[192]{0:T(256)} %rows_ref.3) | copy-start | bytes 2308
  11.4 1.2 %copy-start.5 = (s32[192]{0:T(256)S(1)}, s32[192]{0:T(256)}, u32[]{:S(2)}) copy-start(s32[192]{0:T(256)} %cols_ref.3) | copy-start | bytes 2308
  11.4 3.5 %copy-start.2 = (bf16[512,128]{1,0:T(8,128)(2,1)S(1)}, bf16[512,128]{1,0:T(8,128)(2,1)}, u32[]{:S(2)}) copy-start(bf16[512,128]{1,0:T(8,128)(2,1)} %constant.5.clone.fold_ref) | copy-start | bytes 393220
  11.4 3.5 %collective-permute-start.10 = (bf16[4,8,2048]{2,1,0:T(8,128)(2,1)S(1)}, bf16[4,8,2048]{2,1,0:T(8,128)(2,1)S(1)}, u32[]{:S(2)}, u32[]{:S(2)}) collective-permute-start(bf16[4,8,2048]{2,1,0:T(8,128)(2,1)S(1)} %stack_pieces.7.after_ref.same_ref), channel_id=1, source_target_pairs={{0,4},{4,0},{8,12},{12,8},{16,20},{20,16},{24,28},{28,24},{1,5},{5... | collective-permute-start | bytes 393224 | tf_op jit(solution)/shard_map/ppermute | solution.py:385
  14.3 4.6 %collective-permute-start.6 = (f32[2,8,2048]{2,1,0:T(8,128)S(1)}, f32[2,8,2048]{2,1,0:T(8,128)S(1)}, u32[]{:S(2)}, u32[]{:S(2)}) collective-permute-start(f32[2,8,2048]{2,1,0:T(8,128)S(1)} %get-tuple-element.17), channel_id=1, source_target_pairs={{0,4},{4,0},{8,12},{12,8},{16,20},{20,16},{24,28},{28,24},{1,5},{5... | collective-permute-start | bytes 393224 | tf_op jit(solution)/shard_map/ppermute | solution.py:385
  14.7 4.2 %collective-permute-start.5 = (f32[2,8,2048]{2,1,0:T(8,128)S(1)}, f32[2,8,2048]{2,1,0:T(8,128)S(1)}, u32[]{:S(2)}, u32[]{:S(2)}) collective-permute-start(f32[2,8,2048]{2,1,0:T(8,128)S(1)} %get-tuple-element.16.after_ref), channel_id=1, source_target_pairs={{0,4},{4,0},{8,12},{12,8},{16,20},{20,16},{24,28},{28,24},{1,5},{5... | collective-permute-start | bytes 393224 | tf_op jit(solution)/shard_map/ppermute | solution.py:385
  17.5 4.5 %collective-permute-start.11 = (s16[2,8,2176]{2,1,0:T(8,128)(2,1)S(1)}, s16[2,8,2176]{2,1,0:T(8,128)(2,1)S(1)}, u32[]{:S(2)}, u32[]{:S(2)}) collective-permute-start(s16[2,8,2176]{2,1,0:T(8,128)(2,1)S(1)} %get-tuple-element.22), channel_id=1, source_target_pairs={{0,1},{1,0},{2,3},{3,2},{4,5},{5,4},{6,7},{7,6},{8,9},{9,8},{10,11... | collective-permute-start | bytes 208904 | tf_op jit(solution)/shard_map/ppermute | solution.py:385
  18.9 8.4 %collective-permute-start.8 = (f32[8,2048]{1,0:T(8,128)S(1)}, f32[8,2048]{1,0:T(8,128)S(1)}, u32[]{:S(2)}, u32[]{:S(2)}) collective-permute-start(f32[8,2048]{1,0:T(8,128)S(1)} %get-tuple-element.19), channel_id=1, source_target_pairs={{0,20},{4,16},{8,28},{12,24},{16,4},{20,0},{24,12},{28,8},{1,21},{... | collective-permute-start | bytes 196616 | tf_op jit(solution)/shard_map/ppermute | solution.py:385
  20.0 7.3 %collective-permute-start.9 = (f32[8,2048]{1,0:T(8,128)S(1)}, f32[8,2048]{1,0:T(8,128)S(1)}, u32[]{:S(2)}, u32[]{:S(2)}) collective-permute-start(f32[8,2048]{1,0:T(8,128)S(1)} %get-tuple-element.20), channel_id=1, source_target_pairs={{0,28},{4,24},{8,20},{12,16},{16,12},{20,8},{24,4},{28,0},{1,29},{... | collective-permute-start | bytes 196616 | tf_op jit(solution)/shard_map/ppermute | solution.py:385
  21.7 5.6 %collective-permute-start.7 = (f32[8,2048]{1,0:T(8,128)S(1)}, f32[8,2048]{1,0:T(8,128)S(1)}, u32[]{:S(2)}, u32[]{:S(2)}) collective-permute-start(f32[8,2048]{1,0:T(8,128)S(1)} %get-tuple-element.18.after_ref), channel_id=1, source_target_pairs={{0,12},{4,8},{8,4},{12,0},{16,28},{20,24},{24,20},{28,16},{1,13},{... | collective-permute-start | bytes 196616 | tf_op jit(solution)/shard_map/ppermute | solution.py:385
  22.3 5.1 %collective-permute-start.12 = (s16[1,8,2176]{2,1,0:T(8,128)(2,1)S(1)}, s16[1,8,2176]{2,1,0:T(8,128)(2,1)S(1)}, u32[]{:S(2)}, u32[]{:S(2)}) collective-permute-start(s16[1,8,2176]{2,1,0:T(8,128)(2,1)S(1)} %get-tuple-element.24), channel_id=1, source_target_pairs={{0,2},{1,3},{2,0},{3,1},{4,6},{5,7},{6,4},{7,5},{8,10},{9,11},{10,... | collective-permute-start | bytes 104456 | tf_op jit(solution)/shard_map/ppermute | solution.py:385

commit v22 on v19

--- a/solution.py
+++ b/solution.py
@@ -22,12 +22,10 @@
 
 
 def row_spread():
-    out = np.zeros((LANES, 2, 2, GROUP, HALF), np.float32)
-    for q in range(2):
-        for e in range(2):
-            for m in range(HALF):
-                out[q * TILE + 2 * m + e, q, e, :, m] = 1
-    return jnp.asarray(out.reshape(LANES, 4 * LANES), BF16)
+    source = lax.broadcasted_iota(jnp.int32, (LANES, LANES), 0)
+    m = lax.broadcasted_iota(jnp.int32, (LANES, LANES), 1) % HALF
+    blocks = [source == q * TILE + 2 * m + e for q in range(2) for e in range(2)]
+    return jnp.concatenate([block.astype(F32) for block in blocks], axis=1).astype(BF16)
 
 
 def row_fold():
@@ -110,7 +108,7 @@
 
 
 def backward_kernel(
-    rows_ref, cols_ref, count_ref, spread_ref, tiles_ref, seg_ref, after_ref, keep_ref, *refs
+    rows_ref, cols_ref, count_ref, tiles_ref, seg_ref, after_ref, keep_ref, *refs
 ):
     pieces = [seg_ref.at[at] for at in np.argsort(doubled(seg_ref.shape[0]))]
     *give_refs, table, acc_a, acc_b = refs
@@ -119,7 +117,7 @@
     width, piece = pieces[0].shape
     per_piece = piece // TILE
     slots = tiles_ref.shape[0]
-    build_table(pieces, spread_ref[...], table)
+    build_table(pieces, row_spread(), table)
     for acc in (acc_a, acc_b):
         acc[...] = jnp.zeros_like(acc)
     lane = lax.broadcasted_iota(jnp.int32, (2 * width, LANES), 1)
@@ -162,7 +160,7 @@
     quarter = jax.ShapeDtypeStruct((n_out // 4, width, piece), F32)
     return pl.pallas_call(
         backward_kernel,
-        in_specs=[SMEM] * 3 + [VMEM] * 3 + [ANY],
+        in_specs=[SMEM] * 3 + [VMEM] * 2 + [ANY],
         out_specs=[VMEM] * 3,
         out_shape=[half, quarter, quarter],
         scratch_shapes=[
@@ -175,7 +173,7 @@
             flops=2 * tiles.size * 64, bytes_accessed=4 * tiles.size, transcendentals=0
         ),
         name="transpose_product",
-    )(tile_rows, tile_cols, counts, row_spread(), tiles, segment, after)
+    )(tile_rows, tile_cols, counts, tiles, segment, after)
 
 
 def double_table(pieces, table):

time: 28.1 us -> 28.2 us (level)
    unnamed x12 -> x10, local copies, waits for them, and re-layouts: 2.23 us -> 2.22 us
  transfers between devices with their start and end apart: 13 -> 13, of which waited for: 2 -> 1; matrix products, arithmetic and copies ran while one was open for 0% -> 0% of each run, Pallas kernels for 19% -> 19%
where the time goes in v22:
time: 28.2 us; the launch traced here: 28 us
  starting transfers between devices  15.4 us (55%)
  Pallas kernels  6.02 us (21%)
  waiting for transfers between devices  3.56 us (13%)
  local copies, waits for them, and re-layouts  2.22 us (8%)
  between operations  0.79 us (3%)
    ppermute x13, starting transfers between devices, swap(): return lax.ppermute(x, axis, [(i, i ^ d) for i in range(size)])  15.4 us
    ppermute x13, waiting for transfers between devices, swap(): return lax.ppermute(x, axis, [(i, i ^ d) for i in range(size)])  3.56 us
    pallas_call x1, Pallas kernels, forward(): pl.pallas_call(forward_kernel, in_specs=[SMEM] * 3 + [VMEM] * 4 + [ANY],...  2.47 us
    unnamed x10, local copies, waits for them, and re-layouts  2.22 us
    pallas_call x1, Pallas kernels, backward(): pl.pallas_call(backward_kernel, in_specs=[SMEM] * 3 + [VMEM] * 2 + [ANY],...  1.86 us
    pallas_call x1, Pallas kernels, last_sum(): pl.pallas_call(last_sum_kernel, in_specs=[VMEM] * (4 + len(chips)), out_s...  0.74 us
    pallas_call x1, Pallas kernels, prep(): pl.pallas_call(prep_kernel, in_specs=[VMEM], out_specs=VMEM, out_shape=ja...  0.69 us
  transfers between devices with their start and end apart: 13, of which 1 were waited for; matrix products, arithmetic and copies ran while one was open for 0% of the time, Pallas kernels for 19%

profile of v22, /device:TPU:0, one launch (start us, length us, event | category | flops | bytes accessed | tf_op | source)
XLA Modules:
  0.0 28.0 jit_solution(8315593605779845508)
XLA Ops:
  0.0 4.0 %collective-permute-start = (bf16[1,8,2048]{2,1,0:T(8,128)(2,1)}, bf16[1,8,2048]{2,1,0:T(8,128)(2,1)S(1)}, u32[]{:S(2)}, u32[]{:S(2)}) collective-permute-start(bf16[1,8,2048]{2,1,0:T(8,128)(2,1)} %bitcast.5), channel_id=1, source_target_pairs={{0,2},{1,3},{2,0},{3,1},{4,6},{5,7},{6,4},{7,5},{8,10},{9,11},{10,... | collective-permute-start | bytes 98312 | tf_op jit(solution)/shard_map/ppermute | solution.py:382
  4.0 0.7 %collective-permute-start.2 = (bf16[8,2048]{1,0:T(8,128)(2,1)}, bf16[8,2048]{1,0:T(8,128)(2,1)S(1)}, u32[]{:S(2)}, u32[]{:S(2)}) collective-permute-start(bf16[8,2048]{1,0:T(8,128)(2,1)} %refs_0_.1), channel_id=1, source_target_pairs={{0,12},{4,8},{8,4},{12,0},{16,28},{20,24},{24,20},{28,16},{1,13},{... | collective-permute-start | bytes 98312 | tf_op jit(solution)/shard_map/ppermute | solution.py:382
  4.7 2.1 %collective-permute-start.4 = (bf16[8,2048]{1,0:T(8,128)(2,1)}, bf16[8,2048]{1,0:T(8,128)(2,1)S(1)}, u32[]{:S(2)}, u32[]{:S(2)}) collective-permute-start(bf16[8,2048]{1,0:T(8,128)(2,1)} %refs_0_.1), channel_id=1, source_target_pairs={{0,28},{4,24},{8,20},{12,16},{16,12},{20,8},{24,4},{28,0},{1,29},{... | collective-permute-start | bytes 98312 | tf_op jit(solution)/shard_map/ppermute | solution.py:382
  6.7 0.0 collective-permute-start.3
  6.8 0.8 %copy-done.2 = bf16[8,2048]{1,0:T(8,128)(2,1)S(1)} copy-done((bf16[8,2048]{1,0:T(8,128)(2,1)S(1)}, bf16[8,2048]{1,0:T(8,128)(2,1)}, u32[]{:S(2)}) %copy-start.2) | copy-done | bytes 32792
  7.6 1.6 %collective-permute-start.1 = (bf16[2,8,2048]{2,1,0:T(8,128)(2,1)S(1)}, bf16[2,8,2048]{2,1,0:T(8,128)(2,1)S(1)}, u32[]{:S(2)}, u32[]{:S(2)}) collective-permute-start(bf16[2,8,2048]{2,1,0:T(8,128)(2,1)S(1)} %stack_pieces.5.refs_0_), channel_id=1, source_target_pairs={{0,1},{1,0},{2,3},{3,2},{4,5},{5,4},{6,7},{7,6},{8,9},{9,8},{10,11... | collective-permute-start | bytes 196616 | tf_op jit(solution)/shard_map/ppermute | solution.py:382
  9.2 1.4 %copy-done = bf16[192,4096]{1,0:T(8,128)(2,1)S(1)} copy-done((bf16[192,4096]{1,0:T(8,128)(2,1)S(1)}, bf16[192,4096]{1,0:T(8,128)(2,1)}, u32[]{:S(2)}) %copy-start) | copy-done | bytes 1572888
  10.6 0.7 %prep_tiles.1.refs_4_.tiles_ref = bf16[192,32,128]{2,1,0:T(8,128)(2,1)S(1)} custom-call(bf16[24,32,8,128]{3,2,1,0:T(8,128)(2,1)S(1)} %bitcast.4), custom_call_target="tpu_custom_call" | custom-call | bytes 3145728 | tf_op jit(solution)/shard_map/prep_tiles/pallas_call | solution.py:75
  11.3 0.0 copy-start.3
  11.3 0.0 copy-start.4
  11.4 0.0 copy-start.1
  11.4 0.0 collective-permute-done.2.refs_1_
  11.4 0.0 collective-permute-done.4.refs_3_
  11.4 0.4 %collective-permute-start.10 = (bf16[4,8,2048]{2,1,0:T(8,128)(2,1)S(1)}, bf16[4,8,2048]{2,1,0:T(8,128)(2,1)S(1)}, u32[]{:S(2)}, u32[]{:S(2)}) collective-permute-start(bf16[4,8,2048]{2,1,0:T(8,128)(2,1)S(1)} %stack_pieces.7.after_ref.same_ref), channel_id=1, source_target_pairs={{0,4},{4,0},{8,12},{12,8},{16,20},{20,16},{24,28},{28,24},{1,5},{5... | collective-permute-start | bytes 393224 | tf_op jit(solution)/shard_map/ppermute | solution.py:382
  12.4 0.0 collective-permute-done.1.refs_1_
  12.5 1.9 %transpose_product.1 = (f32[4,8,2048]{2,1,0:T(8,128)S(1)}, f32[2,8,2048]{2,1,0:T(8,128)S(1)}, f32[2,8,2048]{2,1,0:T(8,128)S(1)}) custom-call(s32[192]{0:T(256)S(1)} %copy-done.3, s32[192]{0:T(256)S(1)} %copy-done.4, s32[1,1]{1,0:T(1,128)S(6)} %copy.7.count_ref, bf16[192,32,128]{2,1,0:T(8,128)(2,1)S(1)} %prep_tiles.1.refs_4_.tiles_ref, ...), custom_call_target="tpu_custom_call" | custom-call | flops 100663296 | bytes 3145728 | tf_op jit(solution)/shard_map/transpose_product/pallas_call | solution.py:161
  14.4 0.3 %collective-permute-start.6 = (f32[2,8,2048]{2,1,0:T(8,128)S(1)}, f32[2,8,2048]{2,1,0:T(8,128)S(1)}, u32[]{:S(2)}, u32[]{:S(2)}) collective-permute-start(f32[2,8,2048]{2,1,0:T(8,128)S(1)} %get-tuple-element.17), channel_id=1, source_target_pairs={{0,4},{4,0},{8,12},{12,8},{16,20},{20,16},{24,28},{28,24},{1,5},{5... | collective-permute-start | bytes 393224 | tf_op jit(solution)/shard_map/ppermute | solution.py:382
  14.7 0.3 collective-permute-start.5
  14.9 0.0 collective-permute-done.10.other_ref
  14.9 2.5 %forward_product.1 = (f32[2,8,2048]{2,1,0:T(8,128)S(1)}, s16[2,8,2176]{2,1,0:T(8,128)(2,1)S(1)}) custom-call(s32[192]{0:T(256)S(1)} %copy-done.3, s32[192]{0:T(256)S(1)} %copy-done.4, s32[1,1]{1,0:T(1,128)S(6)} %copy.7.count_ref, bf16[512,128]{1,0:T(8,128)(2,1)S(1)} %copy-done.1, bf16[192,32,128]{2,1,0:T(8,128)(2,1)S(1)} %prep_tiles.1.refs_4_.tiles_ref, ...), custom_call_target="tpu_custom_call" | custom-call | flops 100663296 | bytes 3145728 | tf_op jit(solution)/shard_map/forward_product/pallas_call | solution.py:272
  17.4 1.6 %collective-permute-start.11 = (s16[2,8,2176]{2,1,0:T(8,128)(2,1)S(1)}, s16[2,8,2176]{2,1,0:T(8,128)(2,1)S(1)}, u32[]{:S(2)}, u32[]{:S(2)}) collective-permute-start(s16[2,8,2176]{2,1,0:T(8,128)(2,1)S(1)} %get-tuple-element.22), channel_id=1, source_target_pairs={{0,1},{1,0},{2,3},{3,2},{4,5},{5,4},{6,7},{7,6},{8,9},{9,8},{10,11... | collective-permute-start | bytes 208904 | tf_op jit(solution)/shard_map/ppermute | solution.py:382
  19.0 0.0 collective-permute-done.6.refs_1_
  19.0 0.0 collective-permute-done.5.refs_0_.refs_4_
  19.0 0.9 %collective-permute-start.8 = (f32[8,2048]{1,0:T(8,128)S(1)}, f32[8,2048]{1,0:T(8,128)S(1)}, u32[]{:S(2)}, u32[]{:S(2)}) collective-permute-start(f32[8,2048]{1,0:T(8,128)S(1)} %get-tuple-element.19), channel_id=1, source_target_pairs={{0,20},{4,16},{8,28},{12,24},{16,4},{20,0},{24,12},{28,8},{1,21},{... | collective-permute-start | bytes 196616 | tf_op jit(solution)/shard_map/ppermute | solution.py:382
  19.9 1.8 %collective-permute-start.9 = (f32[8,2048]{1,0:T(8,128)S(1)}, f32[8,2048]{1,0:T(8,128)S(1)}, u32[]{:S(2)}, u32[]{:S(2)}) collective-permute-start(f32[8,2048]{1,0:T(8,128)S(1)} %get-tuple-element.20), channel_id=1, source_target_pairs={{0,28},{4,24},{8,20},{12,16},{16,12},{20,8},{24,4},{28,0},{1,29},{... | collective-permute-start | bytes 196616 | tf_op jit(solution)/shard_map/ppermute | solution.py:382
  21.7 0.2 collective-permute-start.7
  21.9 0.0 collective-permute-done.11.got_ref
  21.9 0.2 halving_sum.1
  22.1 1.7 %collective-permute-start.12 = (s16[1,8,2176]{2,1,0:T(8,128)(2,1)S(1)}, s16[1,8,2176]{2,1,0:T(8,128)(2,1)S(1)}, u32[]{:S(2)}, u32[]{:S(2)}) collective-permute-start(s16[1,8,2176]{2,1,0:T(8,128)(2,1)S(1)} %get-tuple-element.24), channel_id=1, source_target_pairs={{0,2},{1,3},{2,0},{3,1},{4,6},{5,7},{6,4},{7,5},{8,10},{9,11},{10,... | collective-permute-start | bytes 104456 | tf_op jit(solution)/shard_map/ppermute | solution.py:382
  23.7 3.5 %collective-permute-done.12.refs_6_ = s16[1,8,2176]{2,1,0:T(8,128)(2,1)S(1)} collective-permute-done((s16[1,8,2176]{2,1,0:T(8,128)(2,1)S(1)}, s16[1,8,2176]{2,1,0:T(8,128)(2,1)S(1)}, u32[]{:S(2)}, u32[]{:S(2)}) %collective-permute-start.12) | collective-permute-done | bytes 34848 | tf_op jit(solution)/shard_map/ppermute | solution.py:382
  27.3 0.0 collective-permute-done.8.refs_1_
  27.3 0.7 %last_sum.1 = f32[8,2048]{1,0:T(8,128)} custom-call(f32[8,2048]{1,0:T(8,128)S(1)} %collective-permute-done.7.refs_0_, f32[8,2048]{1,0:T(8,128)S(1)} %collective-permute-done.8.refs_1_, f32[8,2048]{1,0:T(8,128)S(1)} %collective-permute-done.9.refs_2_, f32[4,8,2048]{2,1,0:T(8,128)S(1)} %get-tuple-element.15.keep_ref.refs_3_, ...), custom_call_target="tpu_custom_call" | custom-call | tf_op jit(solution)/shard_map/last_sum/pallas_call | solution.py:371
  (14 shorter events, 0.1 us)
Async XLA Ops:
  0.0 7.6 %collective-permute-start = (bf16[1,8,2048]{2,1,0:T(8,128)(2,1)}, bf16[1,8,2048]{2,1,0:T(8,128)(2,1)S(1)}, u32[]{:S(2)}, u32[]{:S(2)}) collective-permute-start(bf16[1,8,2048]{2,1,0:T(8,128)(2,1)} %bitcast.5), channel_id=1, source_target_pairs={{0,2},{1,3},{2,0},{3,1},{4,6},{5,7},{6,4},{7,5},{8,10},{9,11},{10,... | collective-permute-start | bytes 98312 | tf_op jit(solution)/shard_map/ppermute | solution.py:382
  4.0 7.3 %collective-permute-start.2 = (bf16[8,2048]{1,0:T(8,128)(2,1)}, bf16[8,2048]{1,0:T(8,128)(2,1)S(1)}, u32[]{:S(2)}, u32[]{:S(2)}) collective-permute-start(bf16[8,2048]{1,0:T(8,128)(2,1)} %refs_0_.1), channel_id=1, source_target_pairs={{0,12},{4,8},{8,4},{12,0},{16,28},{20,24},{24,20},{28,16},{1,13},{... | collective-permute-start | bytes 98312 | tf_op jit(solution)/shard_map/ppermute | solution.py:382
  4.7 6.7 %collective-permute-start.4 = (bf16[8,2048]{1,0:T(8,128)(2,1)}, bf16[8,2048]{1,0:T(8,128)(2,1)S(1)}, u32[]{:S(2)}, u32[]{:S(2)}) collective-permute-start(bf16[8,2048]{1,0:T(8,128)(2,1)} %refs_0_.1), channel_id=1, source_target_pairs={{0,28},{4,24},{8,20},{12,16},{16,12},{20,8},{24,4},{28,0},{1,29},{... | collective-permute-start | bytes 98312 | tf_op jit(solution)/shard_map/ppermute | solution.py:382
  6.7 4.7 %collective-permute-start.3 = (bf16[8,2048]{1,0:T(8,128)(2,1)}, bf16[8,2048]{1,0:T(8,128)(2,1)S(1)}, u32[]{:S(2)}, u32[]{:S(2)}) collective-permute-start(bf16[8,2048]{1,0:T(8,128)(2,1)} %refs_0_.1), channel_id=1, source_target_pairs={{0,20},{4,16},{8,28},{12,24},{16,4},{20,0},{24,12},{28,8},{1,21},{... | collective-permute-start | bytes 98312 | tf_op jit(solution)/shard_map/ppermute | solution.py:382
  6.8 0.8 %copy-start.2 = (bf16[8,2048]{1,0:T(8,128)(2,1)S(1)}, bf16[8,2048]{1,0:T(8,128)(2,1)}, u32[]{:S(2)}) copy-start(bf16[8,2048]{1,0:T(8,128)(2,1)} %refs_0_.1) | copy-start | bytes 98308
  7.6 4.9 %collective-permute-start.1 = (bf16[2,8,2048]{2,1,0:T(8,128)(2,1)S(1)}, bf16[2,8,2048]{2,1,0:T(8,128)(2,1)S(1)}, u32[]{:S(2)}, u32[]{:S(2)}) collective-permute-start(bf16[2,8,2048]{2,1,0:T(8,128)(2,1)S(1)} %stack_pieces.5.refs_0_), channel_id=1, source_target_pairs={{0,1},{1,0},{2,3},{3,2},{4,5},{5,4},{6,7},{7,6},{8,9},{9,8},{10,11... | collective-permute-start | bytes 196616 | tf_op jit(solution)/shard_map/ppermute | solution.py:382
  9.2 1.4 %copy-start = (bf16[192,4096]{1,0:T(8,128)(2,1)S(1)}, bf16[192,4096]{1,0:T(8,128)(2,1)}, u32[]{:S(2)}) copy-start(bf16[192,4096]{1,0:T(8,128)(2,1)} %param.7) | copy-start | bytes 4718596
  11.3 1.1 %copy-start.3 = (s32[192]{0:T(256)S(1)}, s32[192]{0:T(256)}, u32[]{:S(2)}) copy-start(s32[192]{0:T(256)} %rows_ref.3) | copy-start | bytes 2308
  11.3 1.1 %copy-start.4 = (s32[192]{0:T(256)S(1)}, s32[192]{0:T(256)}, u32[]{:S(2)}) copy-start(s32[192]{0:T(256)} %cols_ref.3) | copy-start | bytes 2308
  11.4 3.6 %copy-start.1 = (bf16[512,128]{1,0:T(8,128)(2,1)S(1)}, bf16[512,128]{1,0:T(8,128)(2,1)}, u32[]{:S(2)}) copy-start(bf16[512,128]{1,0:T(8,128)(2,1)} %constant.2.clone.fold_ref) | copy-start | bytes 393220
  11.4 3.5 %collective-permute-start.10 = (bf16[4,8,2048]{2,1,0:T(8,128)(2,1)S(1)}, bf16[4,8,2048]{2,1,0:T(8,128)(2,1)S(1)}, u32[]{:S(2)}, u32[]{:S(2)}) collective-permute-start(bf16[4,8,2048]{2,1,0:T(8,128)(2,1)S(1)} %stack_pieces.7.after_ref.same_ref), channel_id=1, source_target_pairs={{0,4},{4,0},{8,12},{12,8},{16,20},{20,16},{24,28},{28,24},{1,5},{5... | collective-permute-start | bytes 393224 | tf_op jit(solution)/shard_map/ppermute | solution.py:382
  14.4 4.6 %collective-permute-start.6 = (f32[2,8,2048]{2,1,0:T(8,128)S(1)}, f32[2,8,2048]{2,1,0:T(8,128)S(1)}, u32[]{:S(2)}, u32[]{:S(2)}) collective-permute-start(f32[2,8,2048]{2,1,0:T(8,128)S(1)} %get-tuple-element.17), channel_id=1, source_target_pairs={{0,4},{4,0},{8,12},{12,8},{16,20},{20,16},{24,28},{28,24},{1,5},{5... | collective-permute-start | bytes 393224 | tf_op jit(solution)/shard_map/ppermute | solution.py:382
  14.7 4.3 %collective-permute-start.5 = (f32[2,8,2048]{2,1,0:T(8,128)S(1)}, f32[2,8,2048]{2,1,0:T(8,128)S(1)}, u32[]{:S(2)}, u32[]{:S(2)}) collective-permute-start(f32[2,8,2048]{2,1,0:T(8,128)S(1)} %get-tuple-element.16.after_ref), channel_id=1, source_target_pairs={{0,4},{4,0},{8,12},{12,8},{16,20},{20,16},{24,28},{28,24},{1,5},{5... | collective-permute-start | bytes 393224 | tf_op jit(solution)/shard_map/ppermute | solution.py:382
  17.4 4.4 %collective-permute-start.11 = (s16[2,8,2176]{2,1,0:T(8,128)(2,1)S(1)}, s16[2,8,2176]{2,1,0:T(8,128)(2,1)S(1)}, u32[]{:S(2)}, u32[]{:S(2)}) collective-permute-start(s16[2,8,2176]{2,1,0:T(8,128)(2,1)S(1)} %get-tuple-element.22), channel_id=1, source_target_pairs={{0,1},{1,0},{2,3},{3,2},{4,5},{5,4},{6,7},{7,6},{8,9},{9,8},{10,11... | collective-permute-start | bytes 208904 | tf_op jit(solution)/shard_map/ppermute | solution.py:382
  19.0 8.3 %collective-permute-start.8 = (f32[8,2048]{1,0:T(8,128)S(1)}, f32[8,2048]{1,0:T(8,128)S(1)}, u32[]{:S(2)}, u32[]{:S(2)}) collective-permute-start(f32[8,2048]{1,0:T(8,128)S(1)} %get-tuple-element.19), channel_id=1, source_target_pairs={{0,20},{4,16},{8,28},{12,24},{16,4},{20,0},{24,12},{28,8},{1,21},{... | collective-permute-start | bytes 196616 | tf_op jit(solution)/shard_map/ppermute | solution.py:382
  19.9 7.4 %collective-permute-start.9 = (f32[8,2048]{1,0:T(8,128)S(1)}, f32[8,2048]{1,0:T(8,128)S(1)}, u32[]{:S(2)}, u32[]{:S(2)}) collective-permute-start(f32[8,2048]{1,0:T(8,128)S(1)} %get-tuple-element.20), channel_id=1, source_target_pairs={{0,28},{4,24},{8,20},{12,16},{16,12},{20,8},{24,4},{28,0},{1,29},{... | collective-permute-start | bytes 196616 | tf_op jit(solution)/shard_map/ppermute | solution.py:382
  21.7 5.6 %collective-permute-start.7 = (f32[8,2048]{1,0:T(8,128)S(1)}, f32[8,2048]{1,0:T(8,128)S(1)}, u32[]{:S(2)}, u32[]{:S(2)}) collective-permute-start(f32[8,2048]{1,0:T(8,128)S(1)} %get-tuple-element.18.after_ref), channel_id=1, source_target_pairs={{0,12},{4,8},{8,4},{12,0},{16,28},{20,24},{24,20},{28,16},{1,13},{... | collective-permute-start | bytes 196616 | tf_op jit(solution)/shard_map/ppermute | solution.py:382
  22.1 5.2 %collective-permute-start.12 = (s16[1,8,2176]{2,1,0:T(8,128)(2,1)S(1)}, s16[1,8,2176]{2,1,0:T(8,128)(2,1)S(1)}, u32[]{:S(2)}, u32[]{:S(2)}) collective-permute-start(s16[1,8,2176]{2,1,0:T(8,128)(2,1)S(1)} %get-tuple-element.24), channel_id=1, source_target_pairs={{0,2},{1,3},{2,0},{3,1},{4,6},{5,7},{6,4},{7,5},{8,10},{9,11},{10,... | collective-permute-start | bytes 104456 | tf_op jit(solution)/shard_map/ppermute | solution.py:382
